TPU v7x, 128 devices: a whole 4x4x4 slice. The times are simulated.
128 devices in a mesh: ctx: 32 (over x, z, core), head: 4 (over y).
Axes of the slice: x: 4, y: 4, z: 4, core: 2. Of those that a mesh axis runs over, the one named last changes fastest.
Arguments:
- x_in: bfloat16 [32768, 4096], P('ctx', 'head'), may hold values from -6 to 6
- b_in: bfloat16 [32768, 128], P('ctx'), may hold values from -1.796875 to 1.796875
- c_in: bfloat16 [32768, 128], P('ctx'), may hold values from -1.796875 to 1.796875
- d_out: bfloat16 [32768, 4096], P('ctx', 'head'), may hold values from -0.75 to 0.75
- table: float32 [16, 18], replicated, may hold values from 0 to 3, as said below
- level_index: int32 [32768], P('ctx'), may hold values from 0 to 15
Outputs:
- y_out: bfloat16 [32768, 4096], P('ctx', 'head')
- dx_out: bfloat16 [32768, 4096], P('ctx', 'head')
- d_b: float32 [32768, 128], P(('ctx', 'head'))
- d_c: float32 [32768, 128], P(('ctx', 'head'))
Inputs may be any that keep to these rules, and one draw needn't show every extreme that they name: `table`: entries are positive.
All inputs are finite; a program needn't handle non-finite values.
Results may differ from a plain program's by a relative error of at most 0.006.
Values sent between devices are 32-bit elements; how exact they have to be, the bound alone decides.
No kernel may reach another device: no remote copies, remote signals or barrier semaphores. Data moves between devices by JAX's collectives and lax.ppermute only.
A program may use at most 128 MiB of HBM per device.

v0:
```python
import jax
import jax.numpy as jnp
from jax import lax
from jax.sharding import PartitionSpec as P


def from_partner(block, axis, bit):
    count = lax.axis_size(axis)
    route = []
    for low in range(count):
        high = low | 1 << bit
        if high != low and high < count:
            route += [(low, high), (high, low)]
    return lax.ppermute(block, axis, route)


def cut_along(value, dim, devices):
    shape = value.shape
    pieces = value.reshape(*shape[:dim], devices, shape[dim] // devices, *shape[dim + 1 :])
    return jnp.moveaxis(pieces, dim, 0)


def summed_on_arrival(value, axis, dim):
    devices = lax.axis_size(axis)
    pieces = lax.all_to_all(cut_along(value, dim, devices), axis, 0, 0, tiled=True)
    return jnp.sum(pieces, axis=0)


def side_by_side(arrays, axis, dim, along):
    ends, at = ([], 0)
    for a in arrays[:-1]:
        at += a.shape[along]
        ends.append(at)
    both = jnp.concatenate(arrays, axis=along)
    return tuple(jnp.split(summed_on_arrival(both, axis, dim), ends, axis=along))


def bit_count(values, bits):
    counted = jnp.zeros(values.shape, jnp.int32)
    for digit_no in range(bits):
        counted = counted + (values >= 1 << digit_no).astype(jnp.int32)
    return counted


def local(x_in, b_in, c_in, d_out, table, level_index):
    tok_rows, feat_width = x_in.shape
    nstate = b_in.shape[1]
    low_bits = tok_rows.bit_length() - 1
    ctx_bits = lax.axis_size("ctx").bit_length() - 1
    my_block = lax.axis_index("ctx")
    table_rows = table.shape[0]
    chooser = (level_index[:, None] == jnp.arange(table_rows, dtype=jnp.int32)[None, :]).astype(
        jnp.float32
    )
    weights_tok = jnp.dot(chooser, table, precision=lax.Precision.HIGHEST)
    far_lam = weights_tok[:, low_bits + 1 : low_bits + 1 + ctx_bits]
    state = jnp.dot(b_in.T, x_in, preferred_element_type=jnp.float32)
    rising = (
        (far_lam[:, :, None] * c_in[:, None, :].astype(jnp.float32))
        .astype(jnp.bfloat16)
        .reshape(tok_rows, ctx_bits * nstate)
    )
    grad_state = jnp.dot(rising.T, d_out, preferred_element_type=jnp.float32).reshape(
        ctx_bits, nstate, feat_width
    )
    block_sum = state
    carry_parts = []
    for digit_no in range(ctx_bits):
        partner = from_partner(block_sum, "ctx", digit_no)
        upper_flag = (my_block >> digit_no & 1).astype(jnp.float32)
        carry_parts.append(partner * upper_flag)
        block_sum = block_sum + partner
    carry_full = jnp.stack(carry_parts)
    carry = carry_full.astype(jnp.bfloat16).reshape(ctx_bits * nstate, feat_width)
    pending = grad_state
    back_sum = jnp.zeros((nstate, feat_width), jnp.float32)
    for digit_no in range(ctx_bits):
        partner = from_partner(pending, "ctx", digit_no)
        lower_flag = (1 - (my_block >> digit_no & 1)).astype(jnp.float32)
        back_sum = back_sum + partner[0] * lower_flag
        pending = (pending + partner)[1:]
    back_state = back_sum.astype(jnp.bfloat16)
    block_rows = min(512, tok_rows)
    positions = jnp.arange(tok_rows, dtype=jnp.int32)
    y_parts = []
    c_parts = []
    dx_accum = jnp.zeros((tok_rows, feat_width), jnp.float32)
    grad_b = jnp.zeros((tok_rows, nstate), jnp.float32)
    for row_start in range(0, tok_rows, block_rows):
        row_stop = row_start + block_rows
        row_pos = positions[row_start:row_stop]
        col_pos = positions[:row_stop]
        level_map = bit_count(row_pos[:, None] ^ col_pos[None, :], low_bits)
        weight = jnp.zeros((block_rows, row_stop), jnp.float32)
        for level_no in range(low_bits + 1):
            weight = weight + jnp.where(
                level_map == level_no, weights_tok[row_start:row_stop, level_no][:, None], 0.0
            )
        weight = jnp.where(col_pos[None, :] <= row_pos[:, None], weight, 0.0)
        scores = jnp.dot(
            c_in[row_start:row_stop], b_in[:row_stop].T, preferred_element_type=jnp.float32
        )
        mixing = (scores * weight).astype(jnp.bfloat16)
        y_rows = jnp.dot(mixing, x_in[:row_stop], preferred_element_type=jnp.float32) + jnp.dot(
            rising[row_start:row_stop], carry, preferred_element_type=jnp.float32
        )
        y_parts.append(y_rows.astype(jnp.bfloat16))
        dx_accum = dx_accum.at[:row_stop].add(
            jnp.dot(mixing.T, d_out[row_start:row_stop], preferred_element_type=jnp.float32)
        )
        d_mix = (
            jnp.dot(
                d_out[row_start:row_stop], x_in[:row_stop].T, preferred_element_type=jnp.float32
            )
            * weight
        ).astype(jnp.bfloat16)
        c_parts.append(jnp.dot(d_mix, b_in[:row_stop], preferred_element_type=jnp.float32))
        grad_b = grad_b.at[:row_stop].add(
            jnp.dot(d_mix.T, c_in[row_start:row_stop], preferred_element_type=jnp.float32)
        )
    y_out = jnp.concatenate(y_parts, axis=0)
    dx_out = (dx_accum + jnp.dot(b_in, back_state, preferred_element_type=jnp.float32)).astype(
        jnp.bfloat16
    )
    far_terms = jnp.dot(d_out, carry.T, preferred_element_type=jnp.float32).reshape(
        tok_rows, ctx_bits, nstate
    )
    grad_c = jnp.concatenate(c_parts, axis=0) + jnp.sum(far_terms * far_lam[:, :, None], axis=1)
    grad_b = grad_b + jnp.dot(x_in, back_state.T, preferred_element_type=jnp.float32)
    d_b, d_c = side_by_side((grad_b, grad_c), "head", 0, 1)
    return (y_out, dx_out, d_b, d_c)


def solution(mesh):
    return jax.shard_map(
        local,
        mesh=mesh,
        in_specs=(
            P("ctx", "head"),
            P("ctx", None),
            P("ctx", None),
            P("ctx", "head"),
            P(),
            P("ctx"),
        ),
        out_specs=(
            P("ctx", "head"),
            P("ctx", "head"),
            P(("ctx", "head"), None),
            P(("ctx", "head"), None),
        ),
        check_vma=False,
    )
```

profile of v0, /device:TPU:0, one launch (start us, length us, event | category | flops | bytes accessed | tf_op | source)
XLA Modules:
  0.0 230.5 jit_solution(13653350192255541427)
XLA Ops:
  0.6 2.2 fusion.50
  4.9 2.1 collective-permute-start.1
  7.0 12.2 %collective-permute-done.1 = f32[128,1024]{1,0:T(8,128)S(1)} collective-permute-done((f32[128,1024]{1,0:T(8,128)S(1)}, f32[128,1024]{1,0:T(8,128)S(1)}, u32[]{:S(2)}, u32[]{:S(2)}) %collective-permute-start.1) | collective-permute-done | bytes 524320 | tf_op jit(solution)/shard_map/ppermute | solution.py:14
  19.3 3.8 %collective-permute-start.2 = (f32[128,1024]{1,0:T(8,128)S(1)}, f32[128,1024]{1,0:T(8,128)S(1)}, u32[]{:S(2)}, u32[]{:S(2)}) collective-permute-start(f32[128,1024]{1,0:T(8,128)S(1)} %add.582), channel_id=1, source_target_pairs={{0,16},{16,0},{4,20},{20,4},{8,24},{24,8},{12,28},{28,12},{32,48},... | collective-permute-start | bytes 1572872 | tf_op jit(solution)/shard_map/ppermute | solution.py:14
  23.1 11.4 %collective-permute-done.2 = f32[128,1024]{1,0:T(8,128)S(1)} collective-permute-done((f32[128,1024]{1,0:T(8,128)S(1)}, f32[128,1024]{1,0:T(8,128)S(1)}, u32[]{:S(2)}, u32[]{:S(2)}) %collective-permute-start.2) | collective-permute-done | bytes 524320 | tf_op jit(solution)/shard_map/ppermute | solution.py:14
  36.7 10.4 %collective-permute-done.3 = f32[128,1024]{1,0:T(8,128)S(1)} collective-permute-done((f32[128,1024]{1,0:T(8,128)S(1)}, f32[128,1024]{1,0:T(8,128)S(1)}, u32[]{:S(2)}, u32[]{:S(2)}) %collective-permute-start.3) | collective-permute-done | bytes 524320 | tf_op jit(solution)/shard_map/ppermute | solution.py:14
  47.2 3.1 %collective-permute-start.4 = (f32[128,1024]{1,0:T(8,128)S(1)}, f32[128,1024]{1,0:T(8,128)S(1)}, u32[]{:S(2)}, u32[]{:S(2)}) collective-permute-start(f32[128,1024]{1,0:T(8,128)S(1)} %add.584), channel_id=1, source_target_pairs={{0,64},{64,0},{4,68},{68,4},{8,72},{72,8},{12,76},{76,12},{16,80},... | collective-permute-start | bytes 1572872 | tf_op jit(solution)/shard_map/ppermute | solution.py:14
  50.4 10.1 %collective-permute-done.4 = f32[128,1024]{1,0:T(8,128)S(1)} collective-permute-done((f32[128,1024]{1,0:T(8,128)S(1)}, f32[128,1024]{1,0:T(8,128)S(1)}, u32[]{:S(2)}, u32[]{:S(2)}) %collective-permute-start.4) | collective-permute-done | bytes 524320 | tf_op jit(solution)/shard_map/ppermute | solution.py:14
  62.2 2.1 copy.22
  64.2 3.0 %multiply_reduce_fusion = (f32[1024,128]{1,0:T(8,128)}, bf16[1024,5,128]{2,0,1:T(8,128)(2,1)S(1)}) fusion(f32[1024,5,128]{2,0,1:T(8,128)} %copy.22, f32[1024,5]{0,1:T(8,128)S(1)} %slice.288, f32[1024,128]{1,0:T(8,128)S(1)} %convert_element_type.544), kind=kLoop, calls=%fused_computation.12 | loop fusion | flops 2490368 | bytes 5001216 | tf_op jit(solution)/shard_map/reduce_sum | solution.py:128
  69.3 2.9 %fusion.1 = f32[5,128,1024]{2,1,0:T(8,128)S(1)} fusion(bf16[1024,1024]{1,0:T(8,128)(2,1)S(1)} %copy-done.18, bf16[1024,5,128]{0,2,1:T(8,128)(2,1)} %copy.18), kind=kOutput, calls=%fused_computation.16 | convolution fusion | flops 1342177280 | bytes 6029312 | tf_op jit(solution)/shard_map/dot_general | solution.py:63
  72.4 4.8 %collective-permute-done.5 = f32[5,128,1024]{2,1,0:T(8,128)S(1)} collective-permute-done((f32[5,128,1024]{2,1,0:T(8,128)S(1)}, f32[5,128,1024]{2,1,0:T(8,128)S(1)}, u32[]{:S(2)}, u32[]{:S(2)}) %collective-permute-start.5) | collective-permute-done | bytes 2621472 | tf_op jit(solution)/shard_map/ppermute | solution.py:14
  79.7 2.7 %fusion.17 = bf16[512,512]{1,0:T(8,128)(2,1)S(1)} fusion(bf16[1024,1024]{1,0:T(8,128)(2,1)S(1)} %copy-done.19, bf16[1024,1024]{1,0:T(8,128)(2,1)S(1)} %copy-done.2, f32[512]{0:T(512)S(1)} %bitcast.118, f32[512]{0:T(512)S(1)} %bitcast.120, f32[512]{0:T(512)S(1)} %bitcast.122, f32[512]{0:T(512)S(1)} %bitcast.124, f32[512]{0:T(512)S(1)} %bitcast.126, ...), kind=kOutput, calls=%fused_computation.43 | convolution fusion | flops 554172416 | bytes 2648064 | tf_op jit(solution)/shard_map/dot_general | solution.py:112
  83.4 3.3 %fusion.16 = bf16[512,512]{1,0:T(8,128)(2,1)} fusion(f32[512]{0:T(512)S(1)} %bitcast.119, f32[512]{0:T(512)S(1)} %bitcast.121, f32[512]{0:T(512)S(1)} %bitcast.123, f32[512]{0:T(512)S(1)} %bitcast.125, f32[512]{0:T(512)S(1)} %bitcast.127, f32[512]{0:T(512)S(1)} %bitcast.129, f32[512]{0:T(512)S(1)} %bitcast.131, f32[512]{0:T(512)S(1)} %bitcast.135, ...), kind=kOutput, calls=%fused_computation.42 | convolution fusion | flops 84410368 | bytes 813056 | tf_op jit(solution)/shard_map/dot_general | solution.py:100
  86.7 7.4 %multiply_convert_fusion.1 = bf16[512,1024]{1,0:T(8,128)(2,1)} fusion(bf16[1024,1024]{1,0:T(8,128)(2,1)S(1)} %copy-done.2, f32[512]{0:T(512)S(1)} %bitcast.94, f32[512]{0:T(512)S(1)} %bitcast.96, f32[512]{0:T(512)S(1)} %bitcast.98, f32[512]{0:T(512)S(1)} %bitcast.100, f32[512]{0:T(512)S(1)} %bitcast.102, f32[512]{0:T(512)S(1)} %bitcast.104, ...), kind=kOutput, calls=%fused_computation.22 | convolution fusion | flops 1108344832 | bytes 4218880 | tf_op jit(solution)/shard_map/dot_general | solution.py:112
  94.0 32.4 %collective-permute-done.6 = f32[4,128,1024]{2,1,0:T(8,128)S(1)} collective-permute-done((f32[4,128,1024]{2,1,0:T(8,128)S(1)}, f32[4,128,1024]{2,1,0:T(8,128)S(1)}, u32[]{:S(2)}, u32[]{:S(2)}) %collective-permute-start.6) | collective-permute-done | bytes 2097184 | tf_op jit(solution)/shard_map/ppermute | solution.py:14
  128.2 2.9 %collective-permute-start.7 = (f32[3,128,1024]{2,1,0:T(8,128)}, f32[3,128,1024]{2,1,0:T(8,128)}, u32[]{:S(2)}, u32[]{:S(2)}) collective-permute-start(f32[3,128,1024]{2,1,0:T(8,128)} %slice_add_fusion.1), channel_id=1, source_target_pairs={{0,16},{16,0},{4,20},{20,4},{8,24},{24,8},{12,28},{28,12},{32,48},... | collective-permute-start | bytes 4718600 | tf_op jit(solution)/shard_map/ppermute | solution.py:14
  132.1 2.4 %fusion.52 = f32[512,128]{0,1:T(8,128)} fusion(bf16[512,1024]{1,0:T(8,128)(2,1)} %multiply_convert_fusion.1, bf16[1024,128]{1,0:T(8,128)(2,1)} %param.19), kind=kOutput, calls=%fused_computation.97 | convolution fusion | flops 134217728 | bytes 1572864 | tf_op jit(solution)/shard_map/dot_general | solution.py:117
  134.6 3.6 %fusion.23 = f32[512,1024]{1,0:T(8,128)} fusion(bf16[512,512]{1,0:T(8,128)(2,1)} %fusion.16, bf16[1024,1024]{1,0:T(8,128)(2,1)} %param.21), kind=kOutput, calls=%fused_computation.56 | convolution fusion | flops 536870912 | bytes 3670016 | tf_op jit(solution)/shard_map/dot_general | solution.py:109
  138.1 5.1 %multiply_convert_fusion.2 = bf16[512,1024]{1,0:T(8,128)(2,1)S(1)} fusion(bf16[1024,128]{1,0:T(8,128)(2,1)S(1)} %copy-done.10, f32[512]{0:T(512)S(1)} %bitcast.95, f32[512]{0:T(512)S(1)} %bitcast.97, f32[512]{0:T(512)S(1)} %bitcast.99, f32[512]{0:T(512)S(1)} %bitcast.101, f32[512]{0:T(512)S(1)} %bitcast.103, f32[512]{0:T(512)S(1)} %bitcast.105, ...), kind=kOutput, calls=%fused_computation.23 | convolution fusion | flops 168820736 | bytes 1466368 | tf_op jit(solution)/shard_map/dot_general | solution.py:100
  143.2 22.4 %collective-permute-done.7 = f32[3,128,1024]{2,1,0:T(8,128)} collective-permute-done((f32[3,128,1024]{2,1,0:T(8,128)}, f32[3,128,1024]{2,1,0:T(8,128)}, u32[]{:S(2)}, u32[]{:S(2)}) %collective-permute-start.7) | collective-permute-done | bytes 1572896 | tf_op jit(solution)/shard_map/ppermute | solution.py:14
  165.6 2.7 %slice_add_fusion.2 = f32[2,128,1024]{2,1,0:T(8,128)} fusion(f32[3,128,1024]{2,1,0:T(8,128)} %collective-permute-done.7, f32[3,128,1024]{2,1,0:T(8,128)} %slice_add_fusion.1), kind=kLoop, calls=%fused_computation.48 | loop fusion | flops 262144 | bytes 3145728 | tf_op jit(solution)/shard_map/add | solution.py:81
  171.7 2.6 %fusion.51 = f32[512,1024]{1,0:T(8,128)} fusion(bf16[512,1024]{1,0:T(8,128)(2,1)S(1)} %multiply_convert_fusion.2, bf16[1024,1024]{1,0:T(8,128)(2,1)S(1)} %copy-done.2), kind=kOutput, calls=%fused_computation.96 | convolution fusion | flops 1073741824 | bytes 5242880 | tf_op jit(solution)/shard_map/dot_general | solution.py:104
  174.3 3.3 %fusion.20 = f32[1024,1024]{1,0:T(8,128)} fusion(bf16[512,1024]{1,0:T(8,128)(2,1)S(1)} %multiply_convert_fusion.2, bf16[1024,1024]{1,0:T(8,128)(2,1)S(1)} %copy-done.20), kind=kOutput, calls=%fused_computation.53 | convolution fusion | flops 1073741824 | bytes 6291456 | tf_op jit(solution)/shard_map/dot_general | solution.py:109
  177.5 2.0 copy.23
  179.6 12.5 %collective-permute-done.8 = f32[2,128,1024]{2,1,0:T(8,128)} collective-permute-done((f32[2,128,1024]{2,1,0:T(8,128)}, f32[2,128,1024]{2,1,0:T(8,128)}, u32[]{:S(2)}, u32[]{:S(2)}) %collective-permute-start.8) | collective-permute-done | bytes 1048608 | tf_op jit(solution)/shard_map/ppermute | solution.py:14
  193.3 3.1 %collective-permute-start.9 = (f32[1,128,1024]{2,1,0:T(8,128)S(1)}, f32[1,128,1024]{2,1,0:T(8,128)S(1)}, u32[]{:S(2)}, u32[]{:S(2)}) collective-permute-start(f32[1,128,1024]{2,1,0:T(8,128)S(1)} %slice_add_fusion.3), channel_id=1, source_target_pairs={{0,64},{64,0},{4,68},{68,4},{8,72},{72,8},{12,76},{76,12},{16,80},... | collective-permute-start | bytes 1572872 | tf_op jit(solution)/shard_map/ppermute | solution.py:14
  197.7 3.3 %fusion.4 = bf16[512,1024]{1,0:T(8,128)(2,1)} fusion(f32[512,1024]{1,0:T(8,128)S(1)} %copy-done.4, bf16[5,128,1024]{2,1,0:T(8,128)(2,1)} %copy-done.5, bf16[1024,5,128]{2,0,1:T(8,128)(2,1)S(1)} %get-tuple-element.97), kind=kOutput, calls=%fused_computation.21 | convolution fusion | flops 672137216 | bytes 5111808 | tf_op jit(solution)/shard_map/dot_general | solution.py:104
  201.0 5.4 %collective-permute-done.9 = f32[1,128,1024]{2,1,0:T(8,128)S(1)} collective-permute-done((f32[1,128,1024]{2,1,0:T(8,128)S(1)}, f32[1,128,1024]{2,1,0:T(8,128)S(1)}, u32[]{:S(2)}, u32[]{:S(2)}) %collective-permute-start.9) | collective-permute-done | bytes 524320 | tf_op jit(solution)/shard_map/ppermute | solution.py:14
  211.2 4.5 %all-to-all-start = ((f32[4,256,256]{1,2,0:T(8,128)}), f32[4,256,256]{1,2,0:T(8,128)}, u32[]{:S(2)}, u32[]{:S(2)}) async-start(f32[4,256,256]{1,2,0:T(8,128)} %bitcast.91), calls=%async_computation | async-start | bytes 2097152 | tf_op jit(solution)/shard_map/all_to_all | solution.py:25
  215.7 2.7 %fusion.3 = bf16[512,1024]{1,0:T(8,128)(2,1)S(1)} fusion(f32[512,1024]{1,0:T(8,128)} %fusion.51, bf16[5,128,1024]{2,1,0:T(8,128)(2,1)S(1)} %copy-done.6, bf16[1024,5,128]{2,0,1:T(8,128)(2,1)S(1)} %get-tuple-element.97), kind=kOutput, calls=%fused_computation.19 | convolution fusion | flops 672137216 | bytes 5111808 | tf_op jit(solution)/shard_map/dot_general | solution.py:104
  223.4 4.2 %all-to-all-done = f32[4,256,256]{1,2,0:T(8,128)} async-done(((f32[4,256,256]{1,2,0:T(8,128)}), f32[4,256,256]{1,2,0:T(8,128)}, u32[]{:S(2)}, u32[]{:S(2)}) %all-to-all-start) | async-done | bytes 1048608 | tf_op jit(solution)/shard_map/all_to_all | solution.py:25
  (102 shorter events, 33.0 us)
Async XLA Ops:
  0.6 35.5 %copy-start = (f32[16,18]{1,0:T(8,128)S(1)}, f32[16,18]{1,0:T(8,128)}, u32[]{:S(2)}) copy-start(f32[16,18]{1,0:T(8,128)} %param.22) | copy-start | bytes 3460
  2.8 33.3 %copy-start.28 = (s32[1024]{0:T(1024)S(1)}, s32[1024]{0:T(1024)}, u32[]{:S(2)}) copy-start(s32[1024]{0:T(1024)} %param.23) | copy-start | bytes 12292
  2.8 33.8 %copy-start.21 = (bf16[1024,128]{1,0:T(8,128)(2,1)S(1)}, bf16[1024,128]{1,0:T(8,128)(2,1)}, u32[]{:S(2)}) copy-start(bf16[1024,128]{1,0:T(8,128)(2,1)} %param.20) | copy-start | bytes 786436
  2.8 2.0 collective-permute-start
  4.9 14.3 %collective-permute-start.1 = (f32[128,1024]{1,0:T(8,128)S(1)}, f32[128,1024]{1,0:T(8,128)S(1)}, u32[]{:S(2)}, u32[]{:S(2)}) collective-permute-start(f32[128,1024]{1,0:T(8,128)S(1)} %add.581), channel_id=1, source_target_pairs={{0,8},{8,0},{4,12},{12,4},{16,24},{24,16},{20,28},{28,20},{32,40},... | collective-permute-start | bytes 1572872 | tf_op jit(solution)/shard_map/ppermute | solution.py:14
  19.3 15.2 %collective-permute-start.2 = (f32[128,1024]{1,0:T(8,128)S(1)}, f32[128,1024]{1,0:T(8,128)S(1)}, u32[]{:S(2)}, u32[]{:S(2)}) collective-permute-start(f32[128,1024]{1,0:T(8,128)S(1)} %add.582), channel_id=1, source_target_pairs={{0,16},{16,0},{4,20},{20,4},{8,24},{24,8},{12,28},{28,12},{32,48},... | collective-permute-start | bytes 1572872 | tf_op jit(solution)/shard_map/ppermute | solution.py:14
  34.5 12.6 %collective-permute-start.3 = (f32[128,1024]{1,0:T(8,128)S(1)}, f32[128,1024]{1,0:T(8,128)S(1)}, u32[]{:S(2)}, u32[]{:S(2)}) collective-permute-start(f32[128,1024]{1,0:T(8,128)S(1)} %add.583), channel_id=1, source_target_pairs={{0,32},{32,0},{4,36},{36,4},{8,40},{40,8},{12,44},{44,12},{16,48},... | collective-permute-start | bytes 1572872 | tf_op jit(solution)/shard_map/ppermute | solution.py:14
  47.2 13.4 %copy-start.17 = (bf16[1024,1024]{1,0:T(8,128)(2,1)S(1)}, bf16[1024,1024]{1,0:T(8,128)(2,1)}, u32[]{:S(2)}) copy-start(bf16[1024,1024]{1,0:T(8,128)(2,1)} %param.21) | copy-start | bytes 6291460
  47.2 13.3 %collective-permute-start.4 = (f32[128,1024]{1,0:T(8,128)S(1)}, f32[128,1024]{1,0:T(8,128)S(1)}, u32[]{:S(2)}, u32[]{:S(2)}) collective-permute-start(f32[128,1024]{1,0:T(8,128)S(1)} %add.584), channel_id=1, source_target_pairs={{0,64},{64,0},{4,68},{68,4},{8,72},{72,8},{12,76},{76,12},{16,80},... | collective-permute-start | bytes 1572872 | tf_op jit(solution)/shard_map/ppermute | solution.py:14
  72.2 5.0 %collective-permute-start.5 = (f32[5,128,1024]{2,1,0:T(8,128)S(1)}, f32[5,128,1024]{2,1,0:T(8,128)S(1)}, u32[]{:S(2)}, u32[]{:S(2)}) collective-permute-start(f32[5,128,1024]{2,1,0:T(8,128)S(1)} %fusion.1), channel_id=1, source_target_pairs={{0,4},{4,0},{8,12},{12,8},{16,20},{20,16},{24,28},{28,24},{32,36},... | collective-permute-start | bytes 7864328 | tf_op jit(solution)/shard_map/ppermute | solution.py:14
  72.4 14.3 %copy-start.26 = (f32[512,1]{0,1:T(1,128)}, f32[512,1]{0,1:T(1,128)S(1)}, u32[]{:S(2)}) copy-start(f32[512,1]{0,1:T(1,128)S(1)} %get-tuple-element.85) | copy-start | bytes 6148
  72.4 7.3 %copy-start.2 = (bf16[1024,1024]{1,0:T(8,128)(2,1)S(1)}, bf16[1024,1024]{1,0:T(8,128)(2,1)}, u32[]{:S(2)}) copy-start(bf16[1024,1024]{1,0:T(8,128)(2,1)} %param.18) | copy-start | bytes 6291460
  72.4 7.3 %copy-start.19 = (bf16[1024,1024]{1,0:T(8,128)(2,1)S(1)}, bf16[1024,1024]{1,0:T(8,128)(2,1)}, u32[]{:S(2)}) copy-start(bf16[1024,1024]{1,0:T(8,128)(2,1)} %param.21) | copy-start | bytes 6291460
  78.7 47.7 %collective-permute-start.6 = (f32[4,128,1024]{2,1,0:T(8,128)S(1)}, f32[4,128,1024]{2,1,0:T(8,128)S(1)}, u32[]{:S(2)}, u32[]{:S(2)}) collective-permute-start(f32[4,128,1024]{2,1,0:T(8,128)S(1)} %slice_add_fusion), channel_id=1, source_target_pairs={{0,8},{8,0},{4,12},{12,4},{16,24},{24,16},{20,28},{28,20},{32,40},... | collective-permute-start | bytes 6291464 | tf_op jit(solution)/shard_map/ppermute | solution.py:14
  79.7 2.7 %copy-start.22 = (bf16[1024,128]{1,0:T(8,128)(2,1)S(1)}, bf16[1024,128]{1,0:T(8,128)(2,1)}, u32[]{:S(2)}) copy-start(bf16[1024,128]{1,0:T(8,128)(2,1)} %param.20) | copy-start | bytes 786436
  79.7 3.7 %copy-start.9 = (bf16[1024,128]{1,0:T(8,128)(2,1)S(1)}, bf16[1024,128]{1,0:T(8,128)(2,1)}, u32[]{:S(2)}) copy-start(bf16[1024,128]{1,0:T(8,128)(2,1)} %param.19) | copy-start | bytes 786436
  128.2 37.4 %collective-permute-start.7 = (f32[3,128,1024]{2,1,0:T(8,128)}, f32[3,128,1024]{2,1,0:T(8,128)}, u32[]{:S(2)}, u32[]{:S(2)}) collective-permute-start(f32[3,128,1024]{2,1,0:T(8,128)} %slice_add_fusion.1), channel_id=1, source_target_pairs={{0,16},{16,0},{4,20},{20,4},{8,24},{24,8},{12,28},{28,12},{32,48},... | collective-permute-start | bytes 4718600 | tf_op jit(solution)/shard_map/ppermute | solution.py:14
  134.6 3.6 %copy-start.10 = (bf16[1024,128]{1,0:T(8,128)(2,1)S(1)}, bf16[1024,128]{1,0:T(8,128)(2,1)}, u32[]{:S(2)}) copy-start(bf16[1024,128]{1,0:T(8,128)(2,1)} %param.19) | copy-start | bytes 786436
  134.6 3.6 %copy-start.23 = (bf16[1024,128]{1,0:T(8,128)(2,1)S(1)}, bf16[1024,128]{1,0:T(8,128)(2,1)}, u32[]{:S(2)}) copy-start(bf16[1024,128]{1,0:T(8,128)(2,1)} %param.20) | copy-start | bytes 786436
  134.6 3.6 %copy-start.27 = (f32[512,1]{0,1:T(1,128)S(1)}, f32[512,1]{0,1:T(1,128)}, u32[]{:S(2)}) copy-start(f32[512,1]{0,1:T(1,128)} %copy-done.26) | copy-start | bytes 6148
  143.2 26.4 %copy-start.15 = (bf16[512,512]{1,0:T(8,128)(2,1)S(1)}, bf16[512,512]{1,0:T(8,128)(2,1)}, u32[]{:S(2)}) copy-start(bf16[512,512]{1,0:T(8,128)(2,1)} %fusion.16) | copy-start | bytes 1572868
  168.3 23.8 %collective-permute-start.8 = (f32[2,128,1024]{2,1,0:T(8,128)}, f32[2,128,1024]{2,1,0:T(8,128)}, u32[]{:S(2)}, u32[]{:S(2)}) collective-permute-start(f32[2,128,1024]{2,1,0:T(8,128)} %slice_add_fusion.2), channel_id=1, source_target_pairs={{0,32},{32,0},{4,36},{36,4},{8,40},{40,8},{12,44},{44,12},{16,48},... | collective-permute-start | bytes 3145736 | tf_op jit(solution)/shard_map/ppermute | solution.py:14
  171.7 2.6 %copy-start.20 = (bf16[1024,1024]{1,0:T(8,128)(2,1)S(1)}, bf16[1024,1024]{1,0:T(8,128)(2,1)}, u32[]{:S(2)}) copy-start(bf16[1024,1024]{1,0:T(8,128)(2,1)} %param.21) | copy-start | bytes 6291460
  179.6 18.1 %copy-start.4 = (f32[512,1024]{1,0:T(8,128)S(1)}, f32[512,1024]{1,0:T(8,128)}, u32[]{:S(2)}) copy-start(f32[512,1024]{1,0:T(8,128)} %fusion.26) | copy-start | bytes 6291460
  193.3 13.1 %collective-permute-start.9 = (f32[1,128,1024]{2,1,0:T(8,128)S(1)}, f32[1,128,1024]{2,1,0:T(8,128)S(1)}, u32[]{:S(2)}, u32[]{:S(2)}) collective-permute-start(f32[1,128,1024]{2,1,0:T(8,128)S(1)} %slice_add_fusion.3), channel_id=1, source_target_pairs={{0,64},{64,0},{4,68},{68,4},{8,72},{72,8},{12,76},{76,12},{16,80},... | collective-permute-start | bytes 1572872 | tf_op jit(solution)/shard_map/ppermute | solution.py:14
  210.1 5.6 %copy-start.6 = (bf16[5,128,1024]{2,1,0:T(8,128)(2,1)S(1)}, bf16[5,128,1024]{2,1,0:T(8,128)(2,1)}, u32[]{:S(2)}) copy-start(bf16[5,128,1024]{2,1,0:T(8,128)(2,1)} %copy-done.5) | copy-start | bytes 3932164
  211.2 16.4 %all-to-all-start = ((f32[4,256,256]{1,2,0:T(8,128)}), f32[4,256,256]{1,2,0:T(8,128)}, u32[]{:S(2)}, u32[]{:S(2)}) async-start(f32[4,256,256]{1,2,0:T(8,128)} %bitcast.91), calls=%async_computation | async-start | bytes 2097152 | tf_op jit(solution)/shard_map/all_to_all | solution.py:25
  215.7 2.8 %copy-start.8 = (bf16[512,1024]{1,0:T(8,128)(2,1)S(1)}, bf16[512,1024]{1,0:T(8,128)(2,1)}, u32[]{:S(2)}) copy-start(bf16[512,1024]{1,0:T(8,128)(2,1)} %fusion.4) | copy-start | bytes 3145732
  215.7 4.3 %copy-start.3 = (f32[512,1024]{1,0:T(8,128)S(1)}, f32[512,1024]{1,0:T(8,128)}, u32[]{:S(2)}) copy-start(f32[512,1024]{1,0:T(8,128)} %fusion.23) | copy-start | bytes 6291460
  215.7 4.3 %copy-start.11 = (bf16[1024,128]{1,0:T(8,128)(2,1)S(1)}, bf16[1024,128]{1,0:T(8,128)(2,1)}, u32[]{:S(2)}) copy-start(bf16[1024,128]{1,0:T(8,128)(2,1)} %param.19) | copy-start | bytes 786436
  215.7 4.3 %copy-start.14 = (bf16[1,128,1024]{2,1,0:T(8,128)(2,1)S(1)}, bf16[1,128,1024]{2,1,0:T(8,128)(2,1)}, u32[]{:S(2)}) copy-start(bf16[1,128,1024]{2,1,0:T(8,128)(2,1)} %copy-done.13) | copy-start | bytes 786436
  218.5 2.9 %copy-start.1 = (f32[1024,1024]{1,0:T(8,128)S(1)}, f32[1024,1024]{1,0:T(8,128)}, u32[]{:S(2)}) copy-start(f32[1024,1024]{1,0:T(8,128)} %fusion.20) | copy-start | bytes 12582916
  (8 other events, 12.9 us)
where the time goes:
time: 231 us
  waiting for transfers between devices  128 us (55%)
  matrix products  50.5 us (22%)
  starting transfers between devices  23.6 us (10%)
  other arithmetic  15.5 us (7%)
  local copies, waits for them, and re-layouts  12.2 us (5%)
    ppermute x10, waiting for transfers between devices, from_partner(): return lax.ppermute(block, axis, route)  123 us
    ppermute x10, starting transfers between devices, from_partner(): return lax.ppermute(block, axis, route)  19.1 us
    dot_general x2, matrix products, local(): jnp.dot(d_out[row_start:row_stop], x_in[:row_stop].T, preferred_element_t...  10 us
    dot_general x2, matrix products, local(): jnp.dot(c_in[row_start:row_stop], b_in[:row_stop].T, preferred_element_ty...  8.34 us
    dot_general x2, matrix products, local(): jnp.dot(mixing.T, d_out[row_start:row_stop], preferred_element_type=jnp.f...  6.83 us
    add x4, other arithmetic, local(): pending = (pending + partner)[1:]  6.06 us
    dot_general x2, matrix products, local(): jnp.dot(rising[row_start:row_stop], carry, preferred_element_type=jnp.flo...  6.05 us
    unnamed x60, local copies, waits for them, and re-layouts  5.47 us
  transfers between devices with their start and end apart: 11, of which 11 were waited for; matrix products, arithmetic and copies ran while one was open for 21% of the time, Pallas kernels for 0%

commit v1 on v0

v1 whole, which is shorter than its diff:
```python
import jax
import jax.numpy as jnp
from jax import lax
from jax.sharding import PartitionSpec as P


def from_xor(block, flip):
    route = [(i, i ^ flip) for i in range(lax.axis_size("ctx"))]
    return lax.ppermute(block, "ctx", route)


CORE, Z, X = 1, (0, 2, 4, 6), (0, 8, 16, 24)


def sibling_sums(slots):
    a0, a1, a2, a3, a4 = slots
    far = jnp.stack([a3, a4])
    near = jnp.stack([a1, a2])
    far_p = far[:, 0] + from_xor(far[:, 1], CORE)
    near_p = near[:, 0] + from_xor(near[:, 1], CORE)
    b0 = from_xor(a0, CORE)[::-1]
    total = far_p[:, 0]
    for m in (2, 1, 3):
        total = total + from_xor(far_p[:, m], Z[m])
    b3 = from_xor(total[0], X[1])
    b4 = from_xor(total[1], X[2]) + from_xor(total[1], X[3])
    b34 = jnp.stack([b3, b4])
    b1 = from_xor(near_p[0], Z[1])
    b1 = jnp.stack([b1[p ^ 1] for p in range(4)])
    r2, r3 = from_xor(near_p[1], Z[2]), from_xor(near_p[1], Z[3])
    b2 = jnp.stack([r2[p ^ 2] + r3[p ^ 3] for p in range(4)])
    b34_all = jnp.stack([b34] + [from_xor(b34, Z[m]) for m in (1, 2, 3)], axis=1)
    mine = jnp.concatenate([jnp.stack([b1, b2]), b34_all])
    other = from_xor(mine, CORE)
    rest = jnp.stack([mine, other], axis=1)
    return jnp.concatenate([b0[None], rest])


def bit_count(values, bits):
    counted = jnp.zeros(values.shape, jnp.int32)
    for digit_no in range(bits):
        counted = counted + (values >= 1 << digit_no).astype(jnp.int32)
    return counted


def local(x_in, b_in, c_in, d_out, table, level_index):
    tok_rows, feat_width = x_in.shape
    nstate = b_in.shape[1]
    low_bits = tok_rows.bit_length() - 1
    ctx_bits = lax.axis_size("ctx").bit_length() - 1
    my_block = lax.axis_index("ctx")
    mask = ((my_block & 1) << 2 | (my_block >> 1 & 3)) * 16
    iota = jnp.arange(nstate, dtype=jnp.int32)
    perm = (iota[:, None] == (iota[None, :] ^ mask)).astype(jnp.bfloat16)
    chooser = (level_index[:, None] == jnp.arange(table.shape[0], dtype=jnp.int32)[None, :]).astype(jnp.float32)
    weights_tok = jnp.dot(chooser, table, precision=lax.Precision.HIGHEST)
    far_lam = weights_tok[:, low_bits + 1 : low_bits + 1 + ctx_bits]
    b_perm = jnp.dot(b_in, perm, preferred_element_type=jnp.bfloat16)
    c_perm = jnp.dot(c_in, perm, preferred_element_type=jnp.bfloat16)
    state = jnp.dot(b_perm.T, x_in, preferred_element_type=jnp.float32)
    rising = (
        (far_lam[:, :, None] * c_perm[:, None, :].astype(jnp.float32))
        .astype(jnp.bfloat16)
        .reshape(tok_rows, ctx_bits * nstate)
    )
    grad_state = jnp.dot(rising.T, d_out, preferred_element_type=jnp.float32).reshape(ctx_bits, nstate, feat_width)
    bits = [my_block >> k & 1 for k in range(ctx_bits)]
    slots = [jnp.where(bits[k] == 1, grad_state[k], state).reshape(2, 4, 16, feat_width) for k in range(ctx_bits)]
    sums = sibling_sums(slots).reshape(ctx_bits, nstate, feat_width)
    set_bits = jnp.stack(bits).astype(jnp.float32)[:, None, None]
    carry3 = (sums * set_bits).astype(jnp.bfloat16)
    carry = carry3.reshape(ctx_bits * nstate, feat_width)
    back_state = jnp.sum(sums * (1 - set_bits), axis=0).astype(jnp.bfloat16)
    block_rows = min(512, tok_rows)
    positions = jnp.arange(tok_rows, dtype=jnp.int32)
    y_parts = []
    c_parts = []
    dx_accum = jnp.zeros((tok_rows, feat_width), jnp.float32)
    grad_b = jnp.zeros((tok_rows, nstate), jnp.float32)
    for row_start in range(0, tok_rows, block_rows):
        row_stop = row_start + block_rows
        row_pos = positions[row_start:row_stop]
        col_pos = positions[:row_stop]
        level_map = bit_count(row_pos[:, None] ^ col_pos[None, :], low_bits)
        weight = jnp.zeros((block_rows, row_stop), jnp.float32)
        for level_no in range(low_bits + 1):
            weight = weight + jnp.where(level_map == level_no, weights_tok[row_start:row_stop, level_no][:, None], 0.0)
        weight = jnp.where(col_pos[None, :] <= row_pos[:, None], weight, 0.0)
        scores = jnp.dot(c_in[row_start:row_stop], b_in[:row_stop].T, preferred_element_type=jnp.float32)
        mixing = (scores * weight).astype(jnp.bfloat16)
        y_rows = jnp.dot(mixing, x_in[:row_stop], preferred_element_type=jnp.float32) + jnp.dot(
            rising[row_start:row_stop], carry, preferred_element_type=jnp.float32
        )
        y_parts.append(y_rows.astype(jnp.bfloat16))
        dx_accum = dx_accum.at[:row_stop].add(jnp.dot(mixing.T, d_out[row_start:row_stop], preferred_element_type=jnp.float32))
        d_mix = (jnp.dot(d_out[row_start:row_stop], x_in[:row_stop].T, preferred_element_type=jnp.float32) * weight).astype(jnp.bfloat16)
        c_parts.append(jnp.dot(d_mix, b_in[:row_stop], preferred_element_type=jnp.float32))
        grad_b = grad_b.at[:row_stop].add(jnp.dot(d_mix.T, c_in[row_start:row_stop], preferred_element_type=jnp.float32))
    y_out = jnp.concatenate(y_parts, axis=0)
    dx_out = (dx_accum + jnp.dot(b_perm, back_state, preferred_element_type=jnp.float32)).astype(jnp.bfloat16)
    carry_nat = jnp.einsum("ij,kjf->kif", perm, carry3, preferred_element_type=jnp.bfloat16)
    back_nat = jnp.dot(perm, back_state, preferred_element_type=jnp.bfloat16)
    far_terms = jnp.dot(d_out, carry_nat.reshape(ctx_bits * nstate, feat_width).T, preferred_element_type=jnp.float32).reshape(
        tok_rows, ctx_bits, nstate
    )
    grad_c = jnp.concatenate(c_parts, axis=0) + jnp.sum(far_terms * far_lam[:, :, None], axis=1)
    grad_b = grad_b + jnp.dot(x_in, back_nat.T, preferred_element_type=jnp.float32)
    both = jnp.concatenate([grad_b, grad_c], axis=1).reshape(4, tok_rows // 4, 2 * nstate)
    mixed = jnp.sum(lax.all_to_all(both, "head", 0, 0, tiled=True), axis=0)
    return (y_out, dx_out, mixed[:, :nstate], mixed[:, nstate:])


def solution(mesh):
    return jax.shard_map(
        local,
        mesh=mesh,
        in_specs=(P("ctx", "head"), P("ctx", None), P("ctx", None), P("ctx", "head"), P(), P("ctx")),
        out_specs=(P("ctx", "head"), P("ctx", "head"), P(("ctx", "head"), None), P(("ctx", "head"), None)),
        check_vma=False,
    )
```

time: 231 us -> 131 us (0.57)
  waiting for transfers between devices: 128 us -> 25.4 us
  other arithmetic: 15.5 us -> 10.4 us
  matrix products: 50.5 us -> 54.2 us
  local copies, waits for them, and re-layouts: 12.2 us -> 14.8 us
    ppermute x10 -> x16, waiting for transfers between devices: 123 us -> 18.5 us  [from_xor(): return lax.ppermute(block, 'ctx', route)]
    add x8 -> x4, other arithmetic: 6.33 us -> 0.18 us  [the longest x1 0.06 us: sibling_sums(): far_p = far[:, 0] + from_xor(far[:, 1], CORE)]
    dot_general x4 -> x5, matrix products: 6.55 us -> 9.76 us  [the longest x1 3.08 us: local(): jnp.dot(d_out, carry_nat.reshape(ctx_bits * nstate, feat_width).T, prefer...]
    unnamed x0 -> x2, matrix products: none -> 3.11 us
    another operation x1 -> x5, other arithmetic: 0.03 us -> 2.82 us  [the longest x2 2.75 us: sibling_sums(): rest = jnp.stack([mine, other], axis=1)]
    all_to_all x1, waiting for transfers between devices: 4.2 us -> 6.92 us  [local(): mixed = jnp.sum(lax.all_to_all(both, 'head', 0, 0, tiled=True), axis=0)]
    dot_general x2, matrix products: 6.05 us -> 3.74 us  [local(): jnp.dot(rising[row_start:row_stop], carry, preferred_element_type=jnp.flo...]
    unnamed x60 -> x44, local copies, waits for them, and re-layouts: 5.47 us -> 6.19 us
  transfers between devices with their start and end apart: 11 -> 17, of which waited for: 11 -> 10; matrix products, arithmetic and copies ran while one was open for 21% -> 32% of each run, Pallas kernels for 0% -> 0%
where the time goes in v1:
time: 131 us; the launch traced here: 130 us
  matrix products  54.2 us (41%)
  waiting for transfers between devices  25.4 us (19%)
  starting transfers between devices  24.2 us (18%)
  local copies, waits for them, and re-layouts  14.8 us (11%)
  other arithmetic  10.4 us (8%)
    ppermute x16, starting transfers between devices, from_xor(): return lax.ppermute(block, 'ctx', route)  19.8 us
    ppermute x16, waiting for transfers between devices, from_xor(): return lax.ppermute(block, 'ctx', route)  18.5 us
    dot_general x2, matrix products, local(): jnp.dot(c_in[row_start:row_stop], b_in[:row_stop].T, preferred_element_ty...  8.43 us
    dot_general x2, matrix products, local(): jnp.dot(d_out[row_start:row_stop], x_in[:row_stop].T, preferred_element_t...  8.28 us
    all_to_all x1, waiting for transfers between devices, local(): mixed = jnp.sum(lax.all_to_all(both, 'head', 0, 0, tiled=True), axis=0)  6.92 us
    unnamed x44, local copies, waits for them, and re-layouts  6.19 us
    dot_general x2, matrix products, local(): jnp.dot(mixing, x_in[:row_stop], preferred_element_type=jnp.float32)  6.01 us
    dot_general x2, matrix products, local(): jnp.dot(mixing.T, d_out[row_start:row_stop], preferred_element_type=jnp.f...  5.32 us
  transfers between devices with their start and end apart: 17, of which 10 were waited for; matrix products, arithmetic and copies ran while one was open for 32% of the time, Pallas kernels for 0%

profile of v1, /device:TPU:0, one launch (start us, length us, event | category | flops | bytes accessed | tf_op | source)
XLA Modules:
  0.0 130.2 jit_solution(5909353996541618996)
XLA Ops:
  2.5 1.9 %convolution_convert_fusion = bf16[128,1024]{1,0:T(8,128)(2,1)} fusion(bf16[1024,128]{1,0:T(8,128)(2,1)} %param.19, s32[128]{0:T(128)S(1)} %iota_xor_fusion.1), kind=kOutput, calls=%fused_computation.45 | convolution fusion | flops 33718272 | bytes 524800
  6.7 1.5 %copy.35 = bf16[1024,5,128]{0,2,1:T(8,128)(2,1)} copy(bf16[1024,5,128]{2,0,1:T(8,128)(2,1)S(1)} %multiply_convert_fusion.1) | data formatting | bytes 2621440 | tf_op jit(solution)/shard_map/convert_element_type | solution.py:63
  8.2 3.7 %fusion.71 = f32[640,1024]{1,0:T(8,128)S(1)} fusion(bf16[1024,640]{0,1:T(8,128)(2,1)} %bitcast.164, bf16[1024,1024]{1,0:T(8,128)(2,1)} %param.21), kind=kOutput, calls=%fused_computation.134 | convolution fusion | flops 1342177280 | bytes 6029312 | tf_op jit(solution)/shard_map/dot_general | solution.py:66
  14.9 2.7 %fusion.13 = bf16[512,512]{1,0:T(8,128)(2,1)S(1)} fusion(bf16[1024,1024]{1,0:T(8,128)(2,1)S(1)} %copy-done.13, bf16[1024,1024]{1,0:T(8,128)(2,1)S(1)} %copy-done.2, f32[512]{0:T(512)S(1)} %bitcast.194, f32[512]{0:T(512)S(1)} %bitcast.196, f32[512]{0:T(512)S(1)} %bitcast.198, f32[512]{0:T(512)S(1)} %bitcast.200, f32[512]{0:T(512)S(1)} %bitcast.202, ...), kind=kOutput, calls=%fused_computation.41 | convolution fusion | flops 554172416 | bytes 2648064 | tf_op jit(solution)/shard_map/dot_general | solution.py:96
  17.6 2.7 %fusion.12 = bf16[512,512]{1,0:T(8,128)(2,1)S(1)} fusion(f32[512]{0:T(512)S(1)} %bitcast.195, f32[512]{0:T(512)S(1)} %bitcast.197, f32[512]{0:T(512)S(1)} %bitcast.199, f32[512]{0:T(512)S(1)} %bitcast.201, f32[512]{0:T(512)S(1)} %bitcast.203, f32[512]{0:T(512)S(1)} %bitcast.205, f32[512]{0:T(512)S(1)} %bitcast.207, f32[512]{0:T(512)S(1)} %bitcast.211, ...), kind=kOutput, calls=%fused_computation.40 | convolution fusion | flops 84410368 | bytes 813056 | tf_op jit(solution)/shard_map/dot_general | solution.py:89
  20.3 5.6 %multiply_convert_fusion.2 = bf16[512,1024]{1,0:T(8,128)(2,1)S(1)} fusion(bf16[1024,1024]{1,0:T(8,128)(2,1)S(1)} %copy-done.2, f32[512]{0:T(512)S(1)} %bitcast.170, f32[512]{0:T(512)S(1)} %bitcast.172, f32[512]{0:T(512)S(1)} %bitcast.174, f32[512]{0:T(512)S(1)} %bitcast.176, f32[512]{0:T(512)S(1)} %bitcast.178, f32[512]{0:T(512)S(1)} %bitcast.180, ...), kind=kOutput, calls=%fused_computation.22 | convolution fusion | flops 1108344832 | bytes 4218880 | tf_op jit(solution)/shard_map/dot_general | solution.py:96
  25.9 5.8 %multiply_convert_fusion.3 = bf16[512,1024]{1,0:T(8,128)(2,1)} fusion(bf16[1024,128]{1,0:T(8,128)(2,1)S(1)} %copy-done.16, f32[512]{0:T(512)S(1)} %bitcast.171, f32[512]{0:T(512)S(1)} %bitcast.173, f32[512]{0:T(512)S(1)} %bitcast.175, f32[512]{0:T(512)S(1)} %bitcast.177, f32[512]{0:T(512)S(1)} %bitcast.179, f32[512]{0:T(512)S(1)} %bitcast.181, ...), kind=kOutput, calls=%fused_computation.23 | convolution fusion | flops 168820736 | bytes 1466368 | tf_op jit(solution)/shard_map/dot_general | solution.py:89
  31.7 2.0 %fusion.23 = f32[512,1024]{1,0:T(8,128)} fusion(bf16[512,512]{1,0:T(8,128)(2,1)S(1)} %fusion.12, bf16[1024,1024]{1,0:T(8,128)(2,1)S(1)} %copy-done.13), kind=kOutput, calls=%fused_computation.63 | convolution fusion | flops 536870912 | bytes 3670016 | tf_op jit(solution)/shard_map/dot_general | solution.py:95
  33.7 2.0 %fusion.26 = f32[512,1024]{1,0:T(8,128)} fusion(bf16[512,512]{1,0:T(8,128)(2,1)S(1)} %fusion.12, bf16[1024,1024]{1,0:T(8,128)(2,1)S(1)} %copy-done.2), kind=kOutput, calls=%fused_computation.66 | convolution fusion | flops 536870912 | bytes 3670016 | tf_op jit(solution)/shard_map/dot_general | solution.py:91
  38.1 4.0 %collective-permute-start.6 = (f32[2,16,1024]{2,1,0:T(8,128)S(1)}, f32[2,16,1024]{2,1,0:T(8,128)S(1)}, u32[]{:S(2)}, u32[]{:S(2)}) collective-permute-start(f32[2,16,1024]{2,1,0:T(8,128)S(1)} %get-tuple-element.87), channel_id=1, source_target_pairs={{0,16},{4,20},{8,24},{12,28},{16,0},{20,4},{24,8},{28,12},{32,48},... | collective-permute-start | bytes 393224 | tf_op jit(solution)/shard_map/ppermute | solution.py:9
  43.2 2.8 %collective-permute-done.6 = f32[2,16,1024]{2,1,0:T(8,128)S(1)} collective-permute-done((f32[2,16,1024]{2,1,0:T(8,128)S(1)}, f32[2,16,1024]{2,1,0:T(8,128)S(1)}, u32[]{:S(2)}, u32[]{:S(2)}) %collective-permute-start.6) | collective-permute-done | bytes 131104 | tf_op jit(solution)/shard_map/ppermute | solution.py:9
  46.0 2.4 %collective-permute-done.8 = f32[2,16,1024]{2,1,0:T(8,128)S(1)} collective-permute-done((f32[2,16,1024]{2,1,0:T(8,128)S(1)}, f32[2,16,1024]{2,1,0:T(8,128)S(1)}, u32[]{:S(2)}, u32[]{:S(2)}) %collective-permute-start.8) | collective-permute-done | bytes 131104 | tf_op jit(solution)/shard_map/ppermute | solution.py:9
  49.3 2.9 %collective-permute-start.11 = (f32[16,1024]{1,0:T(8,128)S(1)}, f32[16,1024]{1,0:T(8,128)S(1)}, u32[]{:S(2)}, u32[]{:S(2)}) collective-permute-start(f32[16,1024]{1,0:T(8,128)S(1)} %get-tuple-element.99), channel_id=1, source_target_pairs={{0,96},{4,100},{8,104},{12,108},{16,112},{20,116},{24,120},{28,124... | collective-permute-start | bytes 196616 | tf_op jit(solution)/shard_map/ppermute | solution.py:9
  53.0 2.7 %collective-permute-start.4 = (f32[4,16,1024]{2,1,0:T(8,128)S(1)}, f32[4,16,1024]{2,1,0:T(8,128)S(1)}, u32[]{:S(2)}, u32[]{:S(2)}) collective-permute-start(f32[4,16,1024]{2,1,0:T(8,128)S(1)} %get-tuple-element.82), channel_id=1, source_target_pairs={{0,24},{4,28},{8,16},{12,20},{16,8},{20,12},{24,0},{28,4},{32,56},... | collective-permute-start | bytes 786440 | tf_op jit(solution)/shard_map/ppermute | solution.py:9
  58.1 4.1 %collective-permute-done.9 = f32[16,1024]{1,0:T(8,128)S(1)} collective-permute-done((f32[16,1024]{1,0:T(8,128)S(1)}, f32[16,1024]{1,0:T(8,128)S(1)}, u32[]{:S(2)}, u32[]{:S(2)}) %collective-permute-start.9) | collective-permute-done | bytes 65568 | tf_op jit(solution)/shard_map/ppermute | solution.py:9
  62.2 2.1 %collective-permute-start.13 = (f32[2,16,1024]{2,1,0:T(8,128)S(1)}, f32[2,16,1024]{2,1,0:T(8,128)S(1)}, u32[]{:S(2)}, u32[]{:S(2)}) collective-permute-start(f32[2,16,1024]{2,1,0:T(8,128)S(1)} %get-tuple-element.97), channel_id=1, source_target_pairs={{0,16},{4,20},{8,24},{12,28},{16,0},{20,4},{24,8},{28,12},{32,48},... | collective-permute-start | bytes 393224 | tf_op jit(solution)/shard_map/ppermute | solution.py:9
  64.3 3.6 %collective-permute-done.4 = f32[4,16,1024]{2,1,0:T(8,128)S(1)} collective-permute-done((f32[4,16,1024]{2,1,0:T(8,128)S(1)}, f32[4,16,1024]{2,1,0:T(8,128)S(1)}, u32[]{:S(2)}, u32[]{:S(2)}) %collective-permute-start.4) | collective-permute-done | bytes 262176 | tf_op jit(solution)/shard_map/ppermute | solution.py:9
  67.9 3.7 %collective-permute-start.14 = (f32[2,16,1024]{2,1,0:T(8,128)S(1)}, f32[2,16,1024]{2,1,0:T(8,128)S(1)}, u32[]{:S(2)}, u32[]{:S(2)}) collective-permute-start(f32[2,16,1024]{2,1,0:T(8,128)S(1)} %get-tuple-element.97), channel_id=1, source_target_pairs={{0,24},{4,28},{8,16},{12,20},{16,8},{20,12},{24,0},{28,4},{32,56},... | collective-permute-start | bytes 393224 | tf_op jit(solution)/shard_map/ppermute | solution.py:9
  73.5 2.3 %collective-permute-done.14 = f32[2,16,1024]{2,1,0:T(8,128)S(1)} collective-permute-done((f32[2,16,1024]{2,1,0:T(8,128)S(1)}, f32[2,16,1024]{2,1,0:T(8,128)S(1)}, u32[]{:S(2)}, u32[]{:S(2)}) %collective-permute-start.14) | collective-permute-done | bytes 131104 | tf_op jit(solution)/shard_map/ppermute | solution.py:9
  78.1 4.0 %fusion.72 = f32[512,1024]{1,0:T(8,128)} fusion(bf16[512,1024]{1,0:T(8,128)(2,1)} %multiply_convert_fusion.3, bf16[1024,1024]{1,0:T(8,128)(2,1)S(1)} %copy-done.2), kind=kOutput, calls=%fused_computation.135 | convolution fusion | flops 1073741824 | bytes 5242880 | tf_op jit(solution)/shard_map/dot_general | solution.py:91
  82.1 3.3 %fusion.20 = f32[1024,1024]{1,0:T(8,128)} fusion(bf16[512,1024]{1,0:T(8,128)(2,1)S(1)} %copy-done.17, bf16[1024,1024]{1,0:T(8,128)(2,1)S(1)} %copy-done.14), kind=kOutput, calls=%fused_computation.60 | convolution fusion | flops 1073741824 | bytes 6291456 | tf_op jit(solution)/shard_map/dot_general | solution.py:95
  85.4 1.9 %rev.3 = f32[2,4,16,1024]{3,2,1,0:T(8,128)} reverse(f32[2,4,16,1024]{3,2,1,0:T(8,128)} %collective-permute-done), dimensions={0} | reverse | bytes 1048576 | tf_op jit(solution)/shard_map/rev | solution.py:21
  91.0 2.7 %convolution_bitcast_fusion = f32[1024,128]{0,1:T(8,128)} fusion(bf16[1024,1024]{1,0:T(8,128)(2,1)S(1)} %copy-done.2, bf16[128,1024]{1,0:T(8,128)(2,1)} %get-tuple-element.77, s32[128]{0:T(128)S(1)} %iota_xor_fusion.1), kind=kOutput, calls=%fused_computation.44 | convolution fusion | flops 302006272 | bytes 2884096 | tf_op jit(solution)/shard_map/dot_general | solution.py:107
  95.3 3.1 %fusion.74 = f32[640,1024]{1,0:T(8,128)} fusion(bf16[640,1024]{1,0:T(8,128)(2,1)S(1)} %bitcast.165, bf16[1024,1024]{1,0:T(8,128)(2,1)S(1)} %copy-done.15), kind=kOutput, calls=%fused_computation.137 | convolution fusion | flops 1342177280 | bytes 6029312 | tf_op jit(solution)/shard_map/dot_general | solution.py:103
  98.4 3.2 %copy.46 = f32[1024,5,128]{2,0,1:T(8,128)} copy(f32[1024,5,128]{0,2,1:T(8,128)} %bitcast.162) | data formatting | bytes 5242880 | tf_op jit(solution)/shard_map/reshape | solution.py:103
  101.6 2.3 %multiply_reduce_fusion = f32[1024,128]{1,0:T(8,128)S(1)} fusion(f32[1024,5,128]{2,0,1:T(8,128)} %copy.46, f32[1024,5]{0,1:T(8,128)S(1)} %slice.387), kind=kLoop, calls=%fused_computation.12 | loop fusion | flops 1179648 | bytes 3166208 | tf_op jit(solution)/shard_map/reduce_sum | solution.py:106
  104.1 1.6 %fusion.14 = f32[1024,128]{0,1:T(8,128)S(1)} fusion(f32[1024,128]{0,1:T(8,128)} %convolution_bitcast_fusion, bf16[512,1024]{1,0:T(8,128)(2,1)S(1)} %copy-done.8, f32[512,128]{0,1:T(8,128)} %fusion.51, bf16[1024,128]{1,0:T(8,128)(2,1)} %param.20), kind=kOutput, calls=%fused_computation.43 | convolution fusion | flops 134479872 | bytes 2490368 | tf_op jit(solution)/shard_map/dot_general | solution.py:98
  106.9 4.5 %all-to-all-start = ((f32[4,256,256]{1,2,0:T(8,128)}), f32[4,256,256]{1,2,0:T(8,128)}, u32[]{:S(2)}, u32[]{:S(2)}) async-start(f32[4,256,256]{1,2,0:T(8,128)} %bitcast.160), calls=%async_computation | async-start | bytes 2097152 | tf_op jit(solution)/shard_map/all_to_all | solution.py:109
  111.4 2.7 %fusion = bf16[512,1024]{1,0:T(8,128)(2,1)S(1)} fusion(f32[512,1024]{1,0:T(8,128)} %fusion.72, bf16[5,128,1024]{2,1,0:T(8,128)(2,1)S(1)} %get-tuple-element.78, bf16[1024,5,128]{2,0,1:T(8,128)(2,1)S(1)} %copy-done.4), kind=kOutput, calls=%fused_computation.19 | convolution fusion | flops 672137216 | bytes 5111808 | tf_op jit(solution)/shard_map/dot_general | solution.py:91
  116.7 1.6 %copy-done.1 = f32[1024,1024]{1,0:T(8,128)S(1)} copy-done((f32[1024,1024]{1,0:T(8,128)S(1)}, f32[1024,1024]{1,0:T(8,128)}, u32[]{:S(2)}) %copy-start.1) | copy-done | bytes 4194328
  118.3 2.1 %add_convert_fusion = bf16[1024,1024]{1,0:T(8,128)(2,1)} fusion(f32[1024,1024]{1,0:T(8,128)S(1)} %copy-done.1, f32[512,1024]{1,0:T(8,128)S(1)} %copy-done.5, bf16[128,1024]{1,0:T(8,128)(2,1)S(1)} %copy-done.11, bf16[128,1024]{1,0:T(8,128)(2,1)S(1)} %copy-done.9), kind=kOutput, calls=%fused_computation.10 | convolution fusion | flops 271581184 | bytes 8912896 | tf_op jit(solution)/shard_map/dot_general | solution.py:100
  120.4 6.9 %all-to-all-done = f32[4,256,256]{1,2,0:T(8,128)} async-done(((f32[4,256,256]{1,2,0:T(8,128)}), f32[4,256,256]{1,2,0:T(8,128)}, u32[]{:S(2)}, u32[]{:S(2)}) %all-to-all-start) | async-done | bytes 1048608 | tf_op jit(solution)/shard_map/all_to_all | solution.py:109
  (110 shorter events, 31.0 us)
Async XLA Ops:
  6.7 5.2 %copy-start.3 = (bf16[1024,5,128]{2,0,1:T(8,128)(2,1)}, bf16[1024,5,128]{2,0,1:T(8,128)(2,1)S(1)}, u32[]{:S(2)}) copy-start(bf16[1024,5,128]{2,0,1:T(8,128)(2,1)S(1)} %multiply_convert_fusion.1) | copy-start | bytes 3932164
  8.2 3.7 %copy-start.2 = (bf16[1024,1024]{1,0:T(8,128)(2,1)S(1)}, bf16[1024,1024]{1,0:T(8,128)(2,1)}, u32[]{:S(2)}) copy-start(bf16[1024,1024]{1,0:T(8,128)(2,1)} %param.18) | copy-start | bytes 6291460
  8.2 3.7 %copy-start.10 = (bf16[128,1024]{1,0:T(8,128)(2,1)S(1)}, bf16[128,1024]{1,0:T(8,128)(2,1)}, u32[]{:S(2)}) copy-start(bf16[128,1024]{1,0:T(8,128)(2,1)} %convolution_convert_fusion) | copy-start | bytes 786436
  13.4 29.8 %collective-permute-start.1 = (f32[2,4,16,1024]{3,2,1,0:T(8,128)S(1)}, f32[2,4,16,1024]{3,2,1,0:T(8,128)S(1)}, u32[]{:S(2)}, u32[]{:S(2)}) collective-permute-start(f32[2,4,16,1024]{3,2,1,0:T(8,128)S(1)} %fusion.37), channel_id=1, source_target_pairs={{0,4},{4,0},{8,12},{12,8},{16,20},{20,16},{24,28},{28,24},{32,36},... | collective-permute-start | bytes 1572872 | tf_op jit(solution)/shard_map/ppermute | solution.py:9
  13.5 24.5 %collective-permute-start.5 = (f32[2,4,16,1024]{3,2,1,0:T(8,128)S(1)}, f32[2,4,16,1024]{3,2,1,0:T(8,128)S(1)}, u32[]{:S(2)}, u32[]{:S(2)}) collective-permute-start(f32[2,4,16,1024]{3,2,1,0:T(8,128)S(1)} %fusion.36), channel_id=1, source_target_pairs={{0,4},{4,0},{8,12},{12,8},{16,20},{20,16},{24,28},{28,24},{32,36},... | collective-permute-start | bytes 1572872 | tf_op jit(solution)/shard_map/ppermute | solution.py:9
  14.1 71.3 %collective-permute-start = (f32[2,4,16,1024]{3,2,1,0:T(8,128)}, f32[2,4,16,1024]{3,2,1,0:T(8,128)}, u32[]{:S(2)}, u32[]{:S(2)}) collective-permute-start(f32[2,4,16,1024]{3,2,1,0:T(8,128)} %bitcast.13), channel_id=1, source_target_pairs={{0,4},{4,0},{8,12},{12,8},{16,20},{20,16},{24,28},{28,24},{32,36},... | collective-permute-start | bytes 1572872 | tf_op jit(solution)/shard_map/ppermute | solution.py:9
  14.9 2.7 %copy-start.16 = (bf16[1024,128]{1,0:T(8,128)(2,1)S(1)}, bf16[1024,128]{1,0:T(8,128)(2,1)}, u32[]{:S(2)}) copy-start(bf16[1024,128]{1,0:T(8,128)(2,1)} %param.19) | copy-start | bytes 786436
  14.9 2.7 %copy-start.18 = (bf16[1024,128]{1,0:T(8,128)(2,1)S(1)}, bf16[1024,128]{1,0:T(8,128)(2,1)}, u32[]{:S(2)}) copy-start(bf16[1024,128]{1,0:T(8,128)(2,1)} %param.20) | copy-start | bytes 786436
  25.9 9.9 %copy-start.7 = (bf16[512,1024]{1,0:T(8,128)(2,1)}, bf16[512,1024]{1,0:T(8,128)(2,1)S(1)}, u32[]{:S(2)}) copy-start(bf16[512,1024]{1,0:T(8,128)(2,1)S(1)} %multiply_convert_fusion.2) | copy-start | bytes 3145732
  38.1 7.9 %collective-permute-start.6 = (f32[2,16,1024]{2,1,0:T(8,128)S(1)}, f32[2,16,1024]{2,1,0:T(8,128)S(1)}, u32[]{:S(2)}, u32[]{:S(2)}) collective-permute-start(f32[2,16,1024]{2,1,0:T(8,128)S(1)} %get-tuple-element.87), channel_id=1, source_target_pairs={{0,16},{4,20},{8,24},{12,28},{16,0},{20,4},{24,8},{28,12},{32,48},... | collective-permute-start | bytes 393224 | tf_op jit(solution)/shard_map/ppermute | solution.py:9
  42.1 6.3 %collective-permute-start.8 = (f32[2,16,1024]{2,1,0:T(8,128)S(1)}, f32[2,16,1024]{2,1,0:T(8,128)S(1)}, u32[]{:S(2)}, u32[]{:S(2)}) collective-permute-start(f32[2,16,1024]{2,1,0:T(8,128)S(1)} %get-tuple-element.88), channel_id=1, source_target_pairs={{0,24},{4,28},{8,16},{12,20},{16,8},{20,12},{24,0},{28,4},{32,56},... | collective-permute-start | bytes 393224 | tf_op jit(solution)/shard_map/ppermute | solution.py:9
  42.8 6.4 %collective-permute-start.7 = (f32[2,16,1024]{2,1,0:T(8,128)S(1)}, f32[2,16,1024]{2,1,0:T(8,128)S(1)}, u32[]{:S(2)}, u32[]{:S(2)}) collective-permute-start(f32[2,16,1024]{2,1,0:T(8,128)S(1)} %get-tuple-element.89), channel_id=1, source_target_pairs={{0,8},{4,12},{8,0},{12,4},{16,24},{20,28},{24,16},{28,20},{32,40},... | collective-permute-start | bytes 393224 | tf_op jit(solution)/shard_map/ppermute | solution.py:9
  49.3 6.9 %collective-permute-start.11 = (f32[16,1024]{1,0:T(8,128)S(1)}, f32[16,1024]{1,0:T(8,128)S(1)}, u32[]{:S(2)}, u32[]{:S(2)}) collective-permute-start(f32[16,1024]{1,0:T(8,128)S(1)} %get-tuple-element.99), channel_id=1, source_target_pairs={{0,96},{4,100},{8,104},{12,108},{16,112},{20,116},{24,120},{28,124... | collective-permute-start | bytes 196616 | tf_op jit(solution)/shard_map/ppermute | solution.py:9
  52.1 5.8 %collective-permute-start.10 = (f32[16,1024]{1,0:T(8,128)S(1)}, f32[16,1024]{1,0:T(8,128)S(1)}, u32[]{:S(2)}, u32[]{:S(2)}) collective-permute-start(f32[16,1024]{1,0:T(8,128)S(1)} %get-tuple-element.99), channel_id=1, source_target_pairs={{0,64},{4,68},{8,72},{12,76},{16,80},{20,84},{24,88},{28,92},{32,9... | collective-permute-start | bytes 196616 | tf_op jit(solution)/shard_map/ppermute | solution.py:9
  53.0 14.9 %collective-permute-start.4 = (f32[4,16,1024]{2,1,0:T(8,128)S(1)}, f32[4,16,1024]{2,1,0:T(8,128)S(1)}, u32[]{:S(2)}, u32[]{:S(2)}) collective-permute-start(f32[4,16,1024]{2,1,0:T(8,128)S(1)} %get-tuple-element.82), channel_id=1, source_target_pairs={{0,24},{4,28},{8,16},{12,20},{16,8},{20,12},{24,0},{28,4},{32,56},... | collective-permute-start | bytes 786440 | tf_op jit(solution)/shard_map/ppermute | solution.py:9
  55.6 12.2 %collective-permute-start.3 = (f32[4,16,1024]{2,1,0:T(8,128)S(1)}, f32[4,16,1024]{2,1,0:T(8,128)S(1)}, u32[]{:S(2)}, u32[]{:S(2)}) collective-permute-start(f32[4,16,1024]{2,1,0:T(8,128)S(1)} %get-tuple-element.82), channel_id=1, source_target_pairs={{0,16},{4,20},{8,24},{12,28},{16,0},{20,4},{24,8},{28,12},{32,48},... | collective-permute-start | bytes 786440 | tf_op jit(solution)/shard_map/ppermute | solution.py:9
  56.1 15.4 %collective-permute-start.2 = (f32[4,16,1024]{2,1,0:T(8,128)S(1)}, f32[4,16,1024]{2,1,0:T(8,128)S(1)}, u32[]{:S(2)}, u32[]{:S(2)}) collective-permute-start(f32[4,16,1024]{2,1,0:T(8,128)S(1)} %get-tuple-element.81), channel_id=1, source_target_pairs={{0,8},{4,12},{8,0},{12,4},{16,24},{20,28},{24,16},{28,20},{32,40},... | collective-permute-start | bytes 786440 | tf_op jit(solution)/shard_map/ppermute | solution.py:9
  57.9 4.3 %collective-permute-start.9 = (f32[16,1024]{1,0:T(8,128)S(1)}, f32[16,1024]{1,0:T(8,128)S(1)}, u32[]{:S(2)}, u32[]{:S(2)}) collective-permute-start(f32[16,1024]{1,0:T(8,128)S(1)} %get-tuple-element.98), channel_id=1, source_target_pairs={{0,32},{4,36},{8,40},{12,44},{16,48},{20,52},{24,56},{28,60},{32,0... | collective-permute-start | bytes 196616 | tf_op jit(solution)/shard_map/ppermute | solution.py:9
  62.2 10.9 %collective-permute-start.13 = (f32[2,16,1024]{2,1,0:T(8,128)S(1)}, f32[2,16,1024]{2,1,0:T(8,128)S(1)}, u32[]{:S(2)}, u32[]{:S(2)}) collective-permute-start(f32[2,16,1024]{2,1,0:T(8,128)S(1)} %get-tuple-element.97), channel_id=1, source_target_pairs={{0,16},{4,20},{8,24},{12,28},{16,0},{20,4},{24,8},{28,12},{32,48},... | collective-permute-start | bytes 393224 | tf_op jit(solution)/shard_map/ppermute | solution.py:9
  67.9 5.6 %collective-permute-start.12 = (f32[2,16,1024]{2,1,0:T(8,128)S(1)}, f32[2,16,1024]{2,1,0:T(8,128)S(1)}, u32[]{:S(2)}, u32[]{:S(2)}) collective-permute-start(f32[2,16,1024]{2,1,0:T(8,128)S(1)} %get-tuple-element.97), channel_id=1, source_target_pairs={{0,8},{4,12},{8,0},{12,4},{16,24},{20,28},{24,16},{28,20},{32,40},... | collective-permute-start | bytes 393224 | tf_op jit(solution)/shard_map/ppermute | solution.py:9
  67.9 7.9 %collective-permute-start.14 = (f32[2,16,1024]{2,1,0:T(8,128)S(1)}, f32[2,16,1024]{2,1,0:T(8,128)S(1)}, u32[]{:S(2)}, u32[]{:S(2)}) collective-permute-start(f32[2,16,1024]{2,1,0:T(8,128)S(1)} %get-tuple-element.97), channel_id=1, source_target_pairs={{0,24},{4,28},{8,16},{12,20},{16,8},{20,12},{24,0},{28,4},{32,56},... | collective-permute-start | bytes 393224 | tf_op jit(solution)/shard_map/ppermute | solution.py:9
  77.0 10.2 %collective-permute-start.15 = (f32[4,4,16,1024]{3,2,0,1:T(8,128)}, f32[4,4,16,1024]{3,2,0,1:T(8,128)}, u32[]{:S(2)}, u32[]{:S(2)}) collective-permute-start(f32[4,4,16,1024]{3,2,0,1:T(8,128)} %get-tuple-element.80), channel_id=1, source_target_pairs={{0,4},{4,0},{8,12},{12,8},{16,20},{20,16},{24,28},{28,24},{32,36},... | collective-permute-start | bytes 3145736 | tf_op jit(solution)/shard_map/ppermute | solution.py:9
  78.1 4.0 %copy-start.14 = (bf16[1024,1024]{1,0:T(8,128)(2,1)S(1)}, bf16[1024,1024]{1,0:T(8,128)(2,1)}, u32[]{:S(2)}) copy-start(bf16[1024,1024]{1,0:T(8,128)(2,1)} %param.21) | copy-start | bytes 6291460
  78.1 4.0 %copy-start.17 = (bf16[512,1024]{1,0:T(8,128)(2,1)S(1)}, bf16[512,1024]{1,0:T(8,128)(2,1)}, u32[]{:S(2)}) copy-start(bf16[512,1024]{1,0:T(8,128)(2,1)} %multiply_convert_fusion.3) | copy-start | bytes 3145732
  101.6 2.5 %copy-start.8 = (bf16[512,1024]{1,0:T(8,128)(2,1)S(1)}, bf16[512,1024]{1,0:T(8,128)(2,1)}, u32[]{:S(2)}) copy-start(bf16[512,1024]{1,0:T(8,128)(2,1)} %copy-done.7) | copy-start | bytes 3145732
  105.8 5.6 %copy-start.4 = (bf16[1024,5,128]{2,0,1:T(8,128)(2,1)S(1)}, bf16[1024,5,128]{2,0,1:T(8,128)(2,1)}, u32[]{:S(2)}) copy-start(bf16[1024,5,128]{2,0,1:T(8,128)(2,1)} %copy-done.3) | copy-start | bytes 3932164
  106.9 20.4 %all-to-all-start = ((f32[4,256,256]{1,2,0:T(8,128)}), f32[4,256,256]{1,2,0:T(8,128)}, u32[]{:S(2)}, u32[]{:S(2)}) async-start(f32[4,256,256]{1,2,0:T(8,128)} %bitcast.160), calls=%async_computation | async-start | bytes 2097152 | tf_op jit(solution)/shard_map/all_to_all | solution.py:109
  111.4 2.8 %copy-start.6 = (f32[512,1024]{1,0:T(8,128)S(1)}, f32[512,1024]{1,0:T(8,128)}, u32[]{:S(2)}) copy-start(f32[512,1024]{1,0:T(8,128)} %fusion.26) | copy-start | bytes 6291460
  114.2 2.5 %copy-start.5 = (f32[512,1024]{1,0:T(8,128)S(1)}, f32[512,1024]{1,0:T(8,128)}, u32[]{:S(2)}) copy-start(f32[512,1024]{1,0:T(8,128)} %fusion.23) | copy-start | bytes 6291460
  114.2 2.5 %copy-start.9 = (bf16[128,1024]{1,0:T(8,128)(2,1)S(1)}, bf16[128,1024]{1,0:T(8,128)(2,1)}, u32[]{:S(2)}) copy-start(bf16[128,1024]{1,0:T(8,128)(2,1)} %get-tuple-element.77) | copy-start | bytes 786436
  114.2 2.5 %copy-start.11 = (bf16[128,1024]{1,0:T(8,128)(2,1)S(1)}, bf16[128,1024]{1,0:T(8,128)(2,1)}, u32[]{:S(2)}) copy-start(bf16[128,1024]{1,0:T(8,128)(2,1)} %convolution_convert_fusion) | copy-start | bytes 786436
  115.2 3.1 %copy-start.1 = (f32[1024,1024]{1,0:T(8,128)S(1)}, f32[1024,1024]{1,0:T(8,128)}, u32[]{:S(2)}) copy-start(f32[1024,1024]{1,0:T(8,128)} %fusion.20) | copy-start | bytes 12582916
  (6 other events, 8.1 us)

commit v2 on v1

v2 whole, which is shorter than its diff:
```python
import jax
import jax.numpy as jnp
from jax import lax
from jax.experimental import pallas as pl
from jax.experimental.pallas import tpu as pltpu
from jax.sharding import PartitionSpec as P

F32, BF16 = jnp.float32, jnp.bfloat16
CORE, Z, X = 1, (0, 2, 4, 6), (0, 8, 16, 24)
TILE = 256
VMEM = pl.BlockSpec(memory_space=pltpu.VMEM)
SMEM = pl.BlockSpec(memory_space=pltpu.SMEM)


def from_xor(block, flip):
    route = [(i, i ^ flip) for i in range(lax.axis_size("ctx"))]
    return lax.ppermute(block, "ctx", route)


def dot_nt(a, b):
    return lax.dot_general(a, b, (((1,), (1,)), ((), ())), preferred_element_type=F32)


def dot_tn(a, b):
    return lax.dot_general(a, b, (((0,), (0,)), ((), ())), preferred_element_type=F32)


def dot_nn(a, b):
    return jnp.dot(a, b, preferred_element_type=F32)


def one_hot(level_ref, rows):
    ids = lax.broadcasted_iota(jnp.int32, (rows, level_ref.shape[1]), 0)
    return (ids == level_ref[...]).astype(F32)


def call(kernel, out_shape, in_specs, flops, scratch=()):
    return pl.pallas_call(
        kernel,
        out_shape=out_shape,
        in_specs=in_specs,
        out_specs=jax.tree.map(lambda _: VMEM, out_shape),
        scratch_shapes=list(scratch),
        compiler_params=pltpu.CompilerParams(vmem_limit_bytes=32 << 20),
        cost_estimate=pl.CostEstimate(flops=flops, bytes_accessed=8 << 20, transcendentals=0),
    )


def own_bits(me):
    return [lax.shift_right_logical(me, k) & 1 for k in range(5)]


def row_mask(me):
    bits = own_bits(me)
    return bits[0] * 64 + bits[2] * 32 + bits[1] * 16


def state_kernel(me_ref, x_ref, b_ref, c_ref, d_ref, table_t_ref, level_ref, a0_ref, near_keep, near_send, far_keep, far_send, left):
    me = me_ref[0]
    bits = own_bits(me)
    n = b_ref.shape[1]
    rows = lax.broadcasted_iota(jnp.int32, (n, n), 0)
    cols = lax.broadcasted_iota(jnp.int32, (n, n), 1)
    perm = (cols == (rows ^ row_mask(me))).astype(F32).astype(BF16)
    c_t = dot_nt(perm, c_ref[...])
    b_t = dot_nt(perm, b_ref[...]).astype(BF16)
    lam_t = jnp.dot(table_t_ref[...], one_hot(level_ref, table_t_ref.shape[1]), precision=lax.Precision.HIGHEST, preferred_element_type=F32)
    for k in range(5):
        left[k * n : (k + 1) * n, :] = (lam_t[11 + k : 12 + k, :] * c_t).astype(BF16)
    half = n // 2
    for at in range(0, x_ref.shape[1], TILE):
        here = slice(at, at + TILE)
        state = dot_nn(b_t, x_ref[:, here])
        grads = dot_nn(left[...], d_ref[:, here])
        for k in range(5):
            value = jnp.where(bits[k] == 1, grads[k * n : (k + 1) * n], state)
            if k == 0:
                a0_ref[:, here] = value
                continue
            keep, send = (near_keep, near_send) if k < 3 else (far_keep, far_send)
            keep[(k - 1) % 2, :, here] = value[:half]
            send[(k - 1) % 2, :, here] = value[half:]


def local_kernel(x_ref, b_ref, c_ref, d_ref, table_ref, level_ref, mix_ref, grad_b_ref, grad_c_ref):
    lam = lax.dot_general(
        one_hot(level_ref, table_ref.shape[0]),
        table_ref[...],
        (((0,), (0,)), ((), ())),
        precision=lax.Precision.HIGHEST,
        preferred_element_type=F32,
    )
    rows = lax.broadcasted_iota(jnp.int32, (TILE, TILE), 0)
    cols = lax.broadcasted_iota(jnp.int32, (TILE, TILE), 1)
    gap = rows ^ cols
    tiles = x_ref.shape[0] // TILE
    for i in range(tiles):
        mine = slice(i * TILE, (i + 1) * TILE)
        lam_i = lam[mine]
        c_i = c_ref[mine, :]
        d_i = d_ref[mine, :]
        grad_c = None
        for j in range(i + 1):
            theirs = slice(j * TILE, (j + 1) * TILE)
            b_j = b_ref[theirs, :]
            if j == i:
                weight = jnp.broadcast_to(lam_i[:, 0:1], (TILE, TILE))
                for level in range(1, 9):
                    weight = jnp.where(gap >= (1 << (level - 1)), lam_i[:, level : level + 1], weight)
                weight = jnp.where(cols <= rows, weight, 0.0)
            else:
                level = 8 + (i ^ j).bit_length()
                weight = lam_i[:, level : level + 1]
            mix_ref[mine, theirs] = (dot_nt(c_i, b_j) * weight).astype(BF16)
            d_mix = (dot_nt(d_i, x_ref[theirs, :]) * weight).astype(BF16)
            term = dot_nn(d_mix, b_j)
            grad_c = term if grad_c is None else grad_c + term
            back = dot_tn(d_mix, c_i)
            if j == i:
                grad_b_ref[theirs, :] = back
            else:
                grad_b_ref[theirs, :] += back
        grad_c_ref[mine, :] = grad_c


def grad_kernel(me_ref, b0_ref, near_ref, near_other, far_ref, far_other, x_ref, d_ref, table_ref, level_ref, gb_ref, gc_ref, both_ref, carry_ref, back_ref):
    me = me_ref[0]
    bits = own_bits(me)
    mask = row_mask(me) // 16
    n = gb_ref.shape[1]
    for p in range(8):
        to = pl.ds(pl.multiple_of((p ^ mask) * 16, 16), 16)
        half, q = p // 4, slice(p % 4 * 16, p % 4 * 16 + 16)
        q0 = slice((p ^ 4) * 16, (p ^ 4) * 16 + 16)
        near, far = (near_ref, far_ref) if half == 0 else (near_other, far_other)
        parts = [b0_ref[q0, :], near[0, q, :], near[1, q, :], far[0, q, :], far[1, q, :]]
        back = None
        for k in range(5):
            carry_ref[k, to, :] = jnp.where(bits[k] == 1, parts[k], 0.0).astype(BF16)
            low = jnp.where(bits[k] == 1, 0.0, parts[k])
            back = low if back is None else back + low
        back_ref[to, :] = back.astype(BF16)
    lam = lax.dot_general(
        one_hot(level_ref, table_ref.shape[0]),
        table_ref[...],
        (((0,), (0,)), ((), ())),
        precision=lax.Precision.HIGHEST,
        preferred_element_type=F32,
    )
    for i in range(x_ref.shape[0] // TILE):
        mine = slice(i * TILE, (i + 1) * TILE)
        d_i = d_ref[mine, :]
        grad_c = gc_ref[mine, :]
        for k in range(5):
            grad_c = grad_c + dot_nt(d_i, carry_ref[k]) * lam[mine, 11 + k : 12 + k]
        both_ref[i, 1] = grad_c
        both_ref[i, 0] = gb_ref[mine, :] + dot_nt(x_ref[mine, :], back_ref[...])


def output_kernel(mix_ref, x_ref, b_ref, c_ref, d_ref, table_ref, level_ref, carry_ref, back_ref, y_ref, dx_ref):
    lam = lax.dot_general(
        one_hot(level_ref, table_ref.shape[0]),
        table_ref[...],
        (((0,), (0,)), ((), ())),
        precision=lax.Precision.HIGHEST,
        preferred_element_type=F32,
    )
    rows = x_ref.shape[0]
    for i in range(rows // TILE):
        mine = slice(i * TILE, (i + 1) * TILE)
        c_i = c_ref[mine, :].astype(F32)
        total = dot_nn(mix_ref[mine, : (i + 1) * TILE], x_ref[: (i + 1) * TILE, :])
        rising = jnp.concatenate([(c_i * lam[mine, 11 + k : 12 + k]).astype(BF16) for k in range(5)], axis=1)
        carry = carry_ref[...].reshape(5 * carry_ref.shape[1], carry_ref.shape[2])
        y_ref[mine, :] = (total + dot_nn(rising, carry)).astype(BF16)
        total = dot_tn(mix_ref[i * TILE :, mine], d_ref[i * TILE :, :])
        dx_ref[mine, :] = (total + dot_nn(b_ref[mine, :], back_ref[...])).astype(BF16)


def sum_kernel(parts_ref, d_b_ref, d_c_ref):
    d_b_ref[...] = parts_ref[0, 0] + parts_ref[1, 0] + parts_ref[2, 0] + parts_ref[3, 0]
    d_c_ref[...] = parts_ref[0, 1] + parts_ref[1, 1] + parts_ref[2, 1] + parts_ref[3, 1]


def local(x_in, b_in, c_in, d_out, table, level_index):
    rows, width = x_in.shape
    n = b_in.shape[1]
    me = lax.axis_index("ctx").reshape(1)
    level = level_index.reshape(1, rows)
    shape = jax.ShapeDtypeStruct
    half = shape((2, n // 2, width), F32)
    a0, near_keep, near_send, far_keep, far_send = call(
        state_kernel,
        (shape((n, width), F32), half, half, half, half),
        [SMEM] + [VMEM] * 6,
        2 * rows * width * n * 6,
        [pltpu.VMEM((5 * n, rows), BF16)],
    )(me, x_in, b_in, c_in, d_out, table.T, level)
    far = (far_keep + from_xor(far_send, CORE)).reshape(2, 4, n // 8, width)
    near = near_keep + from_xor(near_send, CORE)
    b0 = from_xor(a0, CORE)
    total = far[:, 0]
    for m in (2, 1, 3):
        total = total + from_xor(far[:, m], Z[m])
    b3 = from_xor(total[0], X[1])
    b4 = from_xor(total[1], X[2]) + from_xor(total[1], X[3])
    b34 = jnp.stack([b3, b4])
    near = near.reshape(2, 4, n // 8, width)
    r1, r2, r3 = from_xor(near[0], Z[1]), from_xor(near[1], Z[2]), from_xor(near[1], Z[3])
    near = jnp.stack([jnp.stack([r1[p ^ 1] for p in range(4)]), jnp.stack([r2[p ^ 2] + r3[p ^ 3] for p in range(4)])])
    far = jnp.stack([b34] + [from_xor(b34, Z[m]) for m in (1, 2, 3)], axis=1)
    near, far = near.reshape(2, n // 2, width), far.reshape(2, n // 2, width)
    near_other, far_other = from_xor(near, CORE), from_xor(far, CORE)

    mix, grad_b, grad_c = call(
        local_kernel,
        (shape((rows, rows), BF16), shape((rows, n), F32), shape((rows, n), F32)),
        [VMEM] * 6,
        2 * rows * rows * width // 2,
    )(x_in, b_in, c_in, d_out, table, level)
    both, carry, back = call(
        grad_kernel,
        (shape((4, 2, rows // 4, n), F32), shape((5, n, width), BF16), shape((n, width), BF16)),
        [SMEM] + [VMEM] * 11,
        2 * rows * width * n * 6,
    )(me, b0, near, near_other, far, far_other, x_in, d_out, table, level, grad_b, grad_c)
    parts = lax.all_to_all(both, "head", 0, 0, tiled=True)
    y_out, dx_out = call(
        output_kernel,
        (shape((rows, width), BF16), shape((rows, width), BF16)),
        [VMEM] * 9,
        2 * rows * width * n * 6 + 2 * rows * rows * width,
    )(mix, x_in, b_in, c_in, d_out, table, level, carry, back)
    d_b, d_c = call(sum_kernel, (shape((rows // 4, n), F32), shape((rows // 4, n), F32)), [VMEM], rows * n)(parts)
    return (y_out, dx_out, d_b, d_c)


def solution(mesh):
    return jax.shard_map(
        local,
        mesh=mesh,
        in_specs=(P("ctx", "head"), P("ctx", None), P("ctx", None), P("ctx", "head"), P(), P("ctx")),
        out_specs=(P("ctx", "head"), P("ctx", "head"), P(("ctx", "head"), None), P(("ctx", "head"), None)),
        check_vma=False,
    )
```

time: 131 us -> 87.7 us (0.67)
  matrix products: 54.2 us -> 0 us
  Pallas kernels: 0 us -> 21.5 us
  other arithmetic: 10.4 us -> 0.33 us
  waiting for transfers between devices: 25.4 us -> 22.8 us
  local copies, waits for them, and re-layouts: 14.8 us -> 17.1 us
    dot_general x21 -> x0, matrix products: 51.1 us -> none  [the longest x2 8.43 us: local(): jnp.dot(c_in[row_start:row_stop], b_in[:row_stop].T, preferred_element_ty...]
    pallas_call x0 -> x5, Pallas kernels: none -> 21.5 us  [the longest x1 8.19 us: local(): call(output_kernel, (shape((rows, width), BF16), shape((rows, width), BF1...]
    unnamed x44 -> x39, local copies, waits for them, and re-layouts: 6.19 us -> 17 us
    all_to_all x1, waiting for transfers between devices: 6.92 us -> 1.14 us  [local(): parts = lax.all_to_all(both, 'head', 0, 0, tiled=True)]
    reduce_sum x3 -> x0, other arithmetic: 4.79 us -> none  [the longest x1 2.27 us: local(): jnp.sum(far_terms * far_lam[:, :, None], axis=1)]
    reshape x2 -> x0, local copies, waits for them, and re-layouts: 4.34 us -> none  [the longest x1 3.24 us: local(): jnp.dot(d_out, carry_nat.reshape(ctx_bits * nstate, feat_width).T, prefer...]
    unnamed x2 -> x0, matrix products: 3.11 us -> none
    ppermute x16 -> x17, waiting for transfers between devices: 18.5 us -> 21.6 us  [from_xor(): return lax.ppermute(block, 'ctx', route)]
  transfers between devices with their start and end apart: 17 -> 18, of which waited for: 10 -> 10; matrix products, arithmetic and copies ran while one was open for 32% -> 0% of each run, Pallas kernels for 0% -> 17%
where the time goes in v2:
time: 87.7 us; the launch traced here: 86.9 us
  starting transfers between devices  24.3 us (28%)
  waiting for transfers between devices  22.8 us (26%)
  Pallas kernels  21.5 us (25%)
  local copies, waits for them, and re-layouts  17.1 us (19%)
  between operations  0.88 us (1%)
    ppermute x17, waiting for transfers between devices, from_xor(): return lax.ppermute(block, 'ctx', route)  21.6 us
    ppermute x17, starting transfers between devices, from_xor(): return lax.ppermute(block, 'ctx', route)  19.7 us
    unnamed x39, local copies, waits for them, and re-layouts  17 us
    pallas_call x1, Pallas kernels, local(): call(output_kernel, (shape((rows, width), BF16), shape((rows, width), BF1...  8.19 us
    pallas_call x1, Pallas kernels, local(): call(local_kernel, (shape((rows, rows), BF16), shape((rows, n), F32), sha...  6.27 us
    all_to_all x1, starting transfers between devices, local(): parts = lax.all_to_all(both, 'head', 0, 0, tiled=True)  4.59 us
    pallas_call x1, Pallas kernels, local(): call(grad_kernel, (shape((4, 2, rows // 4, n), F32), shape((5, n, width),...  4.16 us
    pallas_call x1, Pallas kernels, local(): call(state_kernel, (shape((n, width), F32), half, half, half, half), [SME...  2.12 us
  transfers between devices with their start and end apart: 18, of which 10 were waited for; matrix products, arithmetic and copies ran while one was open for 0% of the time, Pallas kernels for 17%

profile of v2, /device:TPU:0, one launch (start us, length us, event | category | flops | bytes accessed | tf_op | source)
XLA Modules:
  0.0 86.9 jit_solution(6523103011128438148)
XLA Ops:
  1.4 1.6 %copy-done = bf16[1024,1024]{1,0:T(8,128)(2,1)S(1)} copy-done((bf16[1024,1024]{1,0:T(8,128)(2,1)S(1)}, bf16[1024,1024]{1,0:T(8,128)(2,1)}, u32[]{:S(2)}) %copy-start) | copy-done | bytes 2097176
  3.0 1.6 %copy-done.2 = bf16[1024,1024]{1,0:T(8,128)(2,1)S(1)} copy-done((bf16[1024,1024]{1,0:T(8,128)(2,1)S(1)}, bf16[1024,1024]{1,0:T(8,128)(2,1)}, u32[]{:S(2)}) %copy-start.2) | copy-done | bytes 2097176
  5.6 0.9 %copy-done.8 = bf16[1024,128]{1,0:T(8,128)(2,1)S(1)} copy-done((bf16[1024,128]{1,0:T(8,128)(2,1)S(1)}, bf16[1024,128]{1,0:T(8,128)(2,1)}, u32[]{:S(2)}) %copy-start.8) | copy-done | bytes 262168
  7.2 2.1 %shard_map.94 = (f32[128,1024]{1,0:T(8,128)S(1)}, f32[2,64,1024]{2,1,0:T(8,128)S(1)}, f32[2,64,1024]{2,1,0:T(8,128)S(1)}, f32[2,64,1024]{2,1,0:T(8,128)S(1)}, f32[2,64,1024]{2,1,0:T(8,128)S(1)}) custom-call(s32[1]{0:T(128)} %bitcast.1.me_ref, bf16[1024,1024]{1,0:T(8,128)(2,1)S(1)} %copy-done, bf16[1024,128]{1,0:T(8,128)(2,1)S(1)} %copy-done.6, ...), custom_call_target="tpu_custom_call" | custom-call | flops 1610612736 | bytes 8388608 | tf_op jit(solution)/shard_map/pallas_call | solution.py:192
  9.9 1.4 %collective-permute-done.6 = f32[2,64,1024]{2,1,0:T(8,128)S(1)} collective-permute-done((f32[2,64,1024]{2,1,0:T(8,128)S(1)}, f32[2,64,1024]{2,1,0:T(8,128)S(1)}, u32[]{:S(2)}, u32[]{:S(2)}) %collective-permute-start.6) | collective-permute-done | bytes 524320 | tf_op jit(solution)/shard_map/ppermute | solution.py:17
  11.4 4.0 %collective-permute-start.7 = (f32[2,16,1024]{2,1,0:T(8,128)S(1)}, f32[2,16,1024]{2,1,0:T(8,128)S(1)}, u32[]{:S(2)}, u32[]{:S(2)}) collective-permute-start(f32[2,16,1024]{2,1,0:T(8,128)S(1)} %get-tuple-element.34), channel_id=1, source_target_pairs={{0,16},{4,20},{8,24},{12,28},{16,0},{20,4},{24,8},{28,12},{32,48},... | collective-permute-start | bytes 393224 | tf_op jit(solution)/shard_map/ppermute | solution.py:17
  15.4 1.0 %collective-permute-start.8 = (f32[2,16,1024]{2,1,0:T(8,128)S(1)}, f32[2,16,1024]{2,1,0:T(8,128)S(1)}, u32[]{:S(2)}, u32[]{:S(2)}) collective-permute-start(f32[2,16,1024]{2,1,0:T(8,128)S(1)} %get-tuple-element.35), channel_id=1, source_target_pairs={{0,8},{4,12},{8,0},{12,4},{16,24},{20,28},{24,16},{28,20},{32,40},... | collective-permute-start | bytes 393224 | tf_op jit(solution)/shard_map/ppermute | solution.py:17
  16.5 3.2 %collective-permute-done.7 = f32[2,16,1024]{2,1,0:T(8,128)S(1)} collective-permute-done((f32[2,16,1024]{2,1,0:T(8,128)S(1)}, f32[2,16,1024]{2,1,0:T(8,128)S(1)}, u32[]{:S(2)}, u32[]{:S(2)}) %collective-permute-start.7) | collective-permute-done | bytes 131104 | tf_op jit(solution)/shard_map/ppermute | solution.py:17
  19.7 3.1 %collective-permute-done.8 = f32[2,16,1024]{2,1,0:T(8,128)S(1)} collective-permute-done((f32[2,16,1024]{2,1,0:T(8,128)S(1)}, f32[2,16,1024]{2,1,0:T(8,128)S(1)}, u32[]{:S(2)}, u32[]{:S(2)}) %collective-permute-start.8) | collective-permute-done | bytes 131104 | tf_op jit(solution)/shard_map/ppermute | solution.py:17
  22.9 2.8 %collective-permute-start.12 = (f32[16,1024]{1,0:T(8,128)S(1)}, f32[16,1024]{1,0:T(8,128)S(1)}, u32[]{:S(2)}, u32[]{:S(2)}) collective-permute-start(f32[16,1024]{1,0:T(8,128)S(1)} %get-tuple-element.50), channel_id=1, source_target_pairs={{0,96},{4,100},{8,104},{12,108},{16,112},{20,116},{24,120},{28,124... | collective-permute-start | bytes 196616 | tf_op jit(solution)/shard_map/ppermute | solution.py:17
  26.5 2.7 %collective-permute-start.4 = (f32[4,16,1024]{2,1,0:T(8,128)S(1)}, f32[4,16,1024]{2,1,0:T(8,128)S(1)}, u32[]{:S(2)}, u32[]{:S(2)}) collective-permute-start(f32[4,16,1024]{2,1,0:T(8,128)S(1)} %bitcast.60), channel_id=1, source_target_pairs={{0,24},{4,28},{8,16},{12,20},{16,8},{20,12},{24,0},{28,4},{32,56},... | collective-permute-start | bytes 786440 | tf_op jit(solution)/shard_map/ppermute | solution.py:17
  29.7 1.0 %collective-permute-start.2 = (f32[4,16,1024]{2,1,0:T(8,128)S(1)}, f32[4,16,1024]{2,1,0:T(8,128)S(1)}, u32[]{:S(2)}, u32[]{:S(2)}) collective-permute-start(f32[4,16,1024]{2,1,0:T(8,128)S(1)} %bitcast.62), channel_id=1, source_target_pairs={{0,8},{4,12},{8,0},{12,4},{16,24},{20,28},{24,16},{28,20},{32,40},... | collective-permute-start | bytes 786440 | tf_op jit(solution)/shard_map/ppermute | solution.py:17
  31.7 4.0 %collective-permute-done.10 = f32[16,1024]{1,0:T(8,128)S(1)} collective-permute-done((f32[16,1024]{1,0:T(8,128)S(1)}, f32[16,1024]{1,0:T(8,128)S(1)}, u32[]{:S(2)}, u32[]{:S(2)}) %collective-permute-start.10) | collective-permute-done | bytes 65568 | tf_op jit(solution)/shard_map/ppermute | solution.py:17
  35.8 2.6 %collective-permute-start.14 = (f32[2,16,1024]{2,1,0:T(8,128)S(1)}, f32[2,16,1024]{2,1,0:T(8,128)S(1)}, u32[]{:S(2)}, u32[]{:S(2)}) collective-permute-start(f32[2,16,1024]{2,1,0:T(8,128)S(1)} %get-tuple-element.48), channel_id=1, source_target_pairs={{0,16},{4,20},{8,24},{12,28},{16,0},{20,4},{24,8},{28,12},{32,48},... | collective-permute-start | bytes 393224 | tf_op jit(solution)/shard_map/ppermute | solution.py:17
  38.3 5.2 %collective-permute-done.2 = f32[4,16,1024]{2,1,0:T(8,128)S(1)} collective-permute-done((f32[4,16,1024]{2,1,0:T(8,128)S(1)}, f32[4,16,1024]{2,1,0:T(8,128)S(1)}, u32[]{:S(2)}, u32[]{:S(2)}) %collective-permute-start.2) | collective-permute-done | bytes 262176 | tf_op jit(solution)/shard_map/ppermute | solution.py:17
  43.6 1.0 %collective-permute-start.13 = (f32[2,16,1024]{2,1,0:T(8,128)S(1)}, f32[2,16,1024]{2,1,0:T(8,128)S(1)}, u32[]{:S(2)}, u32[]{:S(2)}) collective-permute-start(f32[2,16,1024]{2,1,0:T(8,128)S(1)} %get-tuple-element.48), channel_id=1, source_target_pairs={{0,8},{4,12},{8,0},{12,4},{16,24},{20,28},{24,16},{28,20},{32,40},... | collective-permute-start | bytes 393224 | tf_op jit(solution)/shard_map/ppermute | solution.py:17
  44.6 2.1 %collective-permute-start.15 = (f32[2,16,1024]{2,1,0:T(8,128)S(1)}, f32[2,16,1024]{2,1,0:T(8,128)S(1)}, u32[]{:S(2)}, u32[]{:S(2)}) collective-permute-start(f32[2,16,1024]{2,1,0:T(8,128)S(1)} %get-tuple-element.48), channel_id=1, source_target_pairs={{0,24},{4,28},{8,16},{12,20},{16,8},{20,12},{24,0},{28,4},{32,56},... | collective-permute-start | bytes 393224 | tf_op jit(solution)/shard_map/ppermute | solution.py:17
  47.0 1.1 %collective-permute-done.14 = f32[2,16,1024]{2,1,0:T(8,128)S(1)} collective-permute-done((f32[2,16,1024]{2,1,0:T(8,128)S(1)}, f32[2,16,1024]{2,1,0:T(8,128)S(1)}, u32[]{:S(2)}, u32[]{:S(2)}) %collective-permute-start.14) | collective-permute-done | bytes 131104 | tf_op jit(solution)/shard_map/ppermute | solution.py:17
  48.5 2.4 %collective-permute-done.15 = f32[2,16,1024]{2,1,0:T(8,128)S(1)} collective-permute-done((f32[2,16,1024]{2,1,0:T(8,128)S(1)}, f32[2,16,1024]{2,1,0:T(8,128)S(1)}, u32[]{:S(2)}, u32[]{:S(2)}) %collective-permute-start.15) | collective-permute-done | bytes 131104 | tf_op jit(solution)/shard_map/ppermute | solution.py:17
  51.2 6.3 %shard_map.93 = (bf16[1024,1024]{1,0:T(8,128)(2,1)S(1)}, f32[1024,128]{1,0:T(8,128)S(1)}, f32[1024,128]{1,0:T(8,128)S(1)}) custom-call(bf16[1024,1024]{1,0:T(8,128)(2,1)S(1)} %copy-done, bf16[1024,128]{1,0:T(8,128)(2,1)S(1)} %copy-done.6, bf16[1024,128]{1,0:T(8,128)(2,1)S(1)} %copy-done.8, bf16[1024,1024]{1,0:T(8,128)(2,1)S(1)} %copy-done.2, ...), custom_call_target="tpu_custom_call" | custom-call | flops 1073741824 | bytes 8388608 | tf_op jit(solution)/shard_map/pallas_call | solution.py:215
  57.5 1.3 %copy-done.13 = bf16[1024,1024]{1,0:T(8,128)(2,1)} copy-done((bf16[1024,1024]{1,0:T(8,128)(2,1)}, bf16[1024,1024]{1,0:T(8,128)(2,1)S(1)}, u32[]{:S(2)}) %copy-start.13) | copy-done | bytes 2097176
  58.9 4.2 %shard_map.95 = (f32[4,2,256,128]{3,2,1,0:T(8,128)S(1)}, bf16[5,128,1024]{2,1,0:T(8,128)(2,1)S(1)}, bf16[128,1024]{1,0:T(8,128)(2,1)S(1)}) custom-call(s32[1]{0:T(128)} %bitcast.1.me_ref, f32[128,1024]{1,0:T(8,128)S(1)} %collective-permute-done.b0_ref, f32[2,64,1024]{2,1,0:T(8,128)S(1)} %pad_maximum_fusion.near_ref, ...), custom_call_target="tpu_custom_call" | custom-call | flops 1610612736 | bytes 8388608 | tf_op jit(solution)/shard_map/pallas_call | solution.py:221
  63.0 1.0 %copy-done.5 = f32[4,2,256,128]{3,2,1,0:T(8,128)} copy-done((f32[4,2,256,128]{3,2,1,0:T(8,128)}, f32[4,2,256,128]{3,2,1,0:T(8,128)S(1)}, u32[]{:S(2)}) %copy-start.5) | copy-done | bytes 1048600
  64.0 1.1 %copy-done.15 = bf16[5,128,1024]{2,1,0:T(8,128)(2,1)} copy-done((bf16[5,128,1024]{2,1,0:T(8,128)(2,1)}, bf16[5,128,1024]{2,1,0:T(8,128)(2,1)S(1)}, u32[]{:S(2)}) %copy-start.15) | copy-done | bytes 1310744
  65.8 4.6 %all-to-all-start = ((f32[4,2,256,128]{3,2,1,0:T(8,128)}), f32[4,2,256,128]{3,2,1,0:T(8,128)S(1)}, u32[]{:S(2)}, u32[]{:S(2)}) async-start(f32[4,2,256,128]{3,2,1,0:T(8,128)} %copy-done.5), calls=%async_computation | async-start | bytes 2097152 | tf_op jit(solution)/shard_map/all_to_all | solution.py:227
  70.4 1.6 %copy-done.4 = bf16[1024,1024]{1,0:T(8,128)(2,1)S(1)} copy-done((bf16[1024,1024]{1,0:T(8,128)(2,1)S(1)}, bf16[1024,1024]{1,0:T(8,128)(2,1)}, u32[]{:S(2)}) %copy-start.4) | copy-done | bytes 2097176
  72.0 0.9 %copy-done.9 = bf16[1024,128]{1,0:T(8,128)(2,1)S(1)} copy-done((bf16[1024,128]{1,0:T(8,128)(2,1)S(1)}, bf16[1024,128]{1,0:T(8,128)(2,1)}, u32[]{:S(2)}) %copy-start.9) | copy-done | bytes 262168
  73.0 1.6 %copy-done.14 = bf16[1024,1024]{1,0:T(8,128)(2,1)S(1)} copy-done((bf16[1024,1024]{1,0:T(8,128)(2,1)S(1)}, bf16[1024,1024]{1,0:T(8,128)(2,1)}, u32[]{:S(2)}) %copy-start.14) | copy-done | bytes 2097176
  74.5 1.3 %copy-done.16 = bf16[5,128,1024]{2,1,0:T(8,128)(2,1)S(1)} copy-done((bf16[5,128,1024]{2,1,0:T(8,128)(2,1)S(1)}, bf16[5,128,1024]{2,1,0:T(8,128)(2,1)}, u32[]{:S(2)}) %copy-start.16) | copy-done | bytes 1310744
  75.9 0.9 %copy-done.18 = bf16[128,1024]{1,0:T(8,128)(2,1)S(1)} copy-done((bf16[128,1024]{1,0:T(8,128)(2,1)S(1)}, bf16[128,1024]{1,0:T(8,128)(2,1)}, u32[]{:S(2)}) %copy-start.18) | copy-done | bytes 262168
  76.8 8.2 %shard_map.96 = (bf16[1024,1024]{1,0:T(8,128)(2,1)}, bf16[1024,1024]{1,0:T(8,128)(2,1)}) custom-call(bf16[1024,1024]{1,0:T(8,128)(2,1)S(1)} %copy-done.14, bf16[1024,1024]{1,0:T(8,128)(2,1)S(1)} %copy-done.1, bf16[1024,128]{1,0:T(8,128)(2,1)S(1)} %copy-done.7, bf16[1024,128]{1,0:T(8,128)(2,1)S(1)} %copy-done.9, bf16[1024,1024]{1,0:T(8,128)(2,1)S(1)} %copy-done.4, ...), custom_call_target="tpu_custom_call" | custom-call | flops 3758096384 | bytes 8388608 | tf_op jit(solution)/shard_map/pallas_call | solution.py:228
  85.0 1.1 %all-to-all-done.parts_ref = f32[4,2,256,128]{3,2,1,0:T(8,128)S(1)} async-done(((f32[4,2,256,128]{3,2,1,0:T(8,128)}), f32[4,2,256,128]{3,2,1,0:T(8,128)S(1)}, u32[]{:S(2)}, u32[]{:S(2)}) %all-to-all-start) | async-done | bytes 1048608 | tf_op jit(solution)/shard_map/all_to_all | solution.py:227
  (62 shorter events, 8.0 us)
Async XLA Ops:
  1.4 1.6 %copy-start = (bf16[1024,1024]{1,0:T(8,128)(2,1)S(1)}, bf16[1024,1024]{1,0:T(8,128)(2,1)}, u32[]{:S(2)}) copy-start(bf16[1024,1024]{1,0:T(8,128)(2,1)} %x_ref.7) | copy-start | bytes 6291460
  3.0 1.6 %copy-start.2 = (bf16[1024,1024]{1,0:T(8,128)(2,1)S(1)}, bf16[1024,1024]{1,0:T(8,128)(2,1)}, u32[]{:S(2)}) copy-start(bf16[1024,1024]{1,0:T(8,128)(2,1)} %d_ref.7) | copy-start | bytes 6291460
  4.6 0.9 %copy-start.6 = (bf16[1024,128]{1,0:T(8,128)(2,1)S(1)}, bf16[1024,128]{1,0:T(8,128)(2,1)}, u32[]{:S(2)}) copy-start(bf16[1024,128]{1,0:T(8,128)(2,1)} %b_ref.5) | copy-start | bytes 786436
  9.3 2.0 %collective-permute-start.6 = (f32[2,64,1024]{2,1,0:T(8,128)S(1)}, f32[2,64,1024]{2,1,0:T(8,128)S(1)}, u32[]{:S(2)}, u32[]{:S(2)}) collective-permute-start(f32[2,64,1024]{2,1,0:T(8,128)S(1)} %get-tuple-element.24), channel_id=1, source_target_pairs={{0,4},{4,0},{8,12},{12,8},{16,20},{20,16},{24,28},{28,24},{32,36},... | collective-permute-start | bytes 1572872 | tf_op jit(solution)/shard_map/ppermute | solution.py:17
  9.4 7.1 %collective-permute-start.1 = (f32[2,64,1024]{2,1,0:T(8,128)S(1)}, f32[2,64,1024]{2,1,0:T(8,128)S(1)}, u32[]{:S(2)}, u32[]{:S(2)}) collective-permute-start(f32[2,64,1024]{2,1,0:T(8,128)S(1)} %get-tuple-element.22), channel_id=1, source_target_pairs={{0,4},{4,0},{8,12},{12,8},{16,20},{20,16},{24,28},{28,24},{32,36},... | collective-permute-start | bytes 1572872 | tf_op jit(solution)/shard_map/ppermute | solution.py:17
  11.4 8.3 %collective-permute-start.7 = (f32[2,16,1024]{2,1,0:T(8,128)S(1)}, f32[2,16,1024]{2,1,0:T(8,128)S(1)}, u32[]{:S(2)}, u32[]{:S(2)}) collective-permute-start(f32[2,16,1024]{2,1,0:T(8,128)S(1)} %get-tuple-element.34), channel_id=1, source_target_pairs={{0,16},{4,20},{8,24},{12,28},{16,0},{20,4},{24,8},{28,12},{32,48},... | collective-permute-start | bytes 393224 | tf_op jit(solution)/shard_map/ppermute | solution.py:17
  15.4 7.4 %collective-permute-start.8 = (f32[2,16,1024]{2,1,0:T(8,128)S(1)}, f32[2,16,1024]{2,1,0:T(8,128)S(1)}, u32[]{:S(2)}, u32[]{:S(2)}) collective-permute-start(f32[2,16,1024]{2,1,0:T(8,128)S(1)} %get-tuple-element.35), channel_id=1, source_target_pairs={{0,8},{4,12},{8,0},{12,4},{16,24},{20,28},{24,16},{28,20},{32,40},... | collective-permute-start | bytes 393224 | tf_op jit(solution)/shard_map/ppermute | solution.py:17
  16.5 6.4 %collective-permute-start.9 = (f32[2,16,1024]{2,1,0:T(8,128)S(1)}, f32[2,16,1024]{2,1,0:T(8,128)S(1)}, u32[]{:S(2)}, u32[]{:S(2)}) collective-permute-start(f32[2,16,1024]{2,1,0:T(8,128)S(1)} %get-tuple-element.36), channel_id=1, source_target_pairs={{0,24},{4,28},{8,16},{12,20},{16,8},{20,12},{24,0},{28,4},{32,56},... | collective-permute-start | bytes 393224 | tf_op jit(solution)/shard_map/ppermute | solution.py:17
  16.5 42.4 %collective-permute-start = (f32[128,1024]{1,0:T(8,128)S(1)}, f32[128,1024]{1,0:T(8,128)S(1)}, u32[]{:S(2)}, u32[]{:S(2)}) collective-permute-start(f32[128,1024]{1,0:T(8,128)S(1)} %get-tuple-element.20), channel_id=1, source_target_pairs={{0,4},{4,0},{8,12},{12,8},{16,20},{20,16},{24,28},{28,24},{32,36},... | collective-permute-start | bytes 1572872 | tf_op jit(solution)/shard_map/ppermute | solution.py:17
  22.9 6.8 %collective-permute-start.12 = (f32[16,1024]{1,0:T(8,128)S(1)}, f32[16,1024]{1,0:T(8,128)S(1)}, u32[]{:S(2)}, u32[]{:S(2)}) collective-permute-start(f32[16,1024]{1,0:T(8,128)S(1)} %get-tuple-element.50), channel_id=1, source_target_pairs={{0,96},{4,100},{8,104},{12,108},{16,112},{20,116},{24,120},{28,124... | collective-permute-start | bytes 196616 | tf_op jit(solution)/shard_map/ppermute | solution.py:17
  25.7 5.8 %collective-permute-start.11 = (f32[16,1024]{1,0:T(8,128)S(1)}, f32[16,1024]{1,0:T(8,128)S(1)}, u32[]{:S(2)}, u32[]{:S(2)}) collective-permute-start(f32[16,1024]{1,0:T(8,128)S(1)} %get-tuple-element.50), channel_id=1, source_target_pairs={{0,64},{4,68},{8,72},{12,76},{16,80},{20,84},{24,88},{28,92},{32,9... | collective-permute-start | bytes 196616 | tf_op jit(solution)/shard_map/ppermute | solution.py:17
  26.5 18.1 %collective-permute-start.4 = (f32[4,16,1024]{2,1,0:T(8,128)S(1)}, f32[4,16,1024]{2,1,0:T(8,128)S(1)}, u32[]{:S(2)}, u32[]{:S(2)}) collective-permute-start(f32[4,16,1024]{2,1,0:T(8,128)S(1)} %bitcast.60), channel_id=1, source_target_pairs={{0,24},{4,28},{8,16},{12,20},{16,8},{20,12},{24,0},{28,4},{32,56},... | collective-permute-start | bytes 786440 | tf_op jit(solution)/shard_map/ppermute | solution.py:17
  29.3 17.5 %collective-permute-start.3 = (f32[4,16,1024]{2,1,0:T(8,128)S(1)}, f32[4,16,1024]{2,1,0:T(8,128)S(1)}, u32[]{:S(2)}, u32[]{:S(2)}) collective-permute-start(f32[4,16,1024]{2,1,0:T(8,128)S(1)} %bitcast.61), channel_id=1, source_target_pairs={{0,16},{4,20},{8,24},{12,28},{16,0},{20,4},{24,8},{28,12},{32,48},... | collective-permute-start | bytes 786440 | tf_op jit(solution)/shard_map/ppermute | solution.py:17
  29.7 13.8 %collective-permute-start.2 = (f32[4,16,1024]{2,1,0:T(8,128)S(1)}, f32[4,16,1024]{2,1,0:T(8,128)S(1)}, u32[]{:S(2)}, u32[]{:S(2)}) collective-permute-start(f32[4,16,1024]{2,1,0:T(8,128)S(1)} %bitcast.62), channel_id=1, source_target_pairs={{0,8},{4,12},{8,0},{12,4},{16,24},{20,28},{24,16},{28,20},{32,40},... | collective-permute-start | bytes 786440 | tf_op jit(solution)/shard_map/ppermute | solution.py:17
  31.5 4.3 %collective-permute-start.10 = (f32[16,1024]{1,0:T(8,128)S(1)}, f32[16,1024]{1,0:T(8,128)S(1)}, u32[]{:S(2)}, u32[]{:S(2)}) collective-permute-start(f32[16,1024]{1,0:T(8,128)S(1)} %get-tuple-element.49), channel_id=1, source_target_pairs={{0,32},{4,36},{8,40},{12,44},{16,48},{20,52},{24,56},{28,60},{32,0... | collective-permute-start | bytes 196616 | tf_op jit(solution)/shard_map/ppermute | solution.py:17
  35.8 12.3 %collective-permute-start.14 = (f32[2,16,1024]{2,1,0:T(8,128)S(1)}, f32[2,16,1024]{2,1,0:T(8,128)S(1)}, u32[]{:S(2)}, u32[]{:S(2)}) collective-permute-start(f32[2,16,1024]{2,1,0:T(8,128)S(1)} %get-tuple-element.48), channel_id=1, source_target_pairs={{0,16},{4,20},{8,24},{12,28},{16,0},{20,4},{24,8},{28,12},{32,48},... | collective-permute-start | bytes 393224 | tf_op jit(solution)/shard_map/ppermute | solution.py:17
  43.6 5.0 %collective-permute-start.13 = (f32[2,16,1024]{2,1,0:T(8,128)S(1)}, f32[2,16,1024]{2,1,0:T(8,128)S(1)}, u32[]{:S(2)}, u32[]{:S(2)}) collective-permute-start(f32[2,16,1024]{2,1,0:T(8,128)S(1)} %get-tuple-element.48), channel_id=1, source_target_pairs={{0,8},{4,12},{8,0},{12,4},{16,24},{20,28},{24,16},{28,20},{32,40},... | collective-permute-start | bytes 393224 | tf_op jit(solution)/shard_map/ppermute | solution.py:17
  44.6 6.6 %copy-start.10 = (f32[16,18]{1,0:T(8,128)S(1)}, f32[16,18]{1,0:T(8,128)}, u32[]{:S(2)}) copy-start(f32[16,18]{1,0:T(8,128)} %table_ref.5) | copy-start | bytes 3460
  44.6 6.3 %collective-permute-start.15 = (f32[2,16,1024]{2,1,0:T(8,128)S(1)}, f32[2,16,1024]{2,1,0:T(8,128)S(1)}, u32[]{:S(2)}, u32[]{:S(2)}) collective-permute-start(f32[2,16,1024]{2,1,0:T(8,128)S(1)} %get-tuple-element.48), channel_id=1, source_target_pairs={{0,24},{4,28},{8,16},{12,20},{16,8},{20,12},{24,0},{28,4},{32,56},... | collective-permute-start | bytes 393224 | tf_op jit(solution)/shard_map/ppermute | solution.py:17
  46.9 12.0 %collective-permute-start.5 = (f32[2,64,1024]{2,1,0:T(8,128)S(1)}, f32[2,64,1024]{2,1,0:T(8,128)S(1)}, u32[]{:S(2)}, u32[]{:S(2)}) collective-permute-start(f32[2,64,1024]{2,1,0:T(8,128)S(1)} %pad_maximum_fusion.near_ref), channel_id=1, source_target_pairs={{0,4},{4,0},{8,12},{12,8},{16,20},{20,16},{24,28},{28,24},{32,36},... | collective-permute-start | bytes 1572872 | tf_op jit(solution)/shard_map/ppermute | solution.py:17
  50.9 7.9 %copy-start.3 = (bf16[1024,1024]{1,0:T(8,128)(2,1)S(1)}, bf16[1024,1024]{1,0:T(8,128)(2,1)}, u32[]{:S(2)}) copy-start(bf16[1024,1024]{1,0:T(8,128)(2,1)} %d_ref.7) | copy-start | bytes 6291460
  51.0 7.9 %collective-permute-start.16 = (f32[2,64,1024]{2,1,0:T(8,128)S(1)}, f32[2,64,1024]{2,1,0:T(8,128)S(1)}, u32[]{:S(2)}, u32[]{:S(2)}) collective-permute-start(f32[2,64,1024]{2,1,0:T(8,128)S(1)} %bitcast.49), channel_id=1, source_target_pairs={{0,4},{4,0},{8,12},{12,8},{16,20},{20,16},{24,28},{28,24},{32,36},... | collective-permute-start | bytes 1572872 | tf_op jit(solution)/shard_map/ppermute | solution.py:17
  57.5 1.3 %copy-start.13 = (bf16[1024,1024]{1,0:T(8,128)(2,1)}, bf16[1024,1024]{1,0:T(8,128)(2,1)S(1)}, u32[]{:S(2)}) copy-start(bf16[1024,1024]{1,0:T(8,128)(2,1)S(1)} %get-tuple-element.19.mix_ref) | copy-start | bytes 6291460
  58.9 11.5 %copy-start.7 = (bf16[1024,128]{1,0:T(8,128)(2,1)S(1)}, bf16[1024,128]{1,0:T(8,128)(2,1)}, u32[]{:S(2)}) copy-start(bf16[1024,128]{1,0:T(8,128)(2,1)} %b_ref.5) | copy-start | bytes 786436
  63.0 1.0 %copy-start.5 = (f32[4,2,256,128]{3,2,1,0:T(8,128)}, f32[4,2,256,128]{3,2,1,0:T(8,128)S(1)}, u32[]{:S(2)}) copy-start(f32[4,2,256,128]{3,2,1,0:T(8,128)S(1)} %get-tuple-element.31) | copy-start | bytes 3145732
  64.0 1.1 %copy-start.15 = (bf16[5,128,1024]{2,1,0:T(8,128)(2,1)}, bf16[5,128,1024]{2,1,0:T(8,128)(2,1)S(1)}, u32[]{:S(2)}) copy-start(bf16[5,128,1024]{2,1,0:T(8,128)(2,1)S(1)} %get-tuple-element.27.carry_ref) | copy-start | bytes 3932164
  65.8 4.6 %copy-start.1 = (bf16[1024,1024]{1,0:T(8,128)(2,1)S(1)}, bf16[1024,1024]{1,0:T(8,128)(2,1)}, u32[]{:S(2)}) copy-start(bf16[1024,1024]{1,0:T(8,128)(2,1)} %x_ref.7) | copy-start | bytes 6291460
  65.8 4.6 %copy-start.12 = (s32[1024]{0:T(1024)S(1)}, s32[1024]{0:T(1024)}, u32[]{:S(2)}) copy-start(s32[1024]{0:T(1024)} %param.11) | copy-start | bytes 12292
  65.8 20.3 %all-to-all-start = ((f32[4,2,256,128]{3,2,1,0:T(8,128)}), f32[4,2,256,128]{3,2,1,0:T(8,128)S(1)}, u32[]{:S(2)}, u32[]{:S(2)}) async-start(f32[4,2,256,128]{3,2,1,0:T(8,128)} %copy-done.5), calls=%async_computation | async-start | bytes 2097152 | tf_op jit(solution)/shard_map/all_to_all | solution.py:227
  70.4 1.6 %copy-start.4 = (bf16[1024,1024]{1,0:T(8,128)(2,1)S(1)}, bf16[1024,1024]{1,0:T(8,128)(2,1)}, u32[]{:S(2)}) copy-start(bf16[1024,1024]{1,0:T(8,128)(2,1)} %d_ref.7) | copy-start | bytes 6291460
  73.0 1.6 %copy-start.14 = (bf16[1024,1024]{1,0:T(8,128)(2,1)S(1)}, bf16[1024,1024]{1,0:T(8,128)(2,1)}, u32[]{:S(2)}) copy-start(bf16[1024,1024]{1,0:T(8,128)(2,1)} %copy-done.13) | copy-start | bytes 6291460
  74.5 1.3 %copy-start.16 = (bf16[5,128,1024]{2,1,0:T(8,128)(2,1)S(1)}, bf16[5,128,1024]{2,1,0:T(8,128)(2,1)}, u32[]{:S(2)}) copy-start(bf16[5,128,1024]{2,1,0:T(8,128)(2,1)} %copy-done.15) | copy-start | bytes 3932164
  (5 other events, 4.2 us)

commit v3 on v2

v3 whole, which is shorter than its diff:
```python
import jax
import jax.numpy as jnp
from jax import lax
from jax.experimental import pallas as pl
from jax.experimental.pallas import tpu as pltpu
from jax.sharding import PartitionSpec as P

F32, BF16 = jnp.float32, jnp.bfloat16
CORE, Z, X = 1, (0, 2, 4, 6), (0, 8, 16, 24)
TILE = 256
VMEM = pl.BlockSpec(memory_space=pltpu.VMEM)
HBM = pl.BlockSpec(memory_space=pltpu.HBM)
AHEAD = 2
STATE_MIB = 46


def from_xor(block, flip, axis="ctx"):
    route = [(i, i ^ flip) for i in range(lax.axis_size(axis))]
    return lax.ppermute(block, axis, route)


def dot_nt(a, b):
    return lax.dot_general(a, b, (((1,), (1,)), ((), ())), preferred_element_type=F32)


def dot_tn(a, b):
    return lax.dot_general(a, b, (((0,), (0,)), ((), ())), preferred_element_type=F32)


def dot_nn(a, b):
    return jnp.dot(a, b, preferred_element_type=F32)


def one_hot(level_ref, rows):
    ids = lax.broadcasted_iota(jnp.int32, (rows, level_ref.shape[1]), 0)
    return (ids == level_ref[...]).astype(F32)


def call(kernel, outs, in_specs, flops, scratch=(), mib=16):
    return pl.pallas_call(
        kernel,
        out_shape=tuple(jax.ShapeDtypeStruct(shape, dtype) for shape, dtype in outs),
        in_specs=in_specs,
        out_specs=tuple(VMEM for _ in outs),
        scratch_shapes=list(scratch),
        compiler_params=pltpu.CompilerParams(vmem_limit_bytes=mib << 20),
        cost_estimate=pl.CostEstimate(flops=flops, bytes_accessed=1 << 20, transcendentals=0),
    )


def own_bits():
    me = lax.axis_index("ctx")
    return [lax.shift_right_logical(me, k) & 1 for k in range(5)]


def row_mask(bits):
    return bits[0] * 64 + bits[2] * 32 + bits[1] * 16


def level_weights(level_ref, table_ref):
    return lax.dot_general(
        one_hot(level_ref, table_ref.shape[0]),
        table_ref[...],
        (((0,), (0,)), ((), ())),
        precision=lax.Precision.HIGHEST,
        preferred_element_type=F32,
    )


def state_kernel(x_in, b_in, c_in, d_in, table_in, level_in, far_send, far_keep, rest_send, near_keep, x_ref, b_ref, c_ref, d_ref, lam_ref, table_ref, level_ref, left, sems):
    tiles = [slice(at, at + TILE) for at in range(0, x_ref.shape[1], TILE)]
    started = []

    def fetch(pairs):
        copies = [pltpu.make_async_copy(src, dst, sems.at[len(started) + i]) for i, (src, dst) in enumerate(pairs)]
        for copy in copies:
            copy.start()
        started.extend(copies)
        return copies

    small = fetch([(c_in, c_ref), (b_in, b_ref), (table_in, table_ref), (level_in, level_ref)])
    fetch_tile = lambda here: fetch([(d_in.at[:, here], d_ref.at[:, here]), (x_in.at[:, here], x_ref.at[:, here])])
    big = [fetch_tile(here) for here in tiles[:AHEAD]]
    bits = own_bits()
    n = b_ref.shape[1]
    rows = lax.broadcasted_iota(jnp.int32, (n, n), 0)
    cols = lax.broadcasted_iota(jnp.int32, (n, n), 1)
    perm = (cols == (rows ^ row_mask(bits))).astype(F32).astype(BF16)
    for copy in small:
        copy.wait()
    c_t = dot_nt(perm, c_ref[...])
    b_t = dot_nt(perm, b_ref[...]).astype(BF16)
    lam_t = lax.dot_general(
        table_ref[...],
        one_hot(level_ref, table_ref.shape[0]),
        (((0,), (0,)), ((), ())),
        precision=lax.Precision.HIGHEST,
        preferred_element_type=F32,
    )
    lam_ref[...] = level_weights(level_ref, table_ref)
    for k in range(5):
        left[k * n : (k + 1) * n, :] = (lam_t[11 + k : 12 + k, :] * c_t).astype(BF16)
    half = n // 2
    for i, here in enumerate(tiles):
        for copy in big[i]:
            copy.wait()
        if i + AHEAD < len(tiles):
            big.append(fetch_tile(tiles[i + AHEAD]))
        state = dot_nn(b_t, x_ref[:, here])
        grads = dot_nn(left[...], d_ref[:, here])
        for k in range(5):
            value = jnp.where(bits[k] == 1, grads[k * n : (k + 1) * n], state)
            if k == 0:
                rest_send[0, :, here] = value[:half]
                rest_send[1, :, here] = value[half:]
            elif k < 3:
                near_keep[k - 1, :, here] = value[:half]
                rest_send[k + 1, :, here] = value[half:]
            else:
                far_keep[k - 3, :, here] = value[:half]
                far_send[k - 3, :, here] = value[half:]


def local_kernel(x_ref, b_ref, c_ref, d_ref, lam_ref, which, last, outs):
    mix_ref, grad_b_ref, grad_c_ref = outs
    tiles = [slice(at, at + TILE) for at in range(0, x_ref.shape[0], TILE)]
    rows = lax.broadcasted_iota(jnp.int32, (TILE, TILE), 0)
    cols = lax.broadcasted_iota(jnp.int32, (TILE, TILE), 1)
    gap = rows ^ cols
    if last is None:
        first_row = which[0] * TILE
    else:
        first_row = 0
        stop = (which[-1] + 1) * TILE
        grad_b_ref[...] = last[0][...]
        grad_c_ref[stop:, :] = last[1][...]
    for i in which:
        mine = tiles[i]
        lam_i = lam_ref[mine, :]
        c_i = c_ref[mine, :]
        d_i = d_ref[mine, :]
        grad_c = None
        for j in range(i + 1):
            theirs = tiles[j]
            b_j = b_ref[theirs, :]
            if j == i:
                weight = jnp.broadcast_to(lam_i[:, 0:1], (TILE, TILE))
                for level in range(1, 9):
                    weight = jnp.where(gap >= (1 << (level - 1)), lam_i[:, level : level + 1], weight)
                weight = jnp.where(cols <= rows, weight, 0.0)
            else:
                level = 8 + (i ^ j).bit_length()
                weight = lam_i[:, level : level + 1]
            at = slice((i - which[0]) * TILE, (i - which[0] + 1) * TILE)
            mix_ref[at, theirs] = (dot_nt(c_i, b_j) * weight).astype(BF16)
            d_mix = (dot_nt(d_i, x_ref[theirs, :]) * weight).astype(BF16)
            term = dot_nn(d_mix, b_j)
            grad_c = term if grad_c is None else grad_c + term
            back = dot_tn(d_mix, c_i)
            if last is None and i == which[0]:
                grad_b_ref[theirs, :] = back
            else:
                grad_b_ref[theirs, :] += back
        grad_c_ref[i * TILE - first_row : (i + 1) * TILE - first_row, :] = grad_c


def local_last(*refs):
    local_kernel(*refs[:5], (3,), None, refs[5:])


def local_first(last_b, last_c, *refs):
    local_kernel(*refs[:5], (0, 1, 2), (last_b, last_c), refs[5:])


def grad_kernel(rest_ref, near_ref, near_other, far_ref, far_other, gb_ref, gc_ref, x_ref, d_ref, lam_ref, part0, part1, part2, part3, carry_ref, back_ref):
    head = lax.axis_index("head")
    parts = (part0, part1, part2, part3)
    bits = own_bits()
    mask = row_mask(bits) // 16
    n = gb_ref.shape[1]
    for p in range(8):
        to = (p ^ mask) * 16
        half, q = p // 4, slice(p % 4 * 16, p % 4 * 16 + 16)
        near, far = (near_ref, far_ref) if half == 0 else (near_other, far_other)
        sums = [rest_ref[1 - half, q, :], near[0, q, :], near[1, q, :], far[0, q, :], far[1, q, :]]
        back = None
        for k in range(5):
            carry_ref[pl.ds(pl.multiple_of(k * n + to, 16), 16), :] = jnp.where(bits[k] == 1, sums[k], 0.0).astype(BF16)
            low = jnp.where(bits[k] == 1, 0.0, sums[k])
            back = low if back is None else back + low
        back_ref[pl.ds(pl.multiple_of(to, 16), 16), :] = back.astype(BF16)
    for m in (2, 1, 3, 0):
        mine = pl.ds(pl.multiple_of((head ^ m) * TILE, TILE), TILE)
        far_terms = dot_nt(d_ref[mine, :], carry_ref[...])
        lam = lam_ref[mine, :]
        grad_c = gc_ref[mine, :]
        for k in range(5):
            grad_c = grad_c + far_terms[:, k * n : (k + 1) * n] * lam[:, 11 + k : 12 + k]
        parts[m][1] = grad_c
        parts[m][0] = gb_ref[mine, :] + dot_nt(x_ref[mine, :], back_ref[...])


def output_kernel(mix_first, mix_last, x_ref, b_ref, c_ref, d_ref, lam_ref, carry_ref, back_ref, y_ref, dx_ref):
    tiles = [slice(at, at + TILE) for at in range(0, x_ref.shape[0], TILE)]
    count = len(tiles)
    for i, mine in enumerate(tiles):
        lam = lam_ref[mine, :]
        c_i = c_ref[mine, :].astype(F32)
        rising = jnp.concatenate([(c_i * lam[:, 11 + k : 12 + k]).astype(BF16) for k in range(5)], axis=1)
        total = dot_nn(rising, carry_ref[...])
        mix = mix_first[mine, : mine.stop] if i < count - 1 else mix_last[...]
        y_ref[mine, :] = (total + dot_nn(mix, x_ref[: mine.stop, :])).astype(BF16)
    for i, mine in enumerate(tiles):
        total = dot_nn(b_ref[mine, :], back_ref[...]) + dot_tn(mix_last[:, mine], d_ref[tiles[-1], :])
        if i < count - 1:
            total = total + dot_tn(mix_first[mine.start :, mine], d_ref[mine.start : tiles[-1].start, :])
        dx_ref[mine, :] = total.astype(BF16)


def sum_kernel(part0, part1, part2, part3, d_b_ref, d_c_ref):
    d_b_ref[...] = part0[0] + part1[0] + part2[0] + part3[0]
    d_c_ref[...] = part0[1] + part1[1] + part2[1] + part3[1]


def local(x_in, b_in, c_in, d_out, table, level_index):
    rows, width = x_in.shape
    n = b_in.shape[1]
    level = level_index.reshape(1, rows)
    most = rows - TILE
    tie = lax.optimization_barrier
    half = ((2, n // 2, width), F32)
    big, small = ((rows, width), BF16), ((rows, n), BF16)
    far_send, far_keep, rest_send, near_keep, x_in, b_in, c_in, d_out, lam = call(
        state_kernel,
        (half, half, ((4, n // 2, width), F32), half, big, small, small, big, ((rows, table.shape[1]), F32)),
        [HBM] * 6,
        2 * rows * width * n * 6,
        [
            pltpu.VMEM(table.shape, F32),
            pltpu.VMEM((1, rows), jnp.int32),
            pltpu.VMEM((5 * n, rows), BF16),
            pltpu.SemaphoreType.DMA((12,)),
        ],
        STATE_MIB,
    )(x_in, b_in, c_in, d_out, table, level)
    far = (far_keep + from_xor(far_send, CORE)).reshape(2, 4, n // 8, width)
    rest = from_xor(rest_send, CORE)
    near = (near_keep + rest[2:]).reshape(2, 4, n // 8, width)
    taken = [from_xor(far[:, m], Z[m]) for m in (2, 1, 3)]
    local_outs = lambda mix, grad_c_rows: ((mix, BF16), ((rows, n), F32), ((grad_c_rows, n), F32))
    x_tied, far, near = tie((x_in, far, near))
    mix_last, grad_b, grad_c = call(
        local_last,
        local_outs((TILE, rows), TILE),
        [VMEM] * 5,
        rows * rows * width // 2,
    )(x_tied, b_in, c_in, d_out, lam)
    total = far[:, 0]
    for part in taken:
        total = total + part
    total, grad_b = tie((total, grad_b))
    b3 = from_xor(total[0], X[1])
    b4 = from_xor(total[1], X[2]) + from_xor(total[1], X[3])
    b34 = jnp.stack([b3, b4])
    r1, r2, r3 = from_xor(near[0], Z[1]), from_xor(near[1], Z[2]), from_xor(near[1], Z[3])
    gathered = [from_xor(b34, Z[m]) for m in (1, 2, 3)]
    x_tied, b34 = tie((x_in, b34))
    mix_first, grad_b, grad_c = call(
        local_first,
        local_outs((most, most), rows),
        [VMEM] * 7,
        rows * rows * width // 2,
    )(grad_b, grad_c, x_tied, b_in, c_in, d_out, lam)
    r1, r2, r3, gathered, grad_b = tie((r1, r2, r3, gathered, grad_b))
    near = jnp.stack([jnp.stack([r1[p ^ 1] for p in range(4)]), jnp.stack([r2[p ^ 2] + r3[p ^ 3] for p in range(4)])])
    far = jnp.stack([b34] + gathered, axis=1)
    near, far = near.reshape(2, n // 2, width), far.reshape(2, n // 2, width)
    near_other, far_other = from_xor(near, CORE), from_xor(far, CORE)

    piece = ((2, rows // 4, n), F32)
    part0, part1, part2, part3, carry, back = call(
        grad_kernel,
        (piece, piece, piece, piece, ((5 * n, width), BF16), ((n, width), BF16)),
        [VMEM] * 10,
        2 * rows * width * n * 6,
    )(rest, near, near_other, far, far_other, grad_b, grad_c, x_in, d_out, lam)
    part2, part1, part3 = [from_xor(part, m, "head") for part, m in ((part2, 2), (part1, 1), (part3, 3))]
    y_out, dx_out = call(
        output_kernel,
        (((rows, width), BF16), ((rows, width), BF16)),
        [VMEM] * 9,
        2 * rows * width * n * 6 + 2 * rows * rows * width,
    )(mix_first, mix_last, x_in, b_in, c_in, d_out, lam, carry, back)
    piece = ((rows // 4, n), F32)
    d_b, d_c = call(sum_kernel, (piece, piece), [VMEM] * 4, rows * n)(part0, part1, part2, part3)
    return (y_out, dx_out, d_b, d_c)


def solution(mesh):
    return jax.shard_map(
        local,
        mesh=mesh,
        in_specs=(P("ctx", "head"), P("ctx", None), P("ctx", None), P("ctx", "head"), P(), P("ctx")),
        out_specs=(P("ctx", "head"), P("ctx", "head"), P(("ctx", "head"), None), P(("ctx", "head"), None)),
        check_vma=False,
    )
```

time: 87.7 us -> 79.3 us (0.904)
  local copies, waits for them, and re-layouts: 17.1 us -> 3.36 us
  waiting for transfers between devices: 22.8 us -> 30.2 us
  starting transfers between devices: 24.3 us -> 22.6 us
    unnamed x39 -> x10, local copies, waits for them, and re-layouts: 17 us -> 3.28 us
    ppermute x17 -> x19, waiting for transfers between devices: 21.6 us -> 30.2 us  [from_xor(): return lax.ppermute(block, axis, route)]
    all_to_all x1 -> x0, starting transfers between devices: 4.59 us -> none  [local(): parts = lax.all_to_all(both, 'head', 0, 0, tiled=True)]
    ppermute x17 -> x19, starting transfers between devices: 19.7 us -> 22.6 us  [from_xor(): return lax.ppermute(block, axis, route)]
    all_to_all x1 -> x0, waiting for transfers between devices: 1.14 us -> none  [local(): parts = lax.all_to_all(both, 'head', 0, 0, tiled=True)]
    pallas_call x5 -> x6, Pallas kernels: 21.5 us -> 21.7 us  [the longest x1 6.87 us: local(): call(output_kernel, (((rows, width), BF16), ((rows, width), BF16)), [VMEM...]
  transfers between devices with their start and end apart: 18 -> 19, of which waited for: 10 -> 12; matrix products, arithmetic and copies ran while one was open for 0% -> 0% of each run, Pallas kernels for 17% -> 16%
where the time goes in v3:
time: 79.3 us; the launch traced here: 79.1 us
  waiting for transfers between devices  30.2 us (38%)
  starting transfers between devices  22.6 us (28%)
  Pallas kernels  21.7 us (27%)
  local copies, waits for them, and re-layouts  3.36 us (4%)
  between operations  0.81 us (1%)
    ppermute x19, waiting for transfers between devices, from_xor(): return lax.ppermute(block, axis, route)  30.2 us
    ppermute x19, starting transfers between devices, from_xor(): return lax.ppermute(block, axis, route)  22.6 us
    pallas_call x1, Pallas kernels, local(): call(output_kernel, (((rows, width), BF16), ((rows, width), BF16)), [VMEM...  6.87 us
    pallas_call x1, Pallas kernels, local(): call(state_kernel, (half, half, ((4, n // 2, width), F32), half, big, sma...  5.43 us
    pallas_call x1, Pallas kernels, local(): call(local_first, local_outs((most, most), rows), [VMEM] * 7, rows * rows...  3.54 us
    unnamed x10, local copies, waits for them, and re-layouts  3.28 us
    pallas_call x1, Pallas kernels, local(): call(grad_kernel, (piece, piece, piece, piece, ((5 * n, width), BF16), ((...  2.78 us
    pallas_call x1, Pallas kernels, local(): call(local_last, local_outs((TILE, rows), TILE), [VMEM] * 5, rows * rows...  2.38 us
  transfers between devices with their start and end apart: 19, of which 12 were waited for; matrix products, arithmetic and copies ran while one was open for 0% of the time, Pallas kernels for 16%

profile of v3, /device:TPU:0, one launch (start us, length us, event | category | flops | bytes accessed | tf_op | source)
XLA Modules:
  0.0 79.1 jit_solution(12129834763734600344)
XLA Ops:
  0.6 0.9 %copy-done.1 = bf16[1024,128]{1,0:T(8,128)(2,1)S(1)} copy-done((bf16[1024,128]{1,0:T(8,128)(2,1)S(1)}, bf16[1024,128]{1,0:T(8,128)(2,1)}, u32[]{:S(2)}) %copy-start.1) | copy-done | bytes 262168
  1.6 0.9 %copy-done.2 = bf16[1024,128]{1,0:T(8,128)(2,1)S(1)} copy-done((bf16[1024,128]{1,0:T(8,128)(2,1)S(1)}, bf16[1024,128]{1,0:T(8,128)(2,1)}, u32[]{:S(2)}) %copy-start.2) | copy-done | bytes 262168
  2.5 0.7 copy-done.3
  3.2 0.7 copy-done.4
  3.9 5.4 %shard_map.93 = (f32[2,64,1024]{2,1,0:T(8,128)S(1)}, f32[2,64,1024]{2,1,0:T(8,128)S(1)}, f32[4,64,1024]{2,1,0:T(8,128)S(1)}, f32[2,64,1024]{2,1,0:T(8,128)S(1)},...) custom-call(bf16[1024,1024]{1,0:T(8,128)(2,1)} %x_in.1, ...), custom_call_target="tpu_custom_call" | custom-call | flops 1610612736 | bytes 1048576 | tf_op jit(solution)/shard_map/pallas_call | solution.py:233
  10.0 2.9 %collective-permute-done = f32[2,64,1024]{2,1,0:T(8,128)S(1)} collective-permute-done((f32[2,64,1024]{2,1,0:T(8,128)S(1)}, f32[2,64,1024]{2,1,0:T(8,128)S(1)}, u32[]{:S(2)}, u32[]{:S(2)}) %collective-permute-start) | collective-permute-done | bytes 524320 | tf_op jit(solution)/shard_map/ppermute | solution.py:19
  13.0 4.0 %collective-permute-start.2 = (f32[2,16,1024]{2,1,0:T(8,128)S(1)}, f32[2,16,1024]{2,1,0:T(8,128)S(1)}, u32[]{:S(2)}, u32[]{:S(2)}) collective-permute-start(f32[2,16,1024]{2,1,0:T(8,128)S(1)} %get-tuple-element.88), channel_id=1, source_target_pairs={{0,16},{4,20},{8,24},{12,28},{16,0},{20,4},{24,8},{28,12},{32,48},... | collective-permute-start | bytes 393224 | tf_op jit(solution)/shard_map/ppermute | solution.py:19
  17.0 1.0 %collective-permute-start.3 = (f32[2,16,1024]{2,1,0:T(8,128)S(1)}, f32[2,16,1024]{2,1,0:T(8,128)S(1)}, u32[]{:S(2)}, u32[]{:S(2)}) collective-permute-start(f32[2,16,1024]{2,1,0:T(8,128)S(1)} %get-tuple-element.89), channel_id=1, source_target_pairs={{0,8},{4,12},{8,0},{12,4},{16,24},{20,28},{24,16},{28,20},{32,40},... | collective-permute-start | bytes 393224 | tf_op jit(solution)/shard_map/ppermute | solution.py:19
  18.1 2.4 %shard_map.94 = (bf16[256,1024]{1,0:T(8,128)(2,1)S(1)}, f32[1024,128]{1,0:T(8,128)S(1)}, f32[256,128]{1,0:T(8,128)S(1)}) custom-call(bf16[1024,1024]{1,0:T(8,128)(2,1)S(1)} %get-tuple-element.58.refs_0_.x_ref, bf16[1024,128]{1,0:T(8,128)(2,1)S(1)} %get-tuple-element.50.refs_1_.b_ref, bf16[1024,128]{1,0:T(8,128)(2,1)S(1)} %get-tuple-element.51.refs_2_.c_ref, ...), custom_call_target="tpu_custom_call" | custom-call | flops 536870912 | bytes 1048576 | tf_op jit(solution)/shard_map/pallas_call | solution.py:252
  20.5 0.8 collective-permute-done.2
  21.3 3.1 %collective-permute-done.3 = f32[2,16,1024]{2,1,0:T(8,128)S(1)} collective-permute-done((f32[2,16,1024]{2,1,0:T(8,128)S(1)}, f32[2,16,1024]{2,1,0:T(8,128)S(1)}, u32[]{:S(2)}, u32[]{:S(2)}) %collective-permute-start.3) | collective-permute-done | bytes 131104 | tf_op jit(solution)/shard_map/ppermute | solution.py:19
  24.4 2.8 %collective-permute-start.7 = (f32[16,1024]{1,0:T(8,128)S(1)}, f32[16,1024]{1,0:T(8,128)S(1)}, u32[]{:S(2)}, u32[]{:S(2)}) collective-permute-start(f32[16,1024]{1,0:T(8,128)S(1)} %get-tuple-element.96), channel_id=1, source_target_pairs={{0,96},{4,100},{8,104},{12,108},{16,112},{20,116},{24,120},{28,124... | collective-permute-start | bytes 196616 | tf_op jit(solution)/shard_map/ppermute | solution.py:19
  27.3 0.8 %collective-permute-start.6 = (f32[16,1024]{1,0:T(8,128)S(1)}, f32[16,1024]{1,0:T(8,128)S(1)}, u32[]{:S(2)}, u32[]{:S(2)}) collective-permute-start(f32[16,1024]{1,0:T(8,128)S(1)} %get-tuple-element.96), channel_id=1, source_target_pairs={{0,64},{4,68},{8,72},{12,76},{16,80},{20,84},{24,88},{28,92},{32,9... | collective-permute-start | bytes 196616 | tf_op jit(solution)/shard_map/ppermute | solution.py:19
  28.1 0.6 collective-permute-start.5
  28.7 1.3 %collective-permute-done.7 = f32[16,1024]{1,0:T(8,128)S(1)} collective-permute-done((f32[16,1024]{1,0:T(8,128)S(1)}, f32[16,1024]{1,0:T(8,128)S(1)}, u32[]{:S(2)}, u32[]{:S(2)}) %collective-permute-start.7) | collective-permute-done | bytes 65568 | tf_op jit(solution)/shard_map/ppermute | solution.py:19
  30.0 3.1 %collective-permute-done.6 = f32[16,1024]{1,0:T(8,128)S(1)} collective-permute-done((f32[16,1024]{1,0:T(8,128)S(1)}, f32[16,1024]{1,0:T(8,128)S(1)}, u32[]{:S(2)}, u32[]{:S(2)}) %collective-permute-start.6) | collective-permute-done | bytes 65568 | tf_op jit(solution)/shard_map/ppermute | solution.py:19
  33.1 2.9 %collective-permute-start.13 = (f32[2,16,1024]{2,1,0:T(8,128)S(1)}, f32[2,16,1024]{2,1,0:T(8,128)S(1)}, u32[]{:S(2)}, u32[]{:S(2)}) collective-permute-start(f32[2,16,1024]{2,1,0:T(8,128)S(1)} %pad_maximum_fusion.4), channel_id=1, source_target_pairs={{0,24},{4,28},{8,16},{12,20},{16,8},{20,12},{24,0},{28,4},{32,56},... | collective-permute-start | bytes 393224 | tf_op jit(solution)/shard_map/ppermute | solution.py:19
  36.0 0.8 %collective-permute-start.10 = (f32[4,16,1024]{2,1,0:T(8,128)S(1)}, f32[4,16,1024]{2,1,0:T(8,128)S(1)}, u32[]{:S(2)}, u32[]{:S(2)}) collective-permute-start(f32[4,16,1024]{2,1,0:T(8,128)S(1)} %get-tuple-element.86), channel_id=1, source_target_pairs={{0,24},{4,28},{8,16},{12,20},{16,8},{20,12},{24,0},{28,4},{32,56},... | collective-permute-start | bytes 786440 | tf_op jit(solution)/shard_map/ppermute | solution.py:19
  36.8 3.3 %collective-permute-start.9 = (f32[4,16,1024]{2,1,0:T(8,128)S(1)}, f32[4,16,1024]{2,1,0:T(8,128)S(1)}, u32[]{:S(2)}, u32[]{:S(2)}) collective-permute-start(f32[4,16,1024]{2,1,0:T(8,128)S(1)} %get-tuple-element.86), channel_id=1, source_target_pairs={{0,16},{4,20},{8,24},{12,28},{16,0},{20,4},{24,8},{28,12},{32,48},... | collective-permute-start | bytes 786440 | tf_op jit(solution)/shard_map/ppermute | solution.py:19
  40.3 2.0 %collective-permute-done.13 = f32[2,16,1024]{2,1,0:T(8,128)S(1)} collective-permute-done((f32[2,16,1024]{2,1,0:T(8,128)S(1)}, f32[2,16,1024]{2,1,0:T(8,128)S(1)}, u32[]{:S(2)}, u32[]{:S(2)}) %collective-permute-start.13) | collective-permute-done | bytes 131104 | tf_op jit(solution)/shard_map/ppermute | solution.py:19
  42.3 3.5 %shard_map.95 = (bf16[768,768]{1,0:T(8,128)(2,1)S(1)}, f32[1024,128]{1,0:T(8,128)S(1)}, f32[1024,128]{1,0:T(8,128)S(1)}) custom-call(f32[1024,128]{1,0:T(8,128)S(1)} %get-tuple-element.55.last_b, f32[256,128]{1,0:T(8,128)S(1)} %get-tuple-element.56.last_c, bf16[1024,1024]{1,0:T(8,128)(2,1)S(1)} %get-tuple-element.58.refs_0_.x_ref, ...), custom_call_target="tpu_custom_call" | custom-call | flops 536870912 | bytes 1048576 | tf_op jit(solution)/shard_map/pallas_call | solution.py:268
  45.9 6.2 %collective-permute-done.12 = f32[2,16,1024]{2,1,0:T(8,128)S(1)} collective-permute-done((f32[2,16,1024]{2,1,0:T(8,128)S(1)}, f32[2,16,1024]{2,1,0:T(8,128)S(1)}, u32[]{:S(2)}, u32[]{:S(2)}) %collective-permute-start.12) | collective-permute-done | bytes 131104 | tf_op jit(solution)/shard_map/ppermute | solution.py:19
  52.0 1.5 %collective-permute-done.11 = f32[2,16,1024]{2,1,0:T(8,128)S(1)} collective-permute-done((f32[2,16,1024]{2,1,0:T(8,128)S(1)}, f32[2,16,1024]{2,1,0:T(8,128)S(1)}, u32[]{:S(2)}, u32[]{:S(2)}) %collective-permute-start.11) | collective-permute-done | bytes 131104 | tf_op jit(solution)/shard_map/ppermute | solution.py:19
  54.5 1.2 %collective-permute-done.15.far_other = f32[2,64,1024]{2,1,0:T(8,128)S(1)} collective-permute-done((f32[2,64,1024]{2,1,0:T(8,128)S(1)}, f32[2,64,1024]{2,1,0:T(8,128)S(1)}, u32[]{:S(2)}, u32[]{:S(2)}) %collective-permute-start.15) | collective-permute-done | bytes 524320 | tf_op jit(solution)/shard_map/ppermute | solution.py:19
  55.6 0.7 collective-permute-done.14.near_other
  56.4 2.8 %shard_map.96 = (f32[2,256,128]{2,1,0:T(8,128)S(1)}, f32[2,256,128]{2,1,0:T(8,128)S(1)}, f32[2,256,128]{2,1,0:T(8,128)S(1)}, f32[2,256,128]{2,1,0:T(8,128)S(1)},...) custom-call(f32[4,64,1024]{2,1,0:T(8,128)S(1)} %collective-permute-done.1.rest_ref, ...), custom_call_target="tpu_custom_call" | custom-call | flops 1610612736 | bytes 1048576 | tf_op jit(solution)/shard_map/pallas_call | solution.py:281
  59.2 1.7 %collective-permute-start.16 = (f32[2,256,128]{2,1,0:T(8,128)S(1)}, f32[2,256,128]{2,1,0:T(8,128)S(1)}, u32[]{:S(2)}, u32[]{:S(2)}) collective-permute-start(f32[2,256,128]{2,1,0:T(8,128)S(1)} %get-tuple-element.77), channel_id=1, source_target_pairs={{0,1},{1,0},{2,3},{3,2},{4,5},{5,4},{6,7},{7,6},{8,9},{9,8},{10,11... | collective-permute-start | bytes 786440 | tf_op jit(solution)/shard_map/ppermute | solution.py:19
  60.8 2.9 %collective-permute-start.17 = (f32[2,256,128]{2,1,0:T(8,128)S(1)}, f32[2,256,128]{2,1,0:T(8,128)S(1)}, u32[]{:S(2)}, u32[]{:S(2)}) collective-permute-start(f32[2,256,128]{2,1,0:T(8,128)S(1)} %get-tuple-element.78), channel_id=1, source_target_pairs={{0,2},{1,3},{2,0},{3,1},{4,6},{5,7},{6,4},{7,5},{8,10},{9,11},{10,... | collective-permute-start | bytes 786440 | tf_op jit(solution)/shard_map/ppermute | solution.py:19
  63.9 6.9 %shard_map.97 = (bf16[1024,1024]{1,0:T(8,128)(2,1)}, bf16[1024,1024]{1,0:T(8,128)(2,1)}) custom-call(bf16[768,768]{1,0:T(8,128)(2,1)S(1)} %get-tuple-element.59.mix_first, bf16[256,1024]{1,0:T(8,128)(2,1)S(1)} %get-tuple-element.60.mix_last, bf16[1024,1024]{1,0:T(8,128)(2,1)S(1)} %get-tuple-element.58.refs_0_.x_ref, ...), custom_call_target="tpu_custom_call" | custom-call | flops 3758096384 | bytes 1048576 | tf_op jit(solution)/shard_map/pallas_call | solution.py:288
  70.8 4.9 %collective-permute-done.17.part2 = f32[2,256,128]{2,1,0:T(8,128)S(1)} collective-permute-done((f32[2,256,128]{2,1,0:T(8,128)S(1)}, f32[2,256,128]{2,1,0:T(8,128)S(1)}, u32[]{:S(2)}, u32[]{:S(2)}) %collective-permute-start.17) | collective-permute-done | bytes 262176 | tf_op jit(solution)/shard_map/ppermute | solution.py:19
  75.7 2.6 %collective-permute-done.18.part3 = f32[2,256,128]{2,1,0:T(8,128)S(1)} collective-permute-done((f32[2,256,128]{2,1,0:T(8,128)S(1)}, f32[2,256,128]{2,1,0:T(8,128)S(1)}, u32[]{:S(2)}, u32[]{:S(2)}) %collective-permute-start.18) | collective-permute-done | bytes 262176 | tf_op jit(solution)/shard_map/ppermute | solution.py:19
  78.3 0.7 shard_map.98
  (35 shorter events, 2.2 us)
Async XLA Ops:
  0.6 1.0 %copy-start.1 = (bf16[1024,128]{1,0:T(8,128)(2,1)S(1)}, bf16[1024,128]{1,0:T(8,128)(2,1)}, u32[]{:S(2)}) copy-start(bf16[1024,128]{1,0:T(8,128)(2,1)} %b_in.1) | copy-start | bytes 786436
  1.6 0.9 %copy-start.2 = (bf16[1024,128]{1,0:T(8,128)(2,1)S(1)}, bf16[1024,128]{1,0:T(8,128)(2,1)}, u32[]{:S(2)}) copy-start(bf16[1024,128]{1,0:T(8,128)(2,1)} %c_in.1) | copy-start | bytes 786436
  2.5 0.7 copy-start.3
  3.2 0.7 copy-start.4
  9.4 8.8 %copy-start = (bf16[1024,1024]{1,0:T(8,128)(2,1)S(1)}, bf16[1024,1024]{1,0:T(8,128)(2,1)}, u32[]{:S(2)}) copy-start(bf16[1024,1024]{1,0:T(8,128)(2,1)} %get-tuple-element.52.refs_3_.d_ref) | copy-start | bytes 6291460
  9.4 8.7 %collective-permute-start.1 = (f32[4,64,1024]{2,1,0:T(8,128)S(1)}, f32[4,64,1024]{2,1,0:T(8,128)S(1)}, u32[]{:S(2)}, u32[]{:S(2)}) collective-permute-start(f32[4,64,1024]{2,1,0:T(8,128)S(1)} %get-tuple-element.47), channel_id=1, source_target_pairs={{0,4},{4,0},{8,12},{12,8},{16,20},{20,16},{24,28},{28,24},{32,36},... | collective-permute-start | bytes 3145736 | tf_op jit(solution)/shard_map/ppermute | solution.py:19
  9.5 3.4 %collective-permute-start = (f32[2,64,1024]{2,1,0:T(8,128)S(1)}, f32[2,64,1024]{2,1,0:T(8,128)S(1)}, u32[]{:S(2)}, u32[]{:S(2)}) collective-permute-start(f32[2,64,1024]{2,1,0:T(8,128)S(1)} %get-tuple-element.45), channel_id=1, source_target_pairs={{0,4},{4,0},{8,12},{12,8},{16,20},{20,16},{24,28},{28,24},{32,36},... | collective-permute-start | bytes 1572872 | tf_op jit(solution)/shard_map/ppermute | solution.py:19
  13.0 8.3 %collective-permute-start.2 = (f32[2,16,1024]{2,1,0:T(8,128)S(1)}, f32[2,16,1024]{2,1,0:T(8,128)S(1)}, u32[]{:S(2)}, u32[]{:S(2)}) collective-permute-start(f32[2,16,1024]{2,1,0:T(8,128)S(1)} %get-tuple-element.88), channel_id=1, source_target_pairs={{0,16},{4,20},{8,24},{12,28},{16,0},{20,4},{24,8},{28,12},{32,48},... | collective-permute-start | bytes 393224 | tf_op jit(solution)/shard_map/ppermute | solution.py:19
  17.0 7.4 %collective-permute-start.3 = (f32[2,16,1024]{2,1,0:T(8,128)S(1)}, f32[2,16,1024]{2,1,0:T(8,128)S(1)}, u32[]{:S(2)}, u32[]{:S(2)}) collective-permute-start(f32[2,16,1024]{2,1,0:T(8,128)S(1)} %get-tuple-element.89), channel_id=1, source_target_pairs={{0,8},{4,12},{8,0},{12,4},{16,24},{20,28},{24,16},{28,20},{32,40},... | collective-permute-start | bytes 393224 | tf_op jit(solution)/shard_map/ppermute | solution.py:19
  18.0 6.4 %collective-permute-start.4 = (f32[2,16,1024]{2,1,0:T(8,128)S(1)}, f32[2,16,1024]{2,1,0:T(8,128)S(1)}, u32[]{:S(2)}, u32[]{:S(2)}) collective-permute-start(f32[2,16,1024]{2,1,0:T(8,128)S(1)} %get-tuple-element.90), channel_id=1, source_target_pairs={{0,24},{4,28},{8,16},{12,20},{16,8},{20,12},{24,0},{28,4},{32,56},... | collective-permute-start | bytes 393224 | tf_op jit(solution)/shard_map/ppermute | solution.py:19
  24.4 5.6 %collective-permute-start.7 = (f32[16,1024]{1,0:T(8,128)S(1)}, f32[16,1024]{1,0:T(8,128)S(1)}, u32[]{:S(2)}, u32[]{:S(2)}) collective-permute-start(f32[16,1024]{1,0:T(8,128)S(1)} %get-tuple-element.96), channel_id=1, source_target_pairs={{0,96},{4,100},{8,104},{12,108},{16,112},{20,116},{24,120},{28,124... | collective-permute-start | bytes 196616 | tf_op jit(solution)/shard_map/ppermute | solution.py:19
  27.3 5.8 %collective-permute-start.6 = (f32[16,1024]{1,0:T(8,128)S(1)}, f32[16,1024]{1,0:T(8,128)S(1)}, u32[]{:S(2)}, u32[]{:S(2)}) collective-permute-start(f32[16,1024]{1,0:T(8,128)S(1)} %get-tuple-element.96), channel_id=1, source_target_pairs={{0,64},{4,68},{8,72},{12,76},{16,80},{20,84},{24,88},{28,92},{32,9... | collective-permute-start | bytes 196616 | tf_op jit(solution)/shard_map/ppermute | solution.py:19
  28.1 4.9 %collective-permute-start.5 = (f32[16,1024]{1,0:T(8,128)S(1)}, f32[16,1024]{1,0:T(8,128)S(1)}, u32[]{:S(2)}, u32[]{:S(2)}) collective-permute-start(f32[16,1024]{1,0:T(8,128)S(1)} %get-tuple-element.95), channel_id=1, source_target_pairs={{0,32},{4,36},{8,40},{12,44},{16,48},{20,52},{24,56},{28,60},{32,0... | collective-permute-start | bytes 196616 | tf_op jit(solution)/shard_map/ppermute | solution.py:19
  33.1 9.2 %collective-permute-start.13 = (f32[2,16,1024]{2,1,0:T(8,128)S(1)}, f32[2,16,1024]{2,1,0:T(8,128)S(1)}, u32[]{:S(2)}, u32[]{:S(2)}) collective-permute-start(f32[2,16,1024]{2,1,0:T(8,128)S(1)} %pad_maximum_fusion.4), channel_id=1, source_target_pairs={{0,24},{4,28},{8,16},{12,20},{16,8},{20,12},{24,0},{28,4},{32,56},... | collective-permute-start | bytes 393224 | tf_op jit(solution)/shard_map/ppermute | solution.py:19
  36.0 17.6 %collective-permute-start.8 = (f32[4,16,1024]{2,1,0:T(8,128)S(1)}, f32[4,16,1024]{2,1,0:T(8,128)S(1)}, u32[]{:S(2)}, u32[]{:S(2)}) collective-permute-start(f32[4,16,1024]{2,1,0:T(8,128)S(1)} %get-tuple-element.87), channel_id=1, source_target_pairs={{0,8},{4,12},{8,0},{12,4},{16,24},{20,28},{24,16},{28,20},{32,40},... | collective-permute-start | bytes 786440 | tf_op jit(solution)/shard_map/ppermute | solution.py:19
  36.0 17.6 %collective-permute-start.10 = (f32[4,16,1024]{2,1,0:T(8,128)S(1)}, f32[4,16,1024]{2,1,0:T(8,128)S(1)}, u32[]{:S(2)}, u32[]{:S(2)}) collective-permute-start(f32[4,16,1024]{2,1,0:T(8,128)S(1)} %get-tuple-element.86), channel_id=1, source_target_pairs={{0,24},{4,28},{8,16},{12,20},{16,8},{20,12},{24,0},{28,4},{32,56},... | collective-permute-start | bytes 786440 | tf_op jit(solution)/shard_map/ppermute | solution.py:19
  36.8 16.8 %collective-permute-start.9 = (f32[4,16,1024]{2,1,0:T(8,128)S(1)}, f32[4,16,1024]{2,1,0:T(8,128)S(1)}, u32[]{:S(2)}, u32[]{:S(2)}) collective-permute-start(f32[4,16,1024]{2,1,0:T(8,128)S(1)} %get-tuple-element.86), channel_id=1, source_target_pairs={{0,16},{4,20},{8,24},{12,28},{16,0},{20,4},{24,8},{28,12},{32,48},... | collective-permute-start | bytes 786440 | tf_op jit(solution)/shard_map/ppermute | solution.py:19
  40.1 12.0 %collective-permute-start.12 = (f32[2,16,1024]{2,1,0:T(8,128)S(1)}, f32[2,16,1024]{2,1,0:T(8,128)S(1)}, u32[]{:S(2)}, u32[]{:S(2)}) collective-permute-start(f32[2,16,1024]{2,1,0:T(8,128)S(1)} %pad_maximum_fusion.4), channel_id=1, source_target_pairs={{0,16},{4,20},{8,24},{12,28},{16,0},{20,4},{24,8},{28,12},{32,48},... | collective-permute-start | bytes 393224 | tf_op jit(solution)/shard_map/ppermute | solution.py:19
  42.3 11.3 %collective-permute-start.11 = (f32[2,16,1024]{2,1,0:T(8,128)S(1)}, f32[2,16,1024]{2,1,0:T(8,128)S(1)}, u32[]{:S(2)}, u32[]{:S(2)}) collective-permute-start(f32[2,16,1024]{2,1,0:T(8,128)S(1)} %pad_maximum_fusion.4), channel_id=1, source_target_pairs={{0,8},{4,12},{8,0},{12,4},{16,24},{20,28},{24,16},{28,20},{32,40},... | collective-permute-start | bytes 393224 | tf_op jit(solution)/shard_map/ppermute | solution.py:19
  53.6 2.0 %collective-permute-start.15 = (f32[2,64,1024]{2,1,0:T(8,128)S(1)}, f32[2,64,1024]{2,1,0:T(8,128)S(1)}, u32[]{:S(2)}, u32[]{:S(2)}) collective-permute-start(f32[2,64,1024]{2,1,0:T(8,128)S(1)} %bitcast.47), channel_id=1, source_target_pairs={{0,4},{4,0},{8,12},{12,8},{16,20},{20,16},{24,28},{28,24},{32,36},... | collective-permute-start | bytes 1572872 | tf_op jit(solution)/shard_map/ppermute | solution.py:19
  53.9 2.5 %collective-permute-start.14 = (f32[2,64,1024]{2,1,0:T(8,128)S(1)}, f32[2,64,1024]{2,1,0:T(8,128)S(1)}, u32[]{:S(2)}, u32[]{:S(2)}) collective-permute-start(f32[2,64,1024]{2,1,0:T(8,128)S(1)} %pad_maximum_fusion.near_ref), channel_id=1, source_target_pairs={{0,4},{4,0},{8,12},{12,8},{16,20},{20,16},{24,28},{28,24},{32,36},... | collective-permute-start | bytes 1572872 | tf_op jit(solution)/shard_map/ppermute | solution.py:19
  59.2 11.7 %collective-permute-start.16 = (f32[2,256,128]{2,1,0:T(8,128)S(1)}, f32[2,256,128]{2,1,0:T(8,128)S(1)}, u32[]{:S(2)}, u32[]{:S(2)}) collective-permute-start(f32[2,256,128]{2,1,0:T(8,128)S(1)} %get-tuple-element.77), channel_id=1, source_target_pairs={{0,1},{1,0},{2,3},{3,2},{4,5},{5,4},{6,7},{7,6},{8,9},{9,8},{10,11... | collective-permute-start | bytes 786440 | tf_op jit(solution)/shard_map/ppermute | solution.py:19
  60.8 14.9 %collective-permute-start.17 = (f32[2,256,128]{2,1,0:T(8,128)S(1)}, f32[2,256,128]{2,1,0:T(8,128)S(1)}, u32[]{:S(2)}, u32[]{:S(2)}) collective-permute-start(f32[2,256,128]{2,1,0:T(8,128)S(1)} %get-tuple-element.78), channel_id=1, source_target_pairs={{0,2},{1,3},{2,0},{3,1},{4,6},{5,7},{6,4},{7,5},{8,10},{9,11},{10,... | collective-permute-start | bytes 786440 | tf_op jit(solution)/shard_map/ppermute | solution.py:19
  63.7 14.6 %collective-permute-start.18 = (f32[2,256,128]{2,1,0:T(8,128)S(1)}, f32[2,256,128]{2,1,0:T(8,128)S(1)}, u32[]{:S(2)}, u32[]{:S(2)}) collective-permute-start(f32[2,256,128]{2,1,0:T(8,128)S(1)} %get-tuple-element.79), channel_id=1, source_target_pairs={{0,3},{1,2},{2,1},{3,0},{4,7},{5,6},{6,5},{7,4},{8,11},{9,10},{10,... | collective-permute-start | bytes 786440 | tf_op jit(solution)/shard_map/ppermute | solution.py:19

commit v4 on v3

--- a/solution.py
+++ b/solution.py
@@ -9,9 +9,7 @@
 CORE, Z, X = 1, (0, 2, 4, 6), (0, 8, 16, 24)
 TILE = 256
 VMEM = pl.BlockSpec(memory_space=pltpu.VMEM)
-HBM = pl.BlockSpec(memory_space=pltpu.HBM)
-AHEAD = 2
-STATE_MIB = 46
+LONG = 20 * 10**9
 
 
 def from_xor(block, flip, axis="ctx"):
@@ -29,11 +27,6 @@
 
 def dot_nn(a, b):
     return jnp.dot(a, b, preferred_element_type=F32)
-
-
-def one_hot(level_ref, rows):
-    ids = lax.broadcasted_iota(jnp.int32, (rows, level_ref.shape[1]), 0)
-    return (ids == level_ref[...]).astype(F32)
 
 
 def call(kernel, outs, in_specs, flops, scratch=(), mib=16):
@@ -57,55 +50,20 @@
     return bits[0] * 64 + bits[2] * 32 + bits[1] * 16
 
 
-def level_weights(level_ref, table_ref):
-    return lax.dot_general(
-        one_hot(level_ref, table_ref.shape[0]),
-        table_ref[...],
-        (((0,), (0,)), ((), ())),
-        precision=lax.Precision.HIGHEST,
-        preferred_element_type=F32,
-    )
-
-
-def state_kernel(x_in, b_in, c_in, d_in, table_in, level_in, far_send, far_keep, rest_send, near_keep, x_ref, b_ref, c_ref, d_ref, lam_ref, table_ref, level_ref, left, sems):
+def state_kernel(x_ref, bc_ref, d_ref, lam_ref, far_send, far_keep, rest_send, near_keep, left):
     tiles = [slice(at, at + TILE) for at in range(0, x_ref.shape[1], TILE)]
-    started = []
-
-    def fetch(pairs):
-        copies = [pltpu.make_async_copy(src, dst, sems.at[len(started) + i]) for i, (src, dst) in enumerate(pairs)]
-        for copy in copies:
-            copy.start()
-        started.extend(copies)
-        return copies
-
-    small = fetch([(c_in, c_ref), (b_in, b_ref), (table_in, table_ref), (level_in, level_ref)])
-    fetch_tile = lambda here: fetch([(d_in.at[:, here], d_ref.at[:, here]), (x_in.at[:, here], x_ref.at[:, here])])
-    big = [fetch_tile(here) for here in tiles[:AHEAD]]
     bits = own_bits()
-    n = b_ref.shape[1]
+    n = bc_ref.shape[1] // 2
     rows = lax.broadcasted_iota(jnp.int32, (n, n), 0)
     cols = lax.broadcasted_iota(jnp.int32, (n, n), 1)
     perm = (cols == (rows ^ row_mask(bits))).astype(F32).astype(BF16)
-    for copy in small:
-        copy.wait()
-    c_t = dot_nt(perm, c_ref[...])
-    b_t = dot_nt(perm, b_ref[...]).astype(BF16)
-    lam_t = lax.dot_general(
-        table_ref[...],
-        one_hot(level_ref, table_ref.shape[0]),
-        (((0,), (0,)), ((), ())),
-        precision=lax.Precision.HIGHEST,
-        preferred_element_type=F32,
-    )
-    lam_ref[...] = level_weights(level_ref, table_ref)
+    c_t = dot_nt(perm, bc_ref[:, n:])
+    b_t = dot_nt(perm, bc_ref[:, :n]).astype(BF16)
+    lam_t = lam_ref[...].T
     for k in range(5):
         left[k * n : (k + 1) * n, :] = (lam_t[11 + k : 12 + k, :] * c_t).astype(BF16)
     half = n // 2
-    for i, here in enumerate(tiles):
-        for copy in big[i]:
-            copy.wait()
-        if i + AHEAD < len(tiles):
-            big.append(fetch_tile(tiles[i + AHEAD]))
+    for here in tiles:
         state = dot_nn(b_t, x_ref[:, here])
         grads = dot_nn(left[...], d_ref[:, here])
         for k in range(5):
@@ -172,9 +130,18 @@
     local_kernel(*refs[:5], (0, 1, 2), (last_b, last_c), refs[5:])
 
 
-def grad_kernel(rest_ref, near_ref, near_other, far_ref, far_other, gb_ref, gc_ref, x_ref, d_ref, lam_ref, part0, part1, part2, part3, carry_ref, back_ref):
-    head = lax.axis_index("head")
-    parts = (part0, part1, part2, part3)
+def shares(m, gb_ref, gc_ref, x_ref, d_ref, lam_ref, carry_ref, back_ref):
+    n = gb_ref.shape[1]
+    mine = pl.ds(pl.multiple_of((lax.axis_index("head") ^ m) * TILE, TILE), TILE)
+    far_terms = dot_nt(d_ref[mine, :], carry_ref[...])
+    lam = lam_ref[mine, :]
+    grad_c = gc_ref[mine, :]
+    for k in range(5):
+        grad_c = grad_c + far_terms[:, k * n : (k + 1) * n] * lam[:, 11 + k : 12 + k]
+    return gb_ref[mine, :] + dot_nt(x_ref[mine, :], back_ref[...]), grad_c
+
+
+def grad_kernel(rest_ref, near_ref, near_other, far_ref, far_other, gb_ref, gc_ref, x_ref, d_ref, lam_ref, part2_b, part2_c, carry_ref, back_ref):
     bits = own_bits()
     mask = row_mask(bits) // 16
     n = gb_ref.shape[1]
@@ -189,15 +156,12 @@
             low = jnp.where(bits[k] == 1, 0.0, sums[k])
             back = low if back is None else back + low
         back_ref[pl.ds(pl.multiple_of(to, 16), 16), :] = back.astype(BF16)
-    for m in (2, 1, 3, 0):
-        mine = pl.ds(pl.multiple_of((head ^ m) * TILE, TILE), TILE)
-        far_terms = dot_nt(d_ref[mine, :], carry_ref[...])
-        lam = lam_ref[mine, :]
-        grad_c = gc_ref[mine, :]
-        for k in range(5):
-            grad_c = grad_c + far_terms[:, k * n : (k + 1) * n] * lam[:, 11 + k : 12 + k]
-        parts[m][1] = grad_c
-        parts[m][0] = gb_ref[mine, :] + dot_nt(x_ref[mine, :], back_ref[...])
+    part2_b[...], part2_c[...] = shares(2, gb_ref, gc_ref, x_ref, d_ref, lam_ref, carry_ref, back_ref)
+
+
+def grad_rest_kernel(gb_ref, gc_ref, x_ref, d_ref, lam_ref, carry_ref, back_ref, part0, part1, part3):
+    for m, part in ((1, part1), (3, part3), (0, part0)):
+        part[0], part[1] = shares(m, gb_ref, gc_ref, x_ref, d_ref, lam_ref, carry_ref, back_ref)
 
 
 def output_kernel(mix_first, mix_last, x_ref, b_ref, c_ref, d_ref, lam_ref, carry_ref, back_ref, y_ref, dx_ref):
@@ -217,33 +181,29 @@
         dx_ref[mine, :] = total.astype(BF16)
 
 
-def sum_kernel(part0, part1, part2, part3, d_b_ref, d_c_ref):
-    d_b_ref[...] = part0[0] + part1[0] + part2[0] + part3[0]
-    d_c_ref[...] = part0[1] + part1[1] + part2[1] + part3[1]
+def sum_kernel(part0, part1, part3, d_b_ref, d_c_ref):
+    d_b_ref[...] = part0[0] + part1[0] + part3[0]
+    d_c_ref[...] = part0[1] + part1[1] + part3[1]
 
 
 def local(x_in, b_in, c_in, d_out, table, level_index):
     rows, width = x_in.shape
     n = b_in.shape[1]
-    level = level_index.reshape(1, rows)
     most = rows - TILE
     tie = lax.optimization_barrier
     half = ((2, n // 2, width), F32)
-    big, small = ((rows, width), BF16), ((rows, n), BF16)
-    far_send, far_keep, rest_send, near_keep, x_in, b_in, c_in, d_out, lam = call(
+    table_rows = jnp.arange(table.shape[0], dtype=jnp.int32)
+    chooser = (level_index[:, None] == table_rows[None, :]).astype(F32)
+    lam = jnp.dot(chooser, table, precision=lax.Precision.HIGHEST)
+    far_send, far_keep, rest_send, near_keep = call(
         state_kernel,
-        (half, half, ((4, n // 2, width), F32), half, big, small, small, big, ((rows, table.shape[1]), F32)),
-        [HBM] * 6,
+        (half, half, ((4, n // 2, width), F32), half),
+        [VMEM] * 4,
         2 * rows * width * n * 6,
-        [
-            pltpu.VMEM(table.shape, F32),
-            pltpu.VMEM((1, rows), jnp.int32),
-            pltpu.VMEM((5 * n, rows), BF16),
-            pltpu.SemaphoreType.DMA((12,)),
-        ],
-        STATE_MIB,
-    )(x_in, b_in, c_in, d_out, table, level)
-    far = (far_keep + from_xor(far_send, CORE)).reshape(2, 4, n // 8, width)
+        [pltpu.VMEM((5 * n, rows), BF16)],
+    )(x_in, jnp.concatenate([b_in, c_in], axis=1), d_out, lam)
+    far, rest_send = tie((from_xor(far_send, CORE), rest_send))
+    far = (far_keep + far).reshape(2, 4, n // 8, width)
     rest = from_xor(rest_send, CORE)
     near = (near_keep + rest[2:]).reshape(2, 4, n // 8, width)
     taken = [from_xor(far[:, m], Z[m]) for m in (2, 1, 3)]
@@ -261,30 +221,40 @@
     total, grad_b = tie((total, grad_b))
     b3 = from_xor(total[0], X[1])
     b4 = from_xor(total[1], X[2]) + from_xor(total[1], X[3])
+    r1, r2, r3 = from_xor(near[0], Z[1]), from_xor(near[1], Z[2]), from_xor(near[1], Z[3])
+    r1, r2, r3, b3, b4 = tie((r1, r2, r3, b3, b4))
     b34 = jnp.stack([b3, b4])
-    r1, r2, r3 = from_xor(near[0], Z[1]), from_xor(near[1], Z[2]), from_xor(near[1], Z[3])
     gathered = [from_xor(b34, Z[m]) for m in (1, 2, 3)]
-    x_tied, b34 = tie((x_in, b34))
+    near = jnp.stack([jnp.stack([r1[p ^ 1] for p in range(4)]), jnp.stack([r2[p ^ 2] + r3[p ^ 3] for p in range(4)])])
+    near = near.reshape(2, n // 2, width)
+    near_other = from_xor(near, CORE)
+    x_tied, near, near_other = tie((x_in, near, near_other))
     mix_first, grad_b, grad_c = call(
         local_first,
         local_outs((most, most), rows),
         [VMEM] * 7,
-        rows * rows * width // 2,
+        LONG,
     )(grad_b, grad_c, x_tied, b_in, c_in, d_out, lam)
-    r1, r2, r3, gathered, grad_b = tie((r1, r2, r3, gathered, grad_b))
-    near = jnp.stack([jnp.stack([r1[p ^ 1] for p in range(4)]), jnp.stack([r2[p ^ 2] + r3[p ^ 3] for p in range(4)])])
-    far = jnp.stack([b34] + gathered, axis=1)
-    near, far = near.reshape(2, n // 2, width), far.reshape(2, n // 2, width)
-    near_other, far_other = from_xor(near, CORE), from_xor(far, CORE)
+    gathered, grad_b = tie((gathered, grad_b))
+    far = jnp.stack([b34] + gathered, axis=1).reshape(2, n // 2, width)
+    far_other = from_xor(far, CORE)
 
     piece = ((2, rows // 4, n), F32)
-    part0, part1, part2, part3, carry, back = call(
+    part2_b, part2_c, carry, back = call(
         grad_kernel,
-        (piece, piece, piece, piece, ((5 * n, width), BF16), ((n, width), BF16)),
+        (((rows // 4, n), F32), ((rows // 4, n), F32), ((5 * n, width), BF16), ((n, width), BF16)),
         [VMEM] * 10,
         2 * rows * width * n * 6,
     )(rest, near, near_other, far, far_other, grad_b, grad_c, x_in, d_out, lam)
-    part2, part1, part3 = [from_xor(part, m, "head") for part, m in ((part2, 2), (part1, 1), (part3, 3))]
+    part0, part1, part3 = call(
+        grad_rest_kernel,
+        (piece, piece, piece),
+        [VMEM] * 7,
+        2 * rows * width * n * 6,
+    )(grad_b, grad_c, x_in, d_out, lam, carry, back)
+    part3 = part3.at[0].add(from_xor(part2_b, 1, "head"))
+    part1 = part1.at[1].add(from_xor(part2_c, 3, "head"))
+    part1, part3 = from_xor(part1, 1, "head"), from_xor(part3, 3, "head")
     y_out, dx_out = call(
         output_kernel,
         (((rows, width), BF16), ((rows, width), BF16)),
@@ -292,7 +262,7 @@
         2 * rows * width * n * 6 + 2 * rows * rows * width,
     )(mix_first, mix_last, x_in, b_in, c_in, d_out, lam, carry, back)
     piece = ((rows // 4, n), F32)
-    d_b, d_c = call(sum_kernel, (piece, piece), [VMEM] * 4, rows * n)(part0, part1, part2, part3)
+    d_b, d_c = call(sum_kernel, (piece, piece), [VMEM] * 3, rows * n)(part0, part1, part3)
     return (y_out, dx_out, d_b, d_c)
 
 

time: 79.3 us -> 70 us (0.88)
  waiting for transfers between devices: 30.2 us -> 21.8 us
  Pallas kernels: 21.7 us -> 18.3 us
  matrix products: 0 us -> 1.14 us
  other arithmetic: 0.38 us -> 1.5 us
    ppermute x19 -> x20, waiting for transfers between devices: 30.2 us -> 21.8 us  [from_xor(): return lax.ppermute(block, axis, route)]
    pallas_call x4 -> x5, Pallas kernels: 12.5 us -> 9.11 us  [the longest x1 3.48 us: local(): call(local_first, local_outs((most, most), rows), [VMEM] * 7, LONG)]
    dot_general x0 -> x1, matrix products: none -> 1.14 us  [local(): lam = jnp.dot(chooser, table, precision=lax.Precision.HIGHEST)]
    concatenate x0 -> x1, other arithmetic: none -> 1.09 us  [local(): jnp.concatenate([b_in, c_in], axis=1)]
    unnamed x10 -> x12, local copies, waits for them, and re-layouts: 3.28 us -> 3.89 us
    ppermute x19 -> x20, starting transfers between devices: 22.6 us -> 22.1 us  [from_xor(): return lax.ppermute(block, axis, route)]
  transfers between devices with their start and end apart: 19 -> 20, of which waited for: 12 -> 11; matrix products, arithmetic and copies ran while one was open for 0% -> 0% of each run, Pallas kernels for 16% -> 21%
where the time goes in v4:
time: 70 us; the launch traced here: 69.7 us
  starting transfers between devices  22.1 us (32%)
  waiting for transfers between devices  21.8 us (31%)
  Pallas kernels  18.3 us (26%)
  local copies, waits for them, and re-layouts  3.97 us (6%)
  other arithmetic  1.5 us (2%)
  matrix products  1.14 us (2%)
  between operations  0.89 us (1%)
    ppermute x20, starting transfers between devices, from_xor(): return lax.ppermute(block, axis, route)  22.1 us
    ppermute x20, waiting for transfers between devices, from_xor(): return lax.ppermute(block, axis, route)  21.8 us
    pallas_call x1, Pallas kernels, local(): call(output_kernel, (((rows, width), BF16), ((rows, width), BF16)), [VMEM...  6.81 us
    unnamed x12, local copies, waits for them, and re-layouts  3.89 us
    pallas_call x1, Pallas kernels, local(): call(local_first, local_outs((most, most), rows), [VMEM] * 7, LONG)  3.48 us
    pallas_call x1, Pallas kernels, local(): call(local_last, local_outs((TILE, rows), TILE), [VMEM] * 5, rows * rows...  2.37 us
    pallas_call x1, Pallas kernels, local(): call(state_kernel, (half, half, ((4, n // 2, width), F32), half), [VMEM]...  2.01 us
    pallas_call x1, Pallas kernels, local(): call(grad_rest_kernel, (piece, piece, piece), [VMEM] * 7, 2 * rows * widt...  1.83 us
  transfers between devices with their start and end apart: 20, of which 11 were waited for; matrix products, arithmetic and copies ran while one was open for 0% of the time, Pallas kernels for 21%

profile of v4, /device:TPU:0, one launch (start us, length us, event | category | flops | bytes accessed | tf_op | source)
XLA Modules:
  0.0 69.7 jit_solution(9179158610146873239)
XLA Ops:
  0.6 0.7 copy-done
  1.3 1.1 %fusion.lam_ref.refs_4_ = f32[1024,18]{1,0:T(8,128)S(1)} fusion(f32[16,18]{1,0:T(8,128)S(1)} %copy-done, s32[1024]{0:T(1024)} %param.15), kind=kOutput, calls=%fused_computation.5 | convolution fusion | flops 3555328 | bytes 78976 | tf_op jit(solution)/shard_map/dot_general | solution.py:197
  2.5 1.1 %pad_maximum_fusion.bc_ref = bf16[1024,256]{1,0:T(8,128)(2,1)S(1)} fusion(bf16[1024,128]{1,0:T(8,128)(2,1)} %c_ref.1, bf16[1024,128]{1,0:T(8,128)(2,1)} %b_ref.1), kind=kLoop, calls=%fused_computation.1 | loop fusion | flops 1048576 | bytes 1048576 | tf_op jit(solution)/shard_map/concatenate | solution.py:204
  3.6 1.6 %copy-done.1 = bf16[1024,1024]{1,0:T(8,128)(2,1)S(1)} copy-done((bf16[1024,1024]{1,0:T(8,128)(2,1)S(1)}, bf16[1024,1024]{1,0:T(8,128)(2,1)}, u32[]{:S(2)}) %copy-start.1) | copy-done | bytes 2097176
  5.2 1.6 %copy-done.2 = bf16[1024,1024]{1,0:T(8,128)(2,1)S(1)} copy-done((bf16[1024,1024]{1,0:T(8,128)(2,1)S(1)}, bf16[1024,1024]{1,0:T(8,128)(2,1)}, u32[]{:S(2)}) %copy-start.2) | copy-done | bytes 2097176
  6.8 2.0 %shard_map.93 = (f32[2,64,1024]{2,1,0:T(8,128)S(1)}, f32[2,64,1024]{2,1,0:T(8,128)S(1)}, f32[4,64,1024]{2,1,0:T(8,128)S(1)}, f32[2,64,1024]{2,1,0:T(8,128)S(1)}) custom-call(bf16[1024,1024]{1,0:T(8,128)(2,1)S(1)} %copy-done.1, bf16[1024,256]{1,0:T(8,128)(2,1)S(1)} %pad_maximum_fusion.bc_ref, bf16[1024,1024]{1,0:T(8,128)(2,1)S(1)} %copy-done.2, ...), custom_call_target="tpu_custom_call" | custom-call | flops 1610612736 | bytes 1048576 | tf_op jit(solution)/shard_map/pallas_call | solution.py:198
  8.9 1.9 %collective-permute-done = f32[2,64,1024]{2,1,0:T(8,128)S(1)} collective-permute-done((f32[2,64,1024]{2,1,0:T(8,128)S(1)}, f32[2,64,1024]{2,1,0:T(8,128)S(1)}, u32[]{:S(2)}, u32[]{:S(2)}) %collective-permute-start) | collective-permute-done | bytes 524320 | tf_op jit(solution)/shard_map/ppermute | solution.py:17
  11.0 4.1 %collective-permute-start.2 = (f32[2,16,1024]{2,1,0:T(8,128)S(1)}, f32[2,16,1024]{2,1,0:T(8,128)S(1)}, u32[]{:S(2)}, u32[]{:S(2)}) collective-permute-start(f32[2,16,1024]{2,1,0:T(8,128)S(1)} %get-tuple-element.114), channel_id=1, source_target_pairs={{0,16},{4,20},{8,24},{12,28},{16,0},{20,4},{24,8},{28,12},{32,48},... | collective-permute-start | bytes 393224 | tf_op jit(solution)/shard_map/ppermute | solution.py:17
  15.1 1.0 %collective-permute-start.3 = (f32[2,16,1024]{2,1,0:T(8,128)S(1)}, f32[2,16,1024]{2,1,0:T(8,128)S(1)}, u32[]{:S(2)}, u32[]{:S(2)}) collective-permute-start(f32[2,16,1024]{2,1,0:T(8,128)S(1)} %get-tuple-element.115), channel_id=1, source_target_pairs={{0,8},{4,12},{8,0},{12,4},{16,24},{20,28},{24,16},{28,20},{32,40},... | collective-permute-start | bytes 393224 | tf_op jit(solution)/shard_map/ppermute | solution.py:17
  16.2 3.3 %collective-permute-start.7 = (f32[4,16,1024]{2,1,0:T(8,128)S(1)}, f32[4,16,1024]{2,1,0:T(8,128)S(1)}, u32[]{:S(2)}, u32[]{:S(2)}) collective-permute-start(f32[4,16,1024]{2,1,0:T(8,128)S(1)} %get-tuple-element.112), channel_id=1, source_target_pairs={{0,24},{4,28},{8,16},{12,20},{16,8},{20,12},{24,0},{28,4},{32,56},... | collective-permute-start | bytes 786440 | tf_op jit(solution)/shard_map/ppermute | solution.py:17
  19.6 2.4 %shard_map.94 = (bf16[256,1024]{1,0:T(8,128)(2,1)S(1)}, f32[1024,128]{1,0:T(8,128)S(1)}, f32[256,128]{1,0:T(8,128)S(1)}) custom-call(bf16[1024,1024]{1,0:T(8,128)(2,1)S(1)} %copy-done.1, bf16[1024,128]{1,0:T(8,128)(2,1)S(1)} %copy-done.4, bf16[1024,128]{1,0:T(8,128)(2,1)S(1)} %copy-done.5, bf16[1024,1024]{1,0:T(8,128)(2,1)S(1)} %copy-done.3, ...), custom_call_target="tpu_custom_call" | custom-call | flops 536870912 | bytes 1048576 | tf_op jit(solution)/shard_map/pallas_call | solution.py:212
  22.0 1.0 %collective-permute-start.5 = (f32[4,16,1024]{2,1,0:T(8,128)S(1)}, f32[4,16,1024]{2,1,0:T(8,128)S(1)}, u32[]{:S(2)}, u32[]{:S(2)}) collective-permute-start(f32[4,16,1024]{2,1,0:T(8,128)S(1)} %get-tuple-element.113), channel_id=1, source_target_pairs={{0,8},{4,12},{8,0},{12,4},{16,24},{20,28},{24,16},{28,20},{32,40},... | collective-permute-start | bytes 786440 | tf_op jit(solution)/shard_map/ppermute | solution.py:17
  23.3 5.1 %collective-permute-done.4 = f32[2,16,1024]{2,1,0:T(8,128)S(1)} collective-permute-done((f32[2,16,1024]{2,1,0:T(8,128)S(1)}, f32[2,16,1024]{2,1,0:T(8,128)S(1)}, u32[]{:S(2)}, u32[]{:S(2)}) %collective-permute-start.4) | collective-permute-done | bytes 131104 | tf_op jit(solution)/shard_map/ppermute | solution.py:17
  28.4 2.8 %collective-permute-start.10 = (f32[16,1024]{1,0:T(8,128)S(1)}, f32[16,1024]{1,0:T(8,128)S(1)}, u32[]{:S(2)}, u32[]{:S(2)}) collective-permute-start(f32[16,1024]{1,0:T(8,128)S(1)} %get-tuple-element.123), channel_id=1, source_target_pairs={{0,96},{4,100},{8,104},{12,108},{16,112},{20,116},{24,120},{28,124... | collective-permute-start | bytes 196616 | tf_op jit(solution)/shard_map/ppermute | solution.py:17
  31.3 0.8 %collective-permute-start.9 = (f32[16,1024]{1,0:T(8,128)S(1)}, f32[16,1024]{1,0:T(8,128)S(1)}, u32[]{:S(2)}, u32[]{:S(2)}) collective-permute-start(f32[16,1024]{1,0:T(8,128)S(1)} %get-tuple-element.123), channel_id=1, source_target_pairs={{0,64},{4,68},{8,72},{12,76},{16,80},{20,84},{24,88},{28,92},{32,9... | collective-permute-start | bytes 196616 | tf_op jit(solution)/shard_map/ppermute | solution.py:17
  32.1 1.9 %collective-permute-done.10 = f32[16,1024]{1,0:T(8,128)S(1)} collective-permute-done((f32[16,1024]{1,0:T(8,128)S(1)}, f32[16,1024]{1,0:T(8,128)S(1)}, u32[]{:S(2)}, u32[]{:S(2)}) %collective-permute-start.10) | collective-permute-done | bytes 65568 | tf_op jit(solution)/shard_map/ppermute | solution.py:17
  34.3 2.8 %collective-permute-done.9 = f32[16,1024]{1,0:T(8,128)S(1)} collective-permute-done((f32[16,1024]{1,0:T(8,128)S(1)}, f32[16,1024]{1,0:T(8,128)S(1)}, u32[]{:S(2)}, u32[]{:S(2)}) %collective-permute-start.9) | collective-permute-done | bytes 65568 | tf_op jit(solution)/shard_map/ppermute | solution.py:17
  37.0 1.2 %collective-permute-done.8 = f32[16,1024]{1,0:T(8,128)S(1)} collective-permute-done((f32[16,1024]{1,0:T(8,128)S(1)}, f32[16,1024]{1,0:T(8,128)S(1)}, u32[]{:S(2)}, u32[]{:S(2)}) %collective-permute-start.8) | collective-permute-done | bytes 65568 | tf_op jit(solution)/shard_map/ppermute | solution.py:17
  38.6 0.6 collective-permute-start.12
  39.2 3.5 %collective-permute-start.14 = (f32[2,16,1024]{2,1,0:T(8,128)S(1)}, f32[2,16,1024]{2,1,0:T(8,128)S(1)}, u32[]{:S(2)}, u32[]{:S(2)}) collective-permute-start(f32[2,16,1024]{2,1,0:T(8,128)S(1)} %get-tuple-element.122), channel_id=1, source_target_pairs={{0,24},{4,28},{8,16},{12,20},{16,8},{20,12},{24,0},{28,4},{32,56},... | collective-permute-start | bytes 393224 | tf_op jit(solution)/shard_map/ppermute | solution.py:17
  42.7 3.5 %shard_map.95 = (bf16[768,768]{1,0:T(8,128)(2,1)S(1)}, f32[1024,128]{1,0:T(8,128)S(1)}, f32[1024,128]{1,0:T(8,128)S(1)}) custom-call(f32[1024,128]{1,0:T(8,128)S(1)} %get-tuple-element.77.last_b, f32[256,128]{1,0:T(8,128)S(1)} %get-tuple-element.78.last_c, bf16[1024,1024]{1,0:T(8,128)(2,1)S(1)} %copy-done.1, bf16[1024,128]{1,0:T(8,128)(2,1)S(1)} %copy-done.4, ...), custom_call_target="tpu_custom_call" | custom-call | flops 20000000000 | bytes 1048576 | tf_op jit(solution)/shard_map/pallas_call | solution.py:232
  46.5 2.4 %collective-permute-done.14 = f32[2,16,1024]{2,1,0:T(8,128)S(1)} collective-permute-done((f32[2,16,1024]{2,1,0:T(8,128)S(1)}, f32[2,16,1024]{2,1,0:T(8,128)S(1)}, u32[]{:S(2)}, u32[]{:S(2)}) %collective-permute-start.14) | collective-permute-done | bytes 131104 | tf_op jit(solution)/shard_map/ppermute | solution.py:17
  48.9 0.3 collective-permute-start.15
  49.2 1.9 %collective-permute-done.15.far_other = f32[2,64,1024]{2,1,0:T(8,128)S(1)} collective-permute-done((f32[2,64,1024]{2,1,0:T(8,128)S(1)}, f32[2,64,1024]{2,1,0:T(8,128)S(1)}, u32[]{:S(2)}, u32[]{:S(2)}) %collective-permute-start.15) | collective-permute-done | bytes 524320 | tf_op jit(solution)/shard_map/ppermute | solution.py:17
  51.0 1.1 %shard_map.96 = (f32[256,128]{1,0:T(8,128)S(1)}, f32[256,128]{1,0:T(8,128)S(1)}, bf16[640,1024]{1,0:T(8,128)(2,1)S(1)}, bf16[128,1024]{1,0:T(8,128)(2,1)S(1)}) custom-call(f32[4,64,1024]{2,1,0:T(8,128)S(1)} %collective-permute-done.1.rest_ref, f32[2,64,1024]{2,1,0:T(8,128)S(1)} %pad_maximum_fusion.1.near_ref, ...), custom_call_target="tpu_custom_call" | custom-call | flops 1610612736 | bytes 1048576 | tf_op jit(solution)/shard_map/pallas_call | solution.py:243
  52.1 3.1 %collective-permute-start.16 = (f32[256,128]{1,0:T(8,128)S(1)}, f32[256,128]{1,0:T(8,128)S(1)}, u32[]{:S(2)}, u32[]{:S(2)}) collective-permute-start(f32[256,128]{1,0:T(8,128)S(1)} %get-tuple-element.103), channel_id=1, source_target_pairs={{0,3},{1,2},{2,1},{3,0},{4,7},{5,6},{6,5},{7,4},{8,11},{9,10},{10,... | collective-permute-start | bytes 393224 | tf_op jit(solution)/shard_map/ppermute | solution.py:17
  55.3 1.8 %shard_map.98 = (f32[2,256,128]{2,1,0:T(8,128)S(1)}, f32[2,256,128]{2,1,0:T(8,128)S(1)}, f32[2,256,128]{2,1,0:T(8,128)S(1)}) custom-call(f32[1024,128]{1,0:T(8,128)S(1)} %get-tuple-element.95.gb_ref, f32[1024,128]{1,0:T(8,128)S(1)} %get-tuple-element.96.gc_ref, bf16[1024,1024]{1,0:T(8,128)(2,1)S(1)} %copy-done.1, bf16[1024,1024]{1,0:T(8,128)(2,1)S(1)} %copy-done.3, ...), custom_call_target="tpu_custom_call" | custom-call | flops 1610612736 | bytes 1048576 | tf_op jit(solution)/shard_map/pallas_call | solution.py:249
  57.2 3.3 %collective-permute-done.18 = f32[256,128]{1,0:T(8,128)S(1)} collective-permute-done((f32[256,128]{1,0:T(8,128)S(1)}, f32[256,128]{1,0:T(8,128)S(1)}, u32[]{:S(2)}, u32[]{:S(2)}) %collective-permute-start.18) | collective-permute-done | bytes 131104 | tf_op jit(solution)/shard_map/ppermute | solution.py:17
  60.5 0.5 collective-permute-start.19
  61.3 6.8 %shard_map.97 = (bf16[1024,1024]{1,0:T(8,128)(2,1)}, bf16[1024,1024]{1,0:T(8,128)(2,1)}) custom-call(bf16[768,768]{1,0:T(8,128)(2,1)S(1)} %get-tuple-element.85.mix_first, bf16[256,1024]{1,0:T(8,128)(2,1)S(1)} %get-tuple-element.86.mix_last, bf16[1024,1024]{1,0:T(8,128)(2,1)S(1)} %copy-done.1, bf16[1024,128]{1,0:T(8,128)(2,1)S(1)} %copy-done.4, ...), custom_call_target="tpu_custom_call" | custom-call | flops 3758096384 | bytes 1048576 | tf_op jit(solution)/shard_map/pallas_call | solution.py:258
  68.1 0.9 %collective-permute-done.19.part3 = f32[2,256,128]{2,1,0:T(8,128)S(1)} collective-permute-done((f32[2,256,128]{2,1,0:T(8,128)S(1)}, f32[2,256,128]{2,1,0:T(8,128)S(1)}, u32[]{:S(2)}, u32[]{:S(2)}) %collective-permute-start.19) | collective-permute-done | bytes 262176 | tf_op jit(solution)/shard_map/ppermute | solution.py:17
  69.0 0.7 %shard_map.99 = (f32[256,128]{1,0:T(8,128)}, f32[256,128]{1,0:T(8,128)}) custom-call(f32[2,256,128]{2,1,0:T(8,128)S(1)} %get-tuple-element.101.part0, f32[2,256,128]{2,1,0:T(8,128)S(1)} %collective-permute-done.17.part1, f32[2,256,128]{2,1,0:T(8,128)S(1)} %collective-permute-done.19.part3), custom_call_target="tpu_custom_call" | custom-call | flops 131072 | bytes 1048576 | tf_op jit(solution)/shard_map/pallas_call | solution.py:265
  (44 shorter events, 2.2 us)
Async XLA Ops:
  0.6 0.7 %copy-start = (f32[16,18]{1,0:T(8,128)S(1)}, f32[16,18]{1,0:T(8,128)}, u32[]{:S(2)}) copy-start(f32[16,18]{1,0:T(8,128)} %param.14) | copy-start | bytes 3460
  3.6 1.6 %copy-start.1 = (bf16[1024,1024]{1,0:T(8,128)(2,1)S(1)}, bf16[1024,1024]{1,0:T(8,128)(2,1)}, u32[]{:S(2)}) copy-start(bf16[1024,1024]{1,0:T(8,128)(2,1)} %x_ref.7) | copy-start | bytes 6291460
  5.2 1.6 %copy-start.2 = (bf16[1024,1024]{1,0:T(8,128)(2,1)S(1)}, bf16[1024,1024]{1,0:T(8,128)(2,1)}, u32[]{:S(2)}) copy-start(bf16[1024,1024]{1,0:T(8,128)(2,1)} %d_ref.7) | copy-start | bytes 6291460
  8.8 2.0 %collective-permute-start = (f32[2,64,1024]{2,1,0:T(8,128)S(1)}, f32[2,64,1024]{2,1,0:T(8,128)S(1)}, u32[]{:S(2)}, u32[]{:S(2)}) collective-permute-start(f32[2,64,1024]{2,1,0:T(8,128)S(1)} %get-tuple-element.69), channel_id=1, source_target_pairs={{0,4},{4,0},{8,12},{12,8},{16,20},{20,16},{24,28},{28,24},{32,36},... | collective-permute-start | bytes 1572872 | tf_op jit(solution)/shard_map/ppermute | solution.py:17
  10.8 5.4 %collective-permute-start.1 = (f32[4,64,1024]{2,1,0:T(8,128)S(1)}, f32[4,64,1024]{2,1,0:T(8,128)S(1)}, u32[]{:S(2)}, u32[]{:S(2)}) collective-permute-start(f32[4,64,1024]{2,1,0:T(8,128)S(1)} %get-tuple-element.73), channel_id=1, source_target_pairs={{0,4},{4,0},{8,12},{12,8},{16,20},{20,16},{24,28},{28,24},{32,36},... | collective-permute-start | bytes 3145736 | tf_op jit(solution)/shard_map/ppermute | solution.py:17
  11.0 8.6 %copy-start.3 = (bf16[1024,1024]{1,0:T(8,128)(2,1)S(1)}, bf16[1024,1024]{1,0:T(8,128)(2,1)}, u32[]{:S(2)}) copy-start(bf16[1024,1024]{1,0:T(8,128)(2,1)} %d_ref.7) | copy-start | bytes 6291460
  11.0 8.6 %copy-start.4 = (bf16[1024,128]{1,0:T(8,128)(2,1)S(1)}, bf16[1024,128]{1,0:T(8,128)(2,1)}, u32[]{:S(2)}) copy-start(bf16[1024,128]{1,0:T(8,128)(2,1)} %b_ref.1) | copy-start | bytes 786436
  11.0 8.6 %copy-start.5 = (bf16[1024,128]{1,0:T(8,128)(2,1)S(1)}, bf16[1024,128]{1,0:T(8,128)(2,1)}, u32[]{:S(2)}) copy-start(bf16[1024,128]{1,0:T(8,128)(2,1)} %c_ref.1) | copy-start | bytes 786436
  11.0 10.9 %collective-permute-start.2 = (f32[2,16,1024]{2,1,0:T(8,128)S(1)}, f32[2,16,1024]{2,1,0:T(8,128)S(1)}, u32[]{:S(2)}, u32[]{:S(2)}) collective-permute-start(f32[2,16,1024]{2,1,0:T(8,128)S(1)} %get-tuple-element.114), channel_id=1, source_target_pairs={{0,16},{4,20},{8,24},{12,28},{16,0},{20,4},{24,8},{28,12},{32,48},... | collective-permute-start | bytes 393224 | tf_op jit(solution)/shard_map/ppermute | solution.py:17
  15.1 8.2 %collective-permute-start.3 = (f32[2,16,1024]{2,1,0:T(8,128)S(1)}, f32[2,16,1024]{2,1,0:T(8,128)S(1)}, u32[]{:S(2)}, u32[]{:S(2)}) collective-permute-start(f32[2,16,1024]{2,1,0:T(8,128)S(1)} %get-tuple-element.115), channel_id=1, source_target_pairs={{0,8},{4,12},{8,0},{12,4},{16,24},{20,28},{24,16},{28,20},{32,40},... | collective-permute-start | bytes 393224 | tf_op jit(solution)/shard_map/ppermute | solution.py:17
  16.1 12.2 %collective-permute-start.4 = (f32[2,16,1024]{2,1,0:T(8,128)S(1)}, f32[2,16,1024]{2,1,0:T(8,128)S(1)}, u32[]{:S(2)}, u32[]{:S(2)}) collective-permute-start(f32[2,16,1024]{2,1,0:T(8,128)S(1)} %get-tuple-element.116), channel_id=1, source_target_pairs={{0,24},{4,28},{8,16},{12,20},{16,8},{20,12},{24,0},{28,4},{32,56},... | collective-permute-start | bytes 393224 | tf_op jit(solution)/shard_map/ppermute | solution.py:17
  16.2 22.0 %collective-permute-start.7 = (f32[4,16,1024]{2,1,0:T(8,128)S(1)}, f32[4,16,1024]{2,1,0:T(8,128)S(1)}, u32[]{:S(2)}, u32[]{:S(2)}) collective-permute-start(f32[4,16,1024]{2,1,0:T(8,128)S(1)} %get-tuple-element.112), channel_id=1, source_target_pairs={{0,24},{4,28},{8,16},{12,20},{16,8},{20,12},{24,0},{28,4},{32,56},... | collective-permute-start | bytes 786440 | tf_op jit(solution)/shard_map/ppermute | solution.py:17
  19.6 18.7 %collective-permute-start.6 = (f32[4,16,1024]{2,1,0:T(8,128)S(1)}, f32[4,16,1024]{2,1,0:T(8,128)S(1)}, u32[]{:S(2)}, u32[]{:S(2)}) collective-permute-start(f32[4,16,1024]{2,1,0:T(8,128)S(1)} %get-tuple-element.112), channel_id=1, source_target_pairs={{0,16},{4,20},{8,24},{12,28},{16,0},{20,4},{24,8},{28,12},{32,48},... | collective-permute-start | bytes 786440 | tf_op jit(solution)/shard_map/ppermute | solution.py:17
  22.0 16.3 %collective-permute-start.5 = (f32[4,16,1024]{2,1,0:T(8,128)S(1)}, f32[4,16,1024]{2,1,0:T(8,128)S(1)}, u32[]{:S(2)}, u32[]{:S(2)}) collective-permute-start(f32[4,16,1024]{2,1,0:T(8,128)S(1)} %get-tuple-element.113), channel_id=1, source_target_pairs={{0,8},{4,12},{8,0},{12,4},{16,24},{20,28},{24,16},{28,20},{32,40},... | collective-permute-start | bytes 786440 | tf_op jit(solution)/shard_map/ppermute | solution.py:17
  28.4 5.6 %collective-permute-start.10 = (f32[16,1024]{1,0:T(8,128)S(1)}, f32[16,1024]{1,0:T(8,128)S(1)}, u32[]{:S(2)}, u32[]{:S(2)}) collective-permute-start(f32[16,1024]{1,0:T(8,128)S(1)} %get-tuple-element.123), channel_id=1, source_target_pairs={{0,96},{4,100},{8,104},{12,108},{16,112},{20,116},{24,120},{28,124... | collective-permute-start | bytes 196616 | tf_op jit(solution)/shard_map/ppermute | solution.py:17
  31.3 5.8 %collective-permute-start.9 = (f32[16,1024]{1,0:T(8,128)S(1)}, f32[16,1024]{1,0:T(8,128)S(1)}, u32[]{:S(2)}, u32[]{:S(2)}) collective-permute-start(f32[16,1024]{1,0:T(8,128)S(1)} %get-tuple-element.123), channel_id=1, source_target_pairs={{0,64},{4,68},{8,72},{12,76},{16,80},{20,84},{24,88},{28,92},{32,9... | collective-permute-start | bytes 196616 | tf_op jit(solution)/shard_map/ppermute | solution.py:17
  34.0 4.3 %collective-permute-start.8 = (f32[16,1024]{1,0:T(8,128)S(1)}, f32[16,1024]{1,0:T(8,128)S(1)}, u32[]{:S(2)}, u32[]{:S(2)}) collective-permute-start(f32[16,1024]{1,0:T(8,128)S(1)} %get-tuple-element.124), channel_id=1, source_target_pairs={{0,32},{4,36},{8,40},{12,44},{16,48},{20,52},{24,56},{28,60},{32,0... | collective-permute-start | bytes 196616 | tf_op jit(solution)/shard_map/ppermute | solution.py:17
  38.4 4.3 %collective-permute-start.11 = (f32[2,64,1024]{2,1,0:T(8,128)S(1)}, f32[2,64,1024]{2,1,0:T(8,128)S(1)}, u32[]{:S(2)}, u32[]{:S(2)}) collective-permute-start(f32[2,64,1024]{2,1,0:T(8,128)S(1)} %pad_maximum_fusion.1.near_ref), channel_id=1, source_target_pairs={{0,4},{4,0},{8,12},{12,8},{16,20},{20,16},{24,28},{28,24},{32,36},... | collective-permute-start | bytes 1572872 | tf_op jit(solution)/shard_map/ppermute | solution.py:17
  38.5 7.9 %collective-permute-start.13 = (f32[2,16,1024]{2,1,0:T(8,128)S(1)}, f32[2,16,1024]{2,1,0:T(8,128)S(1)}, u32[]{:S(2)}, u32[]{:S(2)}) collective-permute-start(f32[2,16,1024]{2,1,0:T(8,128)S(1)} %get-tuple-element.122), channel_id=1, source_target_pairs={{0,16},{4,20},{8,24},{12,28},{16,0},{20,4},{24,8},{28,12},{32,48},... | collective-permute-start | bytes 393224 | tf_op jit(solution)/shard_map/ppermute | solution.py:17
  38.6 7.8 %collective-permute-start.12 = (f32[2,16,1024]{2,1,0:T(8,128)S(1)}, f32[2,16,1024]{2,1,0:T(8,128)S(1)}, u32[]{:S(2)}, u32[]{:S(2)}) collective-permute-start(f32[2,16,1024]{2,1,0:T(8,128)S(1)} %get-tuple-element.122), channel_id=1, source_target_pairs={{0,8},{4,12},{8,0},{12,4},{16,24},{20,28},{24,16},{28,20},{32,40},... | collective-permute-start | bytes 393224 | tf_op jit(solution)/shard_map/ppermute | solution.py:17
  39.2 9.6 %collective-permute-start.14 = (f32[2,16,1024]{2,1,0:T(8,128)S(1)}, f32[2,16,1024]{2,1,0:T(8,128)S(1)}, u32[]{:S(2)}, u32[]{:S(2)}) collective-permute-start(f32[2,16,1024]{2,1,0:T(8,128)S(1)} %get-tuple-element.122), channel_id=1, source_target_pairs={{0,24},{4,28},{8,16},{12,20},{16,8},{20,12},{24,0},{28,4},{32,56},... | collective-permute-start | bytes 393224 | tf_op jit(solution)/shard_map/ppermute | solution.py:17
  48.9 2.2 %collective-permute-start.15 = (f32[2,64,1024]{2,1,0:T(8,128)S(1)}, f32[2,64,1024]{2,1,0:T(8,128)S(1)}, u32[]{:S(2)}, u32[]{:S(2)}) collective-permute-start(f32[2,64,1024]{2,1,0:T(8,128)S(1)} %bitcast.55), channel_id=1, source_target_pairs={{0,4},{4,0},{8,12},{12,8},{16,20},{20,16},{24,28},{28,24},{32,36},... | collective-permute-start | bytes 1572872 | tf_op jit(solution)/shard_map/ppermute | solution.py:17
  52.1 8.8 %collective-permute-start.16 = (f32[256,128]{1,0:T(8,128)S(1)}, f32[256,128]{1,0:T(8,128)S(1)}, u32[]{:S(2)}, u32[]{:S(2)}) collective-permute-start(f32[256,128]{1,0:T(8,128)S(1)} %get-tuple-element.103), channel_id=1, source_target_pairs={{0,3},{1,2},{2,1},{3,0},{4,7},{5,6},{6,5},{7,4},{8,11},{9,10},{10,... | collective-permute-start | bytes 393224 | tf_op jit(solution)/shard_map/ppermute | solution.py:17
  55.2 5.3 %collective-permute-start.18 = (f32[256,128]{1,0:T(8,128)S(1)}, f32[256,128]{1,0:T(8,128)S(1)}, u32[]{:S(2)}, u32[]{:S(2)}) collective-permute-start(f32[256,128]{1,0:T(8,128)S(1)} %get-tuple-element.105), channel_id=1, source_target_pairs={{0,1},{1,0},{2,3},{3,2},{4,5},{5,4},{6,7},{7,6},{8,9},{9,8},{10,11... | collective-permute-start | bytes 393224 | tf_op jit(solution)/shard_map/ppermute | solution.py:17
  60.5 8.5 %collective-permute-start.19 = (f32[2,256,128]{2,1,0:T(8,128)S(1)}, f32[2,256,128]{2,1,0:T(8,128)S(1)}, u32[]{:S(2)}, u32[]{:S(2)}) collective-permute-start(f32[2,256,128]{2,1,0:T(8,128)S(1)} %fusion.5), channel_id=1, source_target_pairs={{0,3},{1,2},{2,1},{3,0},{4,7},{5,6},{6,5},{7,4},{8,11},{9,10},{10,... | collective-permute-start | bytes 786440 | tf_op jit(solution)/shard_map/ppermute | solution.py:17
  61.0 8.0 %collective-permute-start.17 = (f32[2,256,128]{2,1,0:T(8,128)S(1)}, f32[2,256,128]{2,1,0:T(8,128)S(1)}, u32[]{:S(2)}, u32[]{:S(2)}) collective-permute-start(f32[2,256,128]{2,1,0:T(8,128)S(1)} %fusion.6), channel_id=1, source_target_pairs={{0,1},{1,0},{2,3},{3,2},{4,5},{5,4},{6,7},{7,6},{8,9},{9,8},{10,11... | collective-permute-start | bytes 786440 | tf_op jit(solution)/shard_map/ppermute | solution.py:17

commit v5 on v4

--- a/solution.py
+++ b/solution.py
@@ -9,7 +9,7 @@
 CORE, Z, X = 1, (0, 2, 4, 6), (0, 8, 16, 24)
 TILE = 256
 VMEM = pl.BlockSpec(memory_space=pltpu.VMEM)
-LONG = 20 * 10**9
+FIRST, LAST, LONG = 10**9, 10**9, 20 * 10**9
 
 
 def from_xor(block, flip, axis="ctx"):
@@ -86,12 +86,11 @@
     cols = lax.broadcasted_iota(jnp.int32, (TILE, TILE), 1)
     gap = rows ^ cols
     if last is None:
-        first_row = which[0] * TILE
+        grad_b_ref[...] = jnp.zeros(grad_b_ref.shape, F32)
+        grad_c_ref[...] = jnp.zeros(grad_c_ref.shape, F32)
     else:
-        first_row = 0
-        stop = (which[-1] + 1) * TILE
         grad_b_ref[...] = last[0][...]
-        grad_c_ref[stop:, :] = last[1][...]
+        grad_c_ref[...] = last[1][...]
     for i in which:
         mine = tiles[i]
         lam_i = lam_ref[mine, :]
@@ -115,19 +114,20 @@
             term = dot_nn(d_mix, b_j)
             grad_c = term if grad_c is None else grad_c + term
             back = dot_tn(d_mix, c_i)
-            if last is None and i == which[0]:
-                grad_b_ref[theirs, :] = back
-            else:
-                grad_b_ref[theirs, :] += back
-        grad_c_ref[i * TILE - first_row : (i + 1) * TILE - first_row, :] = grad_c
-
-
-def local_last(*refs):
-    local_kernel(*refs[:5], (3,), None, refs[5:])
-
-
-def local_first(last_b, last_c, *refs):
-    local_kernel(*refs[:5], (0, 1, 2), (last_b, last_c), refs[5:])
+            grad_b_ref[theirs, :] += back
+        grad_c_ref[mine, :] = grad_c
+
+
+def local_first(*refs):
+    local_kernel(*refs[:5], (0,), None, refs[5:])
+
+
+def local_last(last_b, last_c, *refs):
+    local_kernel(*refs[:5], (3,), (last_b, last_c), refs[5:])
+
+
+def local_middle(last_b, last_c, *refs):
+    local_kernel(*refs[:5], (1, 2), (last_b, last_c), refs[5:])
 
 
 def shares(m, gb_ref, gc_ref, x_ref, d_ref, lam_ref, carry_ref, back_ref):
@@ -164,20 +164,24 @@
         part[0], part[1] = shares(m, gb_ref, gc_ref, x_ref, d_ref, lam_ref, carry_ref, back_ref)
 
 
-def output_kernel(mix_first, mix_last, x_ref, b_ref, c_ref, d_ref, lam_ref, carry_ref, back_ref, y_ref, dx_ref):
+def output_kernel(mix_first, mix_middle, mix_last, x_ref, b_ref, c_ref, d_ref, lam_ref, carry_ref, back_ref, y_ref, dx_ref):
     tiles = [slice(at, at + TILE) for at in range(0, x_ref.shape[0], TILE)]
-    count = len(tiles)
+    mixes = {0: mix_first[...], 1: mix_middle[:TILE, : 2 * TILE], 2: mix_middle[TILE:, :], 3: mix_last[...]}
     for i, mine in enumerate(tiles):
         lam = lam_ref[mine, :]
         c_i = c_ref[mine, :].astype(F32)
         rising = jnp.concatenate([(c_i * lam[:, 11 + k : 12 + k]).astype(BF16) for k in range(5)], axis=1)
         total = dot_nn(rising, carry_ref[...])
-        mix = mix_first[mine, : mine.stop] if i < count - 1 else mix_last[...]
-        y_ref[mine, :] = (total + dot_nn(mix, x_ref[: mine.stop, :])).astype(BF16)
+        y_ref[mine, :] = (total + dot_nn(mixes[i], x_ref[: mine.stop, :])).astype(BF16)
+    middle = slice(TILE, 3 * TILE)
     for i, mine in enumerate(tiles):
-        total = dot_nn(b_ref[mine, :], back_ref[...]) + dot_tn(mix_last[:, mine], d_ref[tiles[-1], :])
-        if i < count - 1:
-            total = total + dot_tn(mix_first[mine.start :, mine], d_ref[mine.start : tiles[-1].start, :])
+        total = dot_nn(b_ref[mine, :], back_ref[...]) + dot_tn(mix_last[:, mine], d_ref[tiles[3], :])
+        if i < 2:
+            total = total + dot_tn(mix_middle[:, mine], d_ref[middle, :])
+        if i == 2:
+            total = total + dot_tn(mix_middle[TILE:, mine], d_ref[mine, :])
+        if i == 0:
+            total = total + dot_tn(mix_first[...], d_ref[mine, :])
         dx_ref[mine, :] = total.astype(BF16)
 
 
@@ -189,7 +193,6 @@
 def local(x_in, b_in, c_in, d_out, table, level_index):
     rows, width = x_in.shape
     n = b_in.shape[1]
-    most = rows - TILE
     tie = lax.optimization_barrier
     half = ((2, n // 2, width), F32)
     table_rows = jnp.arange(table.shape[0], dtype=jnp.int32)
@@ -207,37 +210,33 @@
     rest = from_xor(rest_send, CORE)
     near = (near_keep + rest[2:]).reshape(2, 4, n // 8, width)
     taken = [from_xor(far[:, m], Z[m]) for m in (2, 1, 3)]
-    local_outs = lambda mix, grad_c_rows: ((mix, BF16), ((rows, n), F32), ((grad_c_rows, n), F32))
+    def local_part(kernel, mix, operands, flops):
+        return call(kernel, ((mix, BF16), ((rows, n), F32), ((rows, n), F32)), [VMEM] * len(operands), flops)(*operands)
+
     x_tied, far, near = tie((x_in, far, near))
-    mix_last, grad_b, grad_c = call(
-        local_last,
-        local_outs((TILE, rows), TILE),
-        [VMEM] * 5,
-        rows * rows * width // 2,
-    )(x_tied, b_in, c_in, d_out, lam)
+    mix_first, grad_b, grad_c = local_part(local_first, (TILE, TILE), (x_tied, b_in, c_in, d_out, lam), FIRST)
     total = far[:, 0]
     for part in taken:
         total = total + part
     total, grad_b = tie((total, grad_b))
     b3 = from_xor(total[0], X[1])
     b4 = from_xor(total[1], X[2]) + from_xor(total[1], X[3])
-    r1, r2, r3 = from_xor(near[0], Z[1]), from_xor(near[1], Z[2]), from_xor(near[1], Z[3])
-    r1, r2, r3, b3, b4 = tie((r1, r2, r3, b3, b4))
+    r1, r3 = from_xor(near[0], Z[1]), from_xor(near[1], Z[3])
+    x_tied, _ = tie((x_in, total))
+    mix_last, grad_b, grad_c = local_part(local_last, (TILE, rows), (grad_b, grad_c, x_tied, b_in, c_in, d_out, lam), LAST)
+    r1, r3, b3, b4, grad_b = tie((r1, r3, b3, b4, grad_b))
     b34 = jnp.stack([b3, b4])
     gathered = [from_xor(b34, Z[m]) for m in (1, 2, 3)]
+    r2 = from_xor(r3, Z[1])
+    x_tied, b34 = tie((x_in, b34))
+    mix_middle, grad_b, grad_c = local_part(
+        local_middle, (2 * TILE, 3 * TILE), (grad_b, grad_c, x_tied, b_in, c_in, d_out, lam), LONG
+    )
     near = jnp.stack([jnp.stack([r1[p ^ 1] for p in range(4)]), jnp.stack([r2[p ^ 2] + r3[p ^ 3] for p in range(4)])])
     near = near.reshape(2, n // 2, width)
-    near_other = from_xor(near, CORE)
-    x_tied, near, near_other = tie((x_in, near, near_other))
-    mix_first, grad_b, grad_c = call(
-        local_first,
-        local_outs((most, most), rows),
-        [VMEM] * 7,
-        LONG,
-    )(grad_b, grad_c, x_tied, b_in, c_in, d_out, lam)
-    gathered, grad_b = tie((gathered, grad_b))
+    gathered, near, grad_b = tie((gathered, near, grad_b))
     far = jnp.stack([b34] + gathered, axis=1).reshape(2, n // 2, width)
-    far_other = from_xor(far, CORE)
+    far_other, near_other = from_xor(far, CORE), from_xor(near, CORE)
 
     piece = ((2, rows // 4, n), F32)
     part2_b, part2_c, carry, back = call(
@@ -258,9 +257,9 @@
     y_out, dx_out = call(
         output_kernel,
         (((rows, width), BF16), ((rows, width), BF16)),
-        [VMEM] * 9,
+        [VMEM] * 10,
         2 * rows * width * n * 6 + 2 * rows * rows * width,
-    )(mix_first, mix_last, x_in, b_in, c_in, d_out, lam, carry, back)
+    )(mix_first, mix_middle, mix_last, x_in, b_in, c_in, d_out, lam, carry, back)
     piece = ((rows // 4, n), F32)
     d_b, d_c = call(sum_kernel, (piece, piece), [VMEM] * 3, rows * n)(part0, part1, part3)
     return (y_out, dx_out, d_b, d_c)

time: 70 us -> 67.4 us (0.963)
  waiting for transfers between devices: 21.8 us -> 19.2 us
    ppermute x20, waiting for transfers between devices: 21.8 us -> 19.2 us  [from_xor(): return lax.ppermute(block, axis, route)]
    pallas_call x2 -> x3, Pallas kernels: 5.85 us -> 5.85 us  [local_part(): call(kernel, ((mix, BF16), ((rows, n), F32), ((rows, n), F32)), [VMEM] *...]
  transfers between devices with their start and end apart: 20 -> 20, of which waited for: 11 -> 9; matrix products, arithmetic and copies ran while one was open for 0% -> 1% of each run, Pallas kernels for 21% -> 22%
where the time goes in v5:
time: 67.4 us; the launch traced here: 67.1 us
  starting transfers between devices  22.1 us (33%)
  waiting for transfers between devices  19.2 us (28%)
  Pallas kernels  18.3 us (27%)
  local copies, waits for them, and re-layouts  3.99 us (6%)
  other arithmetic  1.46 us (2%)
  matrix products  1.14 us (2%)
  between operations  0.94 us (1%)
    ppermute x20, starting transfers between devices, from_xor(): return lax.ppermute(block, axis, route)  22.1 us
    ppermute x20, waiting for transfers between devices, from_xor(): return lax.ppermute(block, axis, route)  19.2 us
    pallas_call x1, Pallas kernels, local(): call(output_kernel, (((rows, width), BF16), ((rows, width), BF16)), [VMEM...  6.82 us
    pallas_call x3, Pallas kernels, local_part(): call(kernel, ((mix, BF16), ((rows, n), F32), ((rows, n), F32)), [VMEM] *...  5.85 us
    unnamed x12, local copies, waits for them, and re-layouts  3.89 us
    pallas_call x1, Pallas kernels, local(): call(state_kernel, (half, half, ((4, n // 2, width), F32), half), [VMEM]...  2.01 us
    pallas_call x1, Pallas kernels, local(): call(grad_rest_kernel, (piece, piece, piece), [VMEM] * 7, 2 * rows * widt...  1.83 us
  transfers between devices with their start and end apart: 20, of which 9 were waited for; matrix products, arithmetic and copies ran while one was open for 1% of the time, Pallas kernels for 22%

profile of v5, /device:TPU:0, one launch (start us, length us, event | category | flops | bytes accessed | tf_op | source)
XLA Modules:
  0.0 67.1 jit_solution(4577257641971755019)
XLA Ops:
  0.6 0.7 %copy-done = f32[16,18]{1,0:T(8,128)S(1)} copy-done((f32[16,18]{1,0:T(8,128)S(1)}, f32[16,18]{1,0:T(8,128)}, u32[]{:S(2)}) %copy-start) | copy-done | bytes 1176
  1.3 1.1 %fusion.lam_ref.refs_4_ = f32[1024,18]{1,0:T(8,128)S(1)} fusion(f32[16,18]{1,0:T(8,128)S(1)} %copy-done, s32[1024]{0:T(1024)} %param.15), kind=kOutput, calls=%fused_computation.5 | convolution fusion | flops 3555328 | bytes 78976 | tf_op jit(solution)/shard_map/dot_general | solution.py:200
  2.5 1.1 %pad_maximum_fusion.bc_ref = bf16[1024,256]{1,0:T(8,128)(2,1)S(1)} fusion(bf16[1024,128]{1,0:T(8,128)(2,1)} %c_ref.1, bf16[1024,128]{1,0:T(8,128)(2,1)} %b_ref.1), kind=kLoop, calls=%fused_computation.1 | loop fusion | flops 1048576 | bytes 1048576 | tf_op jit(solution)/shard_map/concatenate | solution.py:207
  3.6 1.6 %copy-done.1 = bf16[1024,1024]{1,0:T(8,128)(2,1)S(1)} copy-done((bf16[1024,1024]{1,0:T(8,128)(2,1)S(1)}, bf16[1024,1024]{1,0:T(8,128)(2,1)}, u32[]{:S(2)}) %copy-start.1) | copy-done | bytes 2097176
  5.2 1.6 %copy-done.2 = bf16[1024,1024]{1,0:T(8,128)(2,1)S(1)} copy-done((bf16[1024,1024]{1,0:T(8,128)(2,1)S(1)}, bf16[1024,1024]{1,0:T(8,128)(2,1)}, u32[]{:S(2)}) %copy-start.2) | copy-done | bytes 2097176
  6.8 2.0 %shard_map.93 = (f32[2,64,1024]{2,1,0:T(8,128)S(1)}, f32[2,64,1024]{2,1,0:T(8,128)S(1)}, f32[4,64,1024]{2,1,0:T(8,128)S(1)}, f32[2,64,1024]{2,1,0:T(8,128)S(1)}) custom-call(bf16[1024,1024]{1,0:T(8,128)(2,1)S(1)} %copy-done.1, bf16[1024,256]{1,0:T(8,128)(2,1)S(1)} %pad_maximum_fusion.bc_ref, bf16[1024,1024]{1,0:T(8,128)(2,1)S(1)} %copy-done.2, ...), custom_call_target="tpu_custom_call" | custom-call | flops 1610612736 | bytes 1048576 | tf_op jit(solution)/shard_map/pallas_call | solution.py:201
  8.9 1.9 %collective-permute-done = f32[2,64,1024]{2,1,0:T(8,128)S(1)} collective-permute-done((f32[2,64,1024]{2,1,0:T(8,128)S(1)}, f32[2,64,1024]{2,1,0:T(8,128)S(1)}, u32[]{:S(2)}, u32[]{:S(2)}) %collective-permute-start) | collective-permute-done | bytes 524320 | tf_op jit(solution)/shard_map/ppermute | solution.py:17
  11.0 4.1 %collective-permute-start.4 = (f32[2,16,1024]{2,1,0:T(8,128)S(1)}, f32[2,16,1024]{2,1,0:T(8,128)S(1)}, u32[]{:S(2)}, u32[]{:S(2)}) collective-permute-start(f32[2,16,1024]{2,1,0:T(8,128)S(1)} %get-tuple-element.120), channel_id=1, source_target_pairs={{0,16},{4,20},{8,24},{12,28},{16,0},{20,4},{24,8},{28,12},{32,48},... | collective-permute-start | bytes 393224 | tf_op jit(solution)/shard_map/ppermute | solution.py:17
  15.1 1.0 %collective-permute-start.5 = (f32[2,16,1024]{2,1,0:T(8,128)S(1)}, f32[2,16,1024]{2,1,0:T(8,128)S(1)}, u32[]{:S(2)}, u32[]{:S(2)}) collective-permute-start(f32[2,16,1024]{2,1,0:T(8,128)S(1)} %get-tuple-element.121), channel_id=1, source_target_pairs={{0,8},{4,12},{8,0},{12,4},{16,24},{20,28},{24,16},{28,20},{32,40},... | collective-permute-start | bytes 393224 | tf_op jit(solution)/shard_map/ppermute | solution.py:17
  16.2 3.3 %collective-permute-start.3 = (f32[4,16,1024]{2,1,0:T(8,128)S(1)}, f32[4,16,1024]{2,1,0:T(8,128)S(1)}, u32[]{:S(2)}, u32[]{:S(2)}) collective-permute-start(f32[4,16,1024]{2,1,0:T(8,128)S(1)} %get-tuple-element.123), channel_id=1, source_target_pairs={{0,24},{4,28},{8,16},{12,20},{16,8},{20,12},{24,0},{28,4},{32,56},... | collective-permute-start | bytes 786440 | tf_op jit(solution)/shard_map/ppermute | solution.py:17
  19.6 0.7 shard_map.94
  20.2 3.0 %collective-permute-done.5 = f32[2,16,1024]{2,1,0:T(8,128)S(1)} collective-permute-done((f32[2,16,1024]{2,1,0:T(8,128)S(1)}, f32[2,16,1024]{2,1,0:T(8,128)S(1)}, u32[]{:S(2)}, u32[]{:S(2)}) %collective-permute-start.5) | collective-permute-done | bytes 131104 | tf_op jit(solution)/shard_map/ppermute | solution.py:17
  23.8 2.8 %collective-permute-start.9 = (f32[16,1024]{1,0:T(8,128)S(1)}, f32[16,1024]{1,0:T(8,128)S(1)}, u32[]{:S(2)}, u32[]{:S(2)}) collective-permute-start(f32[16,1024]{1,0:T(8,128)S(1)} %get-tuple-element.129), channel_id=1, source_target_pairs={{0,96},{4,100},{8,104},{12,108},{16,112},{20,116},{24,120},{28,124... | collective-permute-start | bytes 196616 | tf_op jit(solution)/shard_map/ppermute | solution.py:17
  26.6 0.8 %collective-permute-start.8 = (f32[16,1024]{1,0:T(8,128)S(1)}, f32[16,1024]{1,0:T(8,128)S(1)}, u32[]{:S(2)}, u32[]{:S(2)}) collective-permute-start(f32[16,1024]{1,0:T(8,128)S(1)} %get-tuple-element.129), channel_id=1, source_target_pairs={{0,64},{4,68},{8,72},{12,76},{16,80},{20,84},{24,88},{28,92},{32,9... | collective-permute-start | bytes 196616 | tf_op jit(solution)/shard_map/ppermute | solution.py:17
  27.4 0.5 collective-permute-start.7
  27.9 2.4 %shard_map.95 = (bf16[256,1024]{1,0:T(8,128)(2,1)S(1)}, f32[1024,128]{1,0:T(8,128)S(1)}, f32[1024,128]{1,0:T(8,128)S(1)}) custom-call(f32[1024,128]{1,0:T(8,128)S(1)} %get-tuple-element.84.last_b, f32[1024,128]{1,0:T(8,128)S(1)} %get-tuple-element.85.last_c, bf16[1024,1024]{1,0:T(8,128)(2,1)S(1)} %copy-done.1, bf16[1024,128]{1,0:T(8,128)(2,1)S(1)} %copy-done.4, ...), custom_call_target="tpu_custom_call" | custom-call | flops 1000000000 | bytes 1048576 | tf_op jit(solution)/shard_map/pallas_call | solution.py:214
  30.3 2.0 %collective-permute-done.8 = f32[16,1024]{1,0:T(8,128)S(1)} collective-permute-done((f32[16,1024]{1,0:T(8,128)S(1)}, f32[16,1024]{1,0:T(8,128)S(1)}, u32[]{:S(2)}, u32[]{:S(2)}) %collective-permute-start.8) | collective-permute-done | bytes 65568 | tf_op jit(solution)/shard_map/ppermute | solution.py:17
  32.4 1.9 %collective-permute-start.12 = (f32[2,16,1024]{2,1,0:T(8,128)S(1)}, f32[2,16,1024]{2,1,0:T(8,128)S(1)}, u32[]{:S(2)}, u32[]{:S(2)}) collective-permute-start(f32[2,16,1024]{2,1,0:T(8,128)S(1)} %pad_maximum_fusion.5), channel_id=1, source_target_pairs={{0,24},{4,28},{8,16},{12,20},{16,8},{20,12},{24,0},{28,4},{32,56},... | collective-permute-start | bytes 393224 | tf_op jit(solution)/shard_map/ppermute | solution.py:17
  34.3 0.8 %collective-permute-start.11 = (f32[2,16,1024]{2,1,0:T(8,128)S(1)}, f32[2,16,1024]{2,1,0:T(8,128)S(1)}, u32[]{:S(2)}, u32[]{:S(2)}) collective-permute-start(f32[2,16,1024]{2,1,0:T(8,128)S(1)} %pad_maximum_fusion.5), channel_id=1, source_target_pairs={{0,16},{4,20},{8,24},{12,28},{16,0},{20,4},{24,8},{28,12},{32,48},... | collective-permute-start | bytes 393224 | tf_op jit(solution)/shard_map/ppermute | solution.py:17
  35.1 1.5 %collective-permute-start.10 = (f32[2,16,1024]{2,1,0:T(8,128)S(1)}, f32[2,16,1024]{2,1,0:T(8,128)S(1)}, u32[]{:S(2)}, u32[]{:S(2)}) collective-permute-start(f32[2,16,1024]{2,1,0:T(8,128)S(1)} %pad_maximum_fusion.5), channel_id=1, source_target_pairs={{0,8},{4,12},{8,0},{12,4},{16,24},{20,28},{24,16},{28,20},{32,40},... | collective-permute-start | bytes 393224 | tf_op jit(solution)/shard_map/ppermute | solution.py:17
  36.6 0.6 collective-permute-start.13
  37.2 2.8 %shard_map.96 = (bf16[512,768]{1,0:T(8,128)(2,1)S(1)}, f32[1024,128]{1,0:T(8,128)S(1)}, f32[1024,128]{1,0:T(8,128)S(1)}) custom-call(f32[1024,128]{1,0:T(8,128)S(1)} %get-tuple-element.88.last_b, f32[1024,128]{1,0:T(8,128)S(1)} %get-tuple-element.89.last_c, bf16[1024,1024]{1,0:T(8,128)(2,1)S(1)} %copy-done.1, bf16[1024,128]{1,0:T(8,128)(2,1)S(1)} %copy-done.4, ...), custom_call_target="tpu_custom_call" | custom-call | flops 20000000000 | bytes 1048576 | tf_op jit(solution)/shard_map/pallas_call | solution.py:214
  40.1 5.5 %collective-permute-done.13 = f32[4,16,1024]{2,1,0:T(8,128)S(1)} collective-permute-done((f32[4,16,1024]{2,1,0:T(8,128)S(1)}, f32[4,16,1024]{2,1,0:T(8,128)S(1)}, u32[]{:S(2)}, u32[]{:S(2)}) %collective-permute-start.13) | collective-permute-done | bytes 262176 | tf_op jit(solution)/shard_map/ppermute | solution.py:17
  46.3 1.4 %collective-permute-done.15.far_other = f32[2,64,1024]{2,1,0:T(8,128)S(1)} collective-permute-done((f32[2,64,1024]{2,1,0:T(8,128)S(1)}, f32[2,64,1024]{2,1,0:T(8,128)S(1)}, u32[]{:S(2)}, u32[]{:S(2)}) %collective-permute-start.15) | collective-permute-done | bytes 524320 | tf_op jit(solution)/shard_map/ppermute | solution.py:17
  47.7 0.7 %collective-permute-done.14.near_other = f32[2,64,1024]{2,1,0:T(8,128)S(1)} collective-permute-done((f32[2,64,1024]{2,1,0:T(8,128)S(1)}, f32[2,64,1024]{2,1,0:T(8,128)S(1)}, u32[]{:S(2)}, u32[]{:S(2)}) %collective-permute-start.14) | collective-permute-done | bytes 524320 | tf_op jit(solution)/shard_map/ppermute | solution.py:17
  48.5 1.1 %shard_map.97 = (f32[256,128]{1,0:T(8,128)S(1)}, f32[256,128]{1,0:T(8,128)S(1)}, bf16[640,1024]{1,0:T(8,128)(2,1)S(1)}, bf16[128,1024]{1,0:T(8,128)(2,1)S(1)}) custom-call(f32[4,64,1024]{2,1,0:T(8,128)S(1)} %collective-permute-done.1.rest_ref, f32[2,64,1024]{2,1,0:T(8,128)S(1)} %pad_maximum_fusion.1.near_ref, ...), custom_call_target="tpu_custom_call" | custom-call | flops 1610612736 | bytes 1048576 | tf_op jit(solution)/shard_map/pallas_call | solution.py:242
  49.5 3.1 %collective-permute-start.16 = (f32[256,128]{1,0:T(8,128)S(1)}, f32[256,128]{1,0:T(8,128)S(1)}, u32[]{:S(2)}, u32[]{:S(2)}) collective-permute-start(f32[256,128]{1,0:T(8,128)S(1)} %get-tuple-element.111), channel_id=1, source_target_pairs={{0,3},{1,2},{2,1},{3,0},{4,7},{5,6},{6,5},{7,4},{8,11},{9,10},{10,... | collective-permute-start | bytes 393224 | tf_op jit(solution)/shard_map/ppermute | solution.py:17
  52.8 1.8 %shard_map.99 = (f32[2,256,128]{2,1,0:T(8,128)S(1)}, f32[2,256,128]{2,1,0:T(8,128)S(1)}, f32[2,256,128]{2,1,0:T(8,128)S(1)}) custom-call(f32[1024,128]{1,0:T(8,128)S(1)} %get-tuple-element.103.gb_ref, f32[1024,128]{1,0:T(8,128)S(1)} %get-tuple-element.104.gc_ref, bf16[1024,1024]{1,0:T(8,128)(2,1)S(1)} %copy-done.1, bf16[1024,1024]{1,0:T(8,128)(2,1)S(1)} %copy-done.3, ...), custom_call_target="tpu_custom_call" | custom-call | flops 1610612736 | bytes 1048576 | tf_op jit(solution)/shard_map/pallas_call | solution.py:248
  54.6 3.3 %collective-permute-done.18 = f32[256,128]{1,0:T(8,128)S(1)} collective-permute-done((f32[256,128]{1,0:T(8,128)S(1)}, f32[256,128]{1,0:T(8,128)S(1)}, u32[]{:S(2)}, u32[]{:S(2)}) %collective-permute-start.18) | collective-permute-done | bytes 131104 | tf_op jit(solution)/shard_map/ppermute | solution.py:17
  58.7 6.8 %shard_map.98 = (bf16[1024,1024]{1,0:T(8,128)(2,1)}, bf16[1024,1024]{1,0:T(8,128)(2,1)}) custom-call(bf16[256,256]{1,0:T(8,128)(2,1)S(1)} %get-tuple-element.79.mix_first, bf16[512,768]{1,0:T(8,128)(2,1)S(1)} %get-tuple-element.93.mix_middle, bf16[256,1024]{1,0:T(8,128)(2,1)S(1)} %get-tuple-element.94.mix_last, bf16[1024,1024]{1,0:T(8,128)(2,1)S(1)} %copy-done.1, ...), custom_call_target="tpu_custom_call" | custom-call | flops 3758096384 | bytes 1048576 | tf_op jit(solution)/shard_map/pallas_call | solution.py:257
  65.5 0.9 %collective-permute-done.19.part3 = f32[2,256,128]{2,1,0:T(8,128)S(1)} collective-permute-done((f32[2,256,128]{2,1,0:T(8,128)S(1)}, f32[2,256,128]{2,1,0:T(8,128)S(1)}, u32[]{:S(2)}, u32[]{:S(2)}) %collective-permute-start.19) | collective-permute-done | bytes 262176 | tf_op jit(solution)/shard_map/ppermute | solution.py:17
  66.4 0.7 %shard_map.100 = (f32[256,128]{1,0:T(8,128)}, f32[256,128]{1,0:T(8,128)}) custom-call(f32[2,256,128]{2,1,0:T(8,128)S(1)} %get-tuple-element.109.part0, f32[2,256,128]{2,1,0:T(8,128)S(1)} %collective-permute-done.17.part1, f32[2,256,128]{2,1,0:T(8,128)S(1)} %collective-permute-done.19.part3), custom_call_target="tpu_custom_call" | custom-call | flops 131072 | bytes 1048576 | tf_op jit(solution)/shard_map/pallas_call | solution.py:264
  (46 shorter events, 2.7 us)
Async XLA Ops:
  0.6 0.7 %copy-start = (f32[16,18]{1,0:T(8,128)S(1)}, f32[16,18]{1,0:T(8,128)}, u32[]{:S(2)}) copy-start(f32[16,18]{1,0:T(8,128)} %param.14) | copy-start | bytes 3460
  3.6 1.6 %copy-start.1 = (bf16[1024,1024]{1,0:T(8,128)(2,1)S(1)}, bf16[1024,1024]{1,0:T(8,128)(2,1)}, u32[]{:S(2)}) copy-start(bf16[1024,1024]{1,0:T(8,128)(2,1)} %x_ref.7) | copy-start | bytes 6291460
  5.2 1.6 %copy-start.2 = (bf16[1024,1024]{1,0:T(8,128)(2,1)S(1)}, bf16[1024,1024]{1,0:T(8,128)(2,1)}, u32[]{:S(2)}) copy-start(bf16[1024,1024]{1,0:T(8,128)(2,1)} %d_ref.7) | copy-start | bytes 6291460
  8.8 2.0 %collective-permute-start = (f32[2,64,1024]{2,1,0:T(8,128)S(1)}, f32[2,64,1024]{2,1,0:T(8,128)S(1)}, u32[]{:S(2)}, u32[]{:S(2)}) collective-permute-start(f32[2,64,1024]{2,1,0:T(8,128)S(1)} %get-tuple-element.73), channel_id=1, source_target_pairs={{0,4},{4,0},{8,12},{12,8},{16,20},{20,16},{24,28},{28,24},{32,36},... | collective-permute-start | bytes 1572872 | tf_op jit(solution)/shard_map/ppermute | solution.py:17
  10.8 5.4 %collective-permute-start.1 = (f32[4,64,1024]{2,1,0:T(8,128)S(1)}, f32[4,64,1024]{2,1,0:T(8,128)S(1)}, u32[]{:S(2)}, u32[]{:S(2)}) collective-permute-start(f32[4,64,1024]{2,1,0:T(8,128)S(1)} %get-tuple-element.77), channel_id=1, source_target_pairs={{0,4},{4,0},{8,12},{12,8},{16,20},{20,16},{24,28},{28,24},{32,36},... | collective-permute-start | bytes 3145736 | tf_op jit(solution)/shard_map/ppermute | solution.py:17
  11.0 8.6 %copy-start.3 = (bf16[1024,1024]{1,0:T(8,128)(2,1)S(1)}, bf16[1024,1024]{1,0:T(8,128)(2,1)}, u32[]{:S(2)}) copy-start(bf16[1024,1024]{1,0:T(8,128)(2,1)} %d_ref.7) | copy-start | bytes 6291460
  11.0 8.6 %copy-start.4 = (bf16[1024,128]{1,0:T(8,128)(2,1)S(1)}, bf16[1024,128]{1,0:T(8,128)(2,1)}, u32[]{:S(2)}) copy-start(bf16[1024,128]{1,0:T(8,128)(2,1)} %b_ref.1) | copy-start | bytes 786436
  11.0 8.6 %copy-start.5 = (bf16[1024,128]{1,0:T(8,128)(2,1)S(1)}, bf16[1024,128]{1,0:T(8,128)(2,1)}, u32[]{:S(2)}) copy-start(bf16[1024,128]{1,0:T(8,128)(2,1)} %c_ref.1) | copy-start | bytes 786436
  11.0 9.2 %collective-permute-start.4 = (f32[2,16,1024]{2,1,0:T(8,128)S(1)}, f32[2,16,1024]{2,1,0:T(8,128)S(1)}, u32[]{:S(2)}, u32[]{:S(2)}) collective-permute-start(f32[2,16,1024]{2,1,0:T(8,128)S(1)} %get-tuple-element.120), channel_id=1, source_target_pairs={{0,16},{4,20},{8,24},{12,28},{16,0},{20,4},{24,8},{28,12},{32,48},... | collective-permute-start | bytes 393224 | tf_op jit(solution)/shard_map/ppermute | solution.py:17
  15.1 8.2 %collective-permute-start.5 = (f32[2,16,1024]{2,1,0:T(8,128)S(1)}, f32[2,16,1024]{2,1,0:T(8,128)S(1)}, u32[]{:S(2)}, u32[]{:S(2)}) collective-permute-start(f32[2,16,1024]{2,1,0:T(8,128)S(1)} %get-tuple-element.121), channel_id=1, source_target_pairs={{0,8},{4,12},{8,0},{12,4},{16,24},{20,28},{24,16},{28,20},{32,40},... | collective-permute-start | bytes 393224 | tf_op jit(solution)/shard_map/ppermute | solution.py:17
  16.1 7.6 %collective-permute-start.6 = (f32[2,16,1024]{2,1,0:T(8,128)S(1)}, f32[2,16,1024]{2,1,0:T(8,128)S(1)}, u32[]{:S(2)}, u32[]{:S(2)}) collective-permute-start(f32[2,16,1024]{2,1,0:T(8,128)S(1)} %get-tuple-element.122), channel_id=1, source_target_pairs={{0,24},{4,28},{8,16},{12,20},{16,8},{20,12},{24,0},{28,4},{32,56},... | collective-permute-start | bytes 393224 | tf_op jit(solution)/shard_map/ppermute | solution.py:17
  16.2 16.2 %collective-permute-start.3 = (f32[4,16,1024]{2,1,0:T(8,128)S(1)}, f32[4,16,1024]{2,1,0:T(8,128)S(1)}, u32[]{:S(2)}, u32[]{:S(2)}) collective-permute-start(f32[4,16,1024]{2,1,0:T(8,128)S(1)} %get-tuple-element.123), channel_id=1, source_target_pairs={{0,24},{4,28},{8,16},{12,20},{16,8},{20,12},{24,0},{28,4},{32,56},... | collective-permute-start | bytes 786440 | tf_op jit(solution)/shard_map/ppermute | solution.py:17
  19.5 12.9 %collective-permute-start.2 = (f32[4,16,1024]{2,1,0:T(8,128)S(1)}, f32[4,16,1024]{2,1,0:T(8,128)S(1)}, u32[]{:S(2)}, u32[]{:S(2)}) collective-permute-start(f32[4,16,1024]{2,1,0:T(8,128)S(1)} %get-tuple-element.124), channel_id=1, source_target_pairs={{0,8},{4,12},{8,0},{12,4},{16,24},{20,28},{24,16},{28,20},{32,40},... | collective-permute-start | bytes 786440 | tf_op jit(solution)/shard_map/ppermute | solution.py:17
  23.8 6.6 %collective-permute-start.9 = (f32[16,1024]{1,0:T(8,128)S(1)}, f32[16,1024]{1,0:T(8,128)S(1)}, u32[]{:S(2)}, u32[]{:S(2)}) collective-permute-start(f32[16,1024]{1,0:T(8,128)S(1)} %get-tuple-element.129), channel_id=1, source_target_pairs={{0,96},{4,100},{8,104},{12,108},{16,112},{20,116},{24,120},{28,124... | collective-permute-start | bytes 196616 | tf_op jit(solution)/shard_map/ppermute | solution.py:17
  26.6 5.8 %collective-permute-start.8 = (f32[16,1024]{1,0:T(8,128)S(1)}, f32[16,1024]{1,0:T(8,128)S(1)}, u32[]{:S(2)}, u32[]{:S(2)}) collective-permute-start(f32[16,1024]{1,0:T(8,128)S(1)} %get-tuple-element.129), channel_id=1, source_target_pairs={{0,64},{4,68},{8,72},{12,76},{16,80},{20,84},{24,88},{28,92},{32,9... | collective-permute-start | bytes 196616 | tf_op jit(solution)/shard_map/ppermute | solution.py:17
  27.4 5.0 %collective-permute-start.7 = (f32[16,1024]{1,0:T(8,128)S(1)}, f32[16,1024]{1,0:T(8,128)S(1)}, u32[]{:S(2)}, u32[]{:S(2)}) collective-permute-start(f32[16,1024]{1,0:T(8,128)S(1)} %get-tuple-element.130), channel_id=1, source_target_pairs={{0,32},{4,36},{8,40},{12,44},{16,48},{20,52},{24,56},{28,60},{32,0... | collective-permute-start | bytes 196616 | tf_op jit(solution)/shard_map/ppermute | solution.py:17
  32.4 13.2 %collective-permute-start.12 = (f32[2,16,1024]{2,1,0:T(8,128)S(1)}, f32[2,16,1024]{2,1,0:T(8,128)S(1)}, u32[]{:S(2)}, u32[]{:S(2)}) collective-permute-start(f32[2,16,1024]{2,1,0:T(8,128)S(1)} %pad_maximum_fusion.5), channel_id=1, source_target_pairs={{0,24},{4,28},{8,16},{12,20},{16,8},{20,12},{24,0},{28,4},{32,56},... | collective-permute-start | bytes 393224 | tf_op jit(solution)/shard_map/ppermute | solution.py:17
  34.3 11.3 %collective-permute-start.11 = (f32[2,16,1024]{2,1,0:T(8,128)S(1)}, f32[2,16,1024]{2,1,0:T(8,128)S(1)}, u32[]{:S(2)}, u32[]{:S(2)}) collective-permute-start(f32[2,16,1024]{2,1,0:T(8,128)S(1)} %pad_maximum_fusion.5), channel_id=1, source_target_pairs={{0,16},{4,20},{8,24},{12,28},{16,0},{20,4},{24,8},{28,12},{32,48},... | collective-permute-start | bytes 393224 | tf_op jit(solution)/shard_map/ppermute | solution.py:17
  35.1 10.5 %collective-permute-start.10 = (f32[2,16,1024]{2,1,0:T(8,128)S(1)}, f32[2,16,1024]{2,1,0:T(8,128)S(1)}, u32[]{:S(2)}, u32[]{:S(2)}) collective-permute-start(f32[2,16,1024]{2,1,0:T(8,128)S(1)} %pad_maximum_fusion.5), channel_id=1, source_target_pairs={{0,8},{4,12},{8,0},{12,4},{16,24},{20,28},{24,16},{28,20},{32,40},... | collective-permute-start | bytes 393224 | tf_op jit(solution)/shard_map/ppermute | solution.py:17
  36.6 8.9 %collective-permute-start.13 = (f32[4,16,1024]{2,1,0:T(8,128)S(1)}, f32[4,16,1024]{2,1,0:T(8,128)S(1)}, u32[]{:S(2)}, u32[]{:S(2)}) collective-permute-start(f32[4,16,1024]{2,1,0:T(8,128)S(1)} %collective-permute-done.3), channel_id=1, source_target_pairs={{0,8},{4,12},{8,0},{12,4},{16,24},{20,28},{24,16},{28,20},{32,40},... | collective-permute-start | bytes 786440 | tf_op jit(solution)/shard_map/ppermute | solution.py:17
  45.7 2.0 %collective-permute-start.15 = (f32[2,64,1024]{2,1,0:T(8,128)S(1)}, f32[2,64,1024]{2,1,0:T(8,128)S(1)}, u32[]{:S(2)}, u32[]{:S(2)}) collective-permute-start(f32[2,64,1024]{2,1,0:T(8,128)S(1)} %bitcast.54), channel_id=1, source_target_pairs={{0,4},{4,0},{8,12},{12,8},{16,20},{20,16},{24,28},{28,24},{32,36},... | collective-permute-start | bytes 1572872 | tf_op jit(solution)/shard_map/ppermute | solution.py:17
  45.8 2.6 %collective-permute-start.14 = (f32[2,64,1024]{2,1,0:T(8,128)S(1)}, f32[2,64,1024]{2,1,0:T(8,128)S(1)}, u32[]{:S(2)}, u32[]{:S(2)}) collective-permute-start(f32[2,64,1024]{2,1,0:T(8,128)S(1)} %pad_maximum_fusion.1.near_ref), channel_id=1, source_target_pairs={{0,4},{4,0},{8,12},{12,8},{16,20},{20,16},{24,28},{28,24},{32,36},... | collective-permute-start | bytes 1572872 | tf_op jit(solution)/shard_map/ppermute | solution.py:17
  49.5 8.8 %collective-permute-start.16 = (f32[256,128]{1,0:T(8,128)S(1)}, f32[256,128]{1,0:T(8,128)S(1)}, u32[]{:S(2)}, u32[]{:S(2)}) collective-permute-start(f32[256,128]{1,0:T(8,128)S(1)} %get-tuple-element.111), channel_id=1, source_target_pairs={{0,3},{1,2},{2,1},{3,0},{4,7},{5,6},{6,5},{7,4},{8,11},{9,10},{10,... | collective-permute-start | bytes 393224 | tf_op jit(solution)/shard_map/ppermute | solution.py:17
  52.6 5.3 %collective-permute-start.18 = (f32[256,128]{1,0:T(8,128)S(1)}, f32[256,128]{1,0:T(8,128)S(1)}, u32[]{:S(2)}, u32[]{:S(2)}) collective-permute-start(f32[256,128]{1,0:T(8,128)S(1)} %get-tuple-element.113), channel_id=1, source_target_pairs={{0,1},{1,0},{2,3},{3,2},{4,5},{5,4},{6,7},{7,6},{8,9},{9,8},{10,11... | collective-permute-start | bytes 393224 | tf_op jit(solution)/shard_map/ppermute | solution.py:17
  57.9 8.5 %collective-permute-start.19 = (f32[2,256,128]{2,1,0:T(8,128)S(1)}, f32[2,256,128]{2,1,0:T(8,128)S(1)}, u32[]{:S(2)}, u32[]{:S(2)}) collective-permute-start(f32[2,256,128]{2,1,0:T(8,128)S(1)} %fusion.5), channel_id=1, source_target_pairs={{0,3},{1,2},{2,1},{3,0},{4,7},{5,6},{6,5},{7,4},{8,11},{9,10},{10,... | collective-permute-start | bytes 786440 | tf_op jit(solution)/shard_map/ppermute | solution.py:17
  58.4 8.0 %collective-permute-start.17 = (f32[2,256,128]{2,1,0:T(8,128)S(1)}, f32[2,256,128]{2,1,0:T(8,128)S(1)}, u32[]{:S(2)}, u32[]{:S(2)}) collective-permute-start(f32[2,256,128]{2,1,0:T(8,128)S(1)} %fusion.6), channel_id=1, source_target_pairs={{0,1},{1,0},{2,3},{3,2},{4,5},{5,4},{6,7},{7,6},{8,9},{9,8},{10,11... | collective-permute-start | bytes 786440 | tf_op jit(solution)/shard_map/ppermute | solution.py:17

commit v6 on v5

--- a/solution.py
+++ b/solution.py
@@ -50,21 +50,26 @@
     return bits[0] * 64 + bits[2] * 32 + bits[1] * 16
 
 
-def state_kernel(x_ref, bc_ref, d_ref, lam_ref, far_send, far_keep, rest_send, near_keep, left):
-    tiles = [slice(at, at + TILE) for at in range(0, x_ref.shape[1], TILE)]
+def rows_kernel(bc_ref, lam_ref, b_t_ref, left):
     bits = own_bits()
     n = bc_ref.shape[1] // 2
     rows = lax.broadcasted_iota(jnp.int32, (n, n), 0)
     cols = lax.broadcasted_iota(jnp.int32, (n, n), 1)
     perm = (cols == (rows ^ row_mask(bits))).astype(F32).astype(BF16)
     c_t = dot_nt(perm, bc_ref[:, n:])
-    b_t = dot_nt(perm, bc_ref[:, :n]).astype(BF16)
+    b_t_ref[...] = dot_nt(perm, bc_ref[:, :n]).astype(BF16)
     lam_t = lam_ref[...].T
     for k in range(5):
         left[k * n : (k + 1) * n, :] = (lam_t[11 + k : 12 + k, :] * c_t).astype(BF16)
+
+
+def state_kernel(x_ref, d_ref, b_t_ref, left, far_send, far_keep, rest_send, near_keep):
+    bits = own_bits()
+    n = b_t_ref.shape[0]
     half = n // 2
-    for here in tiles:
-        state = dot_nn(b_t, x_ref[:, here])
+    for at in range(0, x_ref.shape[1], TILE):
+        here = slice(at, at + TILE)
+        state = dot_nn(b_t_ref[...], x_ref[:, here])
         grads = dot_nn(left[...], d_ref[:, here])
         for k in range(5):
             value = jnp.where(bits[k] == 1, grads[k * n : (k + 1) * n], state)
@@ -198,13 +203,15 @@
     table_rows = jnp.arange(table.shape[0], dtype=jnp.int32)
     chooser = (level_index[:, None] == table_rows[None, :]).astype(F32)
     lam = jnp.dot(chooser, table, precision=lax.Precision.HIGHEST)
+    b_t, left = call(rows_kernel, (((n, rows), BF16), ((5 * n, rows), BF16)), [VMEM] * 2, LONG)(
+        jnp.concatenate([b_in, c_in], axis=1), lam
+    )
     far_send, far_keep, rest_send, near_keep = call(
         state_kernel,
         (half, half, ((4, n // 2, width), F32), half),
         [VMEM] * 4,
         2 * rows * width * n * 6,
-        [pltpu.VMEM((5 * n, rows), BF16)],
-    )(x_in, jnp.concatenate([b_in, c_in], axis=1), d_out, lam)
+    )(x_in, d_out, b_t, left)
     far, rest_send = tie((from_xor(far_send, CORE), rest_send))
     far = (far_keep + far).reshape(2, 4, n // 8, width)
     rest = from_xor(rest_send, CORE)
@@ -218,17 +225,16 @@
     total = far[:, 0]
     for part in taken:
         total = total + part
-    total, grad_b = tie((total, grad_b))
+    near_later, total, grad_b = tie((near[1], total, grad_b))
     b3 = from_xor(total[0], X[1])
     b4 = from_xor(total[1], X[2]) + from_xor(total[1], X[3])
     r1, r3 = from_xor(near[0], Z[1]), from_xor(near[1], Z[3])
-    x_tied, _ = tie((x_in, total))
-    mix_last, grad_b, grad_c = local_part(local_last, (TILE, rows), (grad_b, grad_c, x_tied, b_in, c_in, d_out, lam), LAST)
-    r1, r3, b3, b4, grad_b = tie((r1, r3, b3, b4, grad_b))
+    r2 = from_xor(near_later, Z[2])
+    r1, r3, b3, b4 = tie((r1, r3, b3, b4))
     b34 = jnp.stack([b3, b4])
     gathered = [from_xor(b34, Z[m]) for m in (1, 2, 3)]
-    r2 = from_xor(r3, Z[1])
     x_tied, b34 = tie((x_in, b34))
+    mix_last, grad_b, grad_c = local_part(local_last, (TILE, rows), (grad_b, grad_c, x_tied, b_in, c_in, d_out, lam), LONG)
     mix_middle, grad_b, grad_c = local_part(
         local_middle, (2 * TILE, 3 * TILE), (grad_b, grad_c, x_tied, b_in, c_in, d_out, lam), LONG
     )

time: 67.4 us -> 64.1 us (0.951); the launches traced: 67.1 us -> 63.1 us
  waiting for transfers between devices: 19.2 us -> 15.7 us
  local copies, waits for them, and re-layouts: 3.99 us -> 2.64 us
  starting transfers between devices: 22.1 us -> 22.8 us
    ppermute x20, waiting for transfers between devices: 19.2 us -> 15.7 us  [from_xor(): return lax.ppermute(block, axis, route)]
    unnamed x12 -> x10, local copies, waits for them, and re-layouts: 3.89 us -> 2.56 us
    ppermute x20, starting transfers between devices: 22.1 us -> 22.8 us  [from_xor(): return lax.ppermute(block, axis, route)]
  transfers between devices with their start and end apart: 20 -> 20, of which waited for: 9 -> 11; matrix products, arithmetic and copies ran while one was open for 1% -> 1% of each run, Pallas kernels for 22% -> 23%
where the time goes in v6:
time: 64.1 us; the launch traced here: 63.1 us
  starting transfers between devices  22.8 us (36%)
  Pallas kernels  18.4 us (29%)
  waiting for transfers between devices  15.7 us (24%)
  local copies, waits for them, and re-layouts  2.64 us (4%)
  other arithmetic  1.49 us (2%)
  matrix products  1.14 us (2%)
  between operations  0.91 us (1%)
    ppermute x20, starting transfers between devices, from_xor(): return lax.ppermute(block, axis, route)  22.8 us
    ppermute x20, waiting for transfers between devices, from_xor(): return lax.ppermute(block, axis, route)  15.7 us
    pallas_call x1, Pallas kernels, local(): call(output_kernel, (((rows, width), BF16), ((rows, width), BF16)), [VMEM...  6.81 us
    pallas_call x3, Pallas kernels, local_part(): call(kernel, ((mix, BF16), ((rows, n), F32), ((rows, n), F32)), [VMEM] *...  5.84 us
    unnamed x10, local copies, waits for them, and re-layouts  2.56 us
    pallas_call x1, Pallas kernels, local(): call(grad_rest_kernel, (piece, piece, piece), [VMEM] * 7, 2 * rows * widt...  1.83 us
    pallas_call x1, Pallas kernels, local(): call(state_kernel, (half, half, ((4, n // 2, width), F32), half), [VMEM]...  1.83 us
  transfers between devices with their start and end apart: 20, of which 11 were waited for; matrix products, arithmetic and copies ran while one was open for 1% of the time, Pallas kernels for 23%

profile of v6, /device:TPU:0, one launch (start us, length us, event | category | flops | bytes accessed | tf_op | source)
XLA Modules:
  0.0 63.1 jit_solution(1796264608695978507)
XLA Ops:
  0.6 0.7 %copy-done = f32[16,18]{1,0:T(8,128)S(1)} copy-done((f32[16,18]{1,0:T(8,128)S(1)}, f32[16,18]{1,0:T(8,128)}, u32[]{:S(2)}) %copy-start) | copy-done | bytes 1176
  1.3 1.1 %fusion.lam_ref.refs_4_ = f32[1024,18]{1,0:T(8,128)S(1)} fusion(f32[16,18]{1,0:T(8,128)S(1)} %copy-done, s32[1024]{0:T(1024)} %param.15), kind=kOutput, calls=%fused_computation.5 | convolution fusion | flops 3555328 | bytes 78976 | tf_op jit(solution)/shard_map/dot_general | solution.py:205
  2.5 1.1 %pad_maximum_fusion.bc_ref = bf16[1024,256]{1,0:T(8,128)(2,1)S(1)} fusion(bf16[1024,128]{1,0:T(8,128)(2,1)} %c_ref.1, bf16[1024,128]{1,0:T(8,128)(2,1)} %b_ref.1), kind=kLoop, calls=%fused_computation.1 | loop fusion | flops 1048576 | bytes 1048576 | tf_op jit(solution)/shard_map/concatenate | solution.py:207
  4.0 1.2 %copy-done.1 = bf16[1024,1024]{1,0:T(8,128)(2,1)S(1)} copy-done((bf16[1024,1024]{1,0:T(8,128)(2,1)S(1)}, bf16[1024,1024]{1,0:T(8,128)(2,1)}, u32[]{:S(2)}) %copy-start.1) | copy-done | bytes 2097176
  5.2 0.6 %copy-done.2 = bf16[1024,1024]{1,0:T(8,128)(2,1)S(1)} copy-done((bf16[1024,1024]{1,0:T(8,128)(2,1)S(1)}, bf16[1024,1024]{1,0:T(8,128)(2,1)}, u32[]{:S(2)}) %copy-start.2) | copy-done | bytes 2097176
  5.8 1.8 %shard_map.94 = (f32[2,64,1024]{2,1,0:T(8,128)S(1)}, f32[2,64,1024]{2,1,0:T(8,128)S(1)}, f32[4,64,1024]{2,1,0:T(8,128)S(1)}, f32[2,64,1024]{2,1,0:T(8,128)S(1)}) custom-call(bf16[1024,1024]{1,0:T(8,128)(2,1)S(1)} %copy-done.1, bf16[1024,1024]{1,0:T(8,128)(2,1)S(1)} %copy-done.2, bf16[128,1024]{1,0:T(8,128)(2,1)S(1)} %get-tuple-element.73.b_t_ref, ...), custom_call_target="tpu_custom_call" | custom-call | flops 1610612736 | bytes 1048576 | tf_op jit(solution)/shard_map/pallas_call | solution.py:209
  7.7 1.9 %collective-permute-done = f32[2,64,1024]{2,1,0:T(8,128)S(1)} collective-permute-done((f32[2,64,1024]{2,1,0:T(8,128)S(1)}, f32[2,64,1024]{2,1,0:T(8,128)S(1)}, u32[]{:S(2)}, u32[]{:S(2)}) %collective-permute-start) | collective-permute-done | bytes 524320 | tf_op jit(solution)/shard_map/ppermute | solution.py:17
  9.9 4.1 %collective-permute-start.2 = (f32[2,16,1024]{2,1,0:T(8,128)S(1)}, f32[2,16,1024]{2,1,0:T(8,128)S(1)}, u32[]{:S(2)}, u32[]{:S(2)}) collective-permute-start(f32[2,16,1024]{2,1,0:T(8,128)S(1)} %get-tuple-element.124), channel_id=1, source_target_pairs={{0,16},{4,20},{8,24},{12,28},{16,0},{20,4},{24,8},{28,12},{32,48},... | collective-permute-start | bytes 393224 | tf_op jit(solution)/shard_map/ppermute | solution.py:17
  13.9 1.0 %collective-permute-start.3 = (f32[2,16,1024]{2,1,0:T(8,128)S(1)}, f32[2,16,1024]{2,1,0:T(8,128)S(1)}, u32[]{:S(2)}, u32[]{:S(2)}) collective-permute-start(f32[2,16,1024]{2,1,0:T(8,128)S(1)} %get-tuple-element.125), channel_id=1, source_target_pairs={{0,8},{4,12},{8,0},{12,4},{16,24},{20,28},{24,16},{28,20},{32,40},... | collective-permute-start | bytes 393224 | tf_op jit(solution)/shard_map/ppermute | solution.py:17
  15.1 1.2 %collective-permute-start.5 = (f32[4,16,1024]{2,1,0:T(8,128)S(1)}, f32[4,16,1024]{2,1,0:T(8,128)S(1)}, u32[]{:S(2)}, u32[]{:S(2)}) collective-permute-start(f32[4,16,1024]{2,1,0:T(8,128)S(1)} %get-tuple-element.122), channel_id=1, source_target_pairs={{0,8},{4,12},{8,0},{12,4},{16,24},{20,28},{24,16},{28,20},{32,40},... | collective-permute-start | bytes 786440 | tf_op jit(solution)/shard_map/ppermute | solution.py:17
  16.3 2.5 %collective-permute-start.6 = (f32[4,16,1024]{2,1,0:T(8,128)S(1)}, f32[4,16,1024]{2,1,0:T(8,128)S(1)}, u32[]{:S(2)}, u32[]{:S(2)}) collective-permute-start(f32[4,16,1024]{2,1,0:T(8,128)S(1)} %get-tuple-element.97), channel_id=1, source_target_pairs={{0,24},{4,28},{8,16},{12,20},{16,8},{20,12},{24,0},{28,4},{32,56},... | collective-permute-start | bytes 786440 | tf_op jit(solution)/shard_map/ppermute | solution.py:17
  18.8 0.6 %shard_map.95 = (bf16[256,256]{1,0:T(8,128)(2,1)S(1)}, f32[1024,128]{1,0:T(8,128)S(1)}, f32[1024,128]{1,0:T(8,128)S(1)}) custom-call(bf16[1024,1024]{1,0:T(8,128)(2,1)S(1)} %copy-done.1, bf16[1024,128]{1,0:T(8,128)(2,1)S(1)} %copy-done.3, bf16[1024,128]{1,0:T(8,128)(2,1)S(1)} %copy-done.4, bf16[1024,1024]{1,0:T(8,128)(2,1)S(1)} %copy-done.2, ...), custom_call_target="tpu_custom_call" | custom-call | flops 1000000000 | bytes 1048576 | tf_op jit(solution)/shard_map/pallas_call | solution.py:221
  19.5 2.6 %collective-permute-done.3 = f32[2,16,1024]{2,1,0:T(8,128)S(1)} collective-permute-done((f32[2,16,1024]{2,1,0:T(8,128)S(1)}, f32[2,16,1024]{2,1,0:T(8,128)S(1)}, u32[]{:S(2)}, u32[]{:S(2)}) %collective-permute-start.3) | collective-permute-done | bytes 131104 | tf_op jit(solution)/shard_map/ppermute | solution.py:17
  22.6 2.8 %collective-permute-start.9 = (f32[16,1024]{1,0:T(8,128)S(1)}, f32[16,1024]{1,0:T(8,128)S(1)}, u32[]{:S(2)}, u32[]{:S(2)}) collective-permute-start(f32[16,1024]{1,0:T(8,128)S(1)} %get-tuple-element.131), channel_id=1, source_target_pairs={{0,96},{4,100},{8,104},{12,108},{16,112},{20,116},{24,120},{28,124... | collective-permute-start | bytes 196616 | tf_op jit(solution)/shard_map/ppermute | solution.py:17
  25.5 0.8 %collective-permute-start.8 = (f32[16,1024]{1,0:T(8,128)S(1)}, f32[16,1024]{1,0:T(8,128)S(1)}, u32[]{:S(2)}, u32[]{:S(2)}) collective-permute-start(f32[16,1024]{1,0:T(8,128)S(1)} %get-tuple-element.131), channel_id=1, source_target_pairs={{0,64},{4,68},{8,72},{12,76},{16,80},{20,84},{24,88},{28,92},{32,9... | collective-permute-start | bytes 196616 | tf_op jit(solution)/shard_map/ppermute | solution.py:17
  26.8 2.1 %collective-permute-done.9 = f32[16,1024]{1,0:T(8,128)S(1)} collective-permute-done((f32[16,1024]{1,0:T(8,128)S(1)}, f32[16,1024]{1,0:T(8,128)S(1)}, u32[]{:S(2)}, u32[]{:S(2)}) %collective-permute-start.9) | collective-permute-done | bytes 65568 | tf_op jit(solution)/shard_map/ppermute | solution.py:17
  28.9 0.8 %collective-permute-start.13 = (f32[4,16,1024]{2,1,0:T(8,128)S(1)}, f32[4,16,1024]{2,1,0:T(8,128)S(1)}, u32[]{:S(2)}, u32[]{:S(2)}) collective-permute-start(f32[4,16,1024]{2,1,0:T(8,128)S(1)} %get-tuple-element.97), channel_id=1, source_target_pairs={{0,16},{4,20},{8,24},{12,28},{16,0},{20,4},{24,8},{28,12},{32,48},... | collective-permute-start | bytes 786440 | tf_op jit(solution)/shard_map/ppermute | solution.py:17
  29.7 1.5 %collective-permute-done.8 = f32[16,1024]{1,0:T(8,128)S(1)} collective-permute-done((f32[16,1024]{1,0:T(8,128)S(1)}, f32[16,1024]{1,0:T(8,128)S(1)}, u32[]{:S(2)}, u32[]{:S(2)}) %collective-permute-start.8) | collective-permute-done | bytes 65568 | tf_op jit(solution)/shard_map/ppermute | solution.py:17
  31.3 1.9 %collective-permute-start.12 = (f32[2,16,1024]{2,1,0:T(8,128)S(1)}, f32[2,16,1024]{2,1,0:T(8,128)S(1)}, u32[]{:S(2)}, u32[]{:S(2)}) collective-permute-start(f32[2,16,1024]{2,1,0:T(8,128)S(1)} %pad_maximum_fusion.5), channel_id=1, source_target_pairs={{0,24},{4,28},{8,16},{12,20},{16,8},{20,12},{24,0},{28,4},{32,56},... | collective-permute-start | bytes 393224 | tf_op jit(solution)/shard_map/ppermute | solution.py:17
  33.2 0.8 %collective-permute-start.11 = (f32[2,16,1024]{2,1,0:T(8,128)S(1)}, f32[2,16,1024]{2,1,0:T(8,128)S(1)}, u32[]{:S(2)}, u32[]{:S(2)}) collective-permute-start(f32[2,16,1024]{2,1,0:T(8,128)S(1)} %pad_maximum_fusion.5), channel_id=1, source_target_pairs={{0,16},{4,20},{8,24},{12,28},{16,0},{20,4},{24,8},{28,12},{32,48},... | collective-permute-start | bytes 393224 | tf_op jit(solution)/shard_map/ppermute | solution.py:17
  34.0 1.5 %collective-permute-start.10 = (f32[2,16,1024]{2,1,0:T(8,128)S(1)}, f32[2,16,1024]{2,1,0:T(8,128)S(1)}, u32[]{:S(2)}, u32[]{:S(2)}) collective-permute-start(f32[2,16,1024]{2,1,0:T(8,128)S(1)} %pad_maximum_fusion.5), channel_id=1, source_target_pairs={{0,8},{4,12},{8,0},{12,4},{16,24},{20,28},{24,16},{28,20},{32,40},... | collective-permute-start | bytes 393224 | tf_op jit(solution)/shard_map/ppermute | solution.py:17
  35.5 2.4 %shard_map.96 = (bf16[256,1024]{1,0:T(8,128)(2,1)S(1)}, f32[1024,128]{1,0:T(8,128)S(1)}, f32[1024,128]{1,0:T(8,128)S(1)}) custom-call(f32[1024,128]{1,0:T(8,128)S(1)} %get-tuple-element.86.last_b, f32[1024,128]{1,0:T(8,128)S(1)} %get-tuple-element.87.last_c, bf16[1024,1024]{1,0:T(8,128)(2,1)S(1)} %copy-done.1, bf16[1024,128]{1,0:T(8,128)(2,1)S(1)} %copy-done.3, ...), custom_call_target="tpu_custom_call" | custom-call | flops 20000000000 | bytes 1048576 | tf_op jit(solution)/shard_map/pallas_call | solution.py:221
  37.8 2.8 %shard_map.97 = (bf16[512,768]{1,0:T(8,128)(2,1)S(1)}, f32[1024,128]{1,0:T(8,128)S(1)}, f32[1024,128]{1,0:T(8,128)S(1)}) custom-call(f32[1024,128]{1,0:T(8,128)S(1)} %get-tuple-element.92.last_b, f32[1024,128]{1,0:T(8,128)S(1)} %get-tuple-element.93.last_c, bf16[1024,1024]{1,0:T(8,128)(2,1)S(1)} %copy-done.1, bf16[1024,128]{1,0:T(8,128)(2,1)S(1)} %copy-done.3, ...), custom_call_target="tpu_custom_call" | custom-call | flops 20000000000 | bytes 1048576 | tf_op jit(solution)/shard_map/pallas_call | solution.py:221
  42.3 1.4 %collective-permute-done.15.far_other = f32[2,64,1024]{2,1,0:T(8,128)S(1)} collective-permute-done((f32[2,64,1024]{2,1,0:T(8,128)S(1)}, f32[2,64,1024]{2,1,0:T(8,128)S(1)}, u32[]{:S(2)}, u32[]{:S(2)}) %collective-permute-start.15) | collective-permute-done | bytes 524320 | tf_op jit(solution)/shard_map/ppermute | solution.py:17
  43.7 0.7 %collective-permute-done.14.near_other = f32[2,64,1024]{2,1,0:T(8,128)S(1)} collective-permute-done((f32[2,64,1024]{2,1,0:T(8,128)S(1)}, f32[2,64,1024]{2,1,0:T(8,128)S(1)}, u32[]{:S(2)}, u32[]{:S(2)}) %collective-permute-start.14) | collective-permute-done | bytes 524320 | tf_op jit(solution)/shard_map/ppermute | solution.py:17
  44.5 1.1 %shard_map.98 = (f32[256,128]{1,0:T(8,128)S(1)}, f32[256,128]{1,0:T(8,128)S(1)}, bf16[640,1024]{1,0:T(8,128)(2,1)S(1)}, bf16[128,1024]{1,0:T(8,128)(2,1)S(1)}) custom-call(f32[4,64,1024]{2,1,0:T(8,128)S(1)} %collective-permute-done.1.rest_ref, f32[2,64,1024]{2,1,0:T(8,128)S(1)} %pad_maximum_fusion.1.near_ref, ...), custom_call_target="tpu_custom_call" | custom-call | flops 1610612736 | bytes 1048576 | tf_op jit(solution)/shard_map/pallas_call | solution.py:248
  45.5 3.1 %collective-permute-start.16 = (f32[256,128]{1,0:T(8,128)S(1)}, f32[256,128]{1,0:T(8,128)S(1)}, u32[]{:S(2)}, u32[]{:S(2)}) collective-permute-start(f32[256,128]{1,0:T(8,128)S(1)} %get-tuple-element.113), channel_id=1, source_target_pairs={{0,3},{1,2},{2,1},{3,0},{4,7},{5,6},{6,5},{7,4},{8,11},{9,10},{10,... | collective-permute-start | bytes 393224 | tf_op jit(solution)/shard_map/ppermute | solution.py:17
  48.7 1.8 %shard_map.100 = (f32[2,256,128]{2,1,0:T(8,128)S(1)}, f32[2,256,128]{2,1,0:T(8,128)S(1)}, f32[2,256,128]{2,1,0:T(8,128)S(1)}) custom-call(f32[1024,128]{1,0:T(8,128)S(1)} %get-tuple-element.105.gb_ref, f32[1024,128]{1,0:T(8,128)S(1)} %get-tuple-element.106.gc_ref, bf16[1024,1024]{1,0:T(8,128)(2,1)S(1)} %copy-done.1, bf16[1024,1024]{1,0:T(8,128)(2,1)S(1)} %copy-done.2, ...), custom_call_target="tpu_custom_call" | custom-call | flops 1610612736 | bytes 1048576 | tf_op jit(solution)/shard_map/pallas_call | solution.py:254
  50.6 3.3 %collective-permute-done.18 = f32[256,128]{1,0:T(8,128)S(1)} collective-permute-done((f32[256,128]{1,0:T(8,128)S(1)}, f32[256,128]{1,0:T(8,128)S(1)}, u32[]{:S(2)}, u32[]{:S(2)}) %collective-permute-start.18) | collective-permute-done | bytes 131104 | tf_op jit(solution)/shard_map/ppermute | solution.py:17
  54.7 6.8 %shard_map.99 = (bf16[1024,1024]{1,0:T(8,128)(2,1)}, bf16[1024,1024]{1,0:T(8,128)(2,1)}) custom-call(bf16[256,256]{1,0:T(8,128)(2,1)S(1)} %get-tuple-element.82.mix_first, bf16[512,768]{1,0:T(8,128)(2,1)S(1)} %get-tuple-element.94.mix_middle, bf16[256,1024]{1,0:T(8,128)(2,1)S(1)} %get-tuple-element.95.mix_last, bf16[1024,1024]{1,0:T(8,128)(2,1)S(1)} %copy-done.1, ...), custom_call_target="tpu_custom_call" | custom-call | flops 3758096384 | bytes 1048576 | tf_op jit(solution)/shard_map/pallas_call | solution.py:263
  61.5 0.9 %collective-permute-done.19.part3 = f32[2,256,128]{2,1,0:T(8,128)S(1)} collective-permute-done((f32[2,256,128]{2,1,0:T(8,128)S(1)}, f32[2,256,128]{2,1,0:T(8,128)S(1)}, u32[]{:S(2)}, u32[]{:S(2)}) %collective-permute-start.19) | collective-permute-done | bytes 262176 | tf_op jit(solution)/shard_map/ppermute | solution.py:17
  62.4 0.7 %shard_map.101 = (f32[256,128]{1,0:T(8,128)}, f32[256,128]{1,0:T(8,128)}) custom-call(f32[2,256,128]{2,1,0:T(8,128)S(1)} %get-tuple-element.111.part0, f32[2,256,128]{2,1,0:T(8,128)S(1)} %collective-permute-done.17.part1, f32[2,256,128]{2,1,0:T(8,128)S(1)} %collective-permute-done.19.part3), custom_call_target="tpu_custom_call" | custom-call | flops 131072 | bytes 1048576 | tf_op jit(solution)/shard_map/pallas_call | solution.py:270
  (44 shorter events, 4.4 us)
Async XLA Ops:
  0.6 0.7 %copy-start = (f32[16,18]{1,0:T(8,128)S(1)}, f32[16,18]{1,0:T(8,128)}, u32[]{:S(2)}) copy-start(f32[16,18]{1,0:T(8,128)} %param.14) | copy-start | bytes 3460
  3.6 1.6 %copy-start.1 = (bf16[1024,1024]{1,0:T(8,128)(2,1)S(1)}, bf16[1024,1024]{1,0:T(8,128)(2,1)}, u32[]{:S(2)}) copy-start(bf16[1024,1024]{1,0:T(8,128)(2,1)} %x_ref.7) | copy-start | bytes 6291460
  3.6 2.2 %copy-start.2 = (bf16[1024,1024]{1,0:T(8,128)(2,1)S(1)}, bf16[1024,1024]{1,0:T(8,128)(2,1)}, u32[]{:S(2)}) copy-start(bf16[1024,1024]{1,0:T(8,128)(2,1)} %d_ref.7) | copy-start | bytes 6291460
  7.6 2.0 %collective-permute-start = (f32[2,64,1024]{2,1,0:T(8,128)S(1)}, f32[2,64,1024]{2,1,0:T(8,128)S(1)}, u32[]{:S(2)}, u32[]{:S(2)}) collective-permute-start(f32[2,64,1024]{2,1,0:T(8,128)S(1)} %get-tuple-element.76), channel_id=1, source_target_pairs={{0,4},{4,0},{8,12},{12,8},{16,20},{20,16},{24,28},{28,24},{32,36},... | collective-permute-start | bytes 1572872 | tf_op jit(solution)/shard_map/ppermute | solution.py:17
  9.6 5.3 %collective-permute-start.1 = (f32[4,64,1024]{2,1,0:T(8,128)S(1)}, f32[4,64,1024]{2,1,0:T(8,128)S(1)}, u32[]{:S(2)}, u32[]{:S(2)}) collective-permute-start(f32[4,64,1024]{2,1,0:T(8,128)S(1)} %get-tuple-element.80), channel_id=1, source_target_pairs={{0,4},{4,0},{8,12},{12,8},{16,20},{20,16},{24,28},{28,24},{32,36},... | collective-permute-start | bytes 3145736 | tf_op jit(solution)/shard_map/ppermute | solution.py:17
  9.8 9.0 %copy-start.3 = (bf16[1024,128]{1,0:T(8,128)(2,1)S(1)}, bf16[1024,128]{1,0:T(8,128)(2,1)}, u32[]{:S(2)}) copy-start(bf16[1024,128]{1,0:T(8,128)(2,1)} %b_ref.1) | copy-start | bytes 786436
  9.8 9.0 %copy-start.4 = (bf16[1024,128]{1,0:T(8,128)(2,1)S(1)}, bf16[1024,128]{1,0:T(8,128)(2,1)}, u32[]{:S(2)}) copy-start(bf16[1024,128]{1,0:T(8,128)(2,1)} %c_ref.1) | copy-start | bytes 786436
  9.9 9.6 %collective-permute-start.2 = (f32[2,16,1024]{2,1,0:T(8,128)S(1)}, f32[2,16,1024]{2,1,0:T(8,128)S(1)}, u32[]{:S(2)}, u32[]{:S(2)}) collective-permute-start(f32[2,16,1024]{2,1,0:T(8,128)S(1)} %get-tuple-element.124), channel_id=1, source_target_pairs={{0,16},{4,20},{8,24},{12,28},{16,0},{20,4},{24,8},{28,12},{32,48},... | collective-permute-start | bytes 393224 | tf_op jit(solution)/shard_map/ppermute | solution.py:17
  13.9 8.2 %collective-permute-start.3 = (f32[2,16,1024]{2,1,0:T(8,128)S(1)}, f32[2,16,1024]{2,1,0:T(8,128)S(1)}, u32[]{:S(2)}, u32[]{:S(2)}) collective-permute-start(f32[2,16,1024]{2,1,0:T(8,128)S(1)} %get-tuple-element.125), channel_id=1, source_target_pairs={{0,8},{4,12},{8,0},{12,4},{16,24},{20,28},{24,16},{28,20},{32,40},... | collective-permute-start | bytes 393224 | tf_op jit(solution)/shard_map/ppermute | solution.py:17
  15.0 7.6 %collective-permute-start.4 = (f32[2,16,1024]{2,1,0:T(8,128)S(1)}, f32[2,16,1024]{2,1,0:T(8,128)S(1)}, u32[]{:S(2)}, u32[]{:S(2)}) collective-permute-start(f32[2,16,1024]{2,1,0:T(8,128)S(1)} %get-tuple-element.126), channel_id=1, source_target_pairs={{0,24},{4,28},{8,16},{12,20},{16,8},{20,12},{24,0},{28,4},{32,56},... | collective-permute-start | bytes 393224 | tf_op jit(solution)/shard_map/ppermute | solution.py:17
  15.1 16.2 %collective-permute-start.5 = (f32[4,16,1024]{2,1,0:T(8,128)S(1)}, f32[4,16,1024]{2,1,0:T(8,128)S(1)}, u32[]{:S(2)}, u32[]{:S(2)}) collective-permute-start(f32[4,16,1024]{2,1,0:T(8,128)S(1)} %get-tuple-element.122), channel_id=1, source_target_pairs={{0,8},{4,12},{8,0},{12,4},{16,24},{20,28},{24,16},{28,20},{32,40},... | collective-permute-start | bytes 786440 | tf_op jit(solution)/shard_map/ppermute | solution.py:17
  16.3 15.0 %collective-permute-start.6 = (f32[4,16,1024]{2,1,0:T(8,128)S(1)}, f32[4,16,1024]{2,1,0:T(8,128)S(1)}, u32[]{:S(2)}, u32[]{:S(2)}) collective-permute-start(f32[4,16,1024]{2,1,0:T(8,128)S(1)} %get-tuple-element.97), channel_id=1, source_target_pairs={{0,24},{4,28},{8,16},{12,20},{16,8},{20,12},{24,0},{28,4},{32,56},... | collective-permute-start | bytes 786440 | tf_op jit(solution)/shard_map/ppermute | solution.py:17
  22.6 6.3 %collective-permute-start.9 = (f32[16,1024]{1,0:T(8,128)S(1)}, f32[16,1024]{1,0:T(8,128)S(1)}, u32[]{:S(2)}, u32[]{:S(2)}) collective-permute-start(f32[16,1024]{1,0:T(8,128)S(1)} %get-tuple-element.131), channel_id=1, source_target_pairs={{0,96},{4,100},{8,104},{12,108},{16,112},{20,116},{24,120},{28,124... | collective-permute-start | bytes 196616 | tf_op jit(solution)/shard_map/ppermute | solution.py:17
  25.5 5.8 %collective-permute-start.8 = (f32[16,1024]{1,0:T(8,128)S(1)}, f32[16,1024]{1,0:T(8,128)S(1)}, u32[]{:S(2)}, u32[]{:S(2)}) collective-permute-start(f32[16,1024]{1,0:T(8,128)S(1)} %get-tuple-element.131), channel_id=1, source_target_pairs={{0,64},{4,68},{8,72},{12,76},{16,80},{20,84},{24,88},{28,92},{32,9... | collective-permute-start | bytes 196616 | tf_op jit(solution)/shard_map/ppermute | solution.py:17
  26.3 5.0 %collective-permute-start.7 = (f32[16,1024]{1,0:T(8,128)S(1)}, f32[16,1024]{1,0:T(8,128)S(1)}, u32[]{:S(2)}, u32[]{:S(2)}) collective-permute-start(f32[16,1024]{1,0:T(8,128)S(1)} %get-tuple-element.132), channel_id=1, source_target_pairs={{0,32},{4,36},{8,40},{12,44},{16,48},{20,52},{24,56},{28,60},{32,0... | collective-permute-start | bytes 196616 | tf_op jit(solution)/shard_map/ppermute | solution.py:17
  28.9 11.8 %collective-permute-start.13 = (f32[4,16,1024]{2,1,0:T(8,128)S(1)}, f32[4,16,1024]{2,1,0:T(8,128)S(1)}, u32[]{:S(2)}, u32[]{:S(2)}) collective-permute-start(f32[4,16,1024]{2,1,0:T(8,128)S(1)} %get-tuple-element.97), channel_id=1, source_target_pairs={{0,16},{4,20},{8,24},{12,28},{16,0},{20,4},{24,8},{28,12},{32,48},... | collective-permute-start | bytes 786440 | tf_op jit(solution)/shard_map/ppermute | solution.py:17
  31.3 9.9 %collective-permute-start.12 = (f32[2,16,1024]{2,1,0:T(8,128)S(1)}, f32[2,16,1024]{2,1,0:T(8,128)S(1)}, u32[]{:S(2)}, u32[]{:S(2)}) collective-permute-start(f32[2,16,1024]{2,1,0:T(8,128)S(1)} %pad_maximum_fusion.5), channel_id=1, source_target_pairs={{0,24},{4,28},{8,16},{12,20},{16,8},{20,12},{24,0},{28,4},{32,56},... | collective-permute-start | bytes 393224 | tf_op jit(solution)/shard_map/ppermute | solution.py:17
  33.2 8.0 %collective-permute-start.11 = (f32[2,16,1024]{2,1,0:T(8,128)S(1)}, f32[2,16,1024]{2,1,0:T(8,128)S(1)}, u32[]{:S(2)}, u32[]{:S(2)}) collective-permute-start(f32[2,16,1024]{2,1,0:T(8,128)S(1)} %pad_maximum_fusion.5), channel_id=1, source_target_pairs={{0,16},{4,20},{8,24},{12,28},{16,0},{20,4},{24,8},{28,12},{32,48},... | collective-permute-start | bytes 393224 | tf_op jit(solution)/shard_map/ppermute | solution.py:17
  34.0 7.7 %collective-permute-start.10 = (f32[2,16,1024]{2,1,0:T(8,128)S(1)}, f32[2,16,1024]{2,1,0:T(8,128)S(1)}, u32[]{:S(2)}, u32[]{:S(2)}) collective-permute-start(f32[2,16,1024]{2,1,0:T(8,128)S(1)} %pad_maximum_fusion.5), channel_id=1, source_target_pairs={{0,8},{4,12},{8,0},{12,4},{16,24},{20,28},{24,16},{28,20},{32,40},... | collective-permute-start | bytes 393224 | tf_op jit(solution)/shard_map/ppermute | solution.py:17
  41.7 2.0 %collective-permute-start.15 = (f32[2,64,1024]{2,1,0:T(8,128)S(1)}, f32[2,64,1024]{2,1,0:T(8,128)S(1)}, u32[]{:S(2)}, u32[]{:S(2)}) collective-permute-start(f32[2,64,1024]{2,1,0:T(8,128)S(1)} %bitcast.54), channel_id=1, source_target_pairs={{0,4},{4,0},{8,12},{12,8},{16,20},{20,16},{24,28},{28,24},{32,36},... | collective-permute-start | bytes 1572872 | tf_op jit(solution)/shard_map/ppermute | solution.py:17
  41.8 2.6 %collective-permute-start.14 = (f32[2,64,1024]{2,1,0:T(8,128)S(1)}, f32[2,64,1024]{2,1,0:T(8,128)S(1)}, u32[]{:S(2)}, u32[]{:S(2)}) collective-permute-start(f32[2,64,1024]{2,1,0:T(8,128)S(1)} %pad_maximum_fusion.1.near_ref), channel_id=1, source_target_pairs={{0,4},{4,0},{8,12},{12,8},{16,20},{20,16},{24,28},{28,24},{32,36},... | collective-permute-start | bytes 1572872 | tf_op jit(solution)/shard_map/ppermute | solution.py:17
  45.5 8.8 %collective-permute-start.16 = (f32[256,128]{1,0:T(8,128)S(1)}, f32[256,128]{1,0:T(8,128)S(1)}, u32[]{:S(2)}, u32[]{:S(2)}) collective-permute-start(f32[256,128]{1,0:T(8,128)S(1)} %get-tuple-element.113), channel_id=1, source_target_pairs={{0,3},{1,2},{2,1},{3,0},{4,7},{5,6},{6,5},{7,4},{8,11},{9,10},{10,... | collective-permute-start | bytes 393224 | tf_op jit(solution)/shard_map/ppermute | solution.py:17
  48.6 5.3 %collective-permute-start.18 = (f32[256,128]{1,0:T(8,128)S(1)}, f32[256,128]{1,0:T(8,128)S(1)}, u32[]{:S(2)}, u32[]{:S(2)}) collective-permute-start(f32[256,128]{1,0:T(8,128)S(1)} %get-tuple-element.115), channel_id=1, source_target_pairs={{0,1},{1,0},{2,3},{3,2},{4,5},{5,4},{6,7},{7,6},{8,9},{9,8},{10,11... | collective-permute-start | bytes 393224 | tf_op jit(solution)/shard_map/ppermute | solution.py:17
  53.9 8.5 %collective-permute-start.19 = (f32[2,256,128]{2,1,0:T(8,128)S(1)}, f32[2,256,128]{2,1,0:T(8,128)S(1)}, u32[]{:S(2)}, u32[]{:S(2)}) collective-permute-start(f32[2,256,128]{2,1,0:T(8,128)S(1)} %fusion.5), channel_id=1, source_target_pairs={{0,3},{1,2},{2,1},{3,0},{4,7},{5,6},{6,5},{7,4},{8,11},{9,10},{10,... | collective-permute-start | bytes 786440 | tf_op jit(solution)/shard_map/ppermute | solution.py:17
  54.4 8.0 %collective-permute-start.17 = (f32[2,256,128]{2,1,0:T(8,128)S(1)}, f32[2,256,128]{2,1,0:T(8,128)S(1)}, u32[]{:S(2)}, u32[]{:S(2)}) collective-permute-start(f32[2,256,128]{2,1,0:T(8,128)S(1)} %fusion.6), channel_id=1, source_target_pairs={{0,1},{1,0},{2,3},{3,2},{4,5},{5,4},{6,7},{7,6},{8,9},{9,8},{10,11... | collective-permute-start | bytes 786440 | tf_op jit(solution)/shard_map/ppermute | solution.py:17

commit v7 on v6

--- a/solution.py
+++ b/solution.py
@@ -50,12 +50,15 @@
     return bits[0] * 64 + bits[2] * 32 + bits[1] * 16
 
 
-def rows_kernel(bc_ref, lam_ref, b_t_ref, left):
-    bits = own_bits()
-    n = bc_ref.shape[1] // 2
-    rows = lax.broadcasted_iota(jnp.int32, (n, n), 0)
-    cols = lax.broadcasted_iota(jnp.int32, (n, n), 1)
-    perm = (cols == (rows ^ row_mask(bits))).astype(F32).astype(BF16)
+def order_kernel(perm_ref):
+    rows = lax.broadcasted_iota(jnp.int32, perm_ref.shape, 0)
+    cols = lax.broadcasted_iota(jnp.int32, perm_ref.shape, 1)
+    perm_ref[...] = (cols == (rows ^ row_mask(own_bits()))).astype(F32).astype(BF16)
+
+
+def rows_kernel(bc_ref, lam_ref, perm_ref, b_t_ref, left):
+    n = perm_ref.shape[0]
+    perm = perm_ref[...]
     c_t = dot_nt(perm, bc_ref[:, n:])
     b_t_ref[...] = dot_nt(perm, bc_ref[:, :n]).astype(BF16)
     lam_t = lam_ref[...].T
@@ -200,11 +203,13 @@
     n = b_in.shape[1]
     tie = lax.optimization_barrier
     half = ((2, n // 2, width), F32)
+    (perm,) = call(order_kernel, (((n, n), BF16),), [], LONG)()
+    perm, level_index, b_first, c_first = tie((perm, level_index, b_in, c_in))
     table_rows = jnp.arange(table.shape[0], dtype=jnp.int32)
     chooser = (level_index[:, None] == table_rows[None, :]).astype(F32)
     lam = jnp.dot(chooser, table, precision=lax.Precision.HIGHEST)
-    b_t, left = call(rows_kernel, (((n, rows), BF16), ((5 * n, rows), BF16)), [VMEM] * 2, LONG)(
-        jnp.concatenate([b_in, c_in], axis=1), lam
+    b_t, left = call(rows_kernel, (((n, rows), BF16), ((5 * n, rows), BF16)), [VMEM] * 3, 2 * rows * n * n)(
+        jnp.concatenate([b_first, c_first], axis=1), lam, perm
     )
     far_send, far_keep, rest_send, near_keep = call(
         state_kernel,

time: 64.1 us -> 61.4 us (0.958)
  other arithmetic: 1.49 us -> 0.46 us
  local copies, waits for them, and re-layouts: 2.64 us -> 1.7 us
  matrix products: 1.14 us -> 0.46 us
    concatenate x1, other arithmetic: 1.09 us -> 0.06 us  [local(): jnp.concatenate([b_first, c_first], axis=1)]
    unnamed x10 -> x12, local copies, waits for them, and re-layouts: 2.56 us -> 1.62 us
    dot_general x1, matrix products: 1.14 us -> 0.46 us  [local(): lam = jnp.dot(chooser, table, precision=lax.Precision.HIGHEST)]
  transfers between devices with their start and end apart: 20 -> 20, of which waited for: 11 -> 11; matrix products, arithmetic and copies ran while one was open for 1% -> 1% of each run, Pallas kernels for 23% -> 24%
where the time goes in v7:
time: 61.4 us; the launch traced here: 60.5 us
  starting transfers between devices  22.8 us (37%)
  Pallas kernels  18.5 us (30%)
  waiting for transfers between devices  15.7 us (26%)
  local copies, waits for them, and re-layouts  1.7 us (3%)
  between operations  0.94 us (2%)
    ppermute x20, starting transfers between devices, from_xor(): return lax.ppermute(block, axis, route)  22.8 us
    ppermute x20, waiting for transfers between devices, from_xor(): return lax.ppermute(block, axis, route)  15.7 us
    pallas_call x1, Pallas kernels, local(): call(output_kernel, (((rows, width), BF16), ((rows, width), BF16)), [VMEM...  6.81 us
    pallas_call x3, Pallas kernels, local_part(): call(kernel, ((mix, BF16), ((rows, n), F32), ((rows, n), F32)), [VMEM] *...  5.84 us
    pallas_call x1, Pallas kernels, local(): call(grad_rest_kernel, (piece, piece, piece), [VMEM] * 7, 2 * rows * widt...  1.83 us
    pallas_call x1, Pallas kernels, local(): call(state_kernel, (half, half, ((4, n // 2, width), F32), half), [VMEM]...  1.83 us
    unnamed x12, local copies, waits for them, and re-layouts  1.62 us
  transfers between devices with their start and end apart: 20, of which 11 were waited for; matrix products, arithmetic and copies ran while one was open for 1% of the time, Pallas kernels for 24%

profile of v7, /device:TPU:0, one launch (start us, length us, event | category | flops | bytes accessed | tf_op | source)
XLA Modules:
  0.0 60.5 jit_solution(5103485659660932858)
XLA Ops:
  0.7 0.6 %copy-done = f32[16,18]{1,0:T(8,128)S(1)} copy-done((f32[16,18]{1,0:T(8,128)S(1)}, f32[16,18]{1,0:T(8,128)}, u32[]{:S(2)}) %copy-start) | copy-done | bytes 1176
  2.4 0.8 %copy-done.1 = bf16[1024,1024]{1,0:T(8,128)(2,1)S(1)} copy-done((bf16[1024,1024]{1,0:T(8,128)(2,1)S(1)}, bf16[1024,1024]{1,0:T(8,128)(2,1)}, u32[]{:S(2)}) %copy-start.1) | copy-done | bytes 2097176
  3.2 1.8 %shard_map.95 = (f32[2,64,1024]{2,1,0:T(8,128)S(1)}, f32[2,64,1024]{2,1,0:T(8,128)S(1)}, f32[4,64,1024]{2,1,0:T(8,128)S(1)}, f32[2,64,1024]{2,1,0:T(8,128)S(1)}) custom-call(bf16[1024,1024]{1,0:T(8,128)(2,1)S(1)} %copy-done.1, bf16[1024,1024]{1,0:T(8,128)(2,1)S(1)} %copy-done.2, bf16[128,1024]{1,0:T(8,128)(2,1)S(1)} %get-tuple-element.81.b_t_ref, ...), custom_call_target="tpu_custom_call" | custom-call | flops 1610612736 | bytes 1048576 | tf_op jit(solution)/shard_map/pallas_call | solution.py:214
  5.2 1.9 %collective-permute-done = f32[2,64,1024]{2,1,0:T(8,128)S(1)} collective-permute-done((f32[2,64,1024]{2,1,0:T(8,128)S(1)}, f32[2,64,1024]{2,1,0:T(8,128)S(1)}, u32[]{:S(2)}, u32[]{:S(2)}) %collective-permute-start) | collective-permute-done | bytes 524320 | tf_op jit(solution)/shard_map/ppermute | solution.py:17
  7.3 4.1 %collective-permute-start.2 = (f32[2,16,1024]{2,1,0:T(8,128)S(1)}, f32[2,16,1024]{2,1,0:T(8,128)S(1)}, u32[]{:S(2)}, u32[]{:S(2)}) collective-permute-start(f32[2,16,1024]{2,1,0:T(8,128)S(1)} %get-tuple-element.132), channel_id=1, source_target_pairs={{0,16},{4,20},{8,24},{12,28},{16,0},{20,4},{24,8},{28,12},{32,48},... | collective-permute-start | bytes 393224 | tf_op jit(solution)/shard_map/ppermute | solution.py:17
  11.3 1.0 %collective-permute-start.3 = (f32[2,16,1024]{2,1,0:T(8,128)S(1)}, f32[2,16,1024]{2,1,0:T(8,128)S(1)}, u32[]{:S(2)}, u32[]{:S(2)}) collective-permute-start(f32[2,16,1024]{2,1,0:T(8,128)S(1)} %get-tuple-element.133), channel_id=1, source_target_pairs={{0,8},{4,12},{8,0},{12,4},{16,24},{20,28},{24,16},{28,20},{32,40},... | collective-permute-start | bytes 393224 | tf_op jit(solution)/shard_map/ppermute | solution.py:17
  12.5 1.2 %collective-permute-start.5 = (f32[4,16,1024]{2,1,0:T(8,128)S(1)}, f32[4,16,1024]{2,1,0:T(8,128)S(1)}, u32[]{:S(2)}, u32[]{:S(2)}) collective-permute-start(f32[4,16,1024]{2,1,0:T(8,128)S(1)} %get-tuple-element.130), channel_id=1, source_target_pairs={{0,8},{4,12},{8,0},{12,4},{16,24},{20,28},{24,16},{28,20},{32,40},... | collective-permute-start | bytes 786440 | tf_op jit(solution)/shard_map/ppermute | solution.py:17
  13.7 2.5 %collective-permute-start.6 = (f32[4,16,1024]{2,1,0:T(8,128)S(1)}, f32[4,16,1024]{2,1,0:T(8,128)S(1)}, u32[]{:S(2)}, u32[]{:S(2)}) collective-permute-start(f32[4,16,1024]{2,1,0:T(8,128)S(1)} %get-tuple-element.105), channel_id=1, source_target_pairs={{0,24},{4,28},{8,16},{12,20},{16,8},{20,12},{24,0},{28,4},{32,56},... | collective-permute-start | bytes 786440 | tf_op jit(solution)/shard_map/ppermute | solution.py:17
  16.2 0.7 %shard_map.96 = (bf16[256,256]{1,0:T(8,128)(2,1)S(1)}, f32[1024,128]{1,0:T(8,128)S(1)}, f32[1024,128]{1,0:T(8,128)S(1)}) custom-call(bf16[1024,1024]{1,0:T(8,128)(2,1)S(1)} %copy-done.1, bf16[1024,128]{1,0:T(8,128)(2,1)S(1)} %copy-done.3, bf16[1024,128]{1,0:T(8,128)(2,1)S(1)} %copy-done.4, bf16[1024,1024]{1,0:T(8,128)(2,1)S(1)} %copy-done.2, ...), custom_call_target="tpu_custom_call" | custom-call | flops 1000000000 | bytes 1048576 | tf_op jit(solution)/shard_map/pallas_call | solution.py:226
  16.9 2.6 %collective-permute-done.3 = f32[2,16,1024]{2,1,0:T(8,128)S(1)} collective-permute-done((f32[2,16,1024]{2,1,0:T(8,128)S(1)}, f32[2,16,1024]{2,1,0:T(8,128)S(1)}, u32[]{:S(2)}, u32[]{:S(2)}) %collective-permute-start.3) | collective-permute-done | bytes 131104 | tf_op jit(solution)/shard_map/ppermute | solution.py:17
  20.0 2.8 %collective-permute-start.9 = (f32[16,1024]{1,0:T(8,128)S(1)}, f32[16,1024]{1,0:T(8,128)S(1)}, u32[]{:S(2)}, u32[]{:S(2)}) collective-permute-start(f32[16,1024]{1,0:T(8,128)S(1)} %get-tuple-element.139), channel_id=1, source_target_pairs={{0,96},{4,100},{8,104},{12,108},{16,112},{20,116},{24,120},{28,124... | collective-permute-start | bytes 196616 | tf_op jit(solution)/shard_map/ppermute | solution.py:17
  22.9 0.8 %collective-permute-start.8 = (f32[16,1024]{1,0:T(8,128)S(1)}, f32[16,1024]{1,0:T(8,128)S(1)}, u32[]{:S(2)}, u32[]{:S(2)}) collective-permute-start(f32[16,1024]{1,0:T(8,128)S(1)} %get-tuple-element.139), channel_id=1, source_target_pairs={{0,64},{4,68},{8,72},{12,76},{16,80},{20,84},{24,88},{28,92},{32,9... | collective-permute-start | bytes 196616 | tf_op jit(solution)/shard_map/ppermute | solution.py:17
  23.7 0.5 collective-permute-start.7
  24.2 2.1 %collective-permute-done.9 = f32[16,1024]{1,0:T(8,128)S(1)} collective-permute-done((f32[16,1024]{1,0:T(8,128)S(1)}, f32[16,1024]{1,0:T(8,128)S(1)}, u32[]{:S(2)}, u32[]{:S(2)}) %collective-permute-start.9) | collective-permute-done | bytes 65568 | tf_op jit(solution)/shard_map/ppermute | solution.py:17
  26.3 0.8 %collective-permute-start.13 = (f32[4,16,1024]{2,1,0:T(8,128)S(1)}, f32[4,16,1024]{2,1,0:T(8,128)S(1)}, u32[]{:S(2)}, u32[]{:S(2)}) collective-permute-start(f32[4,16,1024]{2,1,0:T(8,128)S(1)} %get-tuple-element.105), channel_id=1, source_target_pairs={{0,16},{4,20},{8,24},{12,28},{16,0},{20,4},{24,8},{28,12},{32,48},... | collective-permute-start | bytes 786440 | tf_op jit(solution)/shard_map/ppermute | solution.py:17
  27.1 1.5 %collective-permute-done.8 = f32[16,1024]{1,0:T(8,128)S(1)} collective-permute-done((f32[16,1024]{1,0:T(8,128)S(1)}, f32[16,1024]{1,0:T(8,128)S(1)}, u32[]{:S(2)}, u32[]{:S(2)}) %collective-permute-start.8) | collective-permute-done | bytes 65568 | tf_op jit(solution)/shard_map/ppermute | solution.py:17
  28.7 1.9 %collective-permute-start.12 = (f32[2,16,1024]{2,1,0:T(8,128)S(1)}, f32[2,16,1024]{2,1,0:T(8,128)S(1)}, u32[]{:S(2)}, u32[]{:S(2)}) collective-permute-start(f32[2,16,1024]{2,1,0:T(8,128)S(1)} %pad_maximum_fusion.5), channel_id=1, source_target_pairs={{0,24},{4,28},{8,16},{12,20},{16,8},{20,12},{24,0},{28,4},{32,56},... | collective-permute-start | bytes 393224 | tf_op jit(solution)/shard_map/ppermute | solution.py:17
  30.6 0.8 %collective-permute-start.11 = (f32[2,16,1024]{2,1,0:T(8,128)S(1)}, f32[2,16,1024]{2,1,0:T(8,128)S(1)}, u32[]{:S(2)}, u32[]{:S(2)}) collective-permute-start(f32[2,16,1024]{2,1,0:T(8,128)S(1)} %pad_maximum_fusion.5), channel_id=1, source_target_pairs={{0,16},{4,20},{8,24},{12,28},{16,0},{20,4},{24,8},{28,12},{32,48},... | collective-permute-start | bytes 393224 | tf_op jit(solution)/shard_map/ppermute | solution.py:17
  31.4 1.5 %collective-permute-start.10 = (f32[2,16,1024]{2,1,0:T(8,128)S(1)}, f32[2,16,1024]{2,1,0:T(8,128)S(1)}, u32[]{:S(2)}, u32[]{:S(2)}) collective-permute-start(f32[2,16,1024]{2,1,0:T(8,128)S(1)} %pad_maximum_fusion.5), channel_id=1, source_target_pairs={{0,8},{4,12},{8,0},{12,4},{16,24},{20,28},{24,16},{28,20},{32,40},... | collective-permute-start | bytes 393224 | tf_op jit(solution)/shard_map/ppermute | solution.py:17
  32.9 2.4 %shard_map.97 = (bf16[256,1024]{1,0:T(8,128)(2,1)S(1)}, f32[1024,128]{1,0:T(8,128)S(1)}, f32[1024,128]{1,0:T(8,128)S(1)}) custom-call(f32[1024,128]{1,0:T(8,128)S(1)} %get-tuple-element.94.last_b, f32[1024,128]{1,0:T(8,128)S(1)} %get-tuple-element.95.last_c, bf16[1024,1024]{1,0:T(8,128)(2,1)S(1)} %copy-done.1, bf16[1024,128]{1,0:T(8,128)(2,1)S(1)} %copy-done.3, ...), custom_call_target="tpu_custom_call" | custom-call | flops 20000000000 | bytes 1048576 | tf_op jit(solution)/shard_map/pallas_call | solution.py:226
  35.2 2.8 %shard_map.98 = (bf16[512,768]{1,0:T(8,128)(2,1)S(1)}, f32[1024,128]{1,0:T(8,128)S(1)}, f32[1024,128]{1,0:T(8,128)S(1)}) custom-call(f32[1024,128]{1,0:T(8,128)S(1)} %get-tuple-element.100.last_b, f32[1024,128]{1,0:T(8,128)S(1)} %get-tuple-element.101.last_c, bf16[1024,1024]{1,0:T(8,128)(2,1)S(1)} %copy-done.1, bf16[1024,128]{1,0:T(8,128)(2,1)S(1)} %copy-done.3, ...), custom_call_target="tpu_custom_call" | custom-call | flops 20000000000 | bytes 1048576 | tf_op jit(solution)/shard_map/pallas_call | solution.py:226
  38.6 0.5 collective-permute-done.10
  39.2 0.5 collective-permute-start.14
  39.7 1.4 %collective-permute-done.15.far_other = f32[2,64,1024]{2,1,0:T(8,128)S(1)} collective-permute-done((f32[2,64,1024]{2,1,0:T(8,128)S(1)}, f32[2,64,1024]{2,1,0:T(8,128)S(1)}, u32[]{:S(2)}, u32[]{:S(2)}) %collective-permute-start.15) | collective-permute-done | bytes 524320 | tf_op jit(solution)/shard_map/ppermute | solution.py:17
  41.1 0.7 %collective-permute-done.14.near_other = f32[2,64,1024]{2,1,0:T(8,128)S(1)} collective-permute-done((f32[2,64,1024]{2,1,0:T(8,128)S(1)}, f32[2,64,1024]{2,1,0:T(8,128)S(1)}, u32[]{:S(2)}, u32[]{:S(2)}) %collective-permute-start.14) | collective-permute-done | bytes 524320 | tf_op jit(solution)/shard_map/ppermute | solution.py:17
  41.9 1.1 %shard_map.99 = (f32[256,128]{1,0:T(8,128)S(1)}, f32[256,128]{1,0:T(8,128)S(1)}, bf16[640,1024]{1,0:T(8,128)(2,1)S(1)}, bf16[128,1024]{1,0:T(8,128)(2,1)S(1)}) custom-call(f32[4,64,1024]{2,1,0:T(8,128)S(1)} %collective-permute-done.1.rest_ref, f32[2,64,1024]{2,1,0:T(8,128)S(1)} %pad_maximum_fusion.1.near_ref, ...), custom_call_target="tpu_custom_call" | custom-call | flops 1610612736 | bytes 1048576 | tf_op jit(solution)/shard_map/pallas_call | solution.py:253
  42.9 3.1 %collective-permute-start.16 = (f32[256,128]{1,0:T(8,128)S(1)}, f32[256,128]{1,0:T(8,128)S(1)}, u32[]{:S(2)}, u32[]{:S(2)}) collective-permute-start(f32[256,128]{1,0:T(8,128)S(1)} %get-tuple-element.121), channel_id=1, source_target_pairs={{0,3},{1,2},{2,1},{3,0},{4,7},{5,6},{6,5},{7,4},{8,11},{9,10},{10,... | collective-permute-start | bytes 393224 | tf_op jit(solution)/shard_map/ppermute | solution.py:17
  46.2 1.8 %shard_map.101 = (f32[2,256,128]{2,1,0:T(8,128)S(1)}, f32[2,256,128]{2,1,0:T(8,128)S(1)}, f32[2,256,128]{2,1,0:T(8,128)S(1)}) custom-call(f32[1024,128]{1,0:T(8,128)S(1)} %get-tuple-element.113.gb_ref, f32[1024,128]{1,0:T(8,128)S(1)} %get-tuple-element.114.gc_ref, bf16[1024,1024]{1,0:T(8,128)(2,1)S(1)} %copy-done.1, bf16[1024,1024]{1,0:T(8,128)(2,1)S(1)} %copy-done.2, ...), custom_call_target="tpu_custom_call" | custom-call | flops 1610612736 | bytes 1048576 | tf_op jit(solution)/shard_map/pallas_call | solution.py:259
  48.0 3.3 %collective-permute-done.18 = f32[256,128]{1,0:T(8,128)S(1)} collective-permute-done((f32[256,128]{1,0:T(8,128)S(1)}, f32[256,128]{1,0:T(8,128)S(1)}, u32[]{:S(2)}, u32[]{:S(2)}) %collective-permute-start.18) | collective-permute-done | bytes 131104 | tf_op jit(solution)/shard_map/ppermute | solution.py:17
  52.1 6.8 %shard_map.100 = (bf16[1024,1024]{1,0:T(8,128)(2,1)}, bf16[1024,1024]{1,0:T(8,128)(2,1)}) custom-call(bf16[256,256]{1,0:T(8,128)(2,1)S(1)} %get-tuple-element.90.mix_first, bf16[512,768]{1,0:T(8,128)(2,1)S(1)} %get-tuple-element.102.mix_middle, bf16[256,1024]{1,0:T(8,128)(2,1)S(1)} %get-tuple-element.103.mix_last, bf16[1024,1024]{1,0:T(8,128)(2,1)S(1)} %copy-done.1, ...), custom_call_target="tpu_custom_call" | custom-call | flops 3758096384 | bytes 1048576 | tf_op jit(solution)/shard_map/pallas_call | solution.py:268
  58.9 0.9 %collective-permute-done.19.part3 = f32[2,256,128]{2,1,0:T(8,128)S(1)} collective-permute-done((f32[2,256,128]{2,1,0:T(8,128)S(1)}, f32[2,256,128]{2,1,0:T(8,128)S(1)}, u32[]{:S(2)}, u32[]{:S(2)}) %collective-permute-start.19) | collective-permute-done | bytes 262176 | tf_op jit(solution)/shard_map/ppermute | solution.py:17
  59.8 0.7 %shard_map.102 = (f32[256,128]{1,0:T(8,128)}, f32[256,128]{1,0:T(8,128)}) custom-call(f32[2,256,128]{2,1,0:T(8,128)S(1)} %get-tuple-element.119.part0, f32[2,256,128]{2,1,0:T(8,128)S(1)} %collective-permute-done.17.part1, f32[2,256,128]{2,1,0:T(8,128)S(1)} %collective-permute-done.19.part3), custom_call_target="tpu_custom_call" | custom-call | flops 131072 | bytes 1048576 | tf_op jit(solution)/shard_map/pallas_call | solution.py:275
  (47 shorter events, 3.6 us)
Async XLA Ops:
  0.6 0.7 %copy-start = (f32[16,18]{1,0:T(8,128)S(1)}, f32[16,18]{1,0:T(8,128)}, u32[]{:S(2)}) copy-start(f32[16,18]{1,0:T(8,128)} %param.14) | copy-start | bytes 3460
  0.6 1.2 %copy-start.4 = (bf16[1024,128]{1,0:T(8,128)(2,1)S(1)}, bf16[1024,128]{1,0:T(8,128)(2,1)}, u32[]{:S(2)}) copy-start(bf16[1024,128]{1,0:T(8,128)(2,1)} %c_ref.1) | copy-start | bytes 786436
  0.7 1.2 %copy-start.3 = (bf16[1024,128]{1,0:T(8,128)(2,1)S(1)}, bf16[1024,128]{1,0:T(8,128)(2,1)}, u32[]{:S(2)}) copy-start(bf16[1024,128]{1,0:T(8,128)(2,1)} %b_ref.1) | copy-start | bytes 786436
  0.7 0.7 %copy-start.5 = (s32[1024]{0:T(1024)S(1)}, s32[1024]{0:T(1024)}, u32[]{:S(2)}) copy-start(s32[1024]{0:T(1024)} %param.15) | copy-start | bytes 12292
  0.7 1.8 %copy-start.2 = (bf16[1024,1024]{1,0:T(8,128)(2,1)S(1)}, bf16[1024,1024]{1,0:T(8,128)(2,1)}, u32[]{:S(2)}) copy-start(bf16[1024,1024]{1,0:T(8,128)(2,1)} %d_ref.7) | copy-start | bytes 6291460
  1.4 1.8 %copy-start.1 = (bf16[1024,1024]{1,0:T(8,128)(2,1)S(1)}, bf16[1024,1024]{1,0:T(8,128)(2,1)}, u32[]{:S(2)}) copy-start(bf16[1024,1024]{1,0:T(8,128)(2,1)} %x_ref.7) | copy-start | bytes 6291460
  5.1 2.0 %collective-permute-start = (f32[2,64,1024]{2,1,0:T(8,128)S(1)}, f32[2,64,1024]{2,1,0:T(8,128)S(1)}, u32[]{:S(2)}, u32[]{:S(2)}) collective-permute-start(f32[2,64,1024]{2,1,0:T(8,128)S(1)} %get-tuple-element.84), channel_id=1, source_target_pairs={{0,4},{4,0},{8,12},{12,8},{16,20},{20,16},{24,28},{28,24},{32,36},... | collective-permute-start | bytes 1572872 | tf_op jit(solution)/shard_map/ppermute | solution.py:17
  7.1 5.3 %collective-permute-start.1 = (f32[4,64,1024]{2,1,0:T(8,128)S(1)}, f32[4,64,1024]{2,1,0:T(8,128)S(1)}, u32[]{:S(2)}, u32[]{:S(2)}) collective-permute-start(f32[4,64,1024]{2,1,0:T(8,128)S(1)} %get-tuple-element.88), channel_id=1, source_target_pairs={{0,4},{4,0},{8,12},{12,8},{16,20},{20,16},{24,28},{28,24},{32,36},... | collective-permute-start | bytes 3145736 | tf_op jit(solution)/shard_map/ppermute | solution.py:17
  7.3 9.6 %collective-permute-start.2 = (f32[2,16,1024]{2,1,0:T(8,128)S(1)}, f32[2,16,1024]{2,1,0:T(8,128)S(1)}, u32[]{:S(2)}, u32[]{:S(2)}) collective-permute-start(f32[2,16,1024]{2,1,0:T(8,128)S(1)} %get-tuple-element.132), channel_id=1, source_target_pairs={{0,16},{4,20},{8,24},{12,28},{16,0},{20,4},{24,8},{28,12},{32,48},... | collective-permute-start | bytes 393224 | tf_op jit(solution)/shard_map/ppermute | solution.py:17
  11.3 8.2 %collective-permute-start.3 = (f32[2,16,1024]{2,1,0:T(8,128)S(1)}, f32[2,16,1024]{2,1,0:T(8,128)S(1)}, u32[]{:S(2)}, u32[]{:S(2)}) collective-permute-start(f32[2,16,1024]{2,1,0:T(8,128)S(1)} %get-tuple-element.133), channel_id=1, source_target_pairs={{0,8},{4,12},{8,0},{12,4},{16,24},{20,28},{24,16},{28,20},{32,40},... | collective-permute-start | bytes 393224 | tf_op jit(solution)/shard_map/ppermute | solution.py:17
  12.4 7.6 %collective-permute-start.4 = (f32[2,16,1024]{2,1,0:T(8,128)S(1)}, f32[2,16,1024]{2,1,0:T(8,128)S(1)}, u32[]{:S(2)}, u32[]{:S(2)}) collective-permute-start(f32[2,16,1024]{2,1,0:T(8,128)S(1)} %get-tuple-element.134), channel_id=1, source_target_pairs={{0,24},{4,28},{8,16},{12,20},{16,8},{20,12},{24,0},{28,4},{32,56},... | collective-permute-start | bytes 393224 | tf_op jit(solution)/shard_map/ppermute | solution.py:17
  12.5 16.2 %collective-permute-start.5 = (f32[4,16,1024]{2,1,0:T(8,128)S(1)}, f32[4,16,1024]{2,1,0:T(8,128)S(1)}, u32[]{:S(2)}, u32[]{:S(2)}) collective-permute-start(f32[4,16,1024]{2,1,0:T(8,128)S(1)} %get-tuple-element.130), channel_id=1, source_target_pairs={{0,8},{4,12},{8,0},{12,4},{16,24},{20,28},{24,16},{28,20},{32,40},... | collective-permute-start | bytes 786440 | tf_op jit(solution)/shard_map/ppermute | solution.py:17
  13.7 15.0 %collective-permute-start.6 = (f32[4,16,1024]{2,1,0:T(8,128)S(1)}, f32[4,16,1024]{2,1,0:T(8,128)S(1)}, u32[]{:S(2)}, u32[]{:S(2)}) collective-permute-start(f32[4,16,1024]{2,1,0:T(8,128)S(1)} %get-tuple-element.105), channel_id=1, source_target_pairs={{0,24},{4,28},{8,16},{12,20},{16,8},{20,12},{24,0},{28,4},{32,56},... | collective-permute-start | bytes 786440 | tf_op jit(solution)/shard_map/ppermute | solution.py:17
  20.0 6.3 %collective-permute-start.9 = (f32[16,1024]{1,0:T(8,128)S(1)}, f32[16,1024]{1,0:T(8,128)S(1)}, u32[]{:S(2)}, u32[]{:S(2)}) collective-permute-start(f32[16,1024]{1,0:T(8,128)S(1)} %get-tuple-element.139), channel_id=1, source_target_pairs={{0,96},{4,100},{8,104},{12,108},{16,112},{20,116},{24,120},{28,124... | collective-permute-start | bytes 196616 | tf_op jit(solution)/shard_map/ppermute | solution.py:17
  22.9 5.8 %collective-permute-start.8 = (f32[16,1024]{1,0:T(8,128)S(1)}, f32[16,1024]{1,0:T(8,128)S(1)}, u32[]{:S(2)}, u32[]{:S(2)}) collective-permute-start(f32[16,1024]{1,0:T(8,128)S(1)} %get-tuple-element.139), channel_id=1, source_target_pairs={{0,64},{4,68},{8,72},{12,76},{16,80},{20,84},{24,88},{28,92},{32,9... | collective-permute-start | bytes 196616 | tf_op jit(solution)/shard_map/ppermute | solution.py:17
  23.7 5.0 %collective-permute-start.7 = (f32[16,1024]{1,0:T(8,128)S(1)}, f32[16,1024]{1,0:T(8,128)S(1)}, u32[]{:S(2)}, u32[]{:S(2)}) collective-permute-start(f32[16,1024]{1,0:T(8,128)S(1)} %get-tuple-element.140), channel_id=1, source_target_pairs={{0,32},{4,36},{8,40},{12,44},{16,48},{20,52},{24,56},{28,60},{32,0... | collective-permute-start | bytes 196616 | tf_op jit(solution)/shard_map/ppermute | solution.py:17
  26.3 11.8 %collective-permute-start.13 = (f32[4,16,1024]{2,1,0:T(8,128)S(1)}, f32[4,16,1024]{2,1,0:T(8,128)S(1)}, u32[]{:S(2)}, u32[]{:S(2)}) collective-permute-start(f32[4,16,1024]{2,1,0:T(8,128)S(1)} %get-tuple-element.105), channel_id=1, source_target_pairs={{0,16},{4,20},{8,24},{12,28},{16,0},{20,4},{24,8},{28,12},{32,48},... | collective-permute-start | bytes 786440 | tf_op jit(solution)/shard_map/ppermute | solution.py:17
  28.7 9.9 %collective-permute-start.12 = (f32[2,16,1024]{2,1,0:T(8,128)S(1)}, f32[2,16,1024]{2,1,0:T(8,128)S(1)}, u32[]{:S(2)}, u32[]{:S(2)}) collective-permute-start(f32[2,16,1024]{2,1,0:T(8,128)S(1)} %pad_maximum_fusion.5), channel_id=1, source_target_pairs={{0,24},{4,28},{8,16},{12,20},{16,8},{20,12},{24,0},{28,4},{32,56},... | collective-permute-start | bytes 393224 | tf_op jit(solution)/shard_map/ppermute | solution.py:17
  30.6 8.0 %collective-permute-start.11 = (f32[2,16,1024]{2,1,0:T(8,128)S(1)}, f32[2,16,1024]{2,1,0:T(8,128)S(1)}, u32[]{:S(2)}, u32[]{:S(2)}) collective-permute-start(f32[2,16,1024]{2,1,0:T(8,128)S(1)} %pad_maximum_fusion.5), channel_id=1, source_target_pairs={{0,16},{4,20},{8,24},{12,28},{16,0},{20,4},{24,8},{28,12},{32,48},... | collective-permute-start | bytes 393224 | tf_op jit(solution)/shard_map/ppermute | solution.py:17
  31.4 7.7 %collective-permute-start.10 = (f32[2,16,1024]{2,1,0:T(8,128)S(1)}, f32[2,16,1024]{2,1,0:T(8,128)S(1)}, u32[]{:S(2)}, u32[]{:S(2)}) collective-permute-start(f32[2,16,1024]{2,1,0:T(8,128)S(1)} %pad_maximum_fusion.5), channel_id=1, source_target_pairs={{0,8},{4,12},{8,0},{12,4},{16,24},{20,28},{24,16},{28,20},{32,40},... | collective-permute-start | bytes 393224 | tf_op jit(solution)/shard_map/ppermute | solution.py:17
  39.1 2.0 %collective-permute-start.15 = (f32[2,64,1024]{2,1,0:T(8,128)S(1)}, f32[2,64,1024]{2,1,0:T(8,128)S(1)}, u32[]{:S(2)}, u32[]{:S(2)}) collective-permute-start(f32[2,64,1024]{2,1,0:T(8,128)S(1)} %bitcast.54), channel_id=1, source_target_pairs={{0,4},{4,0},{8,12},{12,8},{16,20},{20,16},{24,28},{28,24},{32,36},... | collective-permute-start | bytes 1572872 | tf_op jit(solution)/shard_map/ppermute | solution.py:17
  39.2 2.6 %collective-permute-start.14 = (f32[2,64,1024]{2,1,0:T(8,128)S(1)}, f32[2,64,1024]{2,1,0:T(8,128)S(1)}, u32[]{:S(2)}, u32[]{:S(2)}) collective-permute-start(f32[2,64,1024]{2,1,0:T(8,128)S(1)} %pad_maximum_fusion.1.near_ref), channel_id=1, source_target_pairs={{0,4},{4,0},{8,12},{12,8},{16,20},{20,16},{24,28},{28,24},{32,36},... | collective-permute-start | bytes 1572872 | tf_op jit(solution)/shard_map/ppermute | solution.py:17
  42.9 8.8 %collective-permute-start.16 = (f32[256,128]{1,0:T(8,128)S(1)}, f32[256,128]{1,0:T(8,128)S(1)}, u32[]{:S(2)}, u32[]{:S(2)}) collective-permute-start(f32[256,128]{1,0:T(8,128)S(1)} %get-tuple-element.121), channel_id=1, source_target_pairs={{0,3},{1,2},{2,1},{3,0},{4,7},{5,6},{6,5},{7,4},{8,11},{9,10},{10,... | collective-permute-start | bytes 393224 | tf_op jit(solution)/shard_map/ppermute | solution.py:17
  46.0 5.3 %collective-permute-start.18 = (f32[256,128]{1,0:T(8,128)S(1)}, f32[256,128]{1,0:T(8,128)S(1)}, u32[]{:S(2)}, u32[]{:S(2)}) collective-permute-start(f32[256,128]{1,0:T(8,128)S(1)} %get-tuple-element.123), channel_id=1, source_target_pairs={{0,1},{1,0},{2,3},{3,2},{4,5},{5,4},{6,7},{7,6},{8,9},{9,8},{10,11... | collective-permute-start | bytes 393224 | tf_op jit(solution)/shard_map/ppermute | solution.py:17
  51.3 8.5 %collective-permute-start.19 = (f32[2,256,128]{2,1,0:T(8,128)S(1)}, f32[2,256,128]{2,1,0:T(8,128)S(1)}, u32[]{:S(2)}, u32[]{:S(2)}) collective-permute-start(f32[2,256,128]{2,1,0:T(8,128)S(1)} %fusion.5), channel_id=1, source_target_pairs={{0,3},{1,2},{2,1},{3,0},{4,7},{5,6},{6,5},{7,4},{8,11},{9,10},{10,... | collective-permute-start | bytes 786440 | tf_op jit(solution)/shard_map/ppermute | solution.py:17
  51.8 8.0 %collective-permute-start.17 = (f32[2,256,128]{2,1,0:T(8,128)S(1)}, f32[2,256,128]{2,1,0:T(8,128)S(1)}, u32[]{:S(2)}, u32[]{:S(2)}) collective-permute-start(f32[2,256,128]{2,1,0:T(8,128)S(1)} %fusion.6), channel_id=1, source_target_pairs={{0,1},{1,0},{2,3},{3,2},{4,5},{5,4},{6,7},{7,6},{8,9},{9,8},{10,11... | collective-permute-start | bytes 786440 | tf_op jit(solution)/shard_map/ppermute | solution.py:17

commit v8 on v7

--- a/solution.py
+++ b/solution.py
@@ -66,25 +66,33 @@
         left[k * n : (k + 1) * n, :] = (lam_t[11 + k : 12 + k, :] * c_t).astype(BF16)
 
 
-def state_kernel(x_ref, d_ref, b_t_ref, left, far_send, far_keep, rest_send, near_keep):
+def slots(levels, x_ref, d_ref, b_t_ref, left, here):
     bits = own_bits()
     n = b_t_ref.shape[0]
-    half = n // 2
+    state = dot_nn(b_t_ref[...], x_ref[:, here])
+    grads = dot_nn(left[levels[0] * n : (levels[-1] + 1) * n, :], d_ref[:, here])
+    return [jnp.where(bits[k] == 1, grads[i * n : (i + 1) * n], state) for i, k in enumerate(levels)]
+
+
+def far_kernel(x_ref, d_ref, b_t_ref, left, far_send, far_keep):
+    half = b_t_ref.shape[0] // 2
     for at in range(0, x_ref.shape[1], TILE):
         here = slice(at, at + TILE)
-        state = dot_nn(b_t_ref[...], x_ref[:, here])
-        grads = dot_nn(left[...], d_ref[:, here])
-        for k in range(5):
-            value = jnp.where(bits[k] == 1, grads[k * n : (k + 1) * n], state)
-            if k == 0:
-                rest_send[0, :, here] = value[:half]
-                rest_send[1, :, here] = value[half:]
-            elif k < 3:
-                near_keep[k - 1, :, here] = value[:half]
-                rest_send[k + 1, :, here] = value[half:]
-            else:
-                far_keep[k - 3, :, here] = value[:half]
-                far_send[k - 3, :, here] = value[half:]
+        for k, value in enumerate(slots((3, 4), x_ref, d_ref, b_t_ref, left, here)):
+            far_keep[k, :, here] = value[:half]
+            far_send[k, :, here] = value[half:]
+
+
+def rest_kernel(x_ref, d_ref, b_t_ref, left, rest_send, near_keep):
+    half = b_t_ref.shape[0] // 2
+    for at in range(0, x_ref.shape[1], TILE):
+        here = slice(at, at + TILE)
+        values = slots((0, 1, 2), x_ref, d_ref, b_t_ref, left, here)
+        rest_send[0, :, here] = values[0][:half]
+        rest_send[1, :, here] = values[0][half:]
+        for k in (1, 2):
+            near_keep[k - 1, :, here] = values[k][:half]
+            rest_send[k + 1, :, here] = values[k][half:]
 
 
 def local_kernel(x_ref, b_ref, c_ref, d_ref, lam_ref, which, last, outs):
@@ -211,11 +219,10 @@
     b_t, left = call(rows_kernel, (((n, rows), BF16), ((5 * n, rows), BF16)), [VMEM] * 3, 2 * rows * n * n)(
         jnp.concatenate([b_first, c_first], axis=1), lam, perm
     )
-    far_send, far_keep, rest_send, near_keep = call(
-        state_kernel,
-        (half, half, ((4, n // 2, width), F32), half),
-        [VMEM] * 4,
-        2 * rows * width * n * 6,
+    far_send, far_keep = call(far_kernel, (half, half), [VMEM] * 4, 2 * rows * width * n * 3)(x_in, d_out, b_t, left)
+    far_send, b_t = tie((far_send, b_t))
+    rest_send, near_keep = call(
+        rest_kernel, (((4, n // 2, width), F32), half), [VMEM] * 4, 2 * rows * width * n * 4
     )(x_in, d_out, b_t, left)
     far, rest_send = tie((from_xor(far_send, CORE), rest_send))
     far = (far_keep + far).reshape(2, 4, n // 8, width)

time: 61.4 us -> 60.8 us (level)
  waiting for transfers between devices: 15.7 us -> 14.5 us
    ppermute x20, waiting for transfers between devices: 15.7 us -> 14.5 us  [from_xor(): return lax.ppermute(block, axis, route)]
    pallas_call x1 -> x2, Pallas kernels: 1.83 us -> 2.29 us  [the longest x1 1.28 us: local(): call(rest_kernel, (((4, n // 2, width), F32), half), [VMEM] * 4, 2 * rows...]
  transfers between devices with their start and end apart: 20 -> 20, of which waited for: 11 -> 11; matrix products, arithmetic and copies ran while one was open for 1% -> 1% of each run, Pallas kernels for 24% -> 26%
where the time goes in v8:
time: 60.8 us; the launch traced here: 59.9 us
  starting transfers between devices  22.9 us (38%)
  Pallas kernels  18.9 us (31%)
  waiting for transfers between devices  14.5 us (24%)
  local copies, waits for them, and re-layouts  1.7 us (3%)
  between operations  0.95 us (2%)
    ppermute x20, starting transfers between devices, from_xor(): return lax.ppermute(block, axis, route)  22.9 us
    ppermute x20, waiting for transfers between devices, from_xor(): return lax.ppermute(block, axis, route)  14.5 us
    pallas_call x1, Pallas kernels, local(): call(output_kernel, (((rows, width), BF16), ((rows, width), BF16)), [VMEM...  6.81 us
    pallas_call x3, Pallas kernels, local_part(): call(kernel, ((mix, BF16), ((rows, n), F32), ((rows, n), F32)), [VMEM] *...  5.84 us
    pallas_call x1, Pallas kernels, local(): call(grad_rest_kernel, (piece, piece, piece), [VMEM] * 7, 2 * rows * widt...  1.83 us
    unnamed x12, local copies, waits for them, and re-layouts  1.62 us
    pallas_call x1, Pallas kernels, local(): call(rest_kernel, (((4, n // 2, width), F32), half), [VMEM] * 4, 2 * rows...  1.28 us
  transfers between devices with their start and end apart: 20, of which 11 were waited for; matrix products, arithmetic and copies ran while one was open for 1% of the time, Pallas kernels for 26%

profile of v8, /device:TPU:0, one launch (start us, length us, event | category | flops | bytes accessed | tf_op | source)
XLA Modules:
  0.0 59.9 jit_solution(13650591693991541201)
XLA Ops:
  0.7 0.6 %copy-done = f32[16,18]{1,0:T(8,128)S(1)} copy-done((f32[16,18]{1,0:T(8,128)S(1)}, f32[16,18]{1,0:T(8,128)}, u32[]{:S(2)}) %copy-start) | copy-done | bytes 1176
  2.4 0.8 %copy-done.1 = bf16[1024,1024]{1,0:T(8,128)(2,1)S(1)} copy-done((bf16[1024,1024]{1,0:T(8,128)(2,1)S(1)}, bf16[1024,1024]{1,0:T(8,128)(2,1)}, u32[]{:S(2)}) %copy-start.1) | copy-done | bytes 2097176
  3.2 1.0 %shard_map.95 = (f32[2,64,1024]{2,1,0:T(8,128)S(1)}, f32[2,64,1024]{2,1,0:T(8,128)S(1)}) custom-call(bf16[1024,1024]{1,0:T(8,128)(2,1)S(1)} %copy-done.1, bf16[1024,1024]{1,0:T(8,128)(2,1)S(1)} %copy-done.2, bf16[128,1024]{1,0:T(8,128)(2,1)S(1)} %get-tuple-element.88.b_t_ref, bf16[640,1024]{1,0:T(8,128)(2,1)S(1)} %get-tuple-element.84.left), custom_call_target="tpu_custom_call" | custom-call | flops 805306368 | bytes 1048576 | tf_op jit(solution)/shard_map/pallas_call | solution.py:222
  4.3 1.3 %shard_map.96 = (f32[4,64,1024]{2,1,0:T(8,128)S(1)}, f32[2,64,1024]{2,1,0:T(8,128)S(1)}) custom-call(bf16[1024,1024]{1,0:T(8,128)(2,1)S(1)} %copy-done.1, bf16[1024,1024]{1,0:T(8,128)(2,1)S(1)} %copy-done.2, bf16[128,1024]{1,0:T(8,128)(2,1)S(1)} %get-tuple-element.88.b_t_ref, bf16[640,1024]{1,0:T(8,128)(2,1)S(1)} %get-tuple-element.84.left), custom_call_target="tpu_custom_call" | custom-call | flops 1073741824 | bytes 1048576 | tf_op jit(solution)/shard_map/pallas_call | solution.py:224
  5.6 0.6 %collective-permute-done = f32[2,64,1024]{2,1,0:T(8,128)S(1)} collective-permute-done((f32[2,64,1024]{2,1,0:T(8,128)S(1)}, f32[2,64,1024]{2,1,0:T(8,128)S(1)}, u32[]{:S(2)}, u32[]{:S(2)}) %collective-permute-start) | collective-permute-done | bytes 524320 | tf_op jit(solution)/shard_map/ppermute | solution.py:17
  6.5 4.1 %collective-permute-start.2 = (f32[2,16,1024]{2,1,0:T(8,128)S(1)}, f32[2,16,1024]{2,1,0:T(8,128)S(1)}, u32[]{:S(2)}, u32[]{:S(2)}) collective-permute-start(f32[2,16,1024]{2,1,0:T(8,128)S(1)} %get-tuple-element.136), channel_id=1, source_target_pairs={{0,16},{4,20},{8,24},{12,28},{16,0},{20,4},{24,8},{28,12},{32,48},... | collective-permute-start | bytes 393224 | tf_op jit(solution)/shard_map/ppermute | solution.py:17
  10.5 1.0 %collective-permute-start.3 = (f32[2,16,1024]{2,1,0:T(8,128)S(1)}, f32[2,16,1024]{2,1,0:T(8,128)S(1)}, u32[]{:S(2)}, u32[]{:S(2)}) collective-permute-start(f32[2,16,1024]{2,1,0:T(8,128)S(1)} %get-tuple-element.137), channel_id=1, source_target_pairs={{0,8},{4,12},{8,0},{12,4},{16,24},{20,28},{24,16},{28,20},{32,40},... | collective-permute-start | bytes 393224 | tf_op jit(solution)/shard_map/ppermute | solution.py:17
  11.7 1.2 %collective-permute-start.5 = (f32[4,16,1024]{2,1,0:T(8,128)S(1)}, f32[4,16,1024]{2,1,0:T(8,128)S(1)}, u32[]{:S(2)}, u32[]{:S(2)}) collective-permute-start(f32[4,16,1024]{2,1,0:T(8,128)S(1)} %get-tuple-element.134), channel_id=1, source_target_pairs={{0,8},{4,12},{8,0},{12,4},{16,24},{20,28},{24,16},{28,20},{32,40},... | collective-permute-start | bytes 786440 | tf_op jit(solution)/shard_map/ppermute | solution.py:17
  12.9 2.5 %collective-permute-start.6 = (f32[4,16,1024]{2,1,0:T(8,128)S(1)}, f32[4,16,1024]{2,1,0:T(8,128)S(1)}, u32[]{:S(2)}, u32[]{:S(2)}) collective-permute-start(f32[4,16,1024]{2,1,0:T(8,128)S(1)} %get-tuple-element.109), channel_id=1, source_target_pairs={{0,24},{4,28},{8,16},{12,20},{16,8},{20,12},{24,0},{28,4},{32,56},... | collective-permute-start | bytes 786440 | tf_op jit(solution)/shard_map/ppermute | solution.py:17
  15.4 0.7 %shard_map.97 = (bf16[256,256]{1,0:T(8,128)(2,1)S(1)}, f32[1024,128]{1,0:T(8,128)S(1)}, f32[1024,128]{1,0:T(8,128)S(1)}) custom-call(bf16[1024,1024]{1,0:T(8,128)(2,1)S(1)} %copy-done.1, bf16[1024,128]{1,0:T(8,128)(2,1)S(1)} %copy-done.3, bf16[1024,128]{1,0:T(8,128)(2,1)S(1)} %copy-done.4, bf16[1024,1024]{1,0:T(8,128)(2,1)S(1)} %copy-done.2, ...), custom_call_target="tpu_custom_call" | custom-call | flops 1000000000 | bytes 1048576 | tf_op jit(solution)/shard_map/pallas_call | solution.py:233
  16.1 2.6 %collective-permute-done.3 = f32[2,16,1024]{2,1,0:T(8,128)S(1)} collective-permute-done((f32[2,16,1024]{2,1,0:T(8,128)S(1)}, f32[2,16,1024]{2,1,0:T(8,128)S(1)}, u32[]{:S(2)}, u32[]{:S(2)}) %collective-permute-start.3) | collective-permute-done | bytes 131104 | tf_op jit(solution)/shard_map/ppermute | solution.py:17
  19.2 2.8 %collective-permute-start.9 = (f32[16,1024]{1,0:T(8,128)S(1)}, f32[16,1024]{1,0:T(8,128)S(1)}, u32[]{:S(2)}, u32[]{:S(2)}) collective-permute-start(f32[16,1024]{1,0:T(8,128)S(1)} %get-tuple-element.143), channel_id=1, source_target_pairs={{0,96},{4,100},{8,104},{12,108},{16,112},{20,116},{24,120},{28,124... | collective-permute-start | bytes 196616 | tf_op jit(solution)/shard_map/ppermute | solution.py:17
  22.0 0.8 %collective-permute-start.8 = (f32[16,1024]{1,0:T(8,128)S(1)}, f32[16,1024]{1,0:T(8,128)S(1)}, u32[]{:S(2)}, u32[]{:S(2)}) collective-permute-start(f32[16,1024]{1,0:T(8,128)S(1)} %get-tuple-element.143), channel_id=1, source_target_pairs={{0,64},{4,68},{8,72},{12,76},{16,80},{20,84},{24,88},{28,92},{32,9... | collective-permute-start | bytes 196616 | tf_op jit(solution)/shard_map/ppermute | solution.py:17
  22.8 0.5 collective-permute-start.7
  23.4 2.1 %collective-permute-done.9 = f32[16,1024]{1,0:T(8,128)S(1)} collective-permute-done((f32[16,1024]{1,0:T(8,128)S(1)}, f32[16,1024]{1,0:T(8,128)S(1)}, u32[]{:S(2)}, u32[]{:S(2)}) %collective-permute-start.9) | collective-permute-done | bytes 65568 | tf_op jit(solution)/shard_map/ppermute | solution.py:17
  25.5 0.8 %collective-permute-start.13 = (f32[4,16,1024]{2,1,0:T(8,128)S(1)}, f32[4,16,1024]{2,1,0:T(8,128)S(1)}, u32[]{:S(2)}, u32[]{:S(2)}) collective-permute-start(f32[4,16,1024]{2,1,0:T(8,128)S(1)} %get-tuple-element.109), channel_id=1, source_target_pairs={{0,16},{4,20},{8,24},{12,28},{16,0},{20,4},{24,8},{28,12},{32,48},... | collective-permute-start | bytes 786440 | tf_op jit(solution)/shard_map/ppermute | solution.py:17
  26.3 1.5 %collective-permute-done.8 = f32[16,1024]{1,0:T(8,128)S(1)} collective-permute-done((f32[16,1024]{1,0:T(8,128)S(1)}, f32[16,1024]{1,0:T(8,128)S(1)}, u32[]{:S(2)}, u32[]{:S(2)}) %collective-permute-start.8) | collective-permute-done | bytes 65568 | tf_op jit(solution)/shard_map/ppermute | solution.py:17
  27.9 1.9 %collective-permute-start.12 = (f32[2,16,1024]{2,1,0:T(8,128)S(1)}, f32[2,16,1024]{2,1,0:T(8,128)S(1)}, u32[]{:S(2)}, u32[]{:S(2)}) collective-permute-start(f32[2,16,1024]{2,1,0:T(8,128)S(1)} %pad_maximum_fusion.5), channel_id=1, source_target_pairs={{0,24},{4,28},{8,16},{12,20},{16,8},{20,12},{24,0},{28,4},{32,56},... | collective-permute-start | bytes 393224 | tf_op jit(solution)/shard_map/ppermute | solution.py:17
  29.7 0.8 %collective-permute-start.11 = (f32[2,16,1024]{2,1,0:T(8,128)S(1)}, f32[2,16,1024]{2,1,0:T(8,128)S(1)}, u32[]{:S(2)}, u32[]{:S(2)}) collective-permute-start(f32[2,16,1024]{2,1,0:T(8,128)S(1)} %pad_maximum_fusion.5), channel_id=1, source_target_pairs={{0,16},{4,20},{8,24},{12,28},{16,0},{20,4},{24,8},{28,12},{32,48},... | collective-permute-start | bytes 393224 | tf_op jit(solution)/shard_map/ppermute | solution.py:17
  30.6 1.5 %collective-permute-start.10 = (f32[2,16,1024]{2,1,0:T(8,128)S(1)}, f32[2,16,1024]{2,1,0:T(8,128)S(1)}, u32[]{:S(2)}, u32[]{:S(2)}) collective-permute-start(f32[2,16,1024]{2,1,0:T(8,128)S(1)} %pad_maximum_fusion.5), channel_id=1, source_target_pairs={{0,8},{4,12},{8,0},{12,4},{16,24},{20,28},{24,16},{28,20},{32,40},... | collective-permute-start | bytes 393224 | tf_op jit(solution)/shard_map/ppermute | solution.py:17
  32.0 2.4 %shard_map.98 = (bf16[256,1024]{1,0:T(8,128)(2,1)S(1)}, f32[1024,128]{1,0:T(8,128)S(1)}, f32[1024,128]{1,0:T(8,128)S(1)}) custom-call(f32[1024,128]{1,0:T(8,128)S(1)} %get-tuple-element.98.last_b, f32[1024,128]{1,0:T(8,128)S(1)} %get-tuple-element.99.last_c, bf16[1024,1024]{1,0:T(8,128)(2,1)S(1)} %copy-done.1, bf16[1024,128]{1,0:T(8,128)(2,1)S(1)} %copy-done.3, ...), custom_call_target="tpu_custom_call" | custom-call | flops 20000000000 | bytes 1048576 | tf_op jit(solution)/shard_map/pallas_call | solution.py:233
  34.4 2.8 %shard_map.99 = (bf16[512,768]{1,0:T(8,128)(2,1)S(1)}, f32[1024,128]{1,0:T(8,128)S(1)}, f32[1024,128]{1,0:T(8,128)S(1)}) custom-call(f32[1024,128]{1,0:T(8,128)S(1)} %get-tuple-element.104.last_b, f32[1024,128]{1,0:T(8,128)S(1)} %get-tuple-element.105.last_c, bf16[1024,1024]{1,0:T(8,128)(2,1)S(1)} %copy-done.1, bf16[1024,128]{1,0:T(8,128)(2,1)S(1)} %copy-done.3, ...), custom_call_target="tpu_custom_call" | custom-call | flops 20000000000 | bytes 1048576 | tf_op jit(solution)/shard_map/pallas_call | solution.py:233
  38.6 0.5 collective-permute-start.14
  39.1 1.4 %collective-permute-done.15.far_other = f32[2,64,1024]{2,1,0:T(8,128)S(1)} collective-permute-done((f32[2,64,1024]{2,1,0:T(8,128)S(1)}, f32[2,64,1024]{2,1,0:T(8,128)S(1)}, u32[]{:S(2)}, u32[]{:S(2)}) %collective-permute-start.15) | collective-permute-done | bytes 524320 | tf_op jit(solution)/shard_map/ppermute | solution.py:17
  40.5 0.7 %collective-permute-done.14.near_other = f32[2,64,1024]{2,1,0:T(8,128)S(1)} collective-permute-done((f32[2,64,1024]{2,1,0:T(8,128)S(1)}, f32[2,64,1024]{2,1,0:T(8,128)S(1)}, u32[]{:S(2)}, u32[]{:S(2)}) %collective-permute-start.14) | collective-permute-done | bytes 524320 | tf_op jit(solution)/shard_map/ppermute | solution.py:17
  41.2 1.1 %shard_map.100 = (f32[256,128]{1,0:T(8,128)S(1)}, f32[256,128]{1,0:T(8,128)S(1)}, bf16[640,1024]{1,0:T(8,128)(2,1)S(1)}, bf16[128,1024]{1,0:T(8,128)(2,1)S(1)}) custom-call(f32[4,64,1024]{2,1,0:T(8,128)S(1)} %collective-permute-done.1.rest_ref, f32[2,64,1024]{2,1,0:T(8,128)S(1)} %pad_maximum_fusion.1.near_ref, ...), custom_call_target="tpu_custom_call" | custom-call | flops 1610612736 | bytes 1048576 | tf_op jit(solution)/shard_map/pallas_call | solution.py:260
  42.3 3.1 %collective-permute-start.16 = (f32[256,128]{1,0:T(8,128)S(1)}, f32[256,128]{1,0:T(8,128)S(1)}, u32[]{:S(2)}, u32[]{:S(2)}) collective-permute-start(f32[256,128]{1,0:T(8,128)S(1)} %get-tuple-element.125), channel_id=1, source_target_pairs={{0,3},{1,2},{2,1},{3,0},{4,7},{5,6},{6,5},{7,4},{8,11},{9,10},{10,... | collective-permute-start | bytes 393224 | tf_op jit(solution)/shard_map/ppermute | solution.py:17
  45.5 1.8 %shard_map.102 = (f32[2,256,128]{2,1,0:T(8,128)S(1)}, f32[2,256,128]{2,1,0:T(8,128)S(1)}, f32[2,256,128]{2,1,0:T(8,128)S(1)}) custom-call(f32[1024,128]{1,0:T(8,128)S(1)} %get-tuple-element.117.gb_ref, f32[1024,128]{1,0:T(8,128)S(1)} %get-tuple-element.118.gc_ref, bf16[1024,1024]{1,0:T(8,128)(2,1)S(1)} %copy-done.1, bf16[1024,1024]{1,0:T(8,128)(2,1)S(1)} %copy-done.2, ...), custom_call_target="tpu_custom_call" | custom-call | flops 1610612736 | bytes 1048576 | tf_op jit(solution)/shard_map/pallas_call | solution.py:266
  47.3 3.3 %collective-permute-done.18 = f32[256,128]{1,0:T(8,128)S(1)} collective-permute-done((f32[256,128]{1,0:T(8,128)S(1)}, f32[256,128]{1,0:T(8,128)S(1)}, u32[]{:S(2)}, u32[]{:S(2)}) %collective-permute-start.18) | collective-permute-done | bytes 131104 | tf_op jit(solution)/shard_map/ppermute | solution.py:17
  51.4 6.8 %shard_map.101 = (bf16[1024,1024]{1,0:T(8,128)(2,1)}, bf16[1024,1024]{1,0:T(8,128)(2,1)}) custom-call(bf16[256,256]{1,0:T(8,128)(2,1)S(1)} %get-tuple-element.94.mix_first, bf16[512,768]{1,0:T(8,128)(2,1)S(1)} %get-tuple-element.106.mix_middle, bf16[256,1024]{1,0:T(8,128)(2,1)S(1)} %get-tuple-element.107.mix_last, bf16[1024,1024]{1,0:T(8,128)(2,1)S(1)} %copy-done.1, ...), custom_call_target="tpu_custom_call" | custom-call | flops 3758096384 | bytes 1048576 | tf_op jit(solution)/shard_map/pallas_call | solution.py:275
  58.3 0.9 %collective-permute-done.19.part3 = f32[2,256,128]{2,1,0:T(8,128)S(1)} collective-permute-done((f32[2,256,128]{2,1,0:T(8,128)S(1)}, f32[2,256,128]{2,1,0:T(8,128)S(1)}, u32[]{:S(2)}, u32[]{:S(2)}) %collective-permute-start.19) | collective-permute-done | bytes 262176 | tf_op jit(solution)/shard_map/ppermute | solution.py:17
  59.2 0.7 %shard_map.103 = (f32[256,128]{1,0:T(8,128)}, f32[256,128]{1,0:T(8,128)}) custom-call(f32[2,256,128]{2,1,0:T(8,128)S(1)} %get-tuple-element.123.part0, f32[2,256,128]{2,1,0:T(8,128)S(1)} %collective-permute-done.17.part1, f32[2,256,128]{2,1,0:T(8,128)S(1)} %collective-permute-done.19.part3), custom_call_target="tpu_custom_call" | custom-call | flops 131072 | bytes 1048576 | tf_op jit(solution)/shard_map/pallas_call | solution.py:282
  (48 shorter events, 4.3 us)
Async XLA Ops:
  0.6 0.7 %copy-start = (f32[16,18]{1,0:T(8,128)S(1)}, f32[16,18]{1,0:T(8,128)}, u32[]{:S(2)}) copy-start(f32[16,18]{1,0:T(8,128)} %param.14) | copy-start | bytes 3460
  0.6 1.2 %copy-start.4 = (bf16[1024,128]{1,0:T(8,128)(2,1)S(1)}, bf16[1024,128]{1,0:T(8,128)(2,1)}, u32[]{:S(2)}) copy-start(bf16[1024,128]{1,0:T(8,128)(2,1)} %c_ref.1) | copy-start | bytes 786436
  0.7 1.2 %copy-start.3 = (bf16[1024,128]{1,0:T(8,128)(2,1)S(1)}, bf16[1024,128]{1,0:T(8,128)(2,1)}, u32[]{:S(2)}) copy-start(bf16[1024,128]{1,0:T(8,128)(2,1)} %b_ref.1) | copy-start | bytes 786436
  0.7 0.7 %copy-start.5 = (s32[1024]{0:T(1024)S(1)}, s32[1024]{0:T(1024)}, u32[]{:S(2)}) copy-start(s32[1024]{0:T(1024)} %param.15) | copy-start | bytes 12292
  0.7 1.8 %copy-start.2 = (bf16[1024,1024]{1,0:T(8,128)(2,1)S(1)}, bf16[1024,1024]{1,0:T(8,128)(2,1)}, u32[]{:S(2)}) copy-start(bf16[1024,1024]{1,0:T(8,128)(2,1)} %d_ref.9) | copy-start | bytes 6291460
  1.4 1.8 %copy-start.1 = (bf16[1024,1024]{1,0:T(8,128)(2,1)S(1)}, bf16[1024,1024]{1,0:T(8,128)(2,1)}, u32[]{:S(2)}) copy-start(bf16[1024,1024]{1,0:T(8,128)(2,1)} %x_ref.9) | copy-start | bytes 6291460
  4.2 2.0 %collective-permute-start = (f32[2,64,1024]{2,1,0:T(8,128)S(1)}, f32[2,64,1024]{2,1,0:T(8,128)S(1)}, u32[]{:S(2)}, u32[]{:S(2)}) collective-permute-start(f32[2,64,1024]{2,1,0:T(8,128)S(1)} %get-tuple-element.87), channel_id=1, source_target_pairs={{0,4},{4,0},{8,12},{12,8},{16,20},{20,16},{24,28},{28,24},{32,36},... | collective-permute-start | bytes 1572872 | tf_op jit(solution)/shard_map/ppermute | solution.py:17
  6.2 5.3 %collective-permute-start.1 = (f32[4,64,1024]{2,1,0:T(8,128)S(1)}, f32[4,64,1024]{2,1,0:T(8,128)S(1)}, u32[]{:S(2)}, u32[]{:S(2)}) collective-permute-start(f32[4,64,1024]{2,1,0:T(8,128)S(1)} %get-tuple-element.92), channel_id=1, source_target_pairs={{0,4},{4,0},{8,12},{12,8},{16,20},{20,16},{24,28},{28,24},{32,36},... | collective-permute-start | bytes 3145736 | tf_op jit(solution)/shard_map/ppermute | solution.py:17
  6.5 9.6 %collective-permute-start.2 = (f32[2,16,1024]{2,1,0:T(8,128)S(1)}, f32[2,16,1024]{2,1,0:T(8,128)S(1)}, u32[]{:S(2)}, u32[]{:S(2)}) collective-permute-start(f32[2,16,1024]{2,1,0:T(8,128)S(1)} %get-tuple-element.136), channel_id=1, source_target_pairs={{0,16},{4,20},{8,24},{12,28},{16,0},{20,4},{24,8},{28,12},{32,48},... | collective-permute-start | bytes 393224 | tf_op jit(solution)/shard_map/ppermute | solution.py:17
  10.5 8.2 %collective-permute-start.3 = (f32[2,16,1024]{2,1,0:T(8,128)S(1)}, f32[2,16,1024]{2,1,0:T(8,128)S(1)}, u32[]{:S(2)}, u32[]{:S(2)}) collective-permute-start(f32[2,16,1024]{2,1,0:T(8,128)S(1)} %get-tuple-element.137), channel_id=1, source_target_pairs={{0,8},{4,12},{8,0},{12,4},{16,24},{20,28},{24,16},{28,20},{32,40},... | collective-permute-start | bytes 393224 | tf_op jit(solution)/shard_map/ppermute | solution.py:17
  11.5 7.6 %collective-permute-start.4 = (f32[2,16,1024]{2,1,0:T(8,128)S(1)}, f32[2,16,1024]{2,1,0:T(8,128)S(1)}, u32[]{:S(2)}, u32[]{:S(2)}) collective-permute-start(f32[2,16,1024]{2,1,0:T(8,128)S(1)} %get-tuple-element.138), channel_id=1, source_target_pairs={{0,24},{4,28},{8,16},{12,20},{16,8},{20,12},{24,0},{28,4},{32,56},... | collective-permute-start | bytes 393224 | tf_op jit(solution)/shard_map/ppermute | solution.py:17
  11.7 16.2 %collective-permute-start.5 = (f32[4,16,1024]{2,1,0:T(8,128)S(1)}, f32[4,16,1024]{2,1,0:T(8,128)S(1)}, u32[]{:S(2)}, u32[]{:S(2)}) collective-permute-start(f32[4,16,1024]{2,1,0:T(8,128)S(1)} %get-tuple-element.134), channel_id=1, source_target_pairs={{0,8},{4,12},{8,0},{12,4},{16,24},{20,28},{24,16},{28,20},{32,40},... | collective-permute-start | bytes 786440 | tf_op jit(solution)/shard_map/ppermute | solution.py:17
  12.9 15.0 %collective-permute-start.6 = (f32[4,16,1024]{2,1,0:T(8,128)S(1)}, f32[4,16,1024]{2,1,0:T(8,128)S(1)}, u32[]{:S(2)}, u32[]{:S(2)}) collective-permute-start(f32[4,16,1024]{2,1,0:T(8,128)S(1)} %get-tuple-element.109), channel_id=1, source_target_pairs={{0,24},{4,28},{8,16},{12,20},{16,8},{20,12},{24,0},{28,4},{32,56},... | collective-permute-start | bytes 786440 | tf_op jit(solution)/shard_map/ppermute | solution.py:17
  19.2 6.3 %collective-permute-start.9 = (f32[16,1024]{1,0:T(8,128)S(1)}, f32[16,1024]{1,0:T(8,128)S(1)}, u32[]{:S(2)}, u32[]{:S(2)}) collective-permute-start(f32[16,1024]{1,0:T(8,128)S(1)} %get-tuple-element.143), channel_id=1, source_target_pairs={{0,96},{4,100},{8,104},{12,108},{16,112},{20,116},{24,120},{28,124... | collective-permute-start | bytes 196616 | tf_op jit(solution)/shard_map/ppermute | solution.py:17
  22.0 5.8 %collective-permute-start.8 = (f32[16,1024]{1,0:T(8,128)S(1)}, f32[16,1024]{1,0:T(8,128)S(1)}, u32[]{:S(2)}, u32[]{:S(2)}) collective-permute-start(f32[16,1024]{1,0:T(8,128)S(1)} %get-tuple-element.143), channel_id=1, source_target_pairs={{0,64},{4,68},{8,72},{12,76},{16,80},{20,84},{24,88},{28,92},{32,9... | collective-permute-start | bytes 196616 | tf_op jit(solution)/shard_map/ppermute | solution.py:17
  22.8 5.0 %collective-permute-start.7 = (f32[16,1024]{1,0:T(8,128)S(1)}, f32[16,1024]{1,0:T(8,128)S(1)}, u32[]{:S(2)}, u32[]{:S(2)}) collective-permute-start(f32[16,1024]{1,0:T(8,128)S(1)} %get-tuple-element.144), channel_id=1, source_target_pairs={{0,32},{4,36},{8,40},{12,44},{16,48},{20,52},{24,56},{28,60},{32,0... | collective-permute-start | bytes 196616 | tf_op jit(solution)/shard_map/ppermute | solution.py:17
  25.5 11.8 %collective-permute-start.13 = (f32[4,16,1024]{2,1,0:T(8,128)S(1)}, f32[4,16,1024]{2,1,0:T(8,128)S(1)}, u32[]{:S(2)}, u32[]{:S(2)}) collective-permute-start(f32[4,16,1024]{2,1,0:T(8,128)S(1)} %get-tuple-element.109), channel_id=1, source_target_pairs={{0,16},{4,20},{8,24},{12,28},{16,0},{20,4},{24,8},{28,12},{32,48},... | collective-permute-start | bytes 786440 | tf_op jit(solution)/shard_map/ppermute | solution.py:17
  27.9 9.9 %collective-permute-start.12 = (f32[2,16,1024]{2,1,0:T(8,128)S(1)}, f32[2,16,1024]{2,1,0:T(8,128)S(1)}, u32[]{:S(2)}, u32[]{:S(2)}) collective-permute-start(f32[2,16,1024]{2,1,0:T(8,128)S(1)} %pad_maximum_fusion.5), channel_id=1, source_target_pairs={{0,24},{4,28},{8,16},{12,20},{16,8},{20,12},{24,0},{28,4},{32,56},... | collective-permute-start | bytes 393224 | tf_op jit(solution)/shard_map/ppermute | solution.py:17
  29.7 8.0 %collective-permute-start.11 = (f32[2,16,1024]{2,1,0:T(8,128)S(1)}, f32[2,16,1024]{2,1,0:T(8,128)S(1)}, u32[]{:S(2)}, u32[]{:S(2)}) collective-permute-start(f32[2,16,1024]{2,1,0:T(8,128)S(1)} %pad_maximum_fusion.5), channel_id=1, source_target_pairs={{0,16},{4,20},{8,24},{12,28},{16,0},{20,4},{24,8},{28,12},{32,48},... | collective-permute-start | bytes 393224 | tf_op jit(solution)/shard_map/ppermute | solution.py:17
  30.6 7.7 %collective-permute-start.10 = (f32[2,16,1024]{2,1,0:T(8,128)S(1)}, f32[2,16,1024]{2,1,0:T(8,128)S(1)}, u32[]{:S(2)}, u32[]{:S(2)}) collective-permute-start(f32[2,16,1024]{2,1,0:T(8,128)S(1)} %pad_maximum_fusion.5), channel_id=1, source_target_pairs={{0,8},{4,12},{8,0},{12,4},{16,24},{20,28},{24,16},{28,20},{32,40},... | collective-permute-start | bytes 393224 | tf_op jit(solution)/shard_map/ppermute | solution.py:17
  38.3 2.2 %collective-permute-start.15 = (f32[2,64,1024]{2,1,0:T(8,128)S(1)}, f32[2,64,1024]{2,1,0:T(8,128)S(1)}, u32[]{:S(2)}, u32[]{:S(2)}) collective-permute-start(f32[2,64,1024]{2,1,0:T(8,128)S(1)} %bitcast.54), channel_id=1, source_target_pairs={{0,4},{4,0},{8,12},{12,8},{16,20},{20,16},{24,28},{28,24},{32,36},... | collective-permute-start | bytes 1572872 | tf_op jit(solution)/shard_map/ppermute | solution.py:17
  38.6 2.6 %collective-permute-start.14 = (f32[2,64,1024]{2,1,0:T(8,128)S(1)}, f32[2,64,1024]{2,1,0:T(8,128)S(1)}, u32[]{:S(2)}, u32[]{:S(2)}) collective-permute-start(f32[2,64,1024]{2,1,0:T(8,128)S(1)} %pad_maximum_fusion.1.near_ref), channel_id=1, source_target_pairs={{0,4},{4,0},{8,12},{12,8},{16,20},{20,16},{24,28},{28,24},{32,36},... | collective-permute-start | bytes 1572872 | tf_op jit(solution)/shard_map/ppermute | solution.py:17
  42.3 8.8 %collective-permute-start.16 = (f32[256,128]{1,0:T(8,128)S(1)}, f32[256,128]{1,0:T(8,128)S(1)}, u32[]{:S(2)}, u32[]{:S(2)}) collective-permute-start(f32[256,128]{1,0:T(8,128)S(1)} %get-tuple-element.125), channel_id=1, source_target_pairs={{0,3},{1,2},{2,1},{3,0},{4,7},{5,6},{6,5},{7,4},{8,11},{9,10},{10,... | collective-permute-start | bytes 393224 | tf_op jit(solution)/shard_map/ppermute | solution.py:17
  45.4 5.3 %collective-permute-start.18 = (f32[256,128]{1,0:T(8,128)S(1)}, f32[256,128]{1,0:T(8,128)S(1)}, u32[]{:S(2)}, u32[]{:S(2)}) collective-permute-start(f32[256,128]{1,0:T(8,128)S(1)} %get-tuple-element.127), channel_id=1, source_target_pairs={{0,1},{1,0},{2,3},{3,2},{4,5},{5,4},{6,7},{7,6},{8,9},{9,8},{10,11... | collective-permute-start | bytes 393224 | tf_op jit(solution)/shard_map/ppermute | solution.py:17
  50.7 8.5 %collective-permute-start.19 = (f32[2,256,128]{2,1,0:T(8,128)S(1)}, f32[2,256,128]{2,1,0:T(8,128)S(1)}, u32[]{:S(2)}, u32[]{:S(2)}) collective-permute-start(f32[2,256,128]{2,1,0:T(8,128)S(1)} %fusion.5), channel_id=1, source_target_pairs={{0,3},{1,2},{2,1},{3,0},{4,7},{5,6},{6,5},{7,4},{8,11},{9,10},{10,... | collective-permute-start | bytes 786440 | tf_op jit(solution)/shard_map/ppermute | solution.py:17
  51.1 8.0 %collective-permute-start.17 = (f32[2,256,128]{2,1,0:T(8,128)S(1)}, f32[2,256,128]{2,1,0:T(8,128)S(1)}, u32[]{:S(2)}, u32[]{:S(2)}) collective-permute-start(f32[2,256,128]{2,1,0:T(8,128)S(1)} %fusion.6), channel_id=1, source_target_pairs={{0,1},{1,0},{2,3},{3,2},{4,5},{5,4},{6,7},{7,6},{8,9},{9,8},{10,11... | collective-permute-start | bytes 786440 | tf_op jit(solution)/shard_map/ppermute | solution.py:17

commit v9 on v8

--- a/solution.py
+++ b/solution.py
@@ -157,15 +157,15 @@
     return gb_ref[mine, :] + dot_nt(x_ref[mine, :], back_ref[...]), grad_c
 
 
-def grad_kernel(rest_ref, near_ref, near_other, far_ref, far_other, gb_ref, gc_ref, x_ref, d_ref, lam_ref, part2_b, part2_c, carry_ref, back_ref):
+def grad_kernel(rest_ref, own_ref, other_ref, gb_ref, gc_ref, x_ref, d_ref, lam_ref, part2_b, part2_c, carry_ref, back_ref):
     bits = own_bits()
     mask = row_mask(bits) // 16
     n = gb_ref.shape[1]
     for p in range(8):
         to = (p ^ mask) * 16
         half, q = p // 4, slice(p % 4 * 16, p % 4 * 16 + 16)
-        near, far = (near_ref, far_ref) if half == 0 else (near_other, far_other)
-        sums = [rest_ref[1 - half, q, :], near[0, q, :], near[1, q, :], far[0, q, :], far[1, q, :]]
+        got = own_ref if half == 0 else other_ref
+        sums = [rest_ref[1 - half, q, :], got[0, q, :], got[1, q, :], got[2, q, :], got[3, q, :]]
         back = None
         for k in range(5):
             carry_ref[pl.ds(pl.multiple_of(k * n + to, 16), 16), :] = jnp.where(bits[k] == 1, sums[k], 0.0).astype(BF16)
@@ -254,15 +254,16 @@
     near = near.reshape(2, n // 2, width)
     gathered, near, grad_b = tie((gathered, near, grad_b))
     far = jnp.stack([b34] + gathered, axis=1).reshape(2, n // 2, width)
-    far_other, near_other = from_xor(far, CORE), from_xor(near, CORE)
+    own = jnp.concatenate([near, far])
+    other = from_xor(own, CORE)
 
     piece = ((2, rows // 4, n), F32)
     part2_b, part2_c, carry, back = call(
         grad_kernel,
         (((rows // 4, n), F32), ((rows // 4, n), F32), ((5 * n, width), BF16), ((n, width), BF16)),
-        [VMEM] * 10,
+        [VMEM] * 8,
         2 * rows * width * n * 6,
-    )(rest, near, near_other, far, far_other, grad_b, grad_c, x_in, d_out, lam)
+    )(rest, own, other, grad_b, grad_c, x_in, d_out, lam)
     part0, part1, part3 = call(
         grad_rest_kernel,
         (piece, piece, piece),

time: 60.8 us -> 60.9 us (level)
    ppermute x20 -> x19, waiting for transfers between devices: 14.5 us -> 14.9 us  [from_xor(): return lax.ppermute(block, axis, route)]
    ppermute x20 -> x19, starting transfers between devices: 22.9 us -> 22.4 us  [from_xor(): return lax.ppermute(block, axis, route)]
  transfers between devices with their start and end apart: 20 -> 19, of which waited for: 11 -> 10; matrix products, arithmetic and copies ran while one was open for 1% -> 1% of each run, Pallas kernels for 26% -> 26%
where the time goes in v9:
time: 60.9 us; the launch traced here: 60 us
  starting transfers between devices  22.4 us (37%)
  Pallas kernels  18.9 us (31%)
  waiting for transfers between devices  14.9 us (24%)
  local copies, waits for them, and re-layouts  1.7 us (3%)
  between operations  0.96 us (2%)
    ppermute x19, starting transfers between devices, from_xor(): return lax.ppermute(block, axis, route)  22.4 us
    ppermute x19, waiting for transfers between devices, from_xor(): return lax.ppermute(block, axis, route)  14.9 us
    pallas_call x1, Pallas kernels, local(): call(output_kernel, (((rows, width), BF16), ((rows, width), BF16)), [VMEM...  6.81 us
    pallas_call x3, Pallas kernels, local_part(): call(kernel, ((mix, BF16), ((rows, n), F32), ((rows, n), F32)), [VMEM] *...  5.84 us
    pallas_call x1, Pallas kernels, local(): call(grad_rest_kernel, (piece, piece, piece), [VMEM] * 7, 2 * rows * widt...  1.83 us
    unnamed x12, local copies, waits for them, and re-layouts  1.62 us
    pallas_call x1, Pallas kernels, local(): call(rest_kernel, (((4, n // 2, width), F32), half), [VMEM] * 4, 2 * rows...  1.28 us
  transfers between devices with their start and end apart: 19, of which 10 were waited for; matrix products, arithmetic and copies ran while one was open for 1% of the time, Pallas kernels for 26%

profile of v9, /device:TPU:0, one launch (start us, length us, event | category | flops | bytes accessed | tf_op | source)
XLA Modules:
  0.0 60.0 jit_solution(16654637666197161310)
XLA Ops:
  0.7 0.6 %copy-done = f32[16,18]{1,0:T(8,128)S(1)} copy-done((f32[16,18]{1,0:T(8,128)S(1)}, f32[16,18]{1,0:T(8,128)}, u32[]{:S(2)}) %copy-start) | copy-done | bytes 1176
  2.4 0.8 %copy-done.1 = bf16[1024,1024]{1,0:T(8,128)(2,1)S(1)} copy-done((bf16[1024,1024]{1,0:T(8,128)(2,1)S(1)}, bf16[1024,1024]{1,0:T(8,128)(2,1)}, u32[]{:S(2)}) %copy-start.1) | copy-done | bytes 2097176
  3.2 1.0 %shard_map.95 = (f32[2,64,1024]{2,1,0:T(8,128)S(1)}, f32[2,64,1024]{2,1,0:T(8,128)S(1)}) custom-call(bf16[1024,1024]{1,0:T(8,128)(2,1)S(1)} %copy-done.1, bf16[1024,1024]{1,0:T(8,128)(2,1)S(1)} %copy-done.2, bf16[128,1024]{1,0:T(8,128)(2,1)S(1)} %get-tuple-element.88.b_t_ref, bf16[640,1024]{1,0:T(8,128)(2,1)S(1)} %get-tuple-element.84.left), custom_call_target="tpu_custom_call" | custom-call | flops 805306368 | bytes 1048576 | tf_op jit(solution)/shard_map/pallas_call | solution.py:222
  4.3 1.3 %shard_map.96 = (f32[4,64,1024]{2,1,0:T(8,128)S(1)}, f32[2,64,1024]{2,1,0:T(8,128)S(1)}) custom-call(bf16[1024,1024]{1,0:T(8,128)(2,1)S(1)} %copy-done.1, bf16[1024,1024]{1,0:T(8,128)(2,1)S(1)} %copy-done.2, bf16[128,1024]{1,0:T(8,128)(2,1)S(1)} %get-tuple-element.88.b_t_ref, bf16[640,1024]{1,0:T(8,128)(2,1)S(1)} %get-tuple-element.84.left), custom_call_target="tpu_custom_call" | custom-call | flops 1073741824 | bytes 1048576 | tf_op jit(solution)/shard_map/pallas_call | solution.py:224
  5.6 0.6 %collective-permute-done = f32[2,64,1024]{2,1,0:T(8,128)S(1)} collective-permute-done((f32[2,64,1024]{2,1,0:T(8,128)S(1)}, f32[2,64,1024]{2,1,0:T(8,128)S(1)}, u32[]{:S(2)}, u32[]{:S(2)}) %collective-permute-start) | collective-permute-done | bytes 524320 | tf_op jit(solution)/shard_map/ppermute | solution.py:17
  6.5 4.1 %collective-permute-start.2 = (f32[2,16,1024]{2,1,0:T(8,128)S(1)}, f32[2,16,1024]{2,1,0:T(8,128)S(1)}, u32[]{:S(2)}, u32[]{:S(2)}) collective-permute-start(f32[2,16,1024]{2,1,0:T(8,128)S(1)} %get-tuple-element.136), channel_id=1, source_target_pairs={{0,16},{4,20},{8,24},{12,28},{16,0},{20,4},{24,8},{28,12},{32,48},... | collective-permute-start | bytes 393224 | tf_op jit(solution)/shard_map/ppermute | solution.py:17
  10.5 1.0 %collective-permute-start.3 = (f32[2,16,1024]{2,1,0:T(8,128)S(1)}, f32[2,16,1024]{2,1,0:T(8,128)S(1)}, u32[]{:S(2)}, u32[]{:S(2)}) collective-permute-start(f32[2,16,1024]{2,1,0:T(8,128)S(1)} %get-tuple-element.137), channel_id=1, source_target_pairs={{0,8},{4,12},{8,0},{12,4},{16,24},{20,28},{24,16},{28,20},{32,40},... | collective-permute-start | bytes 393224 | tf_op jit(solution)/shard_map/ppermute | solution.py:17
  11.7 1.2 %collective-permute-start.5 = (f32[4,16,1024]{2,1,0:T(8,128)S(1)}, f32[4,16,1024]{2,1,0:T(8,128)S(1)}, u32[]{:S(2)}, u32[]{:S(2)}) collective-permute-start(f32[4,16,1024]{2,1,0:T(8,128)S(1)} %get-tuple-element.134), channel_id=1, source_target_pairs={{0,8},{4,12},{8,0},{12,4},{16,24},{20,28},{24,16},{28,20},{32,40},... | collective-permute-start | bytes 786440 | tf_op jit(solution)/shard_map/ppermute | solution.py:17
  12.9 2.5 %collective-permute-start.6 = (f32[4,16,1024]{2,1,0:T(8,128)S(1)}, f32[4,16,1024]{2,1,0:T(8,128)S(1)}, u32[]{:S(2)}, u32[]{:S(2)}) collective-permute-start(f32[4,16,1024]{2,1,0:T(8,128)S(1)} %get-tuple-element.109), channel_id=1, source_target_pairs={{0,24},{4,28},{8,16},{12,20},{16,8},{20,12},{24,0},{28,4},{32,56},... | collective-permute-start | bytes 786440 | tf_op jit(solution)/shard_map/ppermute | solution.py:17
  15.4 0.7 %shard_map.97 = (bf16[256,256]{1,0:T(8,128)(2,1)S(1)}, f32[1024,128]{1,0:T(8,128)S(1)}, f32[1024,128]{1,0:T(8,128)S(1)}) custom-call(bf16[1024,1024]{1,0:T(8,128)(2,1)S(1)} %copy-done.1, bf16[1024,128]{1,0:T(8,128)(2,1)S(1)} %copy-done.3, bf16[1024,128]{1,0:T(8,128)(2,1)S(1)} %copy-done.4, bf16[1024,1024]{1,0:T(8,128)(2,1)S(1)} %copy-done.2, ...), custom_call_target="tpu_custom_call" | custom-call | flops 1000000000 | bytes 1048576 | tf_op jit(solution)/shard_map/pallas_call | solution.py:233
  16.1 2.6 %collective-permute-done.3 = f32[2,16,1024]{2,1,0:T(8,128)S(1)} collective-permute-done((f32[2,16,1024]{2,1,0:T(8,128)S(1)}, f32[2,16,1024]{2,1,0:T(8,128)S(1)}, u32[]{:S(2)}, u32[]{:S(2)}) %collective-permute-start.3) | collective-permute-done | bytes 131104 | tf_op jit(solution)/shard_map/ppermute | solution.py:17
  18.7 0.5 collective-permute-done.4
  19.2 2.8 %collective-permute-start.9 = (f32[16,1024]{1,0:T(8,128)S(1)}, f32[16,1024]{1,0:T(8,128)S(1)}, u32[]{:S(2)}, u32[]{:S(2)}) collective-permute-start(f32[16,1024]{1,0:T(8,128)S(1)} %get-tuple-element.143), channel_id=1, source_target_pairs={{0,96},{4,100},{8,104},{12,108},{16,112},{20,116},{24,120},{28,124... | collective-permute-start | bytes 196616 | tf_op jit(solution)/shard_map/ppermute | solution.py:17
  22.0 0.8 %collective-permute-start.8 = (f32[16,1024]{1,0:T(8,128)S(1)}, f32[16,1024]{1,0:T(8,128)S(1)}, u32[]{:S(2)}, u32[]{:S(2)}) collective-permute-start(f32[16,1024]{1,0:T(8,128)S(1)} %get-tuple-element.143), channel_id=1, source_target_pairs={{0,64},{4,68},{8,72},{12,76},{16,80},{20,84},{24,88},{28,92},{32,9... | collective-permute-start | bytes 196616 | tf_op jit(solution)/shard_map/ppermute | solution.py:17
  22.8 0.5 collective-permute-start.7
  23.4 2.1 %collective-permute-done.9 = f32[16,1024]{1,0:T(8,128)S(1)} collective-permute-done((f32[16,1024]{1,0:T(8,128)S(1)}, f32[16,1024]{1,0:T(8,128)S(1)}, u32[]{:S(2)}, u32[]{:S(2)}) %collective-permute-start.9) | collective-permute-done | bytes 65568 | tf_op jit(solution)/shard_map/ppermute | solution.py:17
  25.5 0.8 %collective-permute-start.13 = (f32[4,16,1024]{2,1,0:T(8,128)S(1)}, f32[4,16,1024]{2,1,0:T(8,128)S(1)}, u32[]{:S(2)}, u32[]{:S(2)}) collective-permute-start(f32[4,16,1024]{2,1,0:T(8,128)S(1)} %get-tuple-element.109), channel_id=1, source_target_pairs={{0,16},{4,20},{8,24},{12,28},{16,0},{20,4},{24,8},{28,12},{32,48},... | collective-permute-start | bytes 786440 | tf_op jit(solution)/shard_map/ppermute | solution.py:17
  26.3 1.5 %collective-permute-done.8 = f32[16,1024]{1,0:T(8,128)S(1)} collective-permute-done((f32[16,1024]{1,0:T(8,128)S(1)}, f32[16,1024]{1,0:T(8,128)S(1)}, u32[]{:S(2)}, u32[]{:S(2)}) %collective-permute-start.8) | collective-permute-done | bytes 65568 | tf_op jit(solution)/shard_map/ppermute | solution.py:17
  27.9 1.9 %collective-permute-start.12 = (f32[2,16,1024]{2,1,0:T(8,128)S(1)}, f32[2,16,1024]{2,1,0:T(8,128)S(1)}, u32[]{:S(2)}, u32[]{:S(2)}) collective-permute-start(f32[2,16,1024]{2,1,0:T(8,128)S(1)} %pad_maximum_fusion.6), channel_id=1, source_target_pairs={{0,24},{4,28},{8,16},{12,20},{16,8},{20,12},{24,0},{28,4},{32,56},... | collective-permute-start | bytes 393224 | tf_op jit(solution)/shard_map/ppermute | solution.py:17
  29.7 0.8 %collective-permute-start.11 = (f32[2,16,1024]{2,1,0:T(8,128)S(1)}, f32[2,16,1024]{2,1,0:T(8,128)S(1)}, u32[]{:S(2)}, u32[]{:S(2)}) collective-permute-start(f32[2,16,1024]{2,1,0:T(8,128)S(1)} %pad_maximum_fusion.6), channel_id=1, source_target_pairs={{0,16},{4,20},{8,24},{12,28},{16,0},{20,4},{24,8},{28,12},{32,48},... | collective-permute-start | bytes 393224 | tf_op jit(solution)/shard_map/ppermute | solution.py:17
  30.6 1.5 %collective-permute-start.10 = (f32[2,16,1024]{2,1,0:T(8,128)S(1)}, f32[2,16,1024]{2,1,0:T(8,128)S(1)}, u32[]{:S(2)}, u32[]{:S(2)}) collective-permute-start(f32[2,16,1024]{2,1,0:T(8,128)S(1)} %pad_maximum_fusion.6), channel_id=1, source_target_pairs={{0,8},{4,12},{8,0},{12,4},{16,24},{20,28},{24,16},{28,20},{32,40},... | collective-permute-start | bytes 393224 | tf_op jit(solution)/shard_map/ppermute | solution.py:17
  32.0 2.4 %shard_map.98 = (bf16[256,1024]{1,0:T(8,128)(2,1)S(1)}, f32[1024,128]{1,0:T(8,128)S(1)}, f32[1024,128]{1,0:T(8,128)S(1)}) custom-call(f32[1024,128]{1,0:T(8,128)S(1)} %get-tuple-element.98.last_b, f32[1024,128]{1,0:T(8,128)S(1)} %get-tuple-element.99.last_c, bf16[1024,1024]{1,0:T(8,128)(2,1)S(1)} %copy-done.1, bf16[1024,128]{1,0:T(8,128)(2,1)S(1)} %copy-done.3, ...), custom_call_target="tpu_custom_call" | custom-call | flops 20000000000 | bytes 1048576 | tf_op jit(solution)/shard_map/pallas_call | solution.py:233
  34.4 2.8 %shard_map.99 = (bf16[512,768]{1,0:T(8,128)(2,1)S(1)}, f32[1024,128]{1,0:T(8,128)S(1)}, f32[1024,128]{1,0:T(8,128)S(1)}) custom-call(f32[1024,128]{1,0:T(8,128)S(1)} %get-tuple-element.104.last_b, f32[1024,128]{1,0:T(8,128)S(1)} %get-tuple-element.105.last_c, bf16[1024,1024]{1,0:T(8,128)(2,1)S(1)} %copy-done.1, bf16[1024,128]{1,0:T(8,128)(2,1)S(1)} %copy-done.3, ...), custom_call_target="tpu_custom_call" | custom-call | flops 20000000000 | bytes 1048576 | tf_op jit(solution)/shard_map/pallas_call | solution.py:233
  37.8 0.5 collective-permute-done.10
  38.7 2.6 %collective-permute-done.14.other_ref = f32[4,64,1024]{2,1,0:T(8,128)S(1)} collective-permute-done((f32[4,64,1024]{2,1,0:T(8,128)S(1)}, f32[4,64,1024]{2,1,0:T(8,128)S(1)}, u32[]{:S(2)}, u32[]{:S(2)}) %collective-permute-start.14) | collective-permute-done | bytes 1048608 | tf_op jit(solution)/shard_map/ppermute | solution.py:17
  41.3 1.1 %shard_map.100 = (f32[256,128]{1,0:T(8,128)S(1)}, f32[256,128]{1,0:T(8,128)S(1)}, bf16[640,1024]{1,0:T(8,128)(2,1)S(1)}, bf16[128,1024]{1,0:T(8,128)(2,1)S(1)}) custom-call(f32[4,64,1024]{2,1,0:T(8,128)S(1)} %collective-permute-done.1.rest_ref, f32[4,64,1024]{2,1,0:T(8,128)S(1)} %pad_maximum_fusion.own_ref, ...), custom_call_target="tpu_custom_call" | custom-call | flops 1610612736 | bytes 1048576 | tf_op jit(solution)/shard_map/pallas_call | solution.py:261
  42.4 3.1 %collective-permute-start.15 = (f32[256,128]{1,0:T(8,128)S(1)}, f32[256,128]{1,0:T(8,128)S(1)}, u32[]{:S(2)}, u32[]{:S(2)}) collective-permute-start(f32[256,128]{1,0:T(8,128)S(1)} %get-tuple-element.125), channel_id=1, source_target_pairs={{0,3},{1,2},{2,1},{3,0},{4,7},{5,6},{6,5},{7,4},{8,11},{9,10},{10,... | collective-permute-start | bytes 393224 | tf_op jit(solution)/shard_map/ppermute | solution.py:17
  45.6 1.8 %shard_map.102 = (f32[2,256,128]{2,1,0:T(8,128)S(1)}, f32[2,256,128]{2,1,0:T(8,128)S(1)}, f32[2,256,128]{2,1,0:T(8,128)S(1)}) custom-call(f32[1024,128]{1,0:T(8,128)S(1)} %get-tuple-element.117.gb_ref, f32[1024,128]{1,0:T(8,128)S(1)} %get-tuple-element.118.gc_ref, bf16[1024,1024]{1,0:T(8,128)(2,1)S(1)} %copy-done.1, bf16[1024,1024]{1,0:T(8,128)(2,1)S(1)} %copy-done.2, ...), custom_call_target="tpu_custom_call" | custom-call | flops 1610612736 | bytes 1048576 | tf_op jit(solution)/shard_map/pallas_call | solution.py:267
  47.4 3.3 %collective-permute-done.17 = f32[256,128]{1,0:T(8,128)S(1)} collective-permute-done((f32[256,128]{1,0:T(8,128)S(1)}, f32[256,128]{1,0:T(8,128)S(1)}, u32[]{:S(2)}, u32[]{:S(2)}) %collective-permute-start.17) | collective-permute-done | bytes 131104 | tf_op jit(solution)/shard_map/ppermute | solution.py:17
  51.5 6.8 %shard_map.101 = (bf16[1024,1024]{1,0:T(8,128)(2,1)}, bf16[1024,1024]{1,0:T(8,128)(2,1)}) custom-call(bf16[256,256]{1,0:T(8,128)(2,1)S(1)} %get-tuple-element.94.mix_first, bf16[512,768]{1,0:T(8,128)(2,1)S(1)} %get-tuple-element.106.mix_middle, bf16[256,1024]{1,0:T(8,128)(2,1)S(1)} %get-tuple-element.107.mix_last, bf16[1024,1024]{1,0:T(8,128)(2,1)S(1)} %copy-done.1, ...), custom_call_target="tpu_custom_call" | custom-call | flops 3758096384 | bytes 1048576 | tf_op jit(solution)/shard_map/pallas_call | solution.py:276
  58.3 0.9 %collective-permute-done.18.part3 = f32[2,256,128]{2,1,0:T(8,128)S(1)} collective-permute-done((f32[2,256,128]{2,1,0:T(8,128)S(1)}, f32[2,256,128]{2,1,0:T(8,128)S(1)}, u32[]{:S(2)}, u32[]{:S(2)}) %collective-permute-start.18) | collective-permute-done | bytes 262176 | tf_op jit(solution)/shard_map/ppermute | solution.py:17
  59.2 0.7 %shard_map.103 = (f32[256,128]{1,0:T(8,128)}, f32[256,128]{1,0:T(8,128)}) custom-call(f32[2,256,128]{2,1,0:T(8,128)S(1)} %get-tuple-element.123.part0, f32[2,256,128]{2,1,0:T(8,128)S(1)} %collective-permute-done.16.part1, f32[2,256,128]{2,1,0:T(8,128)S(1)} %collective-permute-done.18.part3), custom_call_target="tpu_custom_call" | custom-call | flops 131072 | bytes 1048576 | tf_op jit(solution)/shard_map/pallas_call | solution.py:283
  (47 shorter events, 3.4 us)
Async XLA Ops:
  0.6 0.7 %copy-start = (f32[16,18]{1,0:T(8,128)S(1)}, f32[16,18]{1,0:T(8,128)}, u32[]{:S(2)}) copy-start(f32[16,18]{1,0:T(8,128)} %param.14) | copy-start | bytes 3460
  0.6 1.2 %copy-start.4 = (bf16[1024,128]{1,0:T(8,128)(2,1)S(1)}, bf16[1024,128]{1,0:T(8,128)(2,1)}, u32[]{:S(2)}) copy-start(bf16[1024,128]{1,0:T(8,128)(2,1)} %c_ref.1) | copy-start | bytes 786436
  0.7 1.2 %copy-start.3 = (bf16[1024,128]{1,0:T(8,128)(2,1)S(1)}, bf16[1024,128]{1,0:T(8,128)(2,1)}, u32[]{:S(2)}) copy-start(bf16[1024,128]{1,0:T(8,128)(2,1)} %b_ref.1) | copy-start | bytes 786436
  0.7 0.7 %copy-start.5 = (s32[1024]{0:T(1024)S(1)}, s32[1024]{0:T(1024)}, u32[]{:S(2)}) copy-start(s32[1024]{0:T(1024)} %param.15) | copy-start | bytes 12292
  0.7 1.8 %copy-start.2 = (bf16[1024,1024]{1,0:T(8,128)(2,1)S(1)}, bf16[1024,1024]{1,0:T(8,128)(2,1)}, u32[]{:S(2)}) copy-start(bf16[1024,1024]{1,0:T(8,128)(2,1)} %d_ref.9) | copy-start | bytes 6291460
  1.4 1.8 %copy-start.1 = (bf16[1024,1024]{1,0:T(8,128)(2,1)S(1)}, bf16[1024,1024]{1,0:T(8,128)(2,1)}, u32[]{:S(2)}) copy-start(bf16[1024,1024]{1,0:T(8,128)(2,1)} %x_ref.9) | copy-start | bytes 6291460
  4.2 2.0 %collective-permute-start = (f32[2,64,1024]{2,1,0:T(8,128)S(1)}, f32[2,64,1024]{2,1,0:T(8,128)S(1)}, u32[]{:S(2)}, u32[]{:S(2)}) collective-permute-start(f32[2,64,1024]{2,1,0:T(8,128)S(1)} %get-tuple-element.87), channel_id=1, source_target_pairs={{0,4},{4,0},{8,12},{12,8},{16,20},{20,16},{24,28},{28,24},{32,36},... | collective-permute-start | bytes 1572872 | tf_op jit(solution)/shard_map/ppermute | solution.py:17
  6.2 5.3 %collective-permute-start.1 = (f32[4,64,1024]{2,1,0:T(8,128)S(1)}, f32[4,64,1024]{2,1,0:T(8,128)S(1)}, u32[]{:S(2)}, u32[]{:S(2)}) collective-permute-start(f32[4,64,1024]{2,1,0:T(8,128)S(1)} %get-tuple-element.92), channel_id=1, source_target_pairs={{0,4},{4,0},{8,12},{12,8},{16,20},{20,16},{24,28},{28,24},{32,36},... | collective-permute-start | bytes 3145736 | tf_op jit(solution)/shard_map/ppermute | solution.py:17
  6.5 9.6 %collective-permute-start.2 = (f32[2,16,1024]{2,1,0:T(8,128)S(1)}, f32[2,16,1024]{2,1,0:T(8,128)S(1)}, u32[]{:S(2)}, u32[]{:S(2)}) collective-permute-start(f32[2,16,1024]{2,1,0:T(8,128)S(1)} %get-tuple-element.136), channel_id=1, source_target_pairs={{0,16},{4,20},{8,24},{12,28},{16,0},{20,4},{24,8},{28,12},{32,48},... | collective-permute-start | bytes 393224 | tf_op jit(solution)/shard_map/ppermute | solution.py:17
  10.5 8.2 %collective-permute-start.3 = (f32[2,16,1024]{2,1,0:T(8,128)S(1)}, f32[2,16,1024]{2,1,0:T(8,128)S(1)}, u32[]{:S(2)}, u32[]{:S(2)}) collective-permute-start(f32[2,16,1024]{2,1,0:T(8,128)S(1)} %get-tuple-element.137), channel_id=1, source_target_pairs={{0,8},{4,12},{8,0},{12,4},{16,24},{20,28},{24,16},{28,20},{32,40},... | collective-permute-start | bytes 393224 | tf_op jit(solution)/shard_map/ppermute | solution.py:17
  11.5 7.6 %collective-permute-start.4 = (f32[2,16,1024]{2,1,0:T(8,128)S(1)}, f32[2,16,1024]{2,1,0:T(8,128)S(1)}, u32[]{:S(2)}, u32[]{:S(2)}) collective-permute-start(f32[2,16,1024]{2,1,0:T(8,128)S(1)} %get-tuple-element.138), channel_id=1, source_target_pairs={{0,24},{4,28},{8,16},{12,20},{16,8},{20,12},{24,0},{28,4},{32,56},... | collective-permute-start | bytes 393224 | tf_op jit(solution)/shard_map/ppermute | solution.py:17
  11.7 16.2 %collective-permute-start.5 = (f32[4,16,1024]{2,1,0:T(8,128)S(1)}, f32[4,16,1024]{2,1,0:T(8,128)S(1)}, u32[]{:S(2)}, u32[]{:S(2)}) collective-permute-start(f32[4,16,1024]{2,1,0:T(8,128)S(1)} %get-tuple-element.134), channel_id=1, source_target_pairs={{0,8},{4,12},{8,0},{12,4},{16,24},{20,28},{24,16},{28,20},{32,40},... | collective-permute-start | bytes 786440 | tf_op jit(solution)/shard_map/ppermute | solution.py:17
  12.9 15.0 %collective-permute-start.6 = (f32[4,16,1024]{2,1,0:T(8,128)S(1)}, f32[4,16,1024]{2,1,0:T(8,128)S(1)}, u32[]{:S(2)}, u32[]{:S(2)}) collective-permute-start(f32[4,16,1024]{2,1,0:T(8,128)S(1)} %get-tuple-element.109), channel_id=1, source_target_pairs={{0,24},{4,28},{8,16},{12,20},{16,8},{20,12},{24,0},{28,4},{32,56},... | collective-permute-start | bytes 786440 | tf_op jit(solution)/shard_map/ppermute | solution.py:17
  19.2 6.3 %collective-permute-start.9 = (f32[16,1024]{1,0:T(8,128)S(1)}, f32[16,1024]{1,0:T(8,128)S(1)}, u32[]{:S(2)}, u32[]{:S(2)}) collective-permute-start(f32[16,1024]{1,0:T(8,128)S(1)} %get-tuple-element.143), channel_id=1, source_target_pairs={{0,96},{4,100},{8,104},{12,108},{16,112},{20,116},{24,120},{28,124... | collective-permute-start | bytes 196616 | tf_op jit(solution)/shard_map/ppermute | solution.py:17
  22.0 5.8 %collective-permute-start.8 = (f32[16,1024]{1,0:T(8,128)S(1)}, f32[16,1024]{1,0:T(8,128)S(1)}, u32[]{:S(2)}, u32[]{:S(2)}) collective-permute-start(f32[16,1024]{1,0:T(8,128)S(1)} %get-tuple-element.143), channel_id=1, source_target_pairs={{0,64},{4,68},{8,72},{12,76},{16,80},{20,84},{24,88},{28,92},{32,9... | collective-permute-start | bytes 196616 | tf_op jit(solution)/shard_map/ppermute | solution.py:17
  22.8 5.0 %collective-permute-start.7 = (f32[16,1024]{1,0:T(8,128)S(1)}, f32[16,1024]{1,0:T(8,128)S(1)}, u32[]{:S(2)}, u32[]{:S(2)}) collective-permute-start(f32[16,1024]{1,0:T(8,128)S(1)} %get-tuple-element.144), channel_id=1, source_target_pairs={{0,32},{4,36},{8,40},{12,44},{16,48},{20,52},{24,56},{28,60},{32,0... | collective-permute-start | bytes 196616 | tf_op jit(solution)/shard_map/ppermute | solution.py:17
  25.5 11.8 %collective-permute-start.13 = (f32[4,16,1024]{2,1,0:T(8,128)S(1)}, f32[4,16,1024]{2,1,0:T(8,128)S(1)}, u32[]{:S(2)}, u32[]{:S(2)}) collective-permute-start(f32[4,16,1024]{2,1,0:T(8,128)S(1)} %get-tuple-element.109), channel_id=1, source_target_pairs={{0,16},{4,20},{8,24},{12,28},{16,0},{20,4},{24,8},{28,12},{32,48},... | collective-permute-start | bytes 786440 | tf_op jit(solution)/shard_map/ppermute | solution.py:17
  27.9 9.9 %collective-permute-start.12 = (f32[2,16,1024]{2,1,0:T(8,128)S(1)}, f32[2,16,1024]{2,1,0:T(8,128)S(1)}, u32[]{:S(2)}, u32[]{:S(2)}) collective-permute-start(f32[2,16,1024]{2,1,0:T(8,128)S(1)} %pad_maximum_fusion.6), channel_id=1, source_target_pairs={{0,24},{4,28},{8,16},{12,20},{16,8},{20,12},{24,0},{28,4},{32,56},... | collective-permute-start | bytes 393224 | tf_op jit(solution)/shard_map/ppermute | solution.py:17
  29.7 8.0 %collective-permute-start.11 = (f32[2,16,1024]{2,1,0:T(8,128)S(1)}, f32[2,16,1024]{2,1,0:T(8,128)S(1)}, u32[]{:S(2)}, u32[]{:S(2)}) collective-permute-start(f32[2,16,1024]{2,1,0:T(8,128)S(1)} %pad_maximum_fusion.6), channel_id=1, source_target_pairs={{0,16},{4,20},{8,24},{12,28},{16,0},{20,4},{24,8},{28,12},{32,48},... | collective-permute-start | bytes 393224 | tf_op jit(solution)/shard_map/ppermute | solution.py:17
  30.6 7.7 %collective-permute-start.10 = (f32[2,16,1024]{2,1,0:T(8,128)S(1)}, f32[2,16,1024]{2,1,0:T(8,128)S(1)}, u32[]{:S(2)}, u32[]{:S(2)}) collective-permute-start(f32[2,16,1024]{2,1,0:T(8,128)S(1)} %pad_maximum_fusion.6), channel_id=1, source_target_pairs={{0,8},{4,12},{8,0},{12,4},{16,24},{20,28},{24,16},{28,20},{32,40},... | collective-permute-start | bytes 393224 | tf_op jit(solution)/shard_map/ppermute | solution.py:17
  38.4 2.9 %collective-permute-start.14 = (f32[4,64,1024]{2,1,0:T(8,128)S(1)}, f32[4,64,1024]{2,1,0:T(8,128)S(1)}, u32[]{:S(2)}, u32[]{:S(2)}) collective-permute-start(f32[4,64,1024]{2,1,0:T(8,128)S(1)} %pad_maximum_fusion.own_ref), channel_id=1, source_target_pairs={{0,4},{4,0},{8,12},{12,8},{16,20},{20,16},{24,28},{28,24},{32,36},... | collective-permute-start | bytes 3145736 | tf_op jit(solution)/shard_map/ppermute | solution.py:17
  42.4 8.8 %collective-permute-start.15 = (f32[256,128]{1,0:T(8,128)S(1)}, f32[256,128]{1,0:T(8,128)S(1)}, u32[]{:S(2)}, u32[]{:S(2)}) collective-permute-start(f32[256,128]{1,0:T(8,128)S(1)} %get-tuple-element.125), channel_id=1, source_target_pairs={{0,3},{1,2},{2,1},{3,0},{4,7},{5,6},{6,5},{7,4},{8,11},{9,10},{10,... | collective-permute-start | bytes 393224 | tf_op jit(solution)/shard_map/ppermute | solution.py:17
  45.5 5.3 %collective-permute-start.17 = (f32[256,128]{1,0:T(8,128)S(1)}, f32[256,128]{1,0:T(8,128)S(1)}, u32[]{:S(2)}, u32[]{:S(2)}) collective-permute-start(f32[256,128]{1,0:T(8,128)S(1)} %get-tuple-element.127), channel_id=1, source_target_pairs={{0,1},{1,0},{2,3},{3,2},{4,5},{5,4},{6,7},{7,6},{8,9},{9,8},{10,11... | collective-permute-start | bytes 393224 | tf_op jit(solution)/shard_map/ppermute | solution.py:17
  50.7 8.5 %collective-permute-start.18 = (f32[2,256,128]{2,1,0:T(8,128)S(1)}, f32[2,256,128]{2,1,0:T(8,128)S(1)}, u32[]{:S(2)}, u32[]{:S(2)}) collective-permute-start(f32[2,256,128]{2,1,0:T(8,128)S(1)} %fusion.5), channel_id=1, source_target_pairs={{0,3},{1,2},{2,1},{3,0},{4,7},{5,6},{6,5},{7,4},{8,11},{9,10},{10,... | collective-permute-start | bytes 786440 | tf_op jit(solution)/shard_map/ppermute | solution.py:17
  51.2 8.0 %collective-permute-start.16 = (f32[2,256,128]{2,1,0:T(8,128)S(1)}, f32[2,256,128]{2,1,0:T(8,128)S(1)}, u32[]{:S(2)}, u32[]{:S(2)}) collective-permute-start(f32[2,256,128]{2,1,0:T(8,128)S(1)} %fusion.6), channel_id=1, source_target_pairs={{0,1},{1,0},{2,3},{3,2},{4,5},{5,4},{6,7},{7,6},{8,9},{9,8},{10,11... | collective-permute-start | bytes 786440 | tf_op jit(solution)/shard_map/ppermute | solution.py:17
